TPU v7x, 32 devices: a whole 2x2x4 slice. The times are simulated.
32 devices in a mesh: az: 8 (over z, core), el: 4 (over y, x).
Axes of the slice: x: 2, y: 2, z: 4, core: 2. Of those that a mesh axis runs over, the one named last changes fastest.
Arguments:
- points: bfloat16 [8, 2048, 256], P('el', 'az'), may hold values from -6 to 6
- skip: bfloat16 [8, 2048, 256], P('el', 'az'), may hold values from -6 to 6
- tokens: bfloat16 [8, 4, 128, 256], P('az', 'el')
- send_slots: int32 [8, 4, 5, 4, 16], P('az', 'el'), may hold values from 0 to 127
- recv_idx: int32 [8, 2048, 16], P('el', 'az'), may hold values from 0 to 319, as said below
- w_query: bfloat16 [256, 256], replicated, may hold values from -0.375 to 0.375
- w_key: bfloat16 [256, 256], replicated, may hold values from -0.375 to 0.375
- w_value: bfloat16 [256, 256], replicated, may hold values from -0.375 to 0.375
- w_out: bfloat16 [256, 256], replicated, may hold values from -0.375 to 0.375
- w_hid: bfloat16 [256, 1024], replicated, may hold values from -0.375 to 0.375
- w_skip: bfloat16 [256, 1024], replicated, may hold values from -0.375 to 0.375
- w_down: bfloat16 [1024, 256], replicated, may hold values from -0.1875 to 0.1875
- w_conv: bfloat16 [9, 256, 256], replicated, may hold values from -0.125 to 0.125
Outputs:
- refined: bfloat16 [8, 2048, 256], P('el', 'az')
Inputs may be any that keep to these rules, and one draw needn't show every extreme that they name: send_slots[o, e, j, f, k] is the row of owner device (o, e)'s tokens sent as slot k to the device of azimuth block (o + j - 2) mod 8 and elevation block f. `recv_idx`: an entry (j * 4 + e) * 16 + k names slot k of what the device of elevation block e, 2 - j azimuth blocks away, sends to the point's device. For each requesting device and each such owner only the slots below a live count of 1 to 16 are named; each requesting device has its own block's slots from itself all live.
All inputs are finite; a program needn't handle non-finite values.
Results may differ from a plain program's by a relative error of at most 0.01.
Values may be sent and summed in bfloat16 or wider, within the bound.
No kernel may reach another device: no remote copies, remote signals or barrier semaphores. Data moves between devices by JAX's collectives and lax.ppermute only.
A program may use at most 64 MiB of HBM per device.

v0:
```python
import math

import jax
import jax.numpy as jnp
from jax import lax
from jax.sharding import PartitionSpec as P

HEADS = 8
REACH = 2


def passed_along(x, axis, by):
    length = lax.axis_size(axis)
    return lax.ppermute(x, axis, [(i, (i + by) % length) for i in range(length)])


def with_halo(cells, sides, width, closed):
    for axis, dim in sides:
        count = lax.axis_size(axis)
        ends = count if closed else count - 1
        head = lax.slice_in_dim(cells, 0, width, axis=dim)
        tail = lax.slice_in_dim(cells, cells.shape[dim] - width, cells.shape[dim], axis=dim)
        cells = jnp.concatenate(
            [
                lax.ppermute(tail, axis, [(i, (i + 1) % count) for i in range(ends)]),
                cells,
                lax.ppermute(head, axis, [((i + 1) % count, i) for i in range(ends)]),
            ],
            axis=dim,
        )
    return cells


def normalize(features):
    widened = features.astype(jnp.float32)
    return widened * lax.rsqrt(jnp.mean(widened * widened, axis=-1, keepdims=True) + 1e-06)


def project_tokens(token_block, w_key, w_value):
    key_rows = jnp.dot(token_block, w_key, preferred_element_type=jnp.float32).astype(jnp.bfloat16)
    normed_tokens = normalize(token_block).astype(jnp.bfloat16)
    value_rows = jnp.dot(normed_tokens, w_value, preferred_element_type=jnp.float32).astype(
        jnp.bfloat16
    )
    return (key_rows, value_rows)


def per_device(
    points,
    skip,
    tokens,
    send_slots,
    recv_idx,
    w_query,
    w_key,
    w_value,
    w_out,
    w_hid,
    w_skip,
    w_down,
    w_conv,
):
    point_rows, point_cols, feature_width = points.shape
    point_count = point_rows * point_cols
    head_width = feature_width // HEADS
    neighbours = recv_idx.shape[2]
    own_tokens = tokens[0, 0]
    slot_table = send_slots[0, 0]
    offset_count, group_count, capacity = slot_table.shape
    row_width = own_tokens.shape[1]
    payload = jnp.take(own_tokens, slot_table.reshape(-1), axis=0).reshape(
        offset_count, group_count, capacity, row_width
    )
    swapped = lax.all_to_all(payload, "el", split_axis=1, concat_axis=1, tiled=True)
    arrived = []
    for offset in range(offset_count):
        if offset == REACH:
            arrived.append(swapped[offset])
        else:
            arrived.append(passed_along(swapped[offset], "az", offset - REACH))
    received = jnp.stack(arrived)
    table_rows = offset_count * group_count * capacity
    received = received.reshape(table_rows, row_width)
    key_rows, value_rows = project_tokens(received, w_key, w_value)
    key_heads = key_rows.reshape(table_rows, HEADS, head_width)
    value_heads = value_rows.reshape(table_rows, HEADS, head_width)
    flat_points = points.reshape(point_count, feature_width)
    query = jnp.dot(flat_points, w_query, preferred_element_type=jnp.float32).astype(jnp.bfloat16)
    block_size = min(512, point_count)
    block_count = point_count // block_size
    scale_factor = 1.0 / math.sqrt(head_width)
    slot_iota = jnp.arange(table_rows, dtype=jnp.int32)

    def attend(inputs):
        query_block, index_block = inputs
        one_hot = (index_block[:, :, None] == slot_iota[None, None, :]).astype(jnp.bfloat16)
        full_scores = jnp.einsum(
            "bhd,thd->bht", query_block, key_heads, preferred_element_type=jnp.float32
        )
        high_part = full_scores.astype(jnp.bfloat16)
        rest_part = full_scores - high_part.astype(jnp.float32)
        middle_part = rest_part.astype(jnp.bfloat16)
        low_part = (rest_part - middle_part.astype(jnp.float32)).astype(jnp.bfloat16)
        picked = jnp.einsum("bnt,bht->bhn", one_hot, high_part, preferred_element_type=jnp.float32)
        picked = picked + jnp.einsum(
            "bnt,bht->bhn", one_hot, middle_part, preferred_element_type=jnp.float32
        )
        picked = picked + jnp.einsum(
            "bnt,bht->bhn", one_hot, low_part, preferred_element_type=jnp.float32
        )
        scores = picked * scale_factor
        shifted = jnp.exp(scores - jnp.max(scores, axis=-1, keepdims=True))
        weights = (shifted / jnp.sum(shifted, axis=-1, keepdims=True)).astype(jnp.bfloat16)
        spread = jnp.einsum("bhn,bnt->bht", weights, one_hot, preferred_element_type=jnp.float32)
        spread_high = spread.astype(jnp.bfloat16)
        spread_low = (spread - spread_high.astype(jnp.float32)).astype(jnp.bfloat16)
        combined = jnp.einsum(
            "bht,thd->bhd", spread_high, value_heads, preferred_element_type=jnp.float32
        )
        combined = combined + jnp.einsum(
            "bht,thd->bhd", spread_low, value_heads, preferred_element_type=jnp.float32
        )
        return combined.reshape(block_size, feature_width).astype(jnp.bfloat16)

    attended = lax.map(
        attend,
        (
            query.reshape(block_count, block_size, HEADS, head_width),
            recv_idx.reshape(block_count, block_size, neighbours),
        ),
    )
    attended = attended.reshape(point_count, feature_width)
    residual_sum = flat_points.astype(jnp.float32) + jnp.dot(
        attended, w_out, preferred_element_type=jnp.float32
    )
    normed = normalize(residual_sum).astype(jnp.bfloat16)
    flat_skip = skip.reshape(point_count, feature_width)
    hidden_pre = jnp.dot(normed, w_hid, preferred_element_type=jnp.float32) + jnp.dot(
        flat_skip, w_skip, preferred_element_type=jnp.float32
    )
    inner = jax.nn.gelu(hidden_pre, approximate=True).astype(jnp.bfloat16)
    joined = residual_sum + jnp.dot(inner, w_down, preferred_element_type=jnp.float32)
    conv_input = (
        normalize(joined).astype(jnp.bfloat16).reshape(point_rows, point_cols, feature_width)
    )
    widened = with_halo(conv_input, (("az", 1),), 1, True)
    padded = with_halo(widened, (("el", 0),), 1, False)
    refined = joined
    for tap_index in range(9):
        row_step = tap_index // 3
        col_step = tap_index % 3
        window = padded[row_step : row_step + point_rows, col_step : col_step + point_cols].reshape(
            point_count, feature_width
        )
        refined = refined + jnp.dot(window, w_conv[tap_index], preferred_element_type=jnp.float32)
    return refined.astype(jnp.bfloat16).reshape(point_rows, point_cols, feature_width)


def solution(mesh):
    return jax.shard_map(
        per_device,
        mesh=mesh,
        in_specs=(
            P("el", "az", None),
            P("el", "az", None),
            P("az", "el", None, None),
            P("az", "el", None, None, None),
            P("el", "az", None),
            P(),
            P(),
            P(),
            P(),
            P(),
            P(),
            P(),
            P(),
        ),
        out_specs=P("el", "az", None),
        check_vma=False,
    )
```

profile of v0, /device:TPU:2, one launch (start us, length us, event | category | flops | bytes accessed | tf_op | source)
XLA Modules:
  0.0 104.5 jit_solution(5186278834871376806)
XLA Ops:
  0.0 0.9 reshape_squeeze.6
  0.9 0.7 compare_and_fusion
  1.7 2.5 %gather_fusion = bf16[320,256]{1,0:T(8,128)(2,1)S(1)} fusion(bf16[128,256]{1,0:T(8,128)(2,1)} %bitcast.120, s32[1024]{0:T(1024)S(1)} %pad_clamp_fusion), kind=kCustom, calls=%fused_computation | custom fusion | bytes 328960 | tf_op jit(solution)/shard_map/jit(_take)/gather | solution.py:71
  4.3 8.1 %all_to_all.5 = bf16[5,4,16,256]{3,2,0,1:T(8,128)(2,1)S(1)} all-to-all(bf16[5,4,16,256]{3,2,0,1:T(8,128)(2,1)S(1)} %copy_select_fusion), channel_id=1, replica_groups=mesh['az'=8,'el'=4] {'el'}, dimensions={1} | all-to-all | bytes 327680 | tf_op jit(solution)/shard_map/all_to_all | solution.py:74
  12.4 3.7 %collective-permute-start = (bf16[4,16,256]{2,1,0:T(8,128)(2,1)S(1)}, bf16[4,16,256]{2,1,0:T(8,128)(2,1)S(1)}, u32[]{:S(2)}, u32[]{:S(2)}) collective-permute-start(bf16[4,16,256]{2,1,0:T(8,128)(2,1)S(1)} %get-tuple-element.44), channel_id=1, source_target_pairs={{0,24},{4,28},{8,0},{12,4},{16,8},{20,12},{24,16},{28,20},{1,25},{... | collective-permute-start | bytes 98312 | tf_op jit(solution)/shard_map/ppermute | solution.py:14
  16.1 1.0 convolution_convert_fusion
  17.1 0.8 copy.61
  17.9 0.5 collective-permute-start.2
  18.4 1.3 %collective-permute-done.1 = bf16[4,16,256]{2,1,0:T(8,128)(2,1)S(1)} collective-permute-done((bf16[4,16,256]{2,1,0:T(8,128)(2,1)S(1)}, bf16[4,16,256]{2,1,0:T(8,128)(2,1)S(1)}, u32[]{:S(2)}, u32[]{:S(2)}) %collective-permute-start.1) | collective-permute-done | bytes 32800 | tf_op jit(solution)/shard_map/ppermute | solution.py:14
  19.7 3.4 %collective-permute-done.2 = bf16[4,16,256]{2,1,0:T(8,128)(2,1)S(1)} collective-permute-done((bf16[4,16,256]{2,1,0:T(8,128)(2,1)S(1)}, bf16[4,16,256]{2,1,0:T(8,128)(2,1)S(1)}, u32[]{:S(2)}, u32[]{:S(2)}) %collective-permute-start.2) | collective-permute-done | bytes 32800 | tf_op jit(solution)/shard_map/ppermute | solution.py:14
  23.1 1.1 %collective-permute-done.3 = bf16[4,16,256]{2,1,0:T(8,128)(2,1)S(1)} collective-permute-done((bf16[4,16,256]{2,1,0:T(8,128)(2,1)S(1)}, bf16[4,16,256]{2,1,0:T(8,128)(2,1)S(1)}, u32[]{:S(2)}, u32[]{:S(2)}) %collective-permute-start.3) | collective-permute-done | bytes 32800 | tf_op jit(solution)/shard_map/ppermute | solution.py:14
  24.3 0.2 convolution_convert_fusion.1
  24.5 0.2 copy.53
  24.6 4.3 %fusion.9 = (bf16[512,8,320]{0,2,1:T(8,128)(2,1)}, bf16[512,8,320]{0,2,1:T(8,128)(2,1)}, bf16[8,320,512]{2,1,0:T(8,128)(2,1)S(1)}) fusion(bf16[320,8,32]{0,2,1:T(8,128)(2,1)S(1)} %bitcast.142, bf16[512,8,32]{0,2,1:T(8,128)(2,1)} %bitcast.133), kind=kOutput, calls=%fused_computation.15 | convolution fusion | flops 94371840 | bytes 8290304 | tf_op jit(solution)/shard_map/while/body/eval_jaxpr/bhd,thd->bht/dot_general | solution.py:97
  29.0 4.9 %copy.58 = bf16[512,8,320]{2,1,0:T(8,128)(2,1)} copy(bf16[512,8,320]{0,2,1:T(8,128)(2,1)} %get-tuple-element.18) | data formatting | bytes 5242880 | tf_op jit(solution)/shard_map/while/body/eval_jaxpr/convert_element_type | solution.py:103
  33.9 4.9 %copy.57 = bf16[512,8,320]{2,1,0:T(8,128)(2,1)} copy(bf16[512,8,320]{0,2,1:T(8,128)(2,1)} %get-tuple-element.17) | data formatting | bytes 5242880 | tf_op jit(solution)/shard_map/while/body/eval_jaxpr/convert_element_type | solution.py:102
  38.8 6.2 %fusion.2 = f32[512,8,16]{2,1,0:T(8,128)} fusion(bf16[512,8,320]{2,1,0:T(8,128)(2,1)} %copy.58, s32[512,16]{1,0:T(8,128)} %bitcast.144), kind=kOutput, calls=%fused_computation.4 | convolution fusion | flops 44564480 | bytes 2916352 | tf_op jit(solution)/shard_map/while/body/eval_jaxpr/bnt,bht->bhn/dot_general | solution.py:108
  45.0 4.5 %fusion.3 = f32[512,8,16]{2,1,0:T(8,128)} fusion(bf16[512,8,320]{2,1,0:T(8,128)(2,1)S(1)} %copy-done.2, s32[512,16]{1,0:T(8,128)S(1)} %bitcast.146), kind=kOutput, calls=%fused_computation.5 | convolution fusion | flops 44564480 | bytes 2916352 | tf_op jit(solution)/shard_map/while/body/eval_jaxpr/bnt,bht->bhn/dot_general | solution.py:105
  49.5 3.5 %copy.56 = bf16[512,8,320]{2,1,0:T(8,128)(2,1)} copy(bf16[512,8,320]{0,2,1:T(8,128)(2,1)S(1)} %bitcast.121) | data formatting | bytes 5242880 | tf_op jit(solution)/shard_map/while/body/eval_jaxpr/convert_element_type | solution.py:100
  53.0 9.2 %fusion.71 = (f32[512,8]{1,0:T(8,128)S(1)}, f32[512,8,16]{2,1,0:T(8,128)S(1)}) fusion(f32[512,8,16]{2,1,0:T(8,128)} %fusion.2, f32[512,8,16]{2,1,0:T(8,128)} %fusion.3, bf16[512,8,320]{2,1,0:T(8,128)(2,1)} %copy.56, s32[512,16]{1,0:T(8,128)} %bitcast.145), kind=kOutput, calls=%fused_computation.116 | convolution fusion | flops 44892176 | bytes 3457024 | tf_op jit(solution)/shard_map/while/body/eval_jaxpr/sub | solution.py:112
  62.2 5.8 %fusion.1 = f32[512,8,320]{2,1,0:T(8,128)} fusion(s32[512,16]{1,0:T(8,128)S(1)} %bitcast.147, f32[512,8,16]{2,1,0:T(8,128)S(1)} %get-tuple-element.48, f32[512,8]{1,0:T(8,128)S(1)} %get-tuple-element.47), kind=kOutput, calls=%fused_computation.3 | convolution fusion | flops 44695552 | bytes 5554176 | tf_op jit(solution)/shard_map/while/body/eval_jaxpr/bhn,bnt->bht/dot_general | solution.py:114
  68.0 6.4 %copy.59 = f32[512,8,320]{0,2,1:T(8,128)} copy(f32[512,8,320]{2,1,0:T(8,128)} %fusion.1) | data formatting | bytes 10485760 | tf_op jit(solution)/shard_map/while/body/eval_jaxpr/bhn,bnt->bht/dot_general | solution.py:114
  74.5 0.2 convolution_convert_fusion.2
  74.7 0.2 copy.52
  74.9 4.9 %fusion.10 = f32[8,32,512]{2,1,0:T(8,128)S(1)} fusion(bf16[320,8,32]{0,2,1:T(8,128)(2,1)S(1)} %bitcast.126, f32[512,8,320]{0,2,1:T(8,128)} %copy.59), kind=kOutput, calls=%fused_computation.17 | convolution fusion | flops 89128960 | bytes 5931008 | tf_op jit(solution)/shard_map/while/body/eval_jaxpr/bht,thd->bhd/dot_general | solution.py:120
  79.8 0.6 copy-done.1
  80.5 0.6 fusion.29
  81.0 0.4 copy-done.6
  81.4 0.4 multiply_reduce_fusion.1
  81.9 0.5 fusion.38
  82.3 0.3 copy-done.3
  82.6 2.5 %multiply_reduce_fusion = (f32[512]{0:T(512)S(1)}, f32[512,256]{1,0:T(8,128)S(1)}) fusion(f32[512,256]{1,0:T(8,128)} %copy-done.3, bf16[1024,256]{1,0:T(8,128)(2,1)} %param.24, f32[512,1024]{1,0:T(8,128)S(1)} %fusion.38, bf16[512,256]{1,0:T(8,128)(2,1)S(1)} %bitcast.148, bf16[256,1024]{1,0:T(8,128)(2,1)} %param.23), kind=kOutput, calls=%fused_computation.56 | convolution fusion | flops 542506496 | bytes 4458496 | tf_op jit(solution)/shard_map/dot_general | solution.py:142
  85.1 0.1 multiply_convert_fusion
  85.3 3.5 %collective-permute-start.5 = (bf16[2,1,256]{2,1,0:T(2,128)(2,1)S(1)}, bf16[2,1,256]{2,1,0:T(2,128)(2,1)S(1)}, u32[]{:S(2)}, u32[]{:S(2)}) collective-permute-start(bf16[2,1,256]{2,1,0:T(2,128)(2,1)S(1)} %get-tuple-element.41), channel_id=1, source_target_pairs={{4,0},{8,4},{12,8},{16,12},{20,16},{24,20},{28,24},{0,28},{5,1},{9... | collective-permute-start | bytes 3080 | tf_op jit(solution)/shard_map/ppermute | solution.py:27
  88.9 1.3 %collective-permute-done.4 = bf16[2,1,256]{2,1,0:T(2,128)(2,1)S(1)} collective-permute-done((bf16[2,1,256]{2,1,0:T(2,128)(2,1)S(1)}, bf16[2,1,256]{2,1,0:T(2,128)(2,1)S(1)}, u32[]{:S(2)}, u32[]{:S(2)}) %collective-permute-start.4) | collective-permute-done | bytes 1056 | tf_op jit(solution)/shard_map/ppermute | solution.py:25
  90.3 3.4 %collective-permute-start.6 = (bf16[1,258,256]{2,1,0:T(8,128)(2,1)S(1)}, bf16[1,258,256]{2,1,0:T(8,128)(2,1)S(1)}, u32[]{:S(2)}, u32[]{:S(2)}) collective-permute-start(bf16[1,258,256]{2,1,0:T(8,128)(2,1)S(1)} %get-tuple-element.34), channel_id=1, source_target_pairs={{0,1},{1,2},{2,3},{4,5},{5,6},{6,7},{8,9},{9,10},{10,11},{12,13},{... | collective-permute-start | bytes 396296 | tf_op jit(solution)/shard_map/ppermute | solution.py:25
  93.7 2.5 %collective-permute-start.7 = (bf16[1,258,256]{2,1,0:T(8,128)(2,1)S(1)}, bf16[1,258,256]{2,1,0:T(8,128)(2,1)S(1)}, u32[]{:S(2)}, u32[]{:S(2)}) collective-permute-start(bf16[1,258,256]{2,1,0:T(8,128)(2,1)S(1)} %get-tuple-element.35), channel_id=1, source_target_pairs={{1,0},{2,1},{3,2},{5,4},{6,5},{7,6},{9,8},{10,9},{11,10},{13,12},{... | collective-permute-start | bytes 396296 | tf_op jit(solution)/shard_map/ppermute | solution.py:27
  96.2 1.1 %fusion.46 = f32[512,256]{1,0:T(8,128)S(1)} fusion(bf16[512,256]{1,0:T(8,128)(2,1)S(1)} %multiply_convert_fusion, bf16[9,256,256]{2,1,0:T(8,128)(2,1)} %param.25), kind=kOutput, calls=%fused_computation.75 | convolution fusion | flops 67108864 | bytes 917504 | tf_op jit(solution)/shard_map/dot_general | solution.py:155
  97.4 4.1 %collective-permute-done.7 = bf16[1,258,256]{2,1,0:T(8,128)(2,1)S(1)} collective-permute-done((bf16[1,258,256]{2,1,0:T(8,128)(2,1)S(1)}, bf16[1,258,256]{2,1,0:T(8,128)(2,1)S(1)}, u32[]{:S(2)}, u32[]{:S(2)}) %collective-permute-start.7) | collective-permute-done | bytes 132128 | tf_op jit(solution)/shard_map/ppermute | solution.py:27
  101.6 0.3 fusion.67
  101.9 0.2 convolution_add_fusion.6
  102.1 0.2 fusion.43
  102.3 0.2 convolution_add_fusion.5
  102.6 0.2 convolution_add_fusion.4
  102.8 0.2 fusion.27
  103.0 0.2 fusion.26
  103.3 0.2 convolution_add_fusion.1
  103.5 0.9 fusion.32
  (53 shorter events, 0.9 us)
Async XLA Ops:
  0.0 81.8 %copy-start = (bf16[256,1024]{1,0:T(8,128)(2,1)S(1)}, bf16[256,1024]{1,0:T(8,128)(2,1)}, u32[]{:S(2)}) copy-start(bf16[256,1024]{1,0:T(8,128)(2,1)} %param.22) | copy-start | bytes 1572868
  0.0 16.1 %copy-start.5 = (bf16[2,256,256]{2,1,0:T(8,128)(2,1)S(1)}, bf16[2,256,256]{2,1,0:T(8,128)(2,1)}, u32[]{:S(2)}) copy-start(bf16[2,256,256]{2,1,0:T(8,128)(2,1)} %param.13) | copy-start | bytes 786436
  0.0 16.1 %copy-start.9 = (bf16[256,256]{1,0:T(8,128)(2,1)S(1)}, bf16[256,256]{1,0:T(8,128)(2,1)}, u32[]{:S(2)}) copy-start(bf16[256,256]{1,0:T(8,128)(2,1)} %param.18) | copy-start | bytes 393220
  0.0 17.1 %copy-start.13 = (s32[2,256,16]{1,2,0:T(8,128)S(1)}, s32[2,256,16]{1,2,0:T(8,128)}, u32[]{:S(2)}) copy-start(s32[2,256,16]{1,2,0:T(8,128)} %param.17) | copy-start | bytes 98308
  0.0 24.2 %copy-start.10 = (bf16[256,256]{1,0:T(8,128)(2,1)S(1)}, bf16[256,256]{1,0:T(8,128)(2,1)}, u32[]{:S(2)}) copy-start(bf16[256,256]{1,0:T(8,128)(2,1)} %param.19) | copy-start | bytes 393220
  12.4 6.0 %collective-permute-start = (bf16[4,16,256]{2,1,0:T(8,128)(2,1)S(1)}, bf16[4,16,256]{2,1,0:T(8,128)(2,1)S(1)}, u32[]{:S(2)}, u32[]{:S(2)}) collective-permute-start(bf16[4,16,256]{2,1,0:T(8,128)(2,1)S(1)} %get-tuple-element.44), channel_id=1, source_target_pairs={{0,24},{4,28},{8,0},{12,4},{16,8},{20,12},{24,16},{28,20},{1,25},{... | collective-permute-start | bytes 98312 | tf_op jit(solution)/shard_map/ppermute | solution.py:14
  17.9 1.8 %collective-permute-start.1 = (bf16[4,16,256]{2,1,0:T(8,128)(2,1)S(1)}, bf16[4,16,256]{2,1,0:T(8,128)(2,1)S(1)}, u32[]{:S(2)}, u32[]{:S(2)}) collective-permute-start(bf16[4,16,256]{2,1,0:T(8,128)(2,1)S(1)} %get-tuple-element.43), channel_id=1, source_target_pairs={{0,28},{4,0},{8,4},{12,8},{16,12},{20,16},{24,20},{28,24},{1,29},{... | collective-permute-start | bytes 98312 | tf_op jit(solution)/shard_map/ppermute | solution.py:14
  17.9 5.1 %collective-permute-start.2 = (bf16[4,16,256]{2,1,0:T(8,128)(2,1)S(1)}, bf16[4,16,256]{2,1,0:T(8,128)(2,1)S(1)}, u32[]{:S(2)}, u32[]{:S(2)}) collective-permute-start(bf16[4,16,256]{2,1,0:T(8,128)(2,1)S(1)} %get-tuple-element.45), channel_id=1, source_target_pairs={{0,4},{4,8},{8,12},{12,16},{16,20},{20,24},{24,28},{28,0},{1,5},{5... | collective-permute-start | bytes 98312 | tf_op jit(solution)/shard_map/ppermute | solution.py:14
  18.4 5.7 %collective-permute-start.3 = (bf16[4,16,256]{2,1,0:T(8,128)(2,1)S(1)}, bf16[4,16,256]{2,1,0:T(8,128)(2,1)S(1)}, u32[]{:S(2)}, u32[]{:S(2)}) collective-permute-start(bf16[4,16,256]{2,1,0:T(8,128)(2,1)S(1)} %get-tuple-element.42), channel_id=1, source_target_pairs={{0,8},{4,12},{8,16},{12,20},{16,24},{20,28},{24,0},{28,4},{1,9},{5... | collective-permute-start | bytes 98312 | tf_op jit(solution)/shard_map/ppermute | solution.py:14
  38.7 6.2 %copy-start.2 = (bf16[512,8,320]{2,1,0:T(8,128)(2,1)S(1)}, bf16[512,8,320]{2,1,0:T(8,128)(2,1)}, u32[]{:S(2)}) copy-start(bf16[512,8,320]{2,1,0:T(8,128)(2,1)} %copy.57) | copy-start | bytes 7864324
  38.7 6.2 %copy-start.7 = (s32[2,256,16]{2,1,0:T(8,128)S(1)}, s32[2,256,16]{2,1,0:T(8,128)}, u32[]{:S(2)}) copy-start(s32[2,256,16]{2,1,0:T(8,128)} %copy.61) | copy-start | bytes 98308
  53.0 9.2 %copy-start.8 = (s32[2,256,16]{2,1,0:T(8,128)S(1)}, s32[2,256,16]{2,1,0:T(8,128)}, u32[]{:S(2)}) copy-start(s32[2,256,16]{2,1,0:T(8,128)} %copy.61) | copy-start | bytes 98308
  68.0 6.5 %copy-start.11 = (bf16[256,256]{1,0:T(8,128)(2,1)S(1)}, bf16[256,256]{1,0:T(8,128)(2,1)}, u32[]{:S(2)}) copy-start(bf16[256,256]{1,0:T(8,128)(2,1)} %param.20) | copy-start | bytes 393220
  74.9 5.5 %copy-start.1 = (f32[512,8,320]{0,2,1:T(8,128)S(1)}, f32[512,8,320]{0,2,1:T(8,128)}, u32[]{:S(2)}) copy-start(f32[512,8,320]{0,2,1:T(8,128)} %copy.59) | copy-start | bytes 15728644
  80.5 0.9 copy-start.6
  80.5 1.0 copy-start.12
  81.4 1.2 %copy-start.14 = (bf16[2,256,256]{2,1,0:T(8,128)(2,1)S(1)}, bf16[2,256,256]{2,1,0:T(8,128)(2,1)}, u32[]{:S(2)}) copy-start(bf16[2,256,256]{2,1,0:T(8,128)(2,1)} %param.14) | copy-start | bytes 786436
  81.8 0.8 copy-start.3
  85.3 4.9 %collective-permute-start.4 = (bf16[2,1,256]{2,1,0:T(2,128)(2,1)S(1)}, bf16[2,1,256]{2,1,0:T(2,128)(2,1)S(1)}, u32[]{:S(2)}, u32[]{:S(2)}) collective-permute-start(bf16[2,1,256]{2,1,0:T(2,128)(2,1)S(1)} %get-tuple-element.40), channel_id=1, source_target_pairs={{0,4},{4,8},{8,12},{12,16},{16,20},{20,24},{24,28},{28,0},{1,5},{5... | collective-permute-start | bytes 3080 | tf_op jit(solution)/shard_map/ppermute | solution.py:25
  85.3 4.8 %collective-permute-start.5 = (bf16[2,1,256]{2,1,0:T(2,128)(2,1)S(1)}, bf16[2,1,256]{2,1,0:T(2,128)(2,1)S(1)}, u32[]{:S(2)}, u32[]{:S(2)}) collective-permute-start(bf16[2,1,256]{2,1,0:T(2,128)(2,1)S(1)} %get-tuple-element.41), channel_id=1, source_target_pairs={{4,0},{8,4},{12,8},{16,12},{20,16},{24,20},{28,24},{0,28},{5,1},{9... | collective-permute-start | bytes 3080 | tf_op jit(solution)/shard_map/ppermute | solution.py:27
  90.3 7.1 %collective-permute-start.6 = (bf16[1,258,256]{2,1,0:T(8,128)(2,1)S(1)}, bf16[1,258,256]{2,1,0:T(8,128)(2,1)S(1)}, u32[]{:S(2)}, u32[]{:S(2)}) collective-permute-start(bf16[1,258,256]{2,1,0:T(8,128)(2,1)S(1)} %get-tuple-element.34), channel_id=1, source_target_pairs={{0,1},{1,2},{2,3},{4,5},{5,6},{6,7},{8,9},{9,10},{10,11},{12,13},{... | collective-permute-start | bytes 396296 | tf_op jit(solution)/shard_map/ppermute | solution.py:25
  93.7 7.8 %collective-permute-start.7 = (bf16[1,258,256]{2,1,0:T(8,128)(2,1)S(1)}, bf16[1,258,256]{2,1,0:T(8,128)(2,1)S(1)}, u32[]{:S(2)}, u32[]{:S(2)}) collective-permute-start(bf16[1,258,256]{2,1,0:T(8,128)(2,1)S(1)} %get-tuple-element.35), channel_id=1, source_target_pairs={{1,0},{2,1},{3,2},{5,4},{6,5},{7,6},{9,8},{10,9},{11,10},{13,12},{... | collective-permute-start | bytes 396296 | tf_op jit(solution)/shard_map/ppermute | solution.py:27
  97.4 4.5 %copy-start.4 = (bf16[9,256,256]{2,1,0:T(8,128)(2,1)S(1)}, bf16[9,256,256]{2,1,0:T(8,128)(2,1)}, u32[]{:S(2)}) copy-start(bf16[9,256,256]{2,1,0:T(8,128)(2,1)} %param.25) | copy-start | bytes 3538948
where the time goes:
time: 106 us; the launch traced here: 104 us
  matrix products  43.9 us (41%)
  local copies, waits for them, and re-layouts  26 us (25%)
  starting transfers between devices  13.6 us (13%)
  waiting for transfers between devices  11.1 us (10%)
  blocking collectives  8.14 us (8%)
  other arithmetic  1.42 us (1%)
    sub x1, matrix products, attend(): shifted = jnp.exp(scores - jnp.max(scores, axis=-1, keepdims=True))  9.18 us
    all_to_all x1, blocking collectives, per_device(): lax.all_to_all(payload, 'el', split_axis=1, concat_axis=1, tiled=True)  8.14 us
    dot_general x1, local copies, waits for them, and re-layouts, attend(): jnp.einsum('bhn,bnt->bht', weights, one_hot, preferred_element_type=jnp.f...  6.43 us
    dot_general x1, matrix products, attend(): jnp.einsum('bnt,bht->bhn', one_hot, low_part, preferred_element_type=jnp....  6.23 us
    ppermute x2, starting transfers between devices, with_halo(): lax.ppermute(head, axis, [((i + 1) % count, i) for i in range(ends)])  6 us
    dot_general x1, matrix products, attend(): jnp.einsum('bhn,bnt->bht', weights, one_hot, preferred_element_type=jnp.f...  5.78 us
    ppermute x4, waiting for transfers between devices, passed_along(): lax.ppermute(x, axis, [(i, (i + by) % length) for i in range(length)])  5.69 us
    dot_general x1, matrix products, attend(): jnp.einsum('bht,thd->bhd', spread_low, value_heads, preferred_element_typ...  4.9 us
  transfers between devices with their start and end apart: 8, of which 5 were waited for; matrix products, arithmetic and copies ran while one was open for 3% of the time, Pallas kernels for 0%

commit v1 on v0

v1 whole, which is shorter than its diff:
```python
import functools
import math

import jax
import jax.numpy as jnp
from jax import lax
from jax.experimental import pallas as pl
from jax.experimental.pallas import tpu as pltpu
from jax.sharding import PartitionSpec as P

HEADS = 8
REACH = 2
BF16 = jnp.bfloat16
F32 = jnp.float32
VMEM = pltpu.VMEM
SMEM = pltpu.SMEM


def ring(x, axis, by):
    length = lax.axis_size(axis)
    return lax.ppermute(x, axis, [(i, (i + by) % length) for i in range(length)])


def line(x, axis, by):
    length = lax.axis_size(axis)
    return lax.ppermute(
        x, axis, [(i, i + by) for i in range(length) if 0 <= i + by < length]
    )


def dot(a, b, contract=((1,), (0,))):
    return lax.dot_general(a, b, (contract, ((), ())), preferred_element_type=F32)


def rms(x):
    return x * lax.rsqrt(jnp.mean(x * x, axis=-1, keepdims=True) + 1e-06)


def call(body, outs, ins, name, cost, spaces=None, scratch=()):
    spaces = spaces or [VMEM] * len(ins)
    flops, transcendentals = cost
    moved = sum(x.size * x.dtype.itemsize for x in list(ins) + list(outs))
    return pl.pallas_call(
        body,
        out_shape=outs,
        in_specs=[pl.BlockSpec(memory_space=s) for s in spaces],
        out_specs=[pl.BlockSpec(memory_space=VMEM) for _ in outs],
        scratch_shapes=list(scratch),
        compiler_params=pltpu.CompilerParams(vmem_limit_bytes=32 * 1024 * 1024),
        cost_estimate=pl.CostEstimate(
            flops=flops, bytes_accessed=moved, transcendentals=transcendentals
        ),
        name=name,
    )(*ins)


def gather_body(me_ref, tokens_ref, slots_ref, *out_refs):
    groups = slots_ref.shape[1]
    offsets, capacity = slots_ref.shape[0], slots_ref.shape[2]
    rows = tokens_ref.shape[0]
    me = me_ref[0]
    tokens = tokens_ref[...]
    eye = (
        lax.broadcasted_iota(jnp.int32, (capacity, capacity), 0)
        == lax.broadcasted_iota(jnp.int32, (capacity, capacity), 1)
    )
    lane = lax.broadcasted_iota(jnp.int32, (capacity, rows), 1).astype(F32)
    for step in range(groups):
        target = lax.rem(me + step, groups)
        picks = []
        for offset in range(offsets):
            row = slots_ref[offset, pl.ds(target, 1), :].astype(F32)
            spread = jnp.broadcast_to(row, (capacity, capacity))
            column = jnp.sum(jnp.where(eye, spread, 0.0), axis=-1, keepdims=True)
            picks.append(jnp.where(column == lane, 1.0, 0.0))
        one_hot = jnp.concatenate(picks, axis=0).astype(BF16)
        chosen = dot(one_hot, tokens).astype(BF16)
        out_refs[step][...] = chosen.reshape(out_refs[step].shape)


def prepare_body(me_ref, points_ref, idx_ref, w_query_ref, q_ref, bias_ref, idx_t_ref, *, groups, capacity):
    count, width = q_ref.shape[1], q_ref.shape[0]
    me = me_ref[0]
    points = points_ref[...].reshape(count, width)
    scale = math.log2(math.e) / math.sqrt(width // HEADS)
    query = dot(points, w_query_ref[...]) * scale
    q_ref[...] = query.T.astype(BF16)
    near = idx_ref.shape[-1]
    idx_t_ref[...] = idx_ref[...].reshape(count, near).T
    lanes = 128
    for step in range(groups):
        source = lax.rem(me + groups - step, groups)
        for offset in range(bias_ref.shape[0] // (groups * capacity)):
            first = (offset * groups + source) * capacity
            slot = first + lax.broadcasted_iota(jnp.int32, (capacity, lanes), 0)
            place = (offset * groups + step) * capacity
            for start in range(0, count, lanes):
                total = jnp.zeros((capacity, lanes), F32)
                for n in range(near):
                    index = idx_t_ref[n : n + 1, start : start + lanes]
                    total = total + jnp.where(slot == index, 1.0, 0.0)
                bias_ref[place : place + capacity, start : start + lanes] = jnp.log2(total)


def main_body(
    *refs, pieces
):
    piece_refs = refs[:pieces]
    (
        q_ref,
        bias_ref,
        points_ref,
        skip_ref,
        w_key_ref,
        w_value_ref,
        w_out_ref,
        w_hid_ref,
        w_skip_ref,
        w_down_ref,
        joined_ref,
        first_ref,
        second_ref,
        left_ref,
        right_ref,
        att_ref,
    ) = refs[pieces:]
    width, count = q_ref.shape
    head_width = width // HEADS
    received = jnp.concatenate(
        [r[...].reshape(-1, width) for r in piece_refs], axis=0
    )
    table = received.shape[0]
    keys = dot(received, w_key_ref[...]).astype(BF16)
    normed_tokens = rms(received.astype(F32)).astype(BF16)
    values_t = dot(w_value_ref[...], normed_tokens, ((0,), (1,))).astype(BF16)
    ones = jnp.ones((16, table), BF16)
    for head in range(HEADS):
        low, high = head * head_width, (head + 1) * head_width
        scores = dot(keys[:, low:high], q_ref[low:high, :]) + bias_ref[...]
        top = jnp.max(scores, axis=0, keepdims=True)
        weights = jnp.exp2(scores - top).astype(BF16)
        lhs = jnp.concatenate([values_t[low:high, :], ones], axis=0)
        mixed = dot(lhs, weights)
        att_ref[low:high, :] = (mixed[:head_width] / mixed[head_width : head_width + 1]).astype(BF16)
    points = points_ref[...].reshape(count, width).astype(F32)
    residual = points + dot(att_ref[...], w_out_ref[...], ((0,), (0,)))
    normed = rms(residual).astype(BF16)
    skip = skip_ref[...].reshape(count, width)
    pre = dot(normed, w_hid_ref[...]) + dot(skip, w_skip_ref[...])
    c1 = math.sqrt(2.0 / math.pi)
    half = 0.5 * pre
    inner = (half + half * jnp.tanh(pre * (c1 + (c1 * 0.044715) * (pre * pre)))).astype(BF16)
    joined = residual + dot(inner, w_down_ref[...])
    conv = rms(joined).astype(BF16)
    joined_ref[...] = joined.reshape(joined_ref.shape)
    cols = count // 2
    first_ref[...] = conv[:cols]
    second_ref[...] = conv[cols:]
    left_ref[0:1, :] = conv[0:1]
    left_ref[1:2, :] = conv[cols : cols + 1]
    right_ref[0:1, :] = conv[cols - 1 : cols]
    right_ref[1:2, :] = conv[2 * cols - 1 : 2 * cols]


def shifted(x, by):
    rolled = pltpu.roll(x, by % x.shape[0], 0)
    row = lax.broadcasted_iota(jnp.int32, x.shape, 0)
    edge = 0 if by > 0 else x.shape[0] - 1
    return jnp.where(row == edge, 0.0, rolled)


def inside_body(first_ref, second_ref, joined_ref, w_conv_ref, out_ref):
    first, second = first_ref[...], second_ref[...]
    for r in range(2):
        taps = []
        for dc in range(3):
            taps.append(
                dot(first, w_conv_ref[3 * (1 - r) + dc])
                + dot(second, w_conv_ref[3 * (2 - r) + dc])
            )
        out_ref[r] = joined_ref[r] + taps[1] + shifted(taps[0], 1) + shifted(taps[2], -1)


def border_body(
    above_ref, below_ref, left_ref, right_ref, corner_up_ref, corner_down_ref, part_ref, w_conv_ref, out_ref
):
    cols, width = above_ref.shape
    row = lax.broadcasted_iota(jnp.int32, (cols, width), 0)
    sides = []
    for side, (ref, at) in enumerate(((left_ref, 0), (right_ref, 1))):
        ends = jnp.concatenate(
            [corner_up_ref[at : at + 1, :], ref[...], corner_down_ref[at : at + 1, :], jnp.zeros((12, width), BF16)],
            axis=0,
        )
        sides.append([dot(ends, w_conv_ref[3 * dr + 2 * side]) for dr in range(3)])
    for r, ref in enumerate((above_ref, below_ref)):
        x = ref[...]
        taps = [dot(x, w_conv_ref[6 * r + dc]) for dc in range(3)]
        total = part_ref[r] + taps[1] + shifted(taps[0], 1) + shifted(taps[2], -1)
        for side in range(2):
            e = sides[side]
            extra = e[0][r : r + 1] + e[1][r + 1 : r + 2] + e[2][r + 2 : r + 3]
            total = total + jnp.where(row == (0, cols - 1)[side], extra, 0.0)
        out_ref[r] = total.astype(BF16)


def per_device(
    points,
    skip,
    tokens,
    send_slots,
    recv_idx,
    w_query,
    w_key,
    w_value,
    w_out,
    w_hid,
    w_skip,
    w_down,
    w_conv,
):
    rows, cols, width = points.shape
    count = rows * cols
    own_tokens = tokens[0, 0]
    slots = send_slots[0, 0]
    offsets, groups, capacity = slots.shape
    table = offsets * groups * capacity
    me = lax.axis_index("el").astype(jnp.int32).reshape(1)
    shape = jax.ShapeDtypeStruct
    sent = call(
        gather_body,
        [shape((offsets, capacity, width), BF16)] * groups,
        [me, own_tokens, slots],
        "gather",
        (2 * table * own_tokens.shape[0] * width, 0),
        [SMEM, VMEM, VMEM],
    )
    got = [sent[0]] + [ring(sent[s], "el", s) for s in range(1, groups)]
    query_t, bias = call(
        functools.partial(prepare_body, groups=groups, capacity=capacity),
        [shape((width, count), BF16), shape((table, count), F32)],
        [me, points, recv_idx, w_query],
        "prepare",
        (table * count * 48, table * count),
        [SMEM, VMEM, VMEM, VMEM],
        [pltpu.VMEM((recv_idx.shape[-1], count), jnp.int32)],
    )
    pieces = []
    for offset in range(offsets):
        bundle = jnp.concatenate([g[offset] for g in got], axis=0)
        pieces.append(bundle if offset == REACH else ring(bundle, "az", offset - REACH))
    joined, first, second, left, right = call(
        functools.partial(main_body, pieces=len(pieces)),
        [
            shape((rows, cols, width), F32),
            shape((cols, width), BF16),
            shape((cols, width), BF16),
            shape((2, width), BF16),
            shape((2, width), BF16),
        ],
        pieces
        + [query_t, bias, points, skip, w_key, w_value, w_out, w_hid, w_skip, w_down],
        "main",
        (10 * table * count * width + 2 * count * width * 13 * width, table * count * HEADS),
        None,
        [pltpu.VMEM((width, count), BF16)],
    )
    from_left = ring(right, "az", 1)
    from_right = ring(left, "az", -1)
    above = line(second, "el", 1)
    below = line(first, "el", -1)
    ends = jnp.stack([from_left, from_right], axis=1)
    corner_up = line(ends[1], "el", 1)
    corner_down = line(ends[0], "el", -1)
    (partial,) = call(
        inside_body,
        [shape((rows, cols, width), F32)],
        [first, second, joined, w_conv],
        "inside",
        (2 * count * width * width * 6, 0),
    )
    (out,) = call(
        border_body,
        [shape((rows, cols, width), BF16)],
        [above, below, from_left, from_right, corner_up, corner_down, partial, w_conv],
        "border",
        (2 * count * width * width * 3, 0),
    )
    return out


def solution(mesh):
    return jax.shard_map(
        per_device,
        mesh=mesh,
        in_specs=(
            P("el", "az", None),
            P("el", "az", None),
            P("az", "el", None, None),
            P("az", "el", None, None, None),
            P("el", "az", None),
            P(),
            P(),
            P(),
            P(),
            P(),
            P(),
            P(),
            P(),
        ),
        out_specs=P("el", "az", None),
        check_vma=False,
    )
```

time: 106 us -> 47.6 us (0.45)
  the two profiles are of different devices: /device:TPU:2 before, /device:TPU:4 now
where the time goes in v1:
time: 47.6 us; the launch traced here: 47.1 us
  starting transfers between devices  23.8 us (50%)
  waiting for transfers between devices  8.18 us (17%)
  Pallas kernels  7.64 us (16%)
  local copies, waits for them, and re-layouts  7.26 us (15%)
    ppermute x4, starting transfers between devices, line(): lax.ppermute(x, axis, [(i, i + by) for i in range(length) if 0 <= i + by...  12.6 us
    ppermute x9, starting transfers between devices, ring(): lax.ppermute(x, axis, [(i, (i + by) % length) for i in range(length)])  11.2 us
    pallas_call x5, Pallas kernels, call(): pl.pallas_call(body, out_shape=outs, in_specs=[pl.BlockSpec(memory_space=...  7.64 us
    unnamed x27, local copies, waits for them, and re-layouts  7.23 us
    ppermute x9, waiting for transfers between devices, ring(): lax.ppermute(x, axis, [(i, (i + by) % length) for i in range(length)])  5.71 us
    ppermute x4, waiting for transfers between devices, line(): lax.ppermute(x, axis, [(i, i + by) for i in range(length) if 0 <= i + by...  2.47 us
  transfers between devices with their start and end apart: 13, of which 5 were waited for; matrix products, arithmetic and copies ran while one was open for 2% of the time, Pallas kernels for 4%

profile of v1, /device:TPU:4, one launch (start us, length us, event | category | flops | bytes accessed | tf_op | source)
XLA Modules:
  0.0 47.1 jit_solution(14471000240973685437)
XLA Ops:
  0.0 0.0 copy-start.2
  0.0 0.9 %copy-done.11 = bf16[1,1,128,256]{3,2,1,0:T(8,128)(2,1)S(1)} copy-done((bf16[1,1,128,256]{3,2,1,0:T(8,128)(2,1)S(1)}, bf16[1,1,128,256]{3,2,1,0:T(8,128)(2,1)}, u32[]{:S(2)}) %copy-start.11) | copy-done | bytes 65560
  0.9 0.7 %copy-done.12 = s32[1,1,5,4,16]{4,3,2,1,0:T(4,128)S(1)} copy-done((s32[1,1,5,4,16]{4,3,2,1,0:T(4,128)S(1)}, s32[1,1,5,4,16]{4,3,2,1,0:T(4,128)}, u32[]{:S(2)}) %copy-start.12) | copy-done | bytes 1304
  1.6 0.3 gather.1
  1.9 1.5 %collective-permute-start = (bf16[5,16,256]{2,1,0:T(8,128)(2,1)S(1)}, bf16[5,16,256]{2,1,0:T(8,128)(2,1)S(1)}, u32[]{:S(2)}, u32[]{:S(2)}) collective-permute-start(bf16[5,16,256]{2,1,0:T(8,128)(2,1)S(1)} %get-tuple-element.17), channel_id=1, source_target_pairs={{0,1},{1,2},{2,3},{3,0},{4,5},{5,6},{6,7},{7,4},{8,9},{9,10},{10,1... | collective-permute-start | bytes 122888 | tf_op jit(solution)/shard_map/ppermute | solution.py:21
  3.4 0.5 %collective-permute-start.1 = (bf16[5,16,256]{2,1,0:T(8,128)(2,1)S(1)}, bf16[5,16,256]{2,1,0:T(8,128)(2,1)S(1)}, u32[]{:S(2)}, u32[]{:S(2)}) collective-permute-start(bf16[5,16,256]{2,1,0:T(8,128)(2,1)S(1)} %get-tuple-element.18), channel_id=1, source_target_pairs={{0,2},{1,3},{2,0},{3,1},{4,6},{5,7},{6,4},{7,5},{8,10},{9,11},{10,... | collective-permute-start | bytes 122888 | tf_op jit(solution)/shard_map/ppermute | solution.py:21
  3.9 1.0 %collective-permute-start.2 = (bf16[5,16,256]{2,1,0:T(8,128)(2,1)S(1)}, bf16[5,16,256]{2,1,0:T(8,128)(2,1)S(1)}, u32[]{:S(2)}, u32[]{:S(2)}) collective-permute-start(bf16[5,16,256]{2,1,0:T(8,128)(2,1)S(1)} %get-tuple-element.19), channel_id=1, source_target_pairs={{0,3},{1,0},{2,1},{3,2},{4,7},{5,4},{6,5},{7,6},{8,11},{9,8},{10,9... | collective-permute-start | bytes 122888 | tf_op jit(solution)/shard_map/ppermute | solution.py:21
  4.9 0.9 %copy.15.idx_ref = s32[2,256,16]{2,1,0:T(8,128)S(1)} copy(s32[2,256,16]{1,2,0:T(8,128)} %param.17) | data formatting | bytes 65536 | tf_op args[4]
  5.8 0.0 copy-start.1
  5.8 0.9 %copy-done.1 = bf16[2,256,256]{2,1,0:T(8,128)(2,1)S(1)} copy-done((bf16[2,256,256]{2,1,0:T(8,128)(2,1)S(1)}, bf16[2,256,256]{2,1,0:T(8,128)(2,1)}, u32[]{:S(2)}) %copy-start.1) | copy-done | bytes 262168
  6.8 0.9 %copy-done.3 = bf16[256,256]{1,0:T(8,128)(2,1)S(1)} copy-done((bf16[256,256]{1,0:T(8,128)(2,1)S(1)}, bf16[256,256]{1,0:T(8,128)(2,1)}, u32[]{:S(2)}) %copy-start.3) | copy-done | bytes 131096
  7.7 1.3 %prepare.1 = (bf16[256,512]{1,0:T(8,128)(2,1)S(1)}, f32[320,512]{1,0:T(8,128)S(1)}) custom-call(s32[1]{0:T(128)} %bitcast.me_ref, bf16[2,256,256]{2,1,0:T(8,128)(2,1)S(1)} %copy-done.1, s32[2,256,16]{2,1,0:T(8,128)S(1)} %copy.15.idx_ref, bf16[256,256]{1,0:T(8,128)(2,1)S(1)} %copy-done.3), custom_call_target="tpu_custom_call" | custom-call | flops 7864320 | bytes 1343492 | tf_op jit(solution)/shard_map/prepare/pallas_call | solution.py:43
  9.0 0.0 collective-permute-done
  9.0 0.0 collective-permute-done.1
  9.1 0.0 collective-permute-done.2
  9.1 4.1 %collective-permute-start.3 = (bf16[64,256]{1,0:T(8,128)(2,1)S(1)}, bf16[64,256]{1,0:T(8,128)(2,1)S(1)}, u32[]{:S(2)}, u32[]{:S(2)}) collective-permute-start(bf16[64,256]{1,0:T(8,128)(2,1)S(1)} %pad_maximum_fusion), channel_id=1, source_target_pairs={{0,24},{4,28},{8,0},{12,4},{16,8},{20,12},{24,16},{28,20},{1,25},{... | collective-permute-start | bytes 98312 | tf_op jit(solution)/shard_map/ppermute | solution.py:21
  13.2 0.0 collective-permute-start.4
  13.2 0.5 %collective-permute-start.5 = (bf16[64,256]{1,0:T(8,128)(2,1)S(1)}, bf16[64,256]{1,0:T(8,128)(2,1)S(1)}, u32[]{:S(2)}, u32[]{:S(2)}) collective-permute-start(bf16[64,256]{1,0:T(8,128)(2,1)S(1)} %pad_maximum_fusion.3), channel_id=1, source_target_pairs={{0,4},{4,8},{8,12},{12,16},{16,20},{20,24},{24,28},{28,0},{1,5},{5... | collective-permute-start | bytes 98312 | tf_op jit(solution)/shard_map/ppermute | solution.py:21
  13.7 0.0 collective-permute-start.6
  13.7 1.2 %collective-permute-done.3.refs_0_ = bf16[64,256]{1,0:T(8,128)(2,1)S(1)} collective-permute-done((bf16[64,256]{1,0:T(8,128)(2,1)S(1)}, bf16[64,256]{1,0:T(8,128)(2,1)S(1)}, u32[]{:S(2)}, u32[]{:S(2)}) %collective-permute-start.3) | collective-permute-done | bytes 32800 | tf_op jit(solution)/shard_map/ppermute | solution.py:21
  14.9 0.5 %collective-permute-done.4.refs_1_ = bf16[64,256]{1,0:T(8,128)(2,1)S(1)} collective-permute-done((bf16[64,256]{1,0:T(8,128)(2,1)S(1)}, bf16[64,256]{1,0:T(8,128)(2,1)S(1)}, u32[]{:S(2)}, u32[]{:S(2)}) %collective-permute-start.4) | collective-permute-done | bytes 32800 | tf_op jit(solution)/shard_map/ppermute | solution.py:21
  15.5 2.9 %collective-permute-done.5.refs_3_ = bf16[64,256]{1,0:T(8,128)(2,1)S(1)} collective-permute-done((bf16[64,256]{1,0:T(8,128)(2,1)S(1)}, bf16[64,256]{1,0:T(8,128)(2,1)S(1)}, u32[]{:S(2)}, u32[]{:S(2)}) %collective-permute-start.5) | collective-permute-done | bytes 32800 | tf_op jit(solution)/shard_map/ppermute | solution.py:21
  18.4 1.0 %collective-permute-done.6.refs_4_ = bf16[64,256]{1,0:T(8,128)(2,1)S(1)} collective-permute-done((bf16[64,256]{1,0:T(8,128)(2,1)S(1)}, bf16[64,256]{1,0:T(8,128)(2,1)S(1)}, u32[]{:S(2)}, u32[]{:S(2)}) %collective-permute-start.6) | collective-permute-done | bytes 32800 | tf_op jit(solution)/shard_map/ppermute | solution.py:21
  19.4 0.0 copy-done.2
  19.4 0.0 copy-done.8
  19.4 0.0 copy-done.4
  19.4 0.0 copy-done.5
  19.4 0.0 copy-done.9
  19.4 0.0 copy-start.6
  19.4 1.0 %copy-done.6 = bf16[1024,256]{1,0:T(8,128)(2,1)S(1)} copy-done((bf16[1024,256]{1,0:T(8,128)(2,1)S(1)}, bf16[1024,256]{1,0:T(8,128)(2,1)}, u32[]{:S(2)}) %copy-start.6) | copy-done | bytes 524312
  20.5 0.9 %copy-done.7 = bf16[2,256,256]{2,1,0:T(8,128)(2,1)S(1)} copy-done((bf16[2,256,256]{2,1,0:T(8,128)(2,1)S(1)}, bf16[2,256,256]{2,1,0:T(8,128)(2,1)}, u32[]{:S(2)}) %copy-start.7) | copy-done | bytes 262168
  21.4 0.9 %copy-done.10 = bf16[256,256]{1,0:T(8,128)(2,1)S(1)} copy-done((bf16[256,256]{1,0:T(8,128)(2,1)S(1)}, bf16[256,256]{1,0:T(8,128)(2,1)}, u32[]{:S(2)}) %copy-start.10) | copy-done | bytes 131096
  22.3 4.3 %main.1 = (f32[2,256,256]{2,1,0:T(8,128)S(1)}, bf16[256,256]{1,0:T(8,128)(2,1)S(1)}, bf16[256,256]{1,0:T(8,128)(2,1)S(1)}, bf16[2,256]{1,0:T(2,128)(2,1)S(1)}, bf16[2,256]{1,0:T(2,128)(2,1)S(1)}) custom-call(bf16[64,256]{1,0:T(8,128)(2,1)S(1)} %collective-permute-done.3.refs_0_, bf16[64,256]{1,0:T(8,128)(2,1)S(1)} %collective-permute-done.4.refs_1_, ...), custom_call_target="tpu_custom_call" | custom-call | flops 1291845632 | bytes 4360192 | tf_op jit(solution)/shard_map/main/pallas_call | solution.py:43
  26.6 0.1 collective-permute-start.9
  26.7 3.5 %collective-permute-start.10 = (bf16[2,256]{1,0:T(2,128)(2,1)S(1)}, bf16[2,256]{1,0:T(2,128)(2,1)S(1)}, u32[]{:S(2)}, u32[]{:S(2)}) collective-permute-start(bf16[2,256]{1,0:T(2,128)(2,1)S(1)} %get-tuple-element.25), channel_id=1, source_target_pairs={{0,28},{4,0},{8,4},{12,8},{16,12},{20,16},{24,20},{28,24},{1,29},{... | collective-permute-start | bytes 3080 | tf_op jit(solution)/shard_map/ppermute | solution.py:21
  30.2 2.7 %collective-permute-start.7 = (bf16[256,256]{1,0:T(8,128)(2,1)S(1)}, bf16[256,256]{1,0:T(8,128)(2,1)S(1)}, u32[]{:S(2)}, u32[]{:S(2)}) collective-permute-start(bf16[256,256]{1,0:T(8,128)(2,1)S(1)} %get-tuple-element.22.second_ref), channel_id=1, source_target_pairs={{0,1},{1,2},{2,3},{4,5},{5,6},{6,7},{8,9},{9,10},{10,11},{12,13},{... | collective-permute-start | bytes 393224 | tf_op jit(solution)/shard_map/ppermute | solution.py:26
  32.9 4.0 %collective-permute-start.8 = (bf16[256,256]{1,0:T(8,128)(2,1)S(1)}, bf16[256,256]{1,0:T(8,128)(2,1)S(1)}, u32[]{:S(2)}, u32[]{:S(2)}) collective-permute-start(bf16[256,256]{1,0:T(8,128)(2,1)S(1)} %get-tuple-element.23.first_ref), channel_id=1, source_target_pairs={{1,0},{2,1},{3,2},{5,4},{6,5},{7,6},{9,8},{10,9},{11,10},{13,12},{... | collective-permute-start | bytes 393224 | tf_op jit(solution)/shard_map/ppermute | solution.py:26
  37.0 0.0 collective-permute-done.9.left_ref
  37.0 0.0 collective-permute-done.10.right_ref
  37.0 2.6 %collective-permute-start.12 = (bf16[2,256]{1,0:T(2,128)(2,1)S(1)}, bf16[2,256]{1,0:T(2,128)(2,1)S(1)}, u32[]{:S(2)}, u32[]{:S(2)}) collective-permute-start(bf16[2,256]{1,0:T(2,128)(2,1)S(1)} %get-tuple-element.47), channel_id=1, source_target_pairs={{1,0},{2,1},{3,2},{5,4},{6,5},{7,6},{9,8},{10,9},{11,10},{13,12},{... | collective-permute-start | bytes 3080 | tf_op jit(solution)/shard_map/ppermute | solution.py:26
  39.6 3.3 %collective-permute-start.11 = (bf16[2,256]{1,0:T(2,128)(2,1)S(1)}, bf16[2,256]{1,0:T(2,128)(2,1)S(1)}, u32[]{:S(2)}, u32[]{:S(2)}) collective-permute-start(bf16[2,256]{1,0:T(2,128)(2,1)S(1)} %get-tuple-element.48), channel_id=1, source_target_pairs={{0,1},{1,2},{2,3},{4,5},{5,6},{6,7},{8,9},{9,10},{10,11},{12,13},{... | collective-permute-start | bytes 3080 | tf_op jit(solution)/shard_map/ppermute | solution.py:26
  42.9 0.0 copy-done
  42.9 0.6 %inside.1.part_ref = f32[2,256,256]{2,1,0:T(8,128)S(1)} custom-call(bf16[256,256]{1,0:T(8,128)(2,1)S(1)} %get-tuple-element.23.first_ref, bf16[256,256]{1,0:T(8,128)(2,1)S(1)} %get-tuple-element.22.second_ref, f32[2,256,256]{2,1,0:T(8,128)S(1)} %get-tuple-element.26.joined_ref, bf16[9,256,256]{2,1,0:T(8,128)(2,1)S(1)} %copy-done), custom_call_target="tpu_custom_call" | custom-call | flops 402653184 | bytes 2490368 | tf_op jit(solution)/shard_map/inside/pallas_call | solution.py:43
  43.5 0.0 collective-permute-done.12.corner_down_ref
  43.5 2.5 %collective-permute-done.11.corner_up_ref = bf16[2,256]{1,0:T(2,128)(2,1)S(1)} collective-permute-done((bf16[2,256]{1,0:T(2,128)(2,1)S(1)}, bf16[2,256]{1,0:T(2,128)(2,1)S(1)}, u32[]{:S(2)}, u32[]{:S(2)}) %collective-permute-start.11) | collective-permute-done | bytes 1056 | tf_op jit(solution)/shard_map/ppermute | solution.py:26
  46.0 0.0 collective-permute-done.7.above_ref
  46.0 0.0 collective-permute-done.8.below_ref
  46.0 1.2 %border.1 = bf16[2,256,256]{2,1,0:T(8,128)(2,1)} custom-call(bf16[256,256]{1,0:T(8,128)(2,1)S(1)} %collective-permute-done.7.above_ref, bf16[256,256]{1,0:T(8,128)(2,1)S(1)} %collective-permute-done.8.below_ref, bf16[2,256]{1,0:T(2,128)(2,1)S(1)} %collective-permute-done.9.left_ref, bf16[2,256]{1,0:T(2,128)(2,1)S(1)} %collective-permute-done.10.right_ref, ...), custom_call_target="tpu_custom_call" | custom-call | flops 201326592 | bytes 2232320 | tf_op jit(solution)/shard_map/border/pallas_call | solution.py:43
  (22 shorter events, 0.1 us)
Async XLA Ops:
  0.0 19.4 %copy-start.2 = (bf16[2,256,256]{2,1,0:T(8,128)(2,1)S(1)}, bf16[2,256,256]{2,1,0:T(8,128)(2,1)}, u32[]{:S(2)}) copy-start(bf16[2,256,256]{2,1,0:T(8,128)(2,1)} %refs_7_.1) | copy-start | bytes 786436
  0.0 19.4 %copy-start.8 = (bf16[256,256]{1,0:T(8,128)(2,1)S(1)}, bf16[256,256]{1,0:T(8,128)(2,1)}, u32[]{:S(2)}) copy-start(bf16[256,256]{1,0:T(8,128)(2,1)} %refs_9_.1) | copy-start | bytes 393220
  0.0 0.9 %copy-start.11 = (bf16[1,1,128,256]{3,2,1,0:T(8,128)(2,1)S(1)}, bf16[1,1,128,256]{3,2,1,0:T(8,128)(2,1)}, u32[]{:S(2)}) copy-start(bf16[1,1,128,256]{3,2,1,0:T(8,128)(2,1)} %param.15) | copy-start | bytes 196612
  0.9 0.7 %copy-start.12 = (s32[1,1,5,4,16]{4,3,2,1,0:T(4,128)S(1)}, s32[1,1,5,4,16]{4,3,2,1,0:T(4,128)}, u32[]{:S(2)}) copy-start(s32[1,1,5,4,16]{4,3,2,1,0:T(4,128)} %param.16) | copy-start | bytes 3844
  1.9 7.2 %collective-permute-start = (bf16[5,16,256]{2,1,0:T(8,128)(2,1)S(1)}, bf16[5,16,256]{2,1,0:T(8,128)(2,1)S(1)}, u32[]{:S(2)}, u32[]{:S(2)}) collective-permute-start(bf16[5,16,256]{2,1,0:T(8,128)(2,1)S(1)} %get-tuple-element.17), channel_id=1, source_target_pairs={{0,1},{1,2},{2,3},{3,0},{4,5},{5,6},{6,7},{7,4},{8,9},{9,10},{10,1... | collective-permute-start | bytes 122888 | tf_op jit(solution)/shard_map/ppermute | solution.py:21
  3.4 5.6 %collective-permute-start.1 = (bf16[5,16,256]{2,1,0:T(8,128)(2,1)S(1)}, bf16[5,16,256]{2,1,0:T(8,128)(2,1)S(1)}, u32[]{:S(2)}, u32[]{:S(2)}) collective-permute-start(bf16[5,16,256]{2,1,0:T(8,128)(2,1)S(1)} %get-tuple-element.18), channel_id=1, source_target_pairs={{0,2},{1,3},{2,0},{3,1},{4,6},{5,7},{6,4},{7,5},{8,10},{9,11},{10,... | collective-permute-start | bytes 122888 | tf_op jit(solution)/shard_map/ppermute | solution.py:21
  3.9 5.2 %collective-permute-start.2 = (bf16[5,16,256]{2,1,0:T(8,128)(2,1)S(1)}, bf16[5,16,256]{2,1,0:T(8,128)(2,1)S(1)}, u32[]{:S(2)}, u32[]{:S(2)}) collective-permute-start(bf16[5,16,256]{2,1,0:T(8,128)(2,1)S(1)} %get-tuple-element.19), channel_id=1, source_target_pairs={{0,3},{1,0},{2,1},{3,2},{4,7},{5,4},{6,5},{7,6},{8,11},{9,8},{10,9... | collective-permute-start | bytes 122888 | tf_op jit(solution)/shard_map/ppermute | solution.py:21
  5.8 1.0 %copy-start.1 = (bf16[2,256,256]{2,1,0:T(8,128)(2,1)S(1)}, bf16[2,256,256]{2,1,0:T(8,128)(2,1)}, u32[]{:S(2)}) copy-start(bf16[2,256,256]{2,1,0:T(8,128)(2,1)} %refs_7_.1) | copy-start | bytes 786436
  6.8 0.9 %copy-start.3 = (bf16[256,256]{1,0:T(8,128)(2,1)S(1)}, bf16[256,256]{1,0:T(8,128)(2,1)}, u32[]{:S(2)}) copy-start(bf16[256,256]{1,0:T(8,128)(2,1)} %w_query_ref.1) | copy-start | bytes 393220
  7.7 11.7 %copy-start.4 = (bf16[256,1024]{1,0:T(8,128)(2,1)S(1)}, bf16[256,1024]{1,0:T(8,128)(2,1)}, u32[]{:S(2)}) copy-start(bf16[256,1024]{1,0:T(8,128)(2,1)} %refs_12_.1) | copy-start | bytes 1572868
  7.7 11.7 %copy-start.5 = (bf16[256,1024]{1,0:T(8,128)(2,1)S(1)}, bf16[256,1024]{1,0:T(8,128)(2,1)}, u32[]{:S(2)}) copy-start(bf16[256,1024]{1,0:T(8,128)(2,1)} %refs_13_.1) | copy-start | bytes 1572868
  7.7 11.7 %copy-start.9 = (bf16[256,256]{1,0:T(8,128)(2,1)S(1)}, bf16[256,256]{1,0:T(8,128)(2,1)}, u32[]{:S(2)}) copy-start(bf16[256,256]{1,0:T(8,128)(2,1)} %refs_10_.1) | copy-start | bytes 393220
  9.1 5.8 %collective-permute-start.3 = (bf16[64,256]{1,0:T(8,128)(2,1)S(1)}, bf16[64,256]{1,0:T(8,128)(2,1)S(1)}, u32[]{:S(2)}, u32[]{:S(2)}) collective-permute-start(bf16[64,256]{1,0:T(8,128)(2,1)S(1)} %pad_maximum_fusion), channel_id=1, source_target_pairs={{0,24},{4,28},{8,0},{12,4},{16,8},{20,12},{24,16},{28,20},{1,25},{... | collective-permute-start | bytes 98312 | tf_op jit(solution)/shard_map/ppermute | solution.py:21
  13.2 2.3 %collective-permute-start.4 = (bf16[64,256]{1,0:T(8,128)(2,1)S(1)}, bf16[64,256]{1,0:T(8,128)(2,1)S(1)}, u32[]{:S(2)}, u32[]{:S(2)}) collective-permute-start(bf16[64,256]{1,0:T(8,128)(2,1)S(1)} %pad_maximum_fusion.1), channel_id=1, source_target_pairs={{0,28},{4,0},{8,4},{12,8},{16,12},{20,16},{24,20},{28,24},{1,29},{... | collective-permute-start | bytes 98312 | tf_op jit(solution)/shard_map/ppermute | solution.py:21
  13.2 5.2 %collective-permute-start.5 = (bf16[64,256]{1,0:T(8,128)(2,1)S(1)}, bf16[64,256]{1,0:T(8,128)(2,1)S(1)}, u32[]{:S(2)}, u32[]{:S(2)}) collective-permute-start(bf16[64,256]{1,0:T(8,128)(2,1)S(1)} %pad_maximum_fusion.3), channel_id=1, source_target_pairs={{0,4},{4,8},{8,12},{12,16},{16,20},{20,24},{24,28},{28,0},{1,5},{5... | collective-permute-start | bytes 98312 | tf_op jit(solution)/shard_map/ppermute | solution.py:21
  13.7 5.7 %collective-permute-start.6 = (bf16[64,256]{1,0:T(8,128)(2,1)S(1)}, bf16[64,256]{1,0:T(8,128)(2,1)S(1)}, u32[]{:S(2)}, u32[]{:S(2)}) collective-permute-start(bf16[64,256]{1,0:T(8,128)(2,1)S(1)} %pad_maximum_fusion.4), channel_id=1, source_target_pairs={{0,8},{4,12},{8,16},{12,20},{16,24},{20,28},{24,0},{28,4},{1,9},{5... | collective-permute-start | bytes 98312 | tf_op jit(solution)/shard_map/ppermute | solution.py:21
  19.4 1.0 %copy-start.6 = (bf16[1024,256]{1,0:T(8,128)(2,1)S(1)}, bf16[1024,256]{1,0:T(8,128)(2,1)}, u32[]{:S(2)}) copy-start(bf16[1024,256]{1,0:T(8,128)(2,1)} %refs_14_.1) | copy-start | bytes 1572868
  20.5 0.9 %copy-start.7 = (bf16[2,256,256]{2,1,0:T(8,128)(2,1)S(1)}, bf16[2,256,256]{2,1,0:T(8,128)(2,1)}, u32[]{:S(2)}) copy-start(bf16[2,256,256]{2,1,0:T(8,128)(2,1)} %refs_8_.1) | copy-start | bytes 786436
  21.4 0.9 %copy-start.10 = (bf16[256,256]{1,0:T(8,128)(2,1)S(1)}, bf16[256,256]{1,0:T(8,128)(2,1)}, u32[]{:S(2)}) copy-start(bf16[256,256]{1,0:T(8,128)(2,1)} %refs_11_.1) | copy-start | bytes 393220
  22.3 20.6 %copy-start = (bf16[9,256,256]{2,1,0:T(8,128)(2,1)S(1)}, bf16[9,256,256]{2,1,0:T(8,128)(2,1)}, u32[]{:S(2)}) copy-start(bf16[9,256,256]{2,1,0:T(8,128)(2,1)} %w_conv_ref.3) | copy-start | bytes 3538948
  26.6 10.3 %collective-permute-start.9 = (bf16[2,256]{1,0:T(2,128)(2,1)S(1)}, bf16[2,256]{1,0:T(2,128)(2,1)S(1)}, u32[]{:S(2)}, u32[]{:S(2)}) collective-permute-start(bf16[2,256]{1,0:T(2,128)(2,1)S(1)} %get-tuple-element.24), channel_id=1, source_target_pairs={{0,4},{4,8},{8,12},{12,16},{16,20},{20,24},{24,28},{28,0},{1,5},{5... | collective-permute-start | bytes 3080 | tf_op jit(solution)/shard_map/ppermute | solution.py:21
  26.7 10.3 %collective-permute-start.10 = (bf16[2,256]{1,0:T(2,128)(2,1)S(1)}, bf16[2,256]{1,0:T(2,128)(2,1)S(1)}, u32[]{:S(2)}, u32[]{:S(2)}) collective-permute-start(bf16[2,256]{1,0:T(2,128)(2,1)S(1)} %get-tuple-element.25), channel_id=1, source_target_pairs={{0,28},{4,0},{8,4},{12,8},{16,12},{20,16},{24,20},{28,24},{1,29},{... | collective-permute-start | bytes 3080 | tf_op jit(solution)/shard_map/ppermute | solution.py:21
  30.2 15.7 %collective-permute-start.7 = (bf16[256,256]{1,0:T(8,128)(2,1)S(1)}, bf16[256,256]{1,0:T(8,128)(2,1)S(1)}, u32[]{:S(2)}, u32[]{:S(2)}) collective-permute-start(bf16[256,256]{1,0:T(8,128)(2,1)S(1)} %get-tuple-element.22.second_ref), channel_id=1, source_target_pairs={{0,1},{1,2},{2,3},{4,5},{5,6},{6,7},{8,9},{9,10},{10,11},{12,13},{... | collective-permute-start | bytes 393224 | tf_op jit(solution)/shard_map/ppermute | solution.py:26
  32.9 13.0 %collective-permute-start.8 = (bf16[256,256]{1,0:T(8,128)(2,1)S(1)}, bf16[256,256]{1,0:T(8,128)(2,1)S(1)}, u32[]{:S(2)}, u32[]{:S(2)}) collective-permute-start(bf16[256,256]{1,0:T(8,128)(2,1)S(1)} %get-tuple-element.23.first_ref), channel_id=1, source_target_pairs={{1,0},{2,1},{3,2},{5,4},{6,5},{7,6},{9,8},{10,9},{11,10},{13,12},{... | collective-permute-start | bytes 393224 | tf_op jit(solution)/shard_map/ppermute | solution.py:26
  37.0 6.5 %collective-permute-start.12 = (bf16[2,256]{1,0:T(2,128)(2,1)S(1)}, bf16[2,256]{1,0:T(2,128)(2,1)S(1)}, u32[]{:S(2)}, u32[]{:S(2)}) collective-permute-start(bf16[2,256]{1,0:T(2,128)(2,1)S(1)} %get-tuple-element.47), channel_id=1, source_target_pairs={{1,0},{2,1},{3,2},{5,4},{6,5},{7,6},{9,8},{10,9},{11,10},{13,12},{... | collective-permute-start | bytes 3080 | tf_op jit(solution)/shard_map/ppermute | solution.py:26
  39.6 6.4 %collective-permute-start.11 = (bf16[2,256]{1,0:T(2,128)(2,1)S(1)}, bf16[2,256]{1,0:T(2,128)(2,1)S(1)}, u32[]{:S(2)}, u32[]{:S(2)}) collective-permute-start(bf16[2,256]{1,0:T(2,128)(2,1)S(1)} %get-tuple-element.48), channel_id=1, source_target_pairs={{0,1},{1,2},{2,3},{4,5},{5,6},{6,7},{8,9},{9,10},{10,11},{12,13},{... | collective-permute-start | bytes 3080 | tf_op jit(solution)/shard_map/ppermute | solution.py:26

commit v2 on v1

v2 whole, which is shorter than its diff:
```python
import functools
import math

import jax
import jax.numpy as jnp
from jax import lax
from jax.experimental import pallas as pl
from jax.experimental.pallas import tpu as pltpu
from jax.sharding import PartitionSpec as P

HEADS = 8
REACH = 2
PAD = 16
BF16 = jnp.bfloat16
F32 = jnp.float32
VMEM = pltpu.VMEM
SMEM = pltpu.SMEM
HBM = pltpu.HBM


def same_chip(i, n):
    return i ^ 1


def next_chip(i, n):
    return (i + 1 if i % 2 else i - 1) % n


def two_on(i, n):
    return (i + 2 if i // 2 % 2 == 0 else i - 2) % n


def two_back(i, n):
    return (i - 2 if i // 2 % 2 == 0 else i + 2) % n


def inner_pair(i, n):
    return i if i in (0, n - 1) else next_chip(i, n)


def swap(x, axis, partner):
    n = lax.axis_size(axis)
    return lax.ppermute(x, axis, [(i, partner(i, n)) for i in range(n)])


def sent_offset(az, piece):
    odd, odd_chip = lax.rem(az, 2), lax.rem(lax.div(az, 2), 2)
    return (REACH, 3 - 2 * odd, 1 + 2 * odd, 4 - 4 * odd_chip, 4 * odd_chip)[piece]


MATCHES = (None, same_chip, next_chip, two_on, two_back)


def dot(a, b, contract=((1,), (0,))):
    return lax.dot_general(a, b, (contract, ((), ())), preferred_element_type=F32)


def rms(x):
    return x * lax.rsqrt(jnp.mean(x * x, axis=-1, keepdims=True) + 1e-06)


def call(body, outs, ins, name, cost, spaces=None, scratch=(), aliases=None):
    spaces = spaces or [VMEM] * len(ins)
    flops, transcendentals = cost
    moved = sum(x.size * x.dtype.itemsize for x in list(ins) + list(outs))
    ins = [
        pltpu.with_memory_space_constraint(x, HBM) if s == HBM else x
        for x, s in zip(ins, spaces)
    ]
    return pl.pallas_call(
        body,
        out_shape=outs,
        in_specs=[pl.BlockSpec(memory_space=s) for s in spaces],
        out_specs=[pl.BlockSpec(memory_space=VMEM) for _ in outs],
        scratch_shapes=list(scratch),
        input_output_aliases=aliases or {},
        compiler_params=pltpu.CompilerParams(vmem_limit_bytes=20 * 1024 * 1024),
        cost_estimate=pl.CostEstimate(
            flops=flops, bytes_accessed=moved, transcendentals=transcendentals
        ),
        name=name,
    )(*ins)


def gather_body(el_ref, az_ref, tokens_hbm, slots_hbm, *refs):
    out_refs, (tokens_ref, slots_ref, sems) = refs[:-3], refs[-3:]
    copies = [
        pltpu.make_async_copy(tokens_hbm, tokens_ref, sems.at[0]),
        pltpu.make_async_copy(slots_hbm, slots_ref, sems.at[1]),
    ]
    for c in copies:
        c.start()
    offsets, groups, capacity = slots_ref.shape
    rows = tokens_ref.shape[0]
    el, az = el_ref[0], az_ref[0]
    eye = lax.broadcasted_iota(jnp.int32, (capacity, capacity), 0) == lax.broadcasted_iota(
        jnp.int32, (capacity, capacity), 1
    )
    lane = lax.broadcasted_iota(jnp.int32, (capacity, rows), 1).astype(F32)
    for c in copies:
        c.wait()
    tokens = tokens_ref[...]
    for step in range(groups):
        target = lax.rem(el + step, groups)
        picks = []
        for piece in range(offsets):
            row = slots_ref[sent_offset(az, piece), pl.ds(target, 1), :].astype(F32)
            spread = jnp.broadcast_to(row, (capacity, capacity))
            column = jnp.sum(jnp.where(eye, spread, 0.0), axis=-1, keepdims=True)
            picks.append(jnp.where(column == lane, 1.0, 0.0))
        one_hot = jnp.concatenate(picks, axis=0).astype(BF16)
        chosen = dot(one_hot, tokens).astype(BF16)
        out_refs[step][...] = chosen.reshape(out_refs[step].shape)


def prepare_body(*refs, groups, capacity, weights):
    el_ref, az_ref, points_hbm, skip_hbm, idx_hbm, w_query_hbm = refs[:6]
    weight_hbm = refs[6 : 6 + weights]
    q_ref, bias_ref, points_ref, skip_ref = refs[6 + weights : 10 + weights]
    weight_refs = refs[10 + weights : 10 + 2 * weights]
    idx_ref, w_query_ref, sems = refs[10 + 2 * weights :]
    el, az = el_ref[0], az_ref[0]
    even = 1 - lax.rem(el, 2)
    cols = points_ref.shape[0] // 2
    first = [
        pltpu.make_async_copy(idx_hbm.at[even], idx_ref.at[0], sems.at[0]),
        pltpu.make_async_copy(idx_hbm.at[1 - even], idx_ref.at[1], sems.at[1]),
        pltpu.make_async_copy(w_query_hbm, w_query_ref, sems.at[2]),
        pltpu.make_async_copy(points_hbm.at[even], points_ref.at[pl.ds(0, cols)], sems.at[3]),
        pltpu.make_async_copy(points_hbm.at[1 - even], points_ref.at[pl.ds(cols, cols)], sems.at[4]),
    ]
    later = [
        pltpu.make_async_copy(skip_hbm.at[even], skip_ref.at[pl.ds(0, cols)], sems.at[5]),
        pltpu.make_async_copy(skip_hbm.at[1 - even], skip_ref.at[pl.ds(cols, cols)], sems.at[6]),
    ]
    for k in range(weights):
        later.append(pltpu.make_async_copy(weight_hbm[k], weight_refs[k], sems.at[7 + k]))
    for c in first + later:
        c.start()
    for c in first:
        c.wait()
    count, width = q_ref.shape[1], q_ref.shape[0]
    scale = math.log2(math.e) / math.sqrt(width // HEADS)
    query = dot(points_ref[...], w_query_ref[...]) * scale
    q_ref[...] = query.T.astype(BF16)
    near = idx_ref.shape[1]
    lanes = 128
    for piece in range(bias_ref.shape[0] // (groups * capacity)):
        offset = 2 * REACH - sent_offset(az, piece)
        for step in range(groups):
            source = lax.rem(el + groups - step, groups)
            low = (offset * groups + source) * capacity
            slot = low + lax.broadcasted_iota(jnp.int32, (capacity, lanes), 0)
            place = (piece * groups + step) * capacity
            for start in range(0, count, lanes):
                row, col = divmod(start, cols)
                total = jnp.zeros((capacity, lanes), F32)
                for n in range(near):
                    index = idx_ref[row, n : n + 1, col : col + lanes]
                    total = total + jnp.where(slot == index, 1.0, 0.0)
                bias_ref[place : place + capacity, start : start + lanes] = jnp.log2(total)
    for c in later:
        c.wait()


def main_body(az_ref, *refs, pieces):
    piece_refs = refs[:pieces]
    (
        q_ref,
        bias_ref,
        points_ref,
        skip_ref,
        w_key_ref,
        w_value_ref,
        w_out_ref,
        w_hid_ref,
        w_skip_ref,
        w_down_ref,
        joined_ref,
        near_ref,
        far_ref,
        inner_edge_ref,
        outer_edge_ref,
        att_ref,
    ) = refs[pieces:]
    width, count = q_ref.shape
    head_width = width // HEADS
    received = jnp.concatenate([r[...] for r in piece_refs], axis=0)
    table = received.shape[0]
    keys = dot(received, w_key_ref[...]).astype(BF16)
    normed_tokens = rms(received.astype(F32)).astype(BF16)
    values_t = dot(w_value_ref[...], normed_tokens, ((0,), (1,))).astype(BF16)
    ones = jnp.ones((16, table), BF16)
    for head in range(HEADS):
        low, high = head * head_width, (head + 1) * head_width
        scores = dot(keys[:, low:high], q_ref[low:high, :]) + bias_ref[...]
        top = jnp.max(scores, axis=0, keepdims=True)
        weights = jnp.exp2(scores - top).astype(BF16)
        lhs = jnp.concatenate([values_t[low:high, :], ones], axis=0)
        mixed = dot(lhs, weights)
        att_ref[low:high, :] = (mixed[:head_width] / mixed[head_width : head_width + 1]).astype(BF16)
    residual = points_ref[...].astype(F32) + dot(att_ref[...], w_out_ref[...], ((0,), (0,)))
    normed = rms(residual).astype(BF16)
    pre = dot(normed, w_hid_ref[...]) + dot(skip_ref[...], w_skip_ref[...])
    c1 = math.sqrt(2.0 / math.pi)
    half = 0.5 * pre
    inner = (half + half * jnp.tanh(pre * (c1 + (c1 * 0.044715) * (pre * pre)))).astype(BF16)
    joined = residual + dot(inner, w_down_ref[...])
    conv = rms(joined)
    joined_ref[...] = joined.reshape(joined_ref.shape)
    cols = count // 2
    near_ref[0:cols] = conv[:cols].astype(BF16)
    far_ref[0:cols] = conv[cols:].astype(BF16)
    left = jnp.concatenate([conv[0:1], conv[cols : cols + 1]], axis=0)
    right = jnp.concatenate([conv[cols - 1 : cols], conv[2 * cols - 1 :]], axis=0)
    odd = lax.rem(az_ref[0], 2) == 1
    inner_edge_ref[...] = jnp.where(odd, left, right).astype(BF16)
    outer_edge_ref[...] = jnp.where(odd, right, left).astype(BF16)


def pack_body(az_ref, inner_ref, outer_ref, near_in, far_in, near_ref, far_ref):
    del near_in, far_in
    odd = lax.rem(az_ref[0], 2) == 1
    inner, outer = inner_ref[...].astype(F32), outer_ref[...].astype(F32)
    right = jnp.where(odd, outer, inner)
    left = jnp.where(odd, inner, outer)
    cols, width = near_ref.shape[0] - PAD, near_ref.shape[1]
    row = lax.broadcasted_iota(jnp.int32, (PAD, width), 0)
    for at, ref in enumerate((near_ref, far_ref)):
        rows = jnp.where(row == 0, right[at : at + 1], 0.0)
        rows = jnp.where(row == PAD - 1, left[at : at + 1], rows)
        ref[cols:, :] = rows.astype(BF16)


def conv_rows(pairs, cols):
    taps = []
    for dc in range(3):
        total = None
        for x, w_ref, base in pairs:
            part = dot(x, w_ref[base + dc])
            total = part if total is None else total + part
        taps.append(total)
    length = taps[0].shape[0]
    shifted = taps[1] + pltpu.roll(taps[0], 1, 0) + pltpu.roll(taps[2], length - 1, 0)
    return shifted[:cols]


def inside_body(el_ref, near_ref, far_ref, joined_ref, w_ref, out_ref):
    odd = lax.rem(el_ref[0], 2)
    cols = joined_ref.shape[1]
    near, far = near_ref[...], far_ref[...]
    out_ref[0] = joined_ref[0] + conv_rows([(near, w_ref, 3), (far, w_ref, 6 * odd)], cols)
    out_ref[1] = joined_ref[1] + conv_rows([(far, w_ref, 3), (near, w_ref, 6 - 6 * odd)], cols)


def border_body(el_ref, near_ref, far_ref, part_ref, w_ref, out_ref, *, last):
    el = el_ref[0]
    odd = lax.rem(el, 2)
    cols = part_ref.shape[1]
    near = part_ref[0] + conv_rows([(near_ref[...], w_ref, 6 - 6 * odd)], cols)
    out_ref[1 - odd] = near.astype(BF16)
    far = conv_rows([(far_ref[...], w_ref, 6 * odd)], cols)
    ends = jnp.logical_or(el == 0, el == last)
    out_ref[odd] = (part_ref[1] + jnp.where(ends, 0.0, far)).astype(BF16)


def per_device(
    points,
    skip,
    tokens,
    send_slots,
    recv_idx,
    w_query,
    w_key,
    w_value,
    w_out,
    w_hid,
    w_skip,
    w_down,
    w_conv,
):
    rows, cols, width = points.shape
    count = rows * cols
    own_tokens = tokens[0, 0]
    slots = send_slots[0, 0]
    offsets, groups, capacity = slots.shape
    table = offsets * groups * capacity
    el = lax.axis_index("el").astype(jnp.int32).reshape(1)
    az = lax.axis_index("az").astype(jnp.int32).reshape(1)
    shape = jax.ShapeDtypeStruct
    dma = pltpu.SemaphoreType.DMA
    sent = call(
        gather_body,
        [shape((offsets, capacity, width), BF16)] * groups,
        [el, az, own_tokens, slots],
        "gather",
        (2 * table * own_tokens.shape[0] * width, 0),
        [SMEM, SMEM, HBM, HBM],
        [VMEM(own_tokens.shape, BF16), VMEM(slots.shape, jnp.int32), dma((2,))],
    )
    got = [sent[0]]
    for s in range(1, groups):
        got.append(swap(sent[s], "el", lambda i, n, s=s: (i + s) % n))
    pieces = []
    for piece in range(offsets):
        bundle = jnp.concatenate([g[piece] for g in got], axis=0)
        pieces.append(swap(bundle, "az", MATCHES[piece]) if piece else bundle)
    weights = [w_key, w_value, w_out, w_hid, w_skip, w_down, w_conv]
    idx = jnp.swapaxes(recv_idx, 1, 2)
    query_t, bias, points_v, skip_v, *held = call(
        functools.partial(prepare_body, groups=groups, capacity=capacity, weights=len(weights)),
        [
            shape((width, count), BF16),
            shape((table, count), F32),
            shape((count, width), BF16),
            shape((count, width), BF16),
        ]
        + [shape(w.shape, BF16) for w in weights],
        [el, az, points, skip, idx, w_query] + weights,
        "prepare",
        (table * count * 48, table * count),
        [SMEM, SMEM] + [HBM] * (4 + len(weights)),
        [VMEM(idx.shape, jnp.int32), VMEM(w_query.shape, BF16), dma((7 + len(weights),))],
    )
    joined, near, far, inner_edge, outer_edge = call(
        functools.partial(main_body, pieces=len(pieces)),
        [
            shape((rows, cols, width), F32),
            shape((cols + PAD, width), BF16),
            shape((cols + PAD, width), BF16),
            shape((2, width), BF16),
            shape((2, width), BF16),
        ],
        [az] + pieces + [query_t, bias, points_v, skip_v] + held[:-1],
        "main",
        (10 * table * count * width + 2 * count * width * 13 * width, table * count * HEADS),
        [SMEM] + [VMEM] * (len(pieces) + 10),
        [VMEM((width, count), BF16)],
    )
    outer_got = swap(outer_edge, "az", next_chip)
    inner_got = swap(inner_edge, "az", same_chip)
    near, far = call(
        pack_body,
        [shape((cols + PAD, width), BF16)] * 2,
        [az, inner_got, outer_got, near, far],
        "pack",
        (4 * PAD * width, 0),
        [SMEM] + [VMEM] * 4,
        (),
        {3: 0, 4: 1},
    )
    far_got = swap(far, "el", inner_pair)
    near_got = swap(near, "el", same_chip)
    (partial,) = call(
        inside_body,
        [shape((rows, cols, width), F32)],
        [el, near, far, joined, held[-1]],
        "inside",
        (2 * count * width * width * 6, 0),
        [SMEM] + [VMEM] * 4,
    )
    (out,) = call(
        functools.partial(border_body, last=lax.axis_size("el") - 1),
        [shape((rows, cols, width), BF16)],
        [el, near_got, far_got, partial, held[-1]],
        "border",
        (2 * count * width * width * 3, 0),
        [SMEM] + [VMEM] * 4,
    )
    return out


def solution(mesh):
    return jax.shard_map(
        per_device,
        mesh=mesh,
        in_specs=(
            P("el", "az", None),
            P("el", "az", None),
            P("az", "el", None, None),
            P("az", "el", None, None, None),
            P("el", "az", None),
            P(),
            P(),
            P(),
            P(),
            P(),
            P(),
            P(),
            P(),
        ),
        out_specs=P("el", "az", None),
        check_vma=False,
    )
```

time: 47.6 us -> 37.7 us (0.79)
  the two profiles are of different devices: /device:TPU:4 before, /device:TPU:2 now
where the time goes in v2:
time: 37.7 us; the launch traced here: 37 us
  starting transfers between devices  15 us (40%)
  waiting for transfers between devices  12.3 us (33%)
  Pallas kernels  9.57 us (25%)
    ppermute x11, starting transfers between devices, swap(): return lax.ppermute(x, axis, [(i, partner(i, n)) for i in range(n)])  15 us
    ppermute x11, waiting for transfers between devices, swap(): return lax.ppermute(x, axis, [(i, partner(i, n)) for i in range(n)])  12.3 us
    pallas_call x6, Pallas kernels, call(): pl.pallas_call(body, out_shape=outs, in_specs=[pl.BlockSpec(memory_space=...  9.57 us
  transfers between devices with their start and end apart: 11, of which 6 were waited for; matrix products, arithmetic and copies ran while one was open for 0% of the time, Pallas kernels for 8%

profile of v2, /device:TPU:2, one launch (start us, length us, event | category | flops | bytes accessed | tf_op | source)
XLA Modules:
  0.0 37.0 jit_solution(11311461516374424418)
XLA Ops:
  0.0 1.1 %gather.1 = (bf16[5,16,256]{2,1,0:T(8,128)(2,1)S(1)}, bf16[5,16,256]{2,1,0:T(8,128)(2,1)S(1)}, bf16[5,16,256]{2,1,0:T(8,128)(2,1)S(1)}, bf16[5,16,256]{2,1,0:T(8,128)(2,1)S(1)}) custom-call(s32[1]{0:T(128)} %bitcast.el_ref.refs_0_, s32[1]{0:T(128)} %bitcast.1.az_ref.refs_1_, bf16[128,256]{1,0:T(8,128)(2,1)} %bitcast.46, s32[5,4,16]{2,1,0:T(4,128)} %bitcast.47), custom_call_target="tpu_custom_call" | custom-call | flops 20971520 | bytes 230664 | tf_op jit(solution)/shard_map/gather/pallas_call | solution.py:70
  1.1 1.5 %collective-permute-start = (bf16[5,16,256]{2,1,0:T(8,128)(2,1)S(1)}, bf16[5,16,256]{2,1,0:T(8,128)(2,1)S(1)}, u32[]{:S(2)}, u32[]{:S(2)}) collective-permute-start(bf16[5,16,256]{2,1,0:T(8,128)(2,1)S(1)} %get-tuple-element.28), channel_id=1, source_target_pairs={{0,1},{1,2},{2,3},{3,0},{4,5},{5,6},{6,7},{7,4},{8,9},{9,10},{10,1... | collective-permute-start | bytes 122888 | tf_op jit(solution)/shard_map/ppermute | solution.py:43
  2.7 0.1 collective-permute-start.1
  2.8 1.9 %collective-permute-start.2 = (bf16[5,16,256]{2,1,0:T(8,128)(2,1)S(1)}, bf16[5,16,256]{2,1,0:T(8,128)(2,1)S(1)}, u32[]{:S(2)}, u32[]{:S(2)}) collective-permute-start(bf16[5,16,256]{2,1,0:T(8,128)(2,1)S(1)} %get-tuple-element.30), channel_id=1, source_target_pairs={{0,3},{1,0},{2,1},{3,2},{4,7},{5,4},{6,5},{7,6},{8,11},{9,8},{10,9... | collective-permute-start | bytes 122888 | tf_op jit(solution)/shard_map/ppermute | solution.py:43
  4.7 2.4 %prepare.1 = (bf16[256,512]{1,0:T(8,128)(2,1)S(1)}, f32[320,512]{1,0:T(8,128)S(1)}, bf16[512,256]{1,0:T(8,128)(2,1)S(1)}, bf16[512,256]{1,0:T(8,128)(2,1)S(1)}, ...) custom-call(s32[1]{0:T(128)} %bitcast.el_ref.refs_0_, ...), custom_call_target="tpu_custom_call" | custom-call | flops 7864320 | bytes 8421384 | tf_op jit(solution)/shard_map/prepare/pallas_call | solution.py:70
  7.1 0.0 collective-permute-done
  7.1 0.0 collective-permute-done.1
  7.2 0.5 %collective-permute-done.2 = bf16[5,16,256]{2,1,0:T(8,128)(2,1)S(1)} collective-permute-done((bf16[5,16,256]{2,1,0:T(8,128)(2,1)S(1)}, bf16[5,16,256]{2,1,0:T(8,128)(2,1)S(1)}, u32[]{:S(2)}, u32[]{:S(2)}) %collective-permute-start.2) | collective-permute-done | bytes 40992 | tf_op jit(solution)/shard_map/ppermute | solution.py:43
  7.7 0.1 collective-permute-start.3
  7.8 4.1 %collective-permute-start.4 = (bf16[64,256]{1,0:T(8,128)(2,1)S(1)}, bf16[64,256]{1,0:T(8,128)(2,1)S(1)}, u32[]{:S(2)}, u32[]{:S(2)}) collective-permute-start(bf16[64,256]{1,0:T(8,128)(2,1)S(1)} %pad_maximum_fusion.2), channel_id=1, source_target_pairs={{0,28},{4,8},{8,4},{12,16},{16,12},{20,24},{24,20},{28,0},{1,29},{... | collective-permute-start | bytes 98312 | tf_op jit(solution)/shard_map/ppermute | solution.py:43
  11.9 0.0 collective-permute-start.5
  11.9 0.9 %collective-permute-start.6 = (bf16[64,256]{1,0:T(8,128)(2,1)S(1)}, bf16[64,256]{1,0:T(8,128)(2,1)S(1)}, u32[]{:S(2)}, u32[]{:S(2)}) collective-permute-start(bf16[64,256]{1,0:T(8,128)(2,1)S(1)} %pad_maximum_fusion.4), channel_id=1, source_target_pairs={{0,24},{4,28},{8,16},{12,20},{16,8},{20,12},{24,0},{28,4},{1,25},{... | collective-permute-start | bytes 98312 | tf_op jit(solution)/shard_map/ppermute | solution.py:43
  12.8 0.0 collective-permute-done.3.refs_1_
  12.8 0.8 %collective-permute-done.4.refs_2_ = bf16[64,256]{1,0:T(8,128)(2,1)S(1)} collective-permute-done((bf16[64,256]{1,0:T(8,128)(2,1)S(1)}, bf16[64,256]{1,0:T(8,128)(2,1)S(1)}, u32[]{:S(2)}, u32[]{:S(2)}) %collective-permute-start.4) | collective-permute-done | bytes 32800 | tf_op jit(solution)/shard_map/ppermute | solution.py:43
  13.6 2.6 %collective-permute-done.5.refs_3_ = bf16[64,256]{1,0:T(8,128)(2,1)S(1)} collective-permute-done((bf16[64,256]{1,0:T(8,128)(2,1)S(1)}, bf16[64,256]{1,0:T(8,128)(2,1)S(1)}, u32[]{:S(2)}, u32[]{:S(2)}) %collective-permute-start.5) | collective-permute-done | bytes 32800 | tf_op jit(solution)/shard_map/ppermute | solution.py:43
  16.1 1.5 %collective-permute-done.6.refs_4_ = bf16[64,256]{1,0:T(8,128)(2,1)S(1)} collective-permute-done((bf16[64,256]{1,0:T(8,128)(2,1)S(1)}, bf16[64,256]{1,0:T(8,128)(2,1)S(1)}, u32[]{:S(2)}, u32[]{:S(2)}) %collective-permute-start.6) | collective-permute-done | bytes 32800 | tf_op jit(solution)/shard_map/ppermute | solution.py:43
  17.7 4.3 %main.1 = (f32[2,256,256]{2,1,0:T(8,128)S(1)}, bf16[272,256]{1,0:T(8,128)(2,1)S(1)}, bf16[272,256]{1,0:T(8,128)(2,1)S(1)}, bf16[2,256]{1,0:T(2,128)(2,1)S(1)}, bf16[2,256]{1,0:T(2,128)(2,1)S(1)}) custom-call(s32[1]{0:T(128)} %bitcast.1.az_ref.refs_1_, bf16[64,256]{1,0:T(8,128)(2,1)S(1)} %pad_maximum_fusion.refs_0_, ...), custom_call_target="tpu_custom_call" | custom-call | flops 1291845632 | bytes 4376580 | tf_op jit(solution)/shard_map/main/pallas_call | solution.py:70
  22.0 0.1 collective-permute-start.7
  22.1 1.3 %collective-permute-start.8 = (bf16[2,256]{1,0:T(2,128)(2,1)S(1)}, bf16[2,256]{1,0:T(2,128)(2,1)S(1)}, u32[]{:S(2)}, u32[]{:S(2)}) collective-permute-start(bf16[2,256]{1,0:T(2,128)(2,1)S(1)} %get-tuple-element.42), channel_id=1, source_target_pairs={{0,28},{4,8},{8,4},{12,16},{16,12},{20,24},{24,20},{28,0},{1,29},{... | collective-permute-start | bytes 3080 | tf_op jit(solution)/shard_map/ppermute | solution.py:43
  23.4 0.0 collective-permute-done.7.inner_ref
  23.4 3.6 %collective-permute-done.8.outer_ref = bf16[2,256]{1,0:T(2,128)(2,1)S(1)} collective-permute-done((bf16[2,256]{1,0:T(2,128)(2,1)S(1)}, bf16[2,256]{1,0:T(2,128)(2,1)S(1)}, u32[]{:S(2)}, u32[]{:S(2)}) %collective-permute-start.8) | collective-permute-done | bytes 1056 | tf_op jit(solution)/shard_map/ppermute | solution.py:43
  27.0 0.7 %collective-permute-start.9 = (bf16[272,256]{1,0:T(8,128)(2,1)S(1)}, bf16[272,256]{1,0:T(8,128)(2,1)S(1)}, u32[]{:S(2)}, u32[]{:S(2)}) collective-permute-start(bf16[272,256]{1,0:T(8,128)(2,1)S(1)} %get-tuple-element.45.near_ref), channel_id=1, source_target_pairs={{0,1},{1,0},{2,3},{3,2},{4,5},{5,4},{6,7},{7,6},{8,9},{9,8},{10,11... | collective-permute-start | bytes 417800 | tf_op jit(solution)/shard_map/ppermute | solution.py:43
  27.7 4.2 %collective-permute-start.10 = (bf16[272,256]{1,0:T(8,128)(2,1)S(1)}, bf16[272,256]{1,0:T(8,128)(2,1)S(1)}, u32[]{:S(2)}, u32[]{:S(2)}) collective-permute-start(bf16[272,256]{1,0:T(8,128)(2,1)S(1)} %get-tuple-element.46.far_ref), channel_id=1, source_target_pairs={{0,0},{1,2},{2,1},{3,3},{4,4},{5,6},{6,5},{7,7},{8,8},{9,10},{10,9... | collective-permute-start | bytes 417800 | tf_op jit(solution)/shard_map/ppermute | solution.py:43
  31.9 0.6 %inside.1.part_ref = f32[2,256,256]{2,1,0:T(8,128)S(1)} custom-call(s32[1]{0:T(128)} %bitcast.el_ref.refs_0_, bf16[272,256]{1,0:T(8,128)(2,1)S(1)} %get-tuple-element.45.near_ref, bf16[272,256]{1,0:T(8,128)(2,1)S(1)} %get-tuple-element.46.far_ref, f32[2,256,256]{2,1,0:T(8,128)S(1)} %get-tuple-element.47.joined_ref, ...), custom_call_target="tpu_custom_call" | custom-call | flops 402653184 | bytes 2506756 | tf_op jit(solution)/shard_map/inside/pallas_call | solution.py:70
  32.5 0.0 collective-permute-done.9.near_ref
  32.5 3.3 %collective-permute-done.10.far_ref = bf16[272,256]{1,0:T(8,128)(2,1)S(1)} collective-permute-done((bf16[272,256]{1,0:T(8,128)(2,1)S(1)}, bf16[272,256]{1,0:T(8,128)(2,1)S(1)}, u32[]{:S(2)}, u32[]{:S(2)}) %collective-permute-start.10) | collective-permute-done | bytes 139296 | tf_op jit(solution)/shard_map/ppermute | solution.py:43
  35.9 1.1 %border.1 = bf16[2,256,256]{2,1,0:T(8,128)(2,1)} custom-call(s32[1]{0:T(128)} %bitcast.el_ref.refs_0_, bf16[272,256]{1,0:T(8,128)(2,1)S(1)} %collective-permute-done.9.near_ref, bf16[272,256]{1,0:T(8,128)(2,1)S(1)} %collective-permute-done.10.far_ref, f32[2,256,256]{2,1,0:T(8,128)S(1)} %inside.1.part_ref, bf16[9,256,256]{2,1,0:T(8,128)(2,1)S(1)} %get-tuple-element.48.w_ref), custom_call_target="tpu_custom_call" | custom-call | flops 201326592 | bytes 2244612 | tf_op jit(solution)/shard_map/border/pallas_call | solution.py:70
  (10 shorter events, 0.1 us)
Async XLA Ops:
  1.1 6.0 %collective-permute-start = (bf16[5,16,256]{2,1,0:T(8,128)(2,1)S(1)}, bf16[5,16,256]{2,1,0:T(8,128)(2,1)S(1)}, u32[]{:S(2)}, u32[]{:S(2)}) collective-permute-start(bf16[5,16,256]{2,1,0:T(8,128)(2,1)S(1)} %get-tuple-element.28), channel_id=1, source_target_pairs={{0,1},{1,2},{2,3},{3,0},{4,5},{5,6},{6,7},{7,4},{8,9},{9,10},{10,1... | collective-permute-start | bytes 122888 | tf_op jit(solution)/shard_map/ppermute | solution.py:43
  2.7 4.5 %collective-permute-start.1 = (bf16[5,16,256]{2,1,0:T(8,128)(2,1)S(1)}, bf16[5,16,256]{2,1,0:T(8,128)(2,1)S(1)}, u32[]{:S(2)}, u32[]{:S(2)}) collective-permute-start(bf16[5,16,256]{2,1,0:T(8,128)(2,1)S(1)} %get-tuple-element.29), channel_id=1, source_target_pairs={{0,2},{1,3},{2,0},{3,1},{4,6},{5,7},{6,4},{7,5},{8,10},{9,11},{10,... | collective-permute-start | bytes 122888 | tf_op jit(solution)/shard_map/ppermute | solution.py:43
  2.8 4.9 %collective-permute-start.2 = (bf16[5,16,256]{2,1,0:T(8,128)(2,1)S(1)}, bf16[5,16,256]{2,1,0:T(8,128)(2,1)S(1)}, u32[]{:S(2)}, u32[]{:S(2)}) collective-permute-start(bf16[5,16,256]{2,1,0:T(8,128)(2,1)S(1)} %get-tuple-element.30), channel_id=1, source_target_pairs={{0,3},{1,0},{2,1},{3,2},{4,7},{5,4},{6,5},{7,6},{8,11},{9,8},{10,9... | collective-permute-start | bytes 122888 | tf_op jit(solution)/shard_map/ppermute | solution.py:43
  7.7 5.1 %collective-permute-start.3 = (bf16[64,256]{1,0:T(8,128)(2,1)S(1)}, bf16[64,256]{1,0:T(8,128)(2,1)S(1)}, u32[]{:S(2)}, u32[]{:S(2)}) collective-permute-start(bf16[64,256]{1,0:T(8,128)(2,1)S(1)} %pad_maximum_fusion.1), channel_id=1, source_target_pairs={{0,4},{4,0},{8,12},{12,8},{16,20},{20,16},{24,28},{28,24},{1,5},{5... | collective-permute-start | bytes 98312 | tf_op jit(solution)/shard_map/ppermute | solution.py:43
  7.8 5.8 %collective-permute-start.4 = (bf16[64,256]{1,0:T(8,128)(2,1)S(1)}, bf16[64,256]{1,0:T(8,128)(2,1)S(1)}, u32[]{:S(2)}, u32[]{:S(2)}) collective-permute-start(bf16[64,256]{1,0:T(8,128)(2,1)S(1)} %pad_maximum_fusion.2), channel_id=1, source_target_pairs={{0,28},{4,8},{8,4},{12,16},{16,12},{20,24},{24,20},{28,0},{1,29},{... | collective-permute-start | bytes 98312 | tf_op jit(solution)/shard_map/ppermute | solution.py:43
  11.9 4.3 %collective-permute-start.5 = (bf16[64,256]{1,0:T(8,128)(2,1)S(1)}, bf16[64,256]{1,0:T(8,128)(2,1)S(1)}, u32[]{:S(2)}, u32[]{:S(2)}) collective-permute-start(bf16[64,256]{1,0:T(8,128)(2,1)S(1)} %pad_maximum_fusion.3), channel_id=1, source_target_pairs={{0,8},{4,12},{8,0},{12,4},{16,24},{20,28},{24,16},{28,20},{1,9},{5... | collective-permute-start | bytes 98312 | tf_op jit(solution)/shard_map/ppermute | solution.py:43
  11.9 5.8 %collective-permute-start.6 = (bf16[64,256]{1,0:T(8,128)(2,1)S(1)}, bf16[64,256]{1,0:T(8,128)(2,1)S(1)}, u32[]{:S(2)}, u32[]{:S(2)}) collective-permute-start(bf16[64,256]{1,0:T(8,128)(2,1)S(1)} %pad_maximum_fusion.4), channel_id=1, source_target_pairs={{0,24},{4,28},{8,16},{12,20},{16,8},{20,12},{24,0},{28,4},{1,25},{... | collective-permute-start | bytes 98312 | tf_op jit(solution)/shard_map/ppermute | solution.py:43
  22.0 1.4 %collective-permute-start.7 = (bf16[2,256]{1,0:T(2,128)(2,1)S(1)}, bf16[2,256]{1,0:T(2,128)(2,1)S(1)}, u32[]{:S(2)}, u32[]{:S(2)}) collective-permute-start(bf16[2,256]{1,0:T(2,128)(2,1)S(1)} %get-tuple-element.41), channel_id=1, source_target_pairs={{0,4},{4,0},{8,12},{12,8},{16,20},{20,16},{24,28},{28,24},{1,5},{5... | collective-permute-start | bytes 3080 | tf_op jit(solution)/shard_map/ppermute | solution.py:43
  22.1 4.9 %collective-permute-start.8 = (bf16[2,256]{1,0:T(2,128)(2,1)S(1)}, bf16[2,256]{1,0:T(2,128)(2,1)S(1)}, u32[]{:S(2)}, u32[]{:S(2)}) collective-permute-start(bf16[2,256]{1,0:T(2,128)(2,1)S(1)} %get-tuple-element.42), channel_id=1, source_target_pairs={{0,28},{4,8},{8,4},{12,16},{16,12},{20,24},{24,20},{28,0},{1,29},{... | collective-permute-start | bytes 3080 | tf_op jit(solution)/shard_map/ppermute | solution.py:43
  27.0 5.6 %collective-permute-start.9 = (bf16[272,256]{1,0:T(8,128)(2,1)S(1)}, bf16[272,256]{1,0:T(8,128)(2,1)S(1)}, u32[]{:S(2)}, u32[]{:S(2)}) collective-permute-start(bf16[272,256]{1,0:T(8,128)(2,1)S(1)} %get-tuple-element.45.near_ref), channel_id=1, source_target_pairs={{0,1},{1,0},{2,3},{3,2},{4,5},{5,4},{6,7},{7,6},{8,9},{9,8},{10,11... | collective-permute-start | bytes 417800 | tf_op jit(solution)/shard_map/ppermute | solution.py:43
  27.7 8.2 %collective-permute-start.10 = (bf16[272,256]{1,0:T(8,128)(2,1)S(1)}, bf16[272,256]{1,0:T(8,128)(2,1)S(1)}, u32[]{:S(2)}, u32[]{:S(2)}) collective-permute-start(bf16[272,256]{1,0:T(8,128)(2,1)S(1)} %get-tuple-element.46.far_ref), channel_id=1, source_target_pairs={{0,0},{1,2},{2,1},{3,3},{4,4},{5,6},{6,5},{7,7},{8,8},{9,10},{10,9... | collective-permute-start | bytes 417800 | tf_op jit(solution)/shard_map/ppermute | solution.py:43

commit v3 on v2

--- a/solution.py
+++ b/solution.py
@@ -45,10 +45,10 @@
 
 def sent_offset(az, piece):
     odd, odd_chip = lax.rem(az, 2), lax.rem(lax.div(az, 2), 2)
-    return (REACH, 3 - 2 * odd, 1 + 2 * odd, 4 - 4 * odd_chip, 4 * odd_chip)[piece]
-
-
-MATCHES = (None, same_chip, next_chip, two_on, two_back)
+    return (REACH, 4 * odd_chip, 1 + 2 * odd, 4 - 4 * odd_chip, 3 - 2 * odd)[piece]
+
+
+MATCHES = (None, two_back, next_chip, two_on, same_chip)
 
 
 def dot(a, b, contract=((1,), (0,))):
@@ -114,11 +114,11 @@
 
 
 def prepare_body(*refs, groups, capacity, weights):
-    el_ref, az_ref, points_hbm, skip_hbm, idx_hbm, w_query_hbm = refs[:6]
-    weight_hbm = refs[6 : 6 + weights]
-    q_ref, bias_ref, points_ref, skip_ref = refs[6 + weights : 10 + weights]
-    weight_refs = refs[10 + weights : 10 + 2 * weights]
-    idx_ref, w_query_ref, sems = refs[10 + 2 * weights :]
+    el_ref, az_ref, points_hbm, skip_hbm, idx_hbm, w_query_hbm, w_skip_hbm = refs[:7]
+    weight_hbm = refs[7 : 7 + weights]
+    q_ref, bias_ref, points_ref, side_ref = refs[8 + weights : 12 + weights]
+    weight_refs = refs[12 + weights : 12 + 2 * weights]
+    idx_ref, w_query_ref, skip_ref, w_skip_ref, sems = refs[12 + 2 * weights :]
     el, az = el_ref[0], az_ref[0]
     even = 1 - lax.rem(el, 2)
     cols = points_ref.shape[0] // 2
@@ -132,9 +132,10 @@
     later = [
         pltpu.make_async_copy(skip_hbm.at[even], skip_ref.at[pl.ds(0, cols)], sems.at[5]),
         pltpu.make_async_copy(skip_hbm.at[1 - even], skip_ref.at[pl.ds(cols, cols)], sems.at[6]),
+        pltpu.make_async_copy(w_skip_hbm, w_skip_ref, sems.at[7]),
     ]
     for k in range(weights):
-        later.append(pltpu.make_async_copy(weight_hbm[k], weight_refs[k], sems.at[7 + k]))
+        later.append(pltpu.make_async_copy(weight_hbm[k], weight_refs[k], sems.at[8 + k]))
     for c in first + later:
         c.start()
     for c in first:
@@ -161,6 +162,7 @@
                 bias_ref[place : place + capacity, start : start + lanes] = jnp.log2(total)
     for c in later:
         c.wait()
+    side_ref[...] = dot(skip_ref[...], w_skip_ref[...])
 
 
 def main_body(az_ref, *refs, pieces):
@@ -169,12 +171,11 @@
         q_ref,
         bias_ref,
         points_ref,
-        skip_ref,
+        side_ref,
         w_key_ref,
         w_value_ref,
         w_out_ref,
         w_hid_ref,
-        w_skip_ref,
         w_down_ref,
         joined_ref,
         near_ref,
@@ -201,7 +202,7 @@
         att_ref[low:high, :] = (mixed[:head_width] / mixed[head_width : head_width + 1]).astype(BF16)
     residual = points_ref[...].astype(F32) + dot(att_ref[...], w_out_ref[...], ((0,), (0,)))
     normed = rms(residual).astype(BF16)
-    pre = dot(normed, w_hid_ref[...]) + dot(skip_ref[...], w_skip_ref[...])
+    pre = dot(normed, w_hid_ref[...]) + side_ref[...]
     c1 = math.sqrt(2.0 / math.pi)
     half = 0.5 * pre
     inner = (half + half * jnp.tanh(pre * (c1 + (c1 * 0.044715) * (pre * pre)))).astype(BF16)
@@ -305,22 +306,28 @@
     for piece in range(offsets):
         bundle = jnp.concatenate([g[piece] for g in got], axis=0)
         pieces.append(swap(bundle, "az", MATCHES[piece]) if piece else bundle)
-    weights = [w_key, w_value, w_out, w_hid, w_skip, w_down, w_conv]
+    weights = [w_key, w_value, w_out, w_hid, w_down, w_conv]
     idx = jnp.swapaxes(recv_idx, 1, 2)
-    query_t, bias, points_v, skip_v, *held = call(
+    query_t, bias, points_v, side, *held = call(
         functools.partial(prepare_body, groups=groups, capacity=capacity, weights=len(weights)),
         [
             shape((width, count), BF16),
             shape((table, count), F32),
             shape((count, width), BF16),
-            shape((count, width), BF16),
+            shape((count, w_skip.shape[1]), F32),
         ]
         + [shape(w.shape, BF16) for w in weights],
-        [el, az, points, skip, idx, w_query] + weights,
+        [el, az, points, skip, idx, w_query, w_skip] + weights + [pieces[0]],
         "prepare",
         (table * count * 48, table * count),
-        [SMEM, SMEM] + [HBM] * (4 + len(weights)),
-        [VMEM(idx.shape, jnp.int32), VMEM(w_query.shape, BF16), dma((7 + len(weights),))],
+        [SMEM, SMEM] + [HBM] * (5 + len(weights)) + [VMEM],
+        [
+            VMEM(idx.shape, jnp.int32),
+            VMEM(w_query.shape, BF16),
+            VMEM((count, width), BF16),
+            VMEM(w_skip.shape, BF16),
+            dma((8 + len(weights),)),
+        ],
     )
     joined, near, far, inner_edge, outer_edge = call(
         functools.partial(main_body, pieces=len(pieces)),
@@ -331,10 +338,10 @@
             shape((2, width), BF16),
             shape((2, width), BF16),
         ],
-        [az] + pieces + [query_t, bias, points_v, skip_v] + held[:-1],
+        [az] + pieces + [query_t, bias, points_v, side] + held[:-1],
         "main",
         (10 * table * count * width + 2 * count * width * 13 * width, table * count * HEADS),
-        [SMEM] + [VMEM] * (len(pieces) + 10),
+        [SMEM] + [VMEM] * (len(pieces) + 9),
         [VMEM((width, count), BF16)],
     )
     outer_got = swap(outer_edge, "az", next_chip)

time: 37.7 us -> 37 us (0.981)
  the two profiles are of different devices: /device:TPU:2 before, /device:TPU:4 now
where the time goes in v3:
time: 37 us; the launch traced here: 36.7 us
  starting transfers between devices  13.8 us (37%)
  waiting for transfers between devices  12.7 us (34%)
  Pallas kernels  10 us (27%)
    ppermute x11, starting transfers between devices, swap(): return lax.ppermute(x, axis, [(i, partner(i, n)) for i in range(n)])  13.8 us
    ppermute x11, waiting for transfers between devices, swap(): return lax.ppermute(x, axis, [(i, partner(i, n)) for i in range(n)])  12.7 us
    pallas_call x6, Pallas kernels, call(): pl.pallas_call(body, out_shape=outs, in_specs=[pl.BlockSpec(memory_space=...  10 us
  transfers between devices with their start and end apart: 11, of which 7 were waited for; matrix products, arithmetic and copies ran while one was open for 0% of the time, Pallas kernels for 9%

profile of v3, /device:TPU:4, one launch (start us, length us, event | category | flops | bytes accessed | tf_op | source)
XLA Modules:
  0.0 36.7 jit_solution(11720087380888567469)
XLA Ops:
  0.0 1.1 %gather.1 = (bf16[5,16,256]{2,1,0:T(8,128)(2,1)S(1)}, bf16[5,16,256]{2,1,0:T(8,128)(2,1)S(1)}, bf16[5,16,256]{2,1,0:T(8,128)(2,1)S(1)}, bf16[5,16,256]{2,1,0:T(8,128)(2,1)S(1)}) custom-call(s32[1]{0:T(128)} %bitcast.el_ref.refs_0_, s32[1]{0:T(128)} %bitcast.1.az_ref.refs_1_, bf16[128,256]{1,0:T(8,128)(2,1)} %bitcast.46, s32[5,4,16]{2,1,0:T(4,128)} %bitcast.47), custom_call_target="tpu_custom_call" | custom-call | flops 20971520 | bytes 230664 | tf_op jit(solution)/shard_map/gather/pallas_call | solution.py:70
  1.1 1.5 %collective-permute-start = (bf16[5,16,256]{2,1,0:T(8,128)(2,1)S(1)}, bf16[5,16,256]{2,1,0:T(8,128)(2,1)S(1)}, u32[]{:S(2)}, u32[]{:S(2)}) collective-permute-start(bf16[5,16,256]{2,1,0:T(8,128)(2,1)S(1)} %get-tuple-element.27), channel_id=1, source_target_pairs={{0,1},{1,2},{2,3},{3,0},{4,5},{5,6},{6,7},{7,4},{8,9},{9,10},{10,1... | collective-permute-start | bytes 122888 | tf_op jit(solution)/shard_map/ppermute | solution.py:43
  2.7 0.5 %collective-permute-start.1 = (bf16[5,16,256]{2,1,0:T(8,128)(2,1)S(1)}, bf16[5,16,256]{2,1,0:T(8,128)(2,1)S(1)}, u32[]{:S(2)}, u32[]{:S(2)}) collective-permute-start(bf16[5,16,256]{2,1,0:T(8,128)(2,1)S(1)} %get-tuple-element.28), channel_id=1, source_target_pairs={{0,2},{1,3},{2,0},{3,1},{4,6},{5,7},{6,4},{7,5},{8,10},{9,11},{10,... | collective-permute-start | bytes 122888 | tf_op jit(solution)/shard_map/ppermute | solution.py:43
  3.2 1.0 %collective-permute-start.2 = (bf16[5,16,256]{2,1,0:T(8,128)(2,1)S(1)}, bf16[5,16,256]{2,1,0:T(8,128)(2,1)S(1)}, u32[]{:S(2)}, u32[]{:S(2)}) collective-permute-start(bf16[5,16,256]{2,1,0:T(8,128)(2,1)S(1)} %get-tuple-element.29), channel_id=1, source_target_pairs={{0,3},{1,0},{2,1},{3,2},{4,7},{5,4},{6,5},{7,6},{8,11},{9,8},{10,9... | collective-permute-start | bytes 122888 | tf_op jit(solution)/shard_map/ppermute | solution.py:43
  4.2 2.0 %collective-permute-done = bf16[5,16,256]{2,1,0:T(8,128)(2,1)S(1)} collective-permute-done((bf16[5,16,256]{2,1,0:T(8,128)(2,1)S(1)}, bf16[5,16,256]{2,1,0:T(8,128)(2,1)S(1)}, u32[]{:S(2)}, u32[]{:S(2)}) %collective-permute-start) | collective-permute-done | bytes 40992 | tf_op jit(solution)/shard_map/ppermute | solution.py:43
  6.3 0.4 %collective-permute-done.1 = bf16[5,16,256]{2,1,0:T(8,128)(2,1)S(1)} collective-permute-done((bf16[5,16,256]{2,1,0:T(8,128)(2,1)S(1)}, bf16[5,16,256]{2,1,0:T(8,128)(2,1)S(1)}, u32[]{:S(2)}, u32[]{:S(2)}) %collective-permute-start.1) | collective-permute-done | bytes 40992 | tf_op jit(solution)/shard_map/ppermute | solution.py:43
  6.7 0.5 %collective-permute-done.2 = bf16[5,16,256]{2,1,0:T(8,128)(2,1)S(1)} collective-permute-done((bf16[5,16,256]{2,1,0:T(8,128)(2,1)S(1)}, bf16[5,16,256]{2,1,0:T(8,128)(2,1)S(1)}, u32[]{:S(2)}, u32[]{:S(2)}) %collective-permute-start.2) | collective-permute-done | bytes 40992 | tf_op jit(solution)/shard_map/ppermute | solution.py:43
  7.2 3.7 %collective-permute-start.3 = (bf16[64,256]{1,0:T(8,128)(2,1)S(1)}, bf16[64,256]{1,0:T(8,128)(2,1)S(1)}, u32[]{:S(2)}, u32[]{:S(2)}) collective-permute-start(bf16[64,256]{1,0:T(8,128)(2,1)S(1)} %pad_maximum_fusion.1), channel_id=1, source_target_pairs={{0,24},{4,28},{8,16},{12,20},{16,8},{20,12},{24,0},{28,4},{1,25},{... | collective-permute-start | bytes 98312 | tf_op jit(solution)/shard_map/ppermute | solution.py:43
  10.9 0.0 collective-permute-start.4
  10.9 0.1 collective-permute-start.5
  11.0 0.1 collective-permute-start.6
  11.1 2.8 %prepare.1 = (bf16[256,512]{1,0:T(8,128)(2,1)S(1)}, f32[320,512]{1,0:T(8,128)S(1)}, bf16[512,256]{1,0:T(8,128)(2,1)S(1)}, f32[512,1024]{1,0:T(8,128)S(1)}, bf16[...) custom-call(s32[1]{0:T(128)} %bitcast.el_ref.refs_0_, ...), custom_call_target="tpu_custom_call" | custom-call | flops 7864320 | bytes 9764872 | tf_op jit(solution)/shard_map/prepare/pallas_call | solution.py:70
  13.9 0.0 collective-permute-done.3.refs_1_
  13.9 2.1 %collective-permute-done.4.refs_2_ = bf16[64,256]{1,0:T(8,128)(2,1)S(1)} collective-permute-done((bf16[64,256]{1,0:T(8,128)(2,1)S(1)}, bf16[64,256]{1,0:T(8,128)(2,1)S(1)}, u32[]{:S(2)}, u32[]{:S(2)}) %collective-permute-start.4) | collective-permute-done | bytes 32800 | tf_op jit(solution)/shard_map/ppermute | solution.py:43
  16.0 0.0 collective-permute-done.5.refs_3_
  16.0 0.0 collective-permute-done.6.refs_4_
  16.0 4.3 %main.1 = (f32[2,256,256]{2,1,0:T(8,128)S(1)}, bf16[272,256]{1,0:T(8,128)(2,1)S(1)}, bf16[272,256]{1,0:T(8,128)(2,1)S(1)}, bf16[2,256]{1,0:T(2,128)(2,1)S(1)}, bf16[2,256]{1,0:T(2,128)(2,1)S(1)}) custom-call(s32[1]{0:T(128)} %bitcast.1.az_ref.refs_1_, bf16[64,256]{1,0:T(8,128)(2,1)S(1)} %pad_maximum_fusion.refs_13_.refs_0_, ...), custom_call_target="tpu_custom_call" | custom-call | flops 1291845632 | bytes 5687300 | tf_op jit(solution)/shard_map/main/pallas_call | solution.py:70
  20.3 0.1 collective-permute-start.7
  20.4 1.9 %collective-permute-start.8 = (bf16[2,256]{1,0:T(2,128)(2,1)S(1)}, bf16[2,256]{1,0:T(2,128)(2,1)S(1)}, u32[]{:S(2)}, u32[]{:S(2)}) collective-permute-start(bf16[2,256]{1,0:T(2,128)(2,1)S(1)} %get-tuple-element.40), channel_id=1, source_target_pairs={{0,28},{4,8},{8,4},{12,16},{16,12},{20,24},{24,20},{28,0},{1,29},{... | collective-permute-start | bytes 3080 | tf_op jit(solution)/shard_map/ppermute | solution.py:43
  22.3 0.0 collective-permute-done.7.inner_ref
  22.3 3.0 %collective-permute-done.8.outer_ref = bf16[2,256]{1,0:T(2,128)(2,1)S(1)} collective-permute-done((bf16[2,256]{1,0:T(2,128)(2,1)S(1)}, bf16[2,256]{1,0:T(2,128)(2,1)S(1)}, u32[]{:S(2)}, u32[]{:S(2)}) %collective-permute-start.8) | collective-permute-done | bytes 1056 | tf_op jit(solution)/shard_map/ppermute | solution.py:43
  25.3 2.5 %collective-permute-start.9 = (bf16[272,256]{1,0:T(8,128)(2,1)S(1)}, bf16[272,256]{1,0:T(8,128)(2,1)S(1)}, u32[]{:S(2)}, u32[]{:S(2)}) collective-permute-start(bf16[272,256]{1,0:T(8,128)(2,1)S(1)} %get-tuple-element.43.near_ref), channel_id=1, source_target_pairs={{0,1},{1,0},{2,3},{3,2},{4,5},{5,4},{6,7},{7,6},{8,9},{9,8},{10,11... | collective-permute-start | bytes 417800 | tf_op jit(solution)/shard_map/ppermute | solution.py:43
  27.7 2.5 %collective-permute-start.10 = (bf16[272,256]{1,0:T(8,128)(2,1)S(1)}, bf16[272,256]{1,0:T(8,128)(2,1)S(1)}, u32[]{:S(2)}, u32[]{:S(2)}) collective-permute-start(bf16[272,256]{1,0:T(8,128)(2,1)S(1)} %get-tuple-element.44.far_ref), channel_id=1, source_target_pairs={{0,0},{1,2},{2,1},{3,3},{4,4},{5,6},{6,5},{7,7},{8,8},{9,10},{10,9... | collective-permute-start | bytes 417800 | tf_op jit(solution)/shard_map/ppermute | solution.py:43
  30.2 0.6 %inside.1.part_ref = f32[2,256,256]{2,1,0:T(8,128)S(1)} custom-call(s32[1]{0:T(128)} %bitcast.el_ref.refs_0_, bf16[272,256]{1,0:T(8,128)(2,1)S(1)} %get-tuple-element.43.near_ref, bf16[272,256]{1,0:T(8,128)(2,1)S(1)} %get-tuple-element.44.far_ref, f32[2,256,256]{2,1,0:T(8,128)S(1)} %get-tuple-element.45.joined_ref, ...), custom_call_target="tpu_custom_call" | custom-call | flops 402653184 | bytes 2506756 | tf_op jit(solution)/shard_map/inside/pallas_call | solution.py:70
  30.9 0.8 %collective-permute-done.9.near_ref = bf16[272,256]{1,0:T(8,128)(2,1)S(1)} collective-permute-done((bf16[272,256]{1,0:T(8,128)(2,1)S(1)}, bf16[272,256]{1,0:T(8,128)(2,1)S(1)}, u32[]{:S(2)}, u32[]{:S(2)}) %collective-permute-start.9) | collective-permute-done | bytes 139296 | tf_op jit(solution)/shard_map/ppermute | solution.py:43
  31.7 3.9 %collective-permute-done.10.far_ref = bf16[272,256]{1,0:T(8,128)(2,1)S(1)} collective-permute-done((bf16[272,256]{1,0:T(8,128)(2,1)S(1)}, bf16[272,256]{1,0:T(8,128)(2,1)S(1)}, u32[]{:S(2)}, u32[]{:S(2)}) %collective-permute-start.10) | collective-permute-done | bytes 139296 | tf_op jit(solution)/shard_map/ppermute | solution.py:43
  35.6 1.1 %border.1 = bf16[2,256,256]{2,1,0:T(8,128)(2,1)} custom-call(s32[1]{0:T(128)} %bitcast.el_ref.refs_0_, bf16[272,256]{1,0:T(8,128)(2,1)S(1)} %collective-permute-done.9.near_ref, bf16[272,256]{1,0:T(8,128)(2,1)S(1)} %collective-permute-done.10.far_ref, f32[2,256,256]{2,1,0:T(8,128)S(1)} %inside.1.part_ref, bf16[9,256,256]{2,1,0:T(8,128)(2,1)S(1)} %get-tuple-element.46.w_ref), custom_call_target="tpu_custom_call" | custom-call | flops 201326592 | bytes 2244612 | tf_op jit(solution)/shard_map/border/pallas_call | solution.py:70
  (10 shorter events, 0.0 us)
Async XLA Ops:
  1.1 5.1 %collective-permute-start = (bf16[5,16,256]{2,1,0:T(8,128)(2,1)S(1)}, bf16[5,16,256]{2,1,0:T(8,128)(2,1)S(1)}, u32[]{:S(2)}, u32[]{:S(2)}) collective-permute-start(bf16[5,16,256]{2,1,0:T(8,128)(2,1)S(1)} %get-tuple-element.27), channel_id=1, source_target_pairs={{0,1},{1,2},{2,3},{3,0},{4,5},{5,6},{6,7},{7,4},{8,9},{9,10},{10,1... | collective-permute-start | bytes 122888 | tf_op jit(solution)/shard_map/ppermute | solution.py:43
  2.7 4.0 %collective-permute-start.1 = (bf16[5,16,256]{2,1,0:T(8,128)(2,1)S(1)}, bf16[5,16,256]{2,1,0:T(8,128)(2,1)S(1)}, u32[]{:S(2)}, u32[]{:S(2)}) collective-permute-start(bf16[5,16,256]{2,1,0:T(8,128)(2,1)S(1)} %get-tuple-element.28), channel_id=1, source_target_pairs={{0,2},{1,3},{2,0},{3,1},{4,6},{5,7},{6,4},{7,5},{8,10},{9,11},{10,... | collective-permute-start | bytes 122888 | tf_op jit(solution)/shard_map/ppermute | solution.py:43
  3.2 4.0 %collective-permute-start.2 = (bf16[5,16,256]{2,1,0:T(8,128)(2,1)S(1)}, bf16[5,16,256]{2,1,0:T(8,128)(2,1)S(1)}, u32[]{:S(2)}, u32[]{:S(2)}) collective-permute-start(bf16[5,16,256]{2,1,0:T(8,128)(2,1)S(1)} %get-tuple-element.29), channel_id=1, source_target_pairs={{0,3},{1,0},{2,1},{3,2},{4,7},{5,4},{6,5},{7,6},{8,11},{9,8},{10,9... | collective-permute-start | bytes 122888 | tf_op jit(solution)/shard_map/ppermute | solution.py:43
  7.2 6.7 %collective-permute-start.3 = (bf16[64,256]{1,0:T(8,128)(2,1)S(1)}, bf16[64,256]{1,0:T(8,128)(2,1)S(1)}, u32[]{:S(2)}, u32[]{:S(2)}) collective-permute-start(bf16[64,256]{1,0:T(8,128)(2,1)S(1)} %pad_maximum_fusion.1), channel_id=1, source_target_pairs={{0,24},{4,28},{8,16},{12,20},{16,8},{20,12},{24,0},{28,4},{1,25},{... | collective-permute-start | bytes 98312 | tf_op jit(solution)/shard_map/ppermute | solution.py:43
  10.9 5.1 %collective-permute-start.4 = (bf16[64,256]{1,0:T(8,128)(2,1)S(1)}, bf16[64,256]{1,0:T(8,128)(2,1)S(1)}, u32[]{:S(2)}, u32[]{:S(2)}) collective-permute-start(bf16[64,256]{1,0:T(8,128)(2,1)S(1)} %pad_maximum_fusion.2), channel_id=1, source_target_pairs={{0,28},{4,8},{8,4},{12,16},{16,12},{20,24},{24,20},{28,0},{1,29},{... | collective-permute-start | bytes 98312 | tf_op jit(solution)/shard_map/ppermute | solution.py:43
  10.9 5.1 %collective-permute-start.5 = (bf16[64,256]{1,0:T(8,128)(2,1)S(1)}, bf16[64,256]{1,0:T(8,128)(2,1)S(1)}, u32[]{:S(2)}, u32[]{:S(2)}) collective-permute-start(bf16[64,256]{1,0:T(8,128)(2,1)S(1)} %pad_maximum_fusion.3), channel_id=1, source_target_pairs={{0,8},{4,12},{8,0},{12,4},{16,24},{20,28},{24,16},{28,20},{1,9},{5... | collective-permute-start | bytes 98312 | tf_op jit(solution)/shard_map/ppermute | solution.py:43
  11.0 5.0 %collective-permute-start.6 = (bf16[64,256]{1,0:T(8,128)(2,1)S(1)}, bf16[64,256]{1,0:T(8,128)(2,1)S(1)}, u32[]{:S(2)}, u32[]{:S(2)}) collective-permute-start(bf16[64,256]{1,0:T(8,128)(2,1)S(1)} %pad_maximum_fusion.4), channel_id=1, source_target_pairs={{0,4},{4,0},{8,12},{12,8},{16,20},{20,16},{24,28},{28,24},{1,5},{5... | collective-permute-start | bytes 98312 | tf_op jit(solution)/shard_map/ppermute | solution.py:43
  20.3 1.9 %collective-permute-start.7 = (bf16[2,256]{1,0:T(2,128)(2,1)S(1)}, bf16[2,256]{1,0:T(2,128)(2,1)S(1)}, u32[]{:S(2)}, u32[]{:S(2)}) collective-permute-start(bf16[2,256]{1,0:T(2,128)(2,1)S(1)} %get-tuple-element.39), channel_id=1, source_target_pairs={{0,4},{4,0},{8,12},{12,8},{16,20},{20,16},{24,28},{28,24},{1,5},{5... | collective-permute-start | bytes 3080 | tf_op jit(solution)/shard_map/ppermute | solution.py:43
  20.4 4.9 %collective-permute-start.8 = (bf16[2,256]{1,0:T(2,128)(2,1)S(1)}, bf16[2,256]{1,0:T(2,128)(2,1)S(1)}, u32[]{:S(2)}, u32[]{:S(2)}) collective-permute-start(bf16[2,256]{1,0:T(2,128)(2,1)S(1)} %get-tuple-element.40), channel_id=1, source_target_pairs={{0,28},{4,8},{8,4},{12,16},{16,12},{20,24},{24,20},{28,0},{1,29},{... | collective-permute-start | bytes 3080 | tf_op jit(solution)/shard_map/ppermute | solution.py:43
  25.3 6.4 %collective-permute-start.9 = (bf16[272,256]{1,0:T(8,128)(2,1)S(1)}, bf16[272,256]{1,0:T(8,128)(2,1)S(1)}, u32[]{:S(2)}, u32[]{:S(2)}) collective-permute-start(bf16[272,256]{1,0:T(8,128)(2,1)S(1)} %get-tuple-element.43.near_ref), channel_id=1, source_target_pairs={{0,1},{1,0},{2,3},{3,2},{4,5},{5,4},{6,7},{7,6},{8,9},{9,8},{10,11... | collective-permute-start | bytes 417800 | tf_op jit(solution)/shard_map/ppermute | solution.py:43
  27.7 7.8 %collective-permute-start.10 = (bf16[272,256]{1,0:T(8,128)(2,1)S(1)}, bf16[272,256]{1,0:T(8,128)(2,1)S(1)}, u32[]{:S(2)}, u32[]{:S(2)}) collective-permute-start(bf16[272,256]{1,0:T(8,128)(2,1)S(1)} %get-tuple-element.44.far_ref), channel_id=1, source_target_pairs={{0,0},{1,2},{2,1},{3,3},{4,4},{5,6},{6,5},{7,7},{8,8},{9,10},{10,9... | collective-permute-start | bytes 417800 | tf_op jit(solution)/shard_map/ppermute | solution.py:43

commit v4 on v3

--- a/solution.py
+++ b/solution.py
@@ -101,7 +101,7 @@
         c.wait()
     tokens = tokens_ref[...]
     for step in range(groups):
-        target = lax.rem(el + step, groups)
+        target = lax.bitwise_xor(el, step)
         picks = []
         for piece in range(offsets):
             row = slots_ref[sent_offset(az, piece), pl.ds(target, 1), :].astype(F32)
@@ -113,43 +113,34 @@
         out_refs[step][...] = chosen.reshape(out_refs[step].shape)
 
 
-def prepare_body(*refs, groups, capacity, weights):
-    el_ref, az_ref, points_hbm, skip_hbm, idx_hbm, w_query_hbm, w_skip_hbm = refs[:7]
-    weight_hbm = refs[7 : 7 + weights]
-    q_ref, bias_ref, points_ref, side_ref = refs[8 + weights : 12 + weights]
-    weight_refs = refs[12 + weights : 12 + 2 * weights]
-    idx_ref, w_query_ref, skip_ref, w_skip_ref, sems = refs[12 + 2 * weights :]
+def load_body(*refs, groups, capacity, held):
+    el_ref, az_ref, points_hbm, skip_hbm, idx_hbm = refs[:5]
+    held_hbm = refs[5 : 5 + held]
+    bias_ref, points_ref, skip_ref = refs[5 + held : 8 + held]
+    held_refs = refs[8 + held : 8 + 2 * held]
+    idx_ref, sems = refs[8 + 2 * held :]
     el, az = el_ref[0], az_ref[0]
     even = 1 - lax.rem(el, 2)
     cols = points_ref.shape[0] // 2
-    first = [
-        pltpu.make_async_copy(idx_hbm.at[even], idx_ref.at[0], sems.at[0]),
-        pltpu.make_async_copy(idx_hbm.at[1 - even], idx_ref.at[1], sems.at[1]),
-        pltpu.make_async_copy(w_query_hbm, w_query_ref, sems.at[2]),
-        pltpu.make_async_copy(points_hbm.at[even], points_ref.at[pl.ds(0, cols)], sems.at[3]),
-        pltpu.make_async_copy(points_hbm.at[1 - even], points_ref.at[pl.ds(cols, cols)], sems.at[4]),
-    ]
-    later = [
-        pltpu.make_async_copy(skip_hbm.at[even], skip_ref.at[pl.ds(0, cols)], sems.at[5]),
-        pltpu.make_async_copy(skip_hbm.at[1 - even], skip_ref.at[pl.ds(cols, cols)], sems.at[6]),
-        pltpu.make_async_copy(w_skip_hbm, w_skip_ref, sems.at[7]),
-    ]
-    for k in range(weights):
-        later.append(pltpu.make_async_copy(weight_hbm[k], weight_refs[k], sems.at[8 + k]))
+    count = 2 * cols
+    first, later = [], []
+    for r, at in enumerate((even, 1 - even)):
+        rows = pl.ds(r * cols, cols)
+        first.append(pltpu.make_async_copy(idx_hbm.at[at], idx_ref.at[r], sems.at[r]))
+        later.append(pltpu.make_async_copy(points_hbm.at[at], points_ref.at[rows], sems.at[2 + r]))
+        later.append(pltpu.make_async_copy(skip_hbm.at[at], skip_ref.at[rows], sems.at[4 + r]))
+    for k in range(held):
+        later.append(pltpu.make_async_copy(held_hbm[k], held_refs[k], sems.at[6 + k]))
     for c in first + later:
         c.start()
     for c in first:
         c.wait()
-    count, width = q_ref.shape[1], q_ref.shape[0]
-    scale = math.log2(math.e) / math.sqrt(width // HEADS)
-    query = dot(points_ref[...], w_query_ref[...]) * scale
-    q_ref[...] = query.T.astype(BF16)
     near = idx_ref.shape[1]
     lanes = 128
     for piece in range(bias_ref.shape[0] // (groups * capacity)):
         offset = 2 * REACH - sent_offset(az, piece)
         for step in range(groups):
-            source = lax.rem(el + groups - step, groups)
+            source = lax.bitwise_xor(el, step)
             low = (offset * groups + source) * capacity
             slot = low + lax.broadcasted_iota(jnp.int32, (capacity, lanes), 0)
             place = (piece * groups + step) * capacity
@@ -162,6 +153,13 @@
                 bias_ref[place : place + capacity, start : start + lanes] = jnp.log2(total)
     for c in later:
         c.wait()
+
+
+def query_body(points_ref, skip_ref, w_query_ref, w_skip_ref, after_ref, q_ref, side_ref):
+    del after_ref
+    scale = math.log2(math.e) / math.sqrt(q_ref.shape[0] // HEADS)
+    query = dot(points_ref[...], w_query_ref[...]) * scale
+    q_ref[...] = query.T.astype(BF16)
     side_ref[...] = dot(skip_ref[...], w_skip_ref[...])
 
 
@@ -299,35 +297,35 @@
         [SMEM, SMEM, HBM, HBM],
         [VMEM(own_tokens.shape, BF16), VMEM(slots.shape, jnp.int32), dma((2,))],
     )
-    got = [sent[0]]
-    for s in range(1, groups):
-        got.append(swap(sent[s], "el", lambda i, n, s=s: (i + s) % n))
+    got = {0: sent[0]}
+    for s in reversed(range(1, groups)):
+        got[s] = swap(sent[s], "el", lambda i, n, s=s: i ^ s)
     pieces = []
     for piece in range(offsets):
-        bundle = jnp.concatenate([g[piece] for g in got], axis=0)
+        bundle = jnp.concatenate([got[s][piece] for s in range(groups)], axis=0)
         pieces.append(swap(bundle, "az", MATCHES[piece]) if piece else bundle)
-    weights = [w_key, w_value, w_out, w_hid, w_down, w_conv]
+    held = [w_query, w_skip, w_key, w_value, w_out, w_hid, w_down, w_conv]
     idx = jnp.swapaxes(recv_idx, 1, 2)
-    query_t, bias, points_v, side, *held = call(
-        functools.partial(prepare_body, groups=groups, capacity=capacity, weights=len(weights)),
+    bias, points_v, skip_v, *held = call(
+        functools.partial(load_body, groups=groups, capacity=capacity, held=len(held)),
         [
-            shape((width, count), BF16),
             shape((table, count), F32),
             shape((count, width), BF16),
-            shape((count, w_skip.shape[1]), F32),
+            shape((count, width), BF16),
         ]
-        + [shape(w.shape, BF16) for w in weights],
-        [el, az, points, skip, idx, w_query, w_skip] + weights + [pieces[0]],
-        "prepare",
+        + [shape(w.shape, BF16) for w in held],
+        [el, az, points, skip, idx] + held,
+        "load",
         (table * count * 48, table * count),
-        [SMEM, SMEM] + [HBM] * (5 + len(weights)) + [VMEM],
-        [
-            VMEM(idx.shape, jnp.int32),
-            VMEM(w_query.shape, BF16),
-            VMEM((count, width), BF16),
-            VMEM(w_skip.shape, BF16),
-            dma((8 + len(weights),)),
-        ],
+        [SMEM, SMEM] + [HBM] * (3 + len(held)),
+        [VMEM(idx.shape, jnp.int32), dma((6 + len(held),))],
+    )
+    query_t, side = call(
+        query_body,
+        [shape((width, count), BF16), shape((count, w_skip.shape[1]), F32)],
+        [points_v, skip_v, held[0], held[1], pieces[0]],
+        "query",
+        (2 * count * width * 5 * width, 0),
     )
     joined, near, far, inner_edge, outer_edge = call(
         functools.partial(main_body, pieces=len(pieces)),
@@ -338,7 +336,7 @@
             shape((2, width), BF16),
             shape((2, width), BF16),
         ],
-        [az] + pieces + [query_t, bias, points_v, side] + held[:-1],
+        [az] + pieces + [query_t, bias, points_v, side] + held[2:-1],
         "main",
         (10 * table * count * width + 2 * count * width * 13 * width, table * count * HEADS),
         [SMEM] + [VMEM] * (len(pieces) + 9),

time: 37 us -> 37 us (level)
  the two profiles are of different devices: /device:TPU:4 before, /device:TPU:2 now
where the time goes in v4:
time: 37 us; the launch traced here: 36.7 us
  waiting for transfers between devices  14 us (38%)
  starting transfers between devices  12.6 us (34%)
  Pallas kernels  10 us (27%)
    ppermute x11, waiting for transfers between devices, swap(): return lax.ppermute(x, axis, [(i, partner(i, n)) for i in range(n)])  14 us
    ppermute x11, starting transfers between devices, swap(): return lax.ppermute(x, axis, [(i, partner(i, n)) for i in range(n)])  12.6 us
    pallas_call x7, Pallas kernels, call(): pl.pallas_call(body, out_shape=outs, in_specs=[pl.BlockSpec(memory_space=...  10 us
  transfers between devices with their start and end apart: 11, of which 6 were waited for; matrix products, arithmetic and copies ran while one was open for 0% of the time, Pallas kernels for 9%

profile of v4, /device:TPU:2, one launch (start us, length us, event | category | flops | bytes accessed | tf_op | source)
XLA Modules:
  0.0 36.7 jit_solution(3051494890177791617)
XLA Ops:
  0.0 1.1 %gather.1 = (bf16[5,16,256]{2,1,0:T(8,128)(2,1)S(1)}, bf16[5,16,256]{2,1,0:T(8,128)(2,1)S(1)}, bf16[5,16,256]{2,1,0:T(8,128)(2,1)S(1)}, bf16[5,16,256]{2,1,0:T(8,128)(2,1)S(1)}) custom-call(s32[1]{0:T(128)} %bitcast.el_ref.refs_0_, s32[1]{0:T(128)} %bitcast.1.az_ref.refs_1_, bf16[128,256]{1,0:T(8,128)(2,1)} %bitcast.46, s32[5,4,16]{2,1,0:T(4,128)} %bitcast.47), custom_call_target="tpu_custom_call" | custom-call | flops 20971520 | bytes 230664 | tf_op jit(solution)/shard_map/gather/pallas_call | solution.py:70
  1.1 0.1 collective-permute-start
  1.2 2.0 %collective-permute-start.1 = (bf16[5,16,256]{2,1,0:T(8,128)(2,1)S(1)}, bf16[5,16,256]{2,1,0:T(8,128)(2,1)S(1)}, u32[]{:S(2)}, u32[]{:S(2)}) collective-permute-start(bf16[5,16,256]{2,1,0:T(8,128)(2,1)S(1)} %get-tuple-element.31), channel_id=1, source_target_pairs={{0,2},{1,3},{2,0},{3,1},{4,6},{5,7},{6,4},{7,5},{8,10},{9,11},{10,... | collective-permute-start | bytes 122888 | tf_op jit(solution)/shard_map/ppermute | solution.py:43
  3.2 1.4 %collective-permute-start.2 = (bf16[5,16,256]{2,1,0:T(8,128)(2,1)S(1)}, bf16[5,16,256]{2,1,0:T(8,128)(2,1)S(1)}, u32[]{:S(2)}, u32[]{:S(2)}) collective-permute-start(bf16[5,16,256]{2,1,0:T(8,128)(2,1)S(1)} %get-tuple-element.32), channel_id=1, source_target_pairs={{0,3},{1,2},{2,1},{3,0},{4,7},{5,6},{6,5},{7,4},{8,11},{9,10},{10,... | collective-permute-start | bytes 122888 | tf_op jit(solution)/shard_map/ppermute | solution.py:43
  4.7 2.3 %load.1 = (f32[320,512]{1,0:T(8,128)S(1)}, bf16[512,256]{1,0:T(8,128)(2,1)S(1)}, bf16[512,256]{1,0:T(8,128)(2,1)S(1)}, bf16[256,256]{1,0:T(8,128)(2,1)S(1)}, bf1...) custom-call(s32[1]{0:T(128)} %bitcast.el_ref.refs_0_, ...), custom_call_target="tpu_custom_call" | custom-call | flops 7864320 | bytes 8290312 | tf_op jit(solution)/shard_map/load/pallas_call | solution.py:70
  7.0 0.0 collective-permute-done
  7.0 0.0 collective-permute-done.1
  7.1 1.1 %collective-permute-done.2 = bf16[5,16,256]{2,1,0:T(8,128)(2,1)S(1)} collective-permute-done((bf16[5,16,256]{2,1,0:T(8,128)(2,1)S(1)}, bf16[5,16,256]{2,1,0:T(8,128)(2,1)S(1)}, u32[]{:S(2)}, u32[]{:S(2)}) %collective-permute-start.2) | collective-permute-done | bytes 40992 | tf_op jit(solution)/shard_map/ppermute | solution.py:43
  8.2 3.7 %collective-permute-start.3 = (bf16[64,256]{1,0:T(8,128)(2,1)S(1)}, bf16[64,256]{1,0:T(8,128)(2,1)S(1)}, u32[]{:S(2)}, u32[]{:S(2)}) collective-permute-start(bf16[64,256]{1,0:T(8,128)(2,1)S(1)} %pad_maximum_fusion.1), channel_id=1, source_target_pairs={{0,24},{4,28},{8,16},{12,20},{16,8},{20,12},{24,0},{28,4},{1,25},{... | collective-permute-start | bytes 98312 | tf_op jit(solution)/shard_map/ppermute | solution.py:43
  11.8 0.0 collective-permute-start.4
  11.8 0.1 collective-permute-start.5
  11.9 0.1 collective-permute-start.6
  12.0 0.5 %query.1 = (bf16[256,512]{1,0:T(8,128)(2,1)S(1)}, f32[512,1024]{1,0:T(8,128)S(1)}) custom-call(bf16[512,256]{1,0:T(8,128)(2,1)S(1)} %get-tuple-element.33.points_ref.refs_7_, bf16[512,256]{1,0:T(8,128)(2,1)S(1)} %get-tuple-element.34.skip_ref, bf16[256,256]{1,0:T(8,128)(2,1)S(1)} %get-tuple-element.35.w_query_ref, ...), custom_call_target="tpu_custom_call" | custom-call | flops 335544320 | bytes 3571712 | tf_op jit(solution)/shard_map/query/pallas_call | solution.py:70
  12.5 1.4 %collective-permute-done.3.refs_1_ = bf16[64,256]{1,0:T(8,128)(2,1)S(1)} collective-permute-done((bf16[64,256]{1,0:T(8,128)(2,1)S(1)}, bf16[64,256]{1,0:T(8,128)(2,1)S(1)}, u32[]{:S(2)}, u32[]{:S(2)}) %collective-permute-start.3) | collective-permute-done | bytes 32800 | tf_op jit(solution)/shard_map/ppermute | solution.py:43
  13.9 3.0 %collective-permute-done.4.refs_2_ = bf16[64,256]{1,0:T(8,128)(2,1)S(1)} collective-permute-done((bf16[64,256]{1,0:T(8,128)(2,1)S(1)}, bf16[64,256]{1,0:T(8,128)(2,1)S(1)}, u32[]{:S(2)}, u32[]{:S(2)}) %collective-permute-start.4) | collective-permute-done | bytes 32800 | tf_op jit(solution)/shard_map/ppermute | solution.py:43
  17.0 0.0 collective-permute-done.5.refs_3_
  17.0 0.0 collective-permute-done.6.refs_4_
  17.0 4.3 %main.1 = (f32[2,256,256]{2,1,0:T(8,128)S(1)}, bf16[272,256]{1,0:T(8,128)(2,1)S(1)}, bf16[272,256]{1,0:T(8,128)(2,1)S(1)}, bf16[2,256]{1,0:T(2,128)(2,1)S(1)}, bf16[2,256]{1,0:T(2,128)(2,1)S(1)}) custom-call(s32[1]{0:T(128)} %bitcast.1.az_ref.refs_1_, bf16[64,256]{1,0:T(8,128)(2,1)S(1)} %pad_maximum_fusion.after_ref.refs_0_, ...), custom_call_target="tpu_custom_call" | custom-call | flops 1291845632 | bytes 5687300 | tf_op jit(solution)/shard_map/main/pallas_call | solution.py:70
  21.3 0.1 collective-permute-start.7
  21.4 1.2 %collective-permute-start.8 = (bf16[2,256]{1,0:T(2,128)(2,1)S(1)}, bf16[2,256]{1,0:T(2,128)(2,1)S(1)}, u32[]{:S(2)}, u32[]{:S(2)}) collective-permute-start(bf16[2,256]{1,0:T(2,128)(2,1)S(1)} %get-tuple-element.46), channel_id=1, source_target_pairs={{0,28},{4,8},{8,4},{12,16},{16,12},{20,24},{24,20},{28,0},{1,29},{... | collective-permute-start | bytes 3080 | tf_op jit(solution)/shard_map/ppermute | solution.py:43
  22.6 0.0 collective-permute-done.7.inner_ref
  22.6 3.6 %collective-permute-done.8.outer_ref = bf16[2,256]{1,0:T(2,128)(2,1)S(1)} collective-permute-done((bf16[2,256]{1,0:T(2,128)(2,1)S(1)}, bf16[2,256]{1,0:T(2,128)(2,1)S(1)}, u32[]{:S(2)}, u32[]{:S(2)}) %collective-permute-start.8) | collective-permute-done | bytes 1056 | tf_op jit(solution)/shard_map/ppermute | solution.py:43
  26.2 1.6 %collective-permute-start.9 = (bf16[272,256]{1,0:T(8,128)(2,1)S(1)}, bf16[272,256]{1,0:T(8,128)(2,1)S(1)}, u32[]{:S(2)}, u32[]{:S(2)}) collective-permute-start(bf16[272,256]{1,0:T(8,128)(2,1)S(1)} %get-tuple-element.49.near_ref), channel_id=1, source_target_pairs={{0,1},{1,0},{2,3},{3,2},{4,5},{5,4},{6,7},{7,6},{8,9},{9,8},{10,11... | collective-permute-start | bytes 417800 | tf_op jit(solution)/shard_map/ppermute | solution.py:43
  27.8 2.4 %collective-permute-start.10 = (bf16[272,256]{1,0:T(8,128)(2,1)S(1)}, bf16[272,256]{1,0:T(8,128)(2,1)S(1)}, u32[]{:S(2)}, u32[]{:S(2)}) collective-permute-start(bf16[272,256]{1,0:T(8,128)(2,1)S(1)} %get-tuple-element.50.far_ref), channel_id=1, source_target_pairs={{0,0},{1,2},{2,1},{3,3},{4,4},{5,6},{6,5},{7,7},{8,8},{9,10},{10,9... | collective-permute-start | bytes 417800 | tf_op jit(solution)/shard_map/ppermute | solution.py:43
  30.2 0.6 %inside.1.part_ref = f32[2,256,256]{2,1,0:T(8,128)S(1)} custom-call(s32[1]{0:T(128)} %bitcast.el_ref.refs_0_, bf16[272,256]{1,0:T(8,128)(2,1)S(1)} %get-tuple-element.49.near_ref, bf16[272,256]{1,0:T(8,128)(2,1)S(1)} %get-tuple-element.50.far_ref, f32[2,256,256]{2,1,0:T(8,128)S(1)} %get-tuple-element.51.joined_ref, ...), custom_call_target="tpu_custom_call" | custom-call | flops 402653184 | bytes 2506756 | tf_op jit(solution)/shard_map/inside/pallas_call | solution.py:70
  30.8 0.8 %collective-permute-done.9.near_ref = bf16[272,256]{1,0:T(8,128)(2,1)S(1)} collective-permute-done((bf16[272,256]{1,0:T(8,128)(2,1)S(1)}, bf16[272,256]{1,0:T(8,128)(2,1)S(1)}, u32[]{:S(2)}, u32[]{:S(2)}) %collective-permute-start.9) | collective-permute-done | bytes 139296 | tf_op jit(solution)/shard_map/ppermute | solution.py:43
  31.6 4.0 %collective-permute-done.10.far_ref = bf16[272,256]{1,0:T(8,128)(2,1)S(1)} collective-permute-done((bf16[272,256]{1,0:T(8,128)(2,1)S(1)}, bf16[272,256]{1,0:T(8,128)(2,1)S(1)}, u32[]{:S(2)}, u32[]{:S(2)}) %collective-permute-start.10) | collective-permute-done | bytes 139296 | tf_op jit(solution)/shard_map/ppermute | solution.py:43
  35.6 1.1 %border.1 = bf16[2,256,256]{2,1,0:T(8,128)(2,1)} custom-call(s32[1]{0:T(128)} %bitcast.el_ref.refs_0_, bf16[272,256]{1,0:T(8,128)(2,1)S(1)} %collective-permute-done.9.near_ref, bf16[272,256]{1,0:T(8,128)(2,1)S(1)} %collective-permute-done.10.far_ref, f32[2,256,256]{2,1,0:T(8,128)S(1)} %inside.1.part_ref, bf16[9,256,256]{2,1,0:T(8,128)(2,1)S(1)} %get-tuple-element.52.w_ref), custom_call_target="tpu_custom_call" | custom-call | flops 201326592 | bytes 2244612 | tf_op jit(solution)/shard_map/border/pallas_call | solution.py:70
  (10 shorter events, 0.1 us)
Async XLA Ops:
  1.1 5.9 %collective-permute-start = (bf16[5,16,256]{2,1,0:T(8,128)(2,1)S(1)}, bf16[5,16,256]{2,1,0:T(8,128)(2,1)S(1)}, u32[]{:S(2)}, u32[]{:S(2)}) collective-permute-start(bf16[5,16,256]{2,1,0:T(8,128)(2,1)S(1)} %get-tuple-element.30), channel_id=1, source_target_pairs={{0,1},{1,0},{2,3},{3,2},{4,5},{5,4},{6,7},{7,6},{8,9},{9,8},{10,11... | collective-permute-start | bytes 122888 | tf_op jit(solution)/shard_map/ppermute | solution.py:43
  1.2 5.8 %collective-permute-start.1 = (bf16[5,16,256]{2,1,0:T(8,128)(2,1)S(1)}, bf16[5,16,256]{2,1,0:T(8,128)(2,1)S(1)}, u32[]{:S(2)}, u32[]{:S(2)}) collective-permute-start(bf16[5,16,256]{2,1,0:T(8,128)(2,1)S(1)} %get-tuple-element.31), channel_id=1, source_target_pairs={{0,2},{1,3},{2,0},{3,1},{4,6},{5,7},{6,4},{7,5},{8,10},{9,11},{10,... | collective-permute-start | bytes 122888 | tf_op jit(solution)/shard_map/ppermute | solution.py:43
  3.2 4.9 %collective-permute-start.2 = (bf16[5,16,256]{2,1,0:T(8,128)(2,1)S(1)}, bf16[5,16,256]{2,1,0:T(8,128)(2,1)S(1)}, u32[]{:S(2)}, u32[]{:S(2)}) collective-permute-start(bf16[5,16,256]{2,1,0:T(8,128)(2,1)S(1)} %get-tuple-element.32), channel_id=1, source_target_pairs={{0,3},{1,2},{2,1},{3,0},{4,7},{5,6},{6,5},{7,4},{8,11},{9,10},{10,... | collective-permute-start | bytes 122888 | tf_op jit(solution)/shard_map/ppermute | solution.py:43
  8.2 5.8 %collective-permute-start.3 = (bf16[64,256]{1,0:T(8,128)(2,1)S(1)}, bf16[64,256]{1,0:T(8,128)(2,1)S(1)}, u32[]{:S(2)}, u32[]{:S(2)}) collective-permute-start(bf16[64,256]{1,0:T(8,128)(2,1)S(1)} %pad_maximum_fusion.1), channel_id=1, source_target_pairs={{0,24},{4,28},{8,16},{12,20},{16,8},{20,12},{24,0},{28,4},{1,25},{... | collective-permute-start | bytes 98312 | tf_op jit(solution)/shard_map/ppermute | solution.py:43
  11.8 5.1 %collective-permute-start.4 = (bf16[64,256]{1,0:T(8,128)(2,1)S(1)}, bf16[64,256]{1,0:T(8,128)(2,1)S(1)}, u32[]{:S(2)}, u32[]{:S(2)}) collective-permute-start(bf16[64,256]{1,0:T(8,128)(2,1)S(1)} %pad_maximum_fusion.2), channel_id=1, source_target_pairs={{0,28},{4,8},{8,4},{12,16},{16,12},{20,24},{24,20},{28,0},{1,29},{... | collective-permute-start | bytes 98312 | tf_op jit(solution)/shard_map/ppermute | solution.py:43
  11.8 5.1 %collective-permute-start.5 = (bf16[64,256]{1,0:T(8,128)(2,1)S(1)}, bf16[64,256]{1,0:T(8,128)(2,1)S(1)}, u32[]{:S(2)}, u32[]{:S(2)}) collective-permute-start(bf16[64,256]{1,0:T(8,128)(2,1)S(1)} %pad_maximum_fusion.3), channel_id=1, source_target_pairs={{0,8},{4,12},{8,0},{12,4},{16,24},{20,28},{24,16},{28,20},{1,9},{5... | collective-permute-start | bytes 98312 | tf_op jit(solution)/shard_map/ppermute | solution.py:43
  11.9 5.0 %collective-permute-start.6 = (bf16[64,256]{1,0:T(8,128)(2,1)S(1)}, bf16[64,256]{1,0:T(8,128)(2,1)S(1)}, u32[]{:S(2)}, u32[]{:S(2)}) collective-permute-start(bf16[64,256]{1,0:T(8,128)(2,1)S(1)} %pad_maximum_fusion.4), channel_id=1, source_target_pairs={{0,4},{4,0},{8,12},{12,8},{16,20},{20,16},{24,28},{28,24},{1,5},{5... | collective-permute-start | bytes 98312 | tf_op jit(solution)/shard_map/ppermute | solution.py:43
  21.3 1.3 %collective-permute-start.7 = (bf16[2,256]{1,0:T(2,128)(2,1)S(1)}, bf16[2,256]{1,0:T(2,128)(2,1)S(1)}, u32[]{:S(2)}, u32[]{:S(2)}) collective-permute-start(bf16[2,256]{1,0:T(2,128)(2,1)S(1)} %get-tuple-element.45), channel_id=1, source_target_pairs={{0,4},{4,0},{8,12},{12,8},{16,20},{20,16},{24,28},{28,24},{1,5},{5... | collective-permute-start | bytes 3080 | tf_op jit(solution)/shard_map/ppermute | solution.py:43
  21.4 4.9 %collective-permute-start.8 = (bf16[2,256]{1,0:T(2,128)(2,1)S(1)}, bf16[2,256]{1,0:T(2,128)(2,1)S(1)}, u32[]{:S(2)}, u32[]{:S(2)}) collective-permute-start(bf16[2,256]{1,0:T(2,128)(2,1)S(1)} %get-tuple-element.46), channel_id=1, source_target_pairs={{0,28},{4,8},{8,4},{12,16},{16,12},{20,24},{24,20},{28,0},{1,29},{... | collective-permute-start | bytes 3080 | tf_op jit(solution)/shard_map/ppermute | solution.py:43
  26.2 5.4 %collective-permute-start.9 = (bf16[272,256]{1,0:T(8,128)(2,1)S(1)}, bf16[272,256]{1,0:T(8,128)(2,1)S(1)}, u32[]{:S(2)}, u32[]{:S(2)}) collective-permute-start(bf16[272,256]{1,0:T(8,128)(2,1)S(1)} %get-tuple-element.49.near_ref), channel_id=1, source_target_pairs={{0,1},{1,0},{2,3},{3,2},{4,5},{5,4},{6,7},{7,6},{8,9},{9,8},{10,11... | collective-permute-start | bytes 417800 | tf_op jit(solution)/shard_map/ppermute | solution.py:43
  27.8 7.8 %collective-permute-start.10 = (bf16[272,256]{1,0:T(8,128)(2,1)S(1)}, bf16[272,256]{1,0:T(8,128)(2,1)S(1)}, u32[]{:S(2)}, u32[]{:S(2)}) collective-permute-start(bf16[272,256]{1,0:T(8,128)(2,1)S(1)} %get-tuple-element.50.far_ref), channel_id=1, source_target_pairs={{0,0},{1,2},{2,1},{3,3},{4,4},{5,6},{6,5},{7,7},{8,8},{9,10},{10,9... | collective-permute-start | bytes 417800 | tf_op jit(solution)/shard_map/ppermute | solution.py:43

commit v5 on v4

--- a/solution.py
+++ b/solution.py
@@ -163,104 +163,137 @@
     side_ref[...] = dot(skip_ref[...], w_skip_ref[...])
 
 
-def main_body(az_ref, *refs, pieces):
-    piece_refs = refs[:pieces]
+def table_body(*refs, pieces):
     (
-        q_ref,
-        bias_ref,
-        points_ref,
-        side_ref,
         w_key_ref,
         w_value_ref,
-        w_out_ref,
-        w_hid_ref,
-        w_down_ref,
-        joined_ref,
-        near_ref,
-        far_ref,
-        inner_edge_ref,
-        outer_edge_ref,
+        *rest,
+        keys_ref,
+        values_ref,
         att_ref,
     ) = refs[pieces:]
-    width, count = q_ref.shape
+    received = jnp.concatenate([r[...] for r in refs[:pieces]], axis=0)
+    keys_ref[...] = dot(received, w_key_ref[...]).astype(BF16)
+    normed_tokens = rms(received.astype(F32)).astype(BF16)
+    values_ref[...] = dot(w_value_ref[...], normed_tokens, ((0,), (1,))).astype(BF16)
+    row_body(keys_ref, values_ref, *rest, att_ref, row=1)
+
+
+def row_body(
+    keys_ref,
+    values_ref,
+    q_ref,
+    bias_ref,
+    points_ref,
+    side_ref,
+    w_out_ref,
+    w_hid_ref,
+    w_down_ref,
+    joined_ref,
+    conv_ref,
+    *refs,
+    row,
+):
+    att_ref = refs[-1]
+    width, cols = att_ref.shape
+    lanes = slice(row * cols, (row + 1) * cols)
     head_width = width // HEADS
-    received = jnp.concatenate([r[...] for r in piece_refs], axis=0)
-    table = received.shape[0]
-    keys = dot(received, w_key_ref[...]).astype(BF16)
-    normed_tokens = rms(received.astype(F32)).astype(BF16)
-    values_t = dot(w_value_ref[...], normed_tokens, ((0,), (1,))).astype(BF16)
-    ones = jnp.ones((16, table), BF16)
+    keys = keys_ref[...]
+    ones = jnp.ones((16, keys.shape[0]), BF16)
     for head in range(HEADS):
         low, high = head * head_width, (head + 1) * head_width
-        scores = dot(keys[:, low:high], q_ref[low:high, :]) + bias_ref[...]
+        scores = dot(keys[:, low:high], q_ref[low:high, lanes]) + bias_ref[:, lanes]
         top = jnp.max(scores, axis=0, keepdims=True)
         weights = jnp.exp2(scores - top).astype(BF16)
-        lhs = jnp.concatenate([values_t[low:high, :], ones], axis=0)
+        lhs = jnp.concatenate([values_ref[low:high, :], ones], axis=0)
         mixed = dot(lhs, weights)
         att_ref[low:high, :] = (mixed[:head_width] / mixed[head_width : head_width + 1]).astype(BF16)
-    residual = points_ref[...].astype(F32) + dot(att_ref[...], w_out_ref[...], ((0,), (0,)))
+    residual = points_ref[lanes].astype(F32) + dot(att_ref[...], w_out_ref[...], ((0,), (0,)))
     normed = rms(residual).astype(BF16)
-    pre = dot(normed, w_hid_ref[...]) + side_ref[...]
+    pre = dot(normed, w_hid_ref[...]) + side_ref[lanes]
     c1 = math.sqrt(2.0 / math.pi)
     half = 0.5 * pre
     inner = (half + half * jnp.tanh(pre * (c1 + (c1 * 0.044715) * (pre * pre)))).astype(BF16)
     joined = residual + dot(inner, w_down_ref[...])
     conv = rms(joined)
-    joined_ref[...] = joined.reshape(joined_ref.shape)
-    cols = count // 2
-    near_ref[0:cols] = conv[:cols].astype(BF16)
-    far_ref[0:cols] = conv[cols:].astype(BF16)
-    left = jnp.concatenate([conv[0:1], conv[cols : cols + 1]], axis=0)
-    right = jnp.concatenate([conv[cols - 1 : cols], conv[2 * cols - 1 :]], axis=0)
+    joined_ref[...] = joined
+    conv_ref[...] = conv.astype(BF16)
+    if len(refs) == 2:
+        refs[0][...] = jnp.concatenate([conv[:1], conv[cols - 1 :]], axis=0).astype(BF16)
+
+
+def ends_of(ref):
+    cols = ref.shape[0]
+    if cols == 2:
+        both = ref[...].astype(F32)
+        return both[:1], both[1:]
+    return ref[:PAD].astype(F32)[:1], ref[cols - PAD :].astype(F32)[PAD - 1 :]
+
+
+def edges_body(az_ref, halo_ends_ref, near_ref, far_ref, far_halo_ref, inner_ref, outer_ref):
+    both = [ends_of(r) for r in (halo_ends_ref, near_ref, far_ref, far_halo_ref)]
+    left = jnp.concatenate([x[0] for x in both], axis=0)
+    right = jnp.concatenate([x[1] for x in both], axis=0)
     odd = lax.rem(az_ref[0], 2) == 1
-    inner_edge_ref[...] = jnp.where(odd, left, right).astype(BF16)
-    outer_edge_ref[...] = jnp.where(odd, right, left).astype(BF16)
-
-
-def pack_body(az_ref, inner_ref, outer_ref, near_in, far_in, near_ref, far_ref):
-    del near_in, far_in
-    odd = lax.rem(az_ref[0], 2) == 1
-    inner, outer = inner_ref[...].astype(F32), outer_ref[...].astype(F32)
-    right = jnp.where(odd, outer, inner)
-    left = jnp.where(odd, inner, outer)
-    cols, width = near_ref.shape[0] - PAD, near_ref.shape[1]
-    row = lax.broadcasted_iota(jnp.int32, (PAD, width), 0)
-    for at, ref in enumerate((near_ref, far_ref)):
-        rows = jnp.where(row == 0, right[at : at + 1], 0.0)
-        rows = jnp.where(row == PAD - 1, left[at : at + 1], rows)
-        ref[cols:, :] = rows.astype(BF16)
-
-
-def conv_rows(pairs, cols):
+    inner_ref[...] = jnp.where(odd, left, right).astype(BF16)
+    outer_ref[...] = jnp.where(odd, right, left).astype(BF16)
+
+
+def conv_rows(pairs, w_ref, left=0.0, right=0.0):
     taps = []
     for dc in range(3):
         total = None
-        for x, w_ref, base in pairs:
+        for x, base in pairs:
             part = dot(x, w_ref[base + dc])
             total = part if total is None else total + part
         taps.append(total)
-    length = taps[0].shape[0]
-    shifted = taps[1] + pltpu.roll(taps[0], 1, 0) + pltpu.roll(taps[2], length - 1, 0)
-    return shifted[:cols]
-
-
-def inside_body(el_ref, near_ref, far_ref, joined_ref, w_ref, out_ref):
+    cols = taps[0].shape[0]
+    row = lax.broadcasted_iota(jnp.int32, taps[0].shape, 0)
+    before = jnp.where(row == 0, left, pltpu.roll(taps[0], 1, 0))
+    after = jnp.where(row == cols - 1, right, pltpu.roll(taps[2], cols - 1, 0))
+    return taps[1] + before + after
+
+
+def inside_body(el_ref, near_ref, far_ref, joined_near_ref, joined_far_ref, w_ref, near_out, far_out):
     odd = lax.rem(el_ref[0], 2)
-    cols = joined_ref.shape[1]
     near, far = near_ref[...], far_ref[...]
-    out_ref[0] = joined_ref[0] + conv_rows([(near, w_ref, 3), (far, w_ref, 6 * odd)], cols)
-    out_ref[1] = joined_ref[1] + conv_rows([(far, w_ref, 3), (near, w_ref, 6 - 6 * odd)], cols)
-
-
-def border_body(el_ref, near_ref, far_ref, part_ref, w_ref, out_ref, *, last):
+    near_out[...] = joined_near_ref[...] + conv_rows([(near, 3), (far, 6 * odd)], w_ref)
+    far_out[...] = joined_far_ref[...] + conv_rows([(far, 3), (near, 6 - 6 * odd)], w_ref)
+
+
+def border_body(
+    el_ref,
+    az_ref,
+    near_ref,
+    far_ref,
+    inner_ref,
+    outer_ref,
+    near_part_ref,
+    far_part_ref,
+    w_ref,
+    out_ref,
+    *,
+    last,
+):
     el = el_ref[0]
     odd = lax.rem(el, 2)
-    cols = part_ref.shape[1]
-    near = part_ref[0] + conv_rows([(near_ref[...], w_ref, 6 - 6 * odd)], cols)
-    out_ref[1 - odd] = near.astype(BF16)
-    far = conv_rows([(far_ref[...], w_ref, 6 * odd)], cols)
-    ends = jnp.logical_or(el == 0, el == last)
-    out_ref[odd] = (part_ref[1] + jnp.where(ends, 0.0, far)).astype(BF16)
+    to_near, to_far = 6 - 6 * odd, 6 * odd
+    outside = jnp.logical_or(el == 0, el == last)
+    inner, outer = inner_ref[...].astype(F32), outer_ref[...].astype(F32)
+    odd_az = lax.rem(az_ref[0], 2) == 1
+    near_ends, far_ends = [], []
+    for side, x in enumerate((jnp.where(odd_az, inner, outer), jnp.where(odd_az, outer, inner))):
+        line = lax.broadcasted_iota(jnp.int32, x.shape, 0)
+        x = jnp.where(jnp.logical_and(outside, line == 3), 0.0, x)
+        x = jnp.concatenate([x, jnp.zeros((PAD - 4, x.shape[1]), F32)], axis=0).astype(BF16)
+        a, m, b = (dot(x, w_ref[base + 2 * side]) for base in (to_near, 3, to_far))
+        near_ends.append(a[0:1] + m[1:2] + b[2:3])
+        far_ends.append(a[1:2] + m[2:3] + b[3:4])
+    far = far_ref[...]
+    far = jnp.where(outside, jnp.zeros_like(far), far)
+    out_ref[odd] = (far_part_ref[...] + conv_rows([(far, to_far)], w_ref, *far_ends)).astype(BF16)
+    near = conv_rows([(near_ref[...], to_near)], w_ref, *near_ends)
+    out_ref[1 - odd] = (near_part_ref[...] + near).astype(BF16)
 
 
 def per_device(
@@ -327,50 +360,56 @@
         "query",
         (2 * count * width * 5 * width, 0),
     )
-    joined, near, far, inner_edge, outer_edge = call(
-        functools.partial(main_body, pieces=len(pieces)),
-        [
-            shape((rows, cols, width), F32),
-            shape((cols + PAD, width), BF16),
-            shape((cols + PAD, width), BF16),
-            shape((2, width), BF16),
-            shape((2, width), BF16),
-        ],
-        [az] + pieces + [query_t, bias, points_v, side] + held[2:-1],
-        "main",
-        (10 * table * count * width + 2 * count * width * 13 * width, table * count * HEADS),
-        [SMEM] + [VMEM] * (len(pieces) + 9),
-        [VMEM((width, count), BF16)],
+    w_key, w_value, w_out, w_hid, w_down, w_conv = held[2:]
+    row_f32, row_bf16 = shape((cols, width), F32), shape((cols, width), BF16)
+    work = (5 * table * count * width + count * width * 9 * width, table * cols * HEADS)
+    shared = [query_t, bias, points_v, side, w_out, w_hid, w_down]
+    joined_far, far, keys, values = call(
+        functools.partial(table_body, pieces=len(pieces)),
+        [row_f32, row_bf16, shape((table, width), BF16), shape((width, table), BF16)],
+        pieces + [w_key, w_value] + shared,
+        "far_row",
+        work,
+        None,
+        [VMEM((width, cols), BF16)],
+    )
+    far_got = swap(far, "el", inner_pair)
+    joined_near, near, near_ends = call(
+        functools.partial(row_body, row=0),
+        [row_f32, row_bf16, shape((2, width), BF16)],
+        [keys, values] + shared,
+        "near_row",
+        work,
+        None,
+        [VMEM((width, cols), BF16)],
+    )
+    halo_ends = swap(near_ends, "el", same_chip)
+    near_got = swap(near, "el", same_chip)
+    inner_edge, outer_edge = call(
+        edges_body,
+        [shape((4, width), BF16)] * 2,
+        [az, halo_ends, near, far, far_got],
+        "edges",
+        (16 * width, 0),
+        [SMEM] + [VMEM] * 4,
     )
     outer_got = swap(outer_edge, "az", next_chip)
     inner_got = swap(inner_edge, "az", same_chip)
-    near, far = call(
-        pack_body,
-        [shape((cols + PAD, width), BF16)] * 2,
-        [az, inner_got, outer_got, near, far],
-        "pack",
-        (4 * PAD * width, 0),
-        [SMEM] + [VMEM] * 4,
-        (),
-        {3: 0, 4: 1},
-    )
-    far_got = swap(far, "el", inner_pair)
-    near_got = swap(near, "el", same_chip)
-    (partial,) = call(
+    near_part, far_part = call(
         inside_body,
-        [shape((rows, cols, width), F32)],
-        [el, near, far, joined, held[-1]],
+        [row_f32, row_f32],
+        [el, near, far, joined_near, joined_far, w_conv],
         "inside",
         (2 * count * width * width * 6, 0),
-        [SMEM] + [VMEM] * 4,
+        [SMEM] + [VMEM] * 5,
     )
     (out,) = call(
         functools.partial(border_body, last=lax.axis_size("el") - 1),
         [shape((rows, cols, width), BF16)],
-        [el, near_got, far_got, partial, held[-1]],
+        [el, az, near_got, far_got, inner_got, outer_got, near_part, far_part, w_conv],
         "border",
         (2 * count * width * width * 3, 0),
-        [SMEM] + [VMEM] * 4,
+        [SMEM, SMEM] + [VMEM] * 7,
     )
     return out
 

time: 37 us -> 40.6 us (1.097)
  the two profiles are of different devices: /device:TPU:2 before, /device:TPU:0 now
where the time goes in v5:
time: 40.6 us; the launch traced here: 40.3 us
  starting transfers between devices  13.9 us (34%)
  waiting for transfers between devices  13.2 us (33%)
  Pallas kernels  12.9 us (32%)
    ppermute x12, starting transfers between devices, swap(): return lax.ppermute(x, axis, [(i, partner(i, n)) for i in range(n)])  13.9 us
    ppermute x12, waiting for transfers between devices, swap(): return lax.ppermute(x, axis, [(i, partner(i, n)) for i in range(n)])  13.2 us
    pallas_call x8, Pallas kernels, call(): pl.pallas_call(body, out_shape=outs, in_specs=[pl.BlockSpec(memory_space=...  12.9 us
  transfers between devices with their start and end apart: 12, of which 6 were waited for; matrix products, arithmetic and copies ran while one was open for 0% of the time, Pallas kernels for 17%

profile of v5, /device:TPU:0, one launch (start us, length us, event | category | flops | bytes accessed | tf_op | source)
XLA Modules:
  0.0 40.3 jit_solution(470503584170254903)
XLA Ops:
  0.0 1.1 %gather.1 = (bf16[5,16,256]{2,1,0:T(8,128)(2,1)S(1)}, bf16[5,16,256]{2,1,0:T(8,128)(2,1)S(1)}, bf16[5,16,256]{2,1,0:T(8,128)(2,1)S(1)}, bf16[5,16,256]{2,1,0:T(8,128)(2,1)S(1)}) custom-call(s32[1]{0:T(128)} %bitcast.el_ref.refs_0_, s32[1]{0:T(128)} %bitcast.1.az_ref.refs_1_, bf16[128,256]{1,0:T(8,128)(2,1)} %bitcast.46, s32[5,4,16]{2,1,0:T(4,128)} %bitcast.47), custom_call_target="tpu_custom_call" | custom-call | flops 20971520 | bytes 230664 | tf_op jit(solution)/shard_map/gather/pallas_call | solution.py:70
  1.1 3.0 %collective-permute-start = (bf16[5,16,256]{2,1,0:T(8,128)(2,1)S(1)}, bf16[5,16,256]{2,1,0:T(8,128)(2,1)S(1)}, u32[]{:S(2)}, u32[]{:S(2)}) collective-permute-start(bf16[5,16,256]{2,1,0:T(8,128)(2,1)S(1)} %get-tuple-element.34), channel_id=1, source_target_pairs={{0,1},{1,0},{2,3},{3,2},{4,5},{5,4},{6,7},{7,6},{8,9},{9,8},{10,11... | collective-permute-start | bytes 122888 | tf_op jit(solution)/shard_map/ppermute | solution.py:43
  4.1 1.5 %collective-permute-start.1 = (bf16[5,16,256]{2,1,0:T(8,128)(2,1)S(1)}, bf16[5,16,256]{2,1,0:T(8,128)(2,1)S(1)}, u32[]{:S(2)}, u32[]{:S(2)}) collective-permute-start(bf16[5,16,256]{2,1,0:T(8,128)(2,1)S(1)} %get-tuple-element.35), channel_id=1, source_target_pairs={{0,2},{1,3},{2,0},{3,1},{4,6},{5,7},{6,4},{7,5},{8,10},{9,11},{10,... | collective-permute-start | bytes 122888 | tf_op jit(solution)/shard_map/ppermute | solution.py:43
  5.6 0.0 collective-permute-start.2
  5.7 2.3 %load.1 = (f32[320,512]{1,0:T(8,128)S(1)}, bf16[512,256]{1,0:T(8,128)(2,1)S(1)}, bf16[512,256]{1,0:T(8,128)(2,1)S(1)}, bf16[256,256]{1,0:T(8,128)(2,1)S(1)}, bf1...) custom-call(s32[1]{0:T(128)} %bitcast.el_ref.refs_0_, ...), custom_call_target="tpu_custom_call" | custom-call | flops 7864320 | bytes 8290312 | tf_op jit(solution)/shard_map/load/pallas_call | solution.py:70
  8.0 0.0 collective-permute-done
  8.0 0.1 collective-permute-done.1
  8.1 2.4 %collective-permute-done.2 = bf16[5,16,256]{2,1,0:T(8,128)(2,1)S(1)} collective-permute-done((bf16[5,16,256]{2,1,0:T(8,128)(2,1)S(1)}, bf16[5,16,256]{2,1,0:T(8,128)(2,1)S(1)}, u32[]{:S(2)}, u32[]{:S(2)}) %collective-permute-start.2) | collective-permute-done | bytes 40992 | tf_op jit(solution)/shard_map/ppermute | solution.py:43
  10.6 3.7 %collective-permute-start.3 = (bf16[64,256]{1,0:T(8,128)(2,1)S(1)}, bf16[64,256]{1,0:T(8,128)(2,1)S(1)}, u32[]{:S(2)}, u32[]{:S(2)}) collective-permute-start(bf16[64,256]{1,0:T(8,128)(2,1)S(1)} %pad_maximum_fusion.1), channel_id=1, source_target_pairs={{0,24},{4,28},{8,16},{12,20},{16,8},{20,12},{24,0},{28,4},{1,25},{... | collective-permute-start | bytes 98312 | tf_op jit(solution)/shard_map/ppermute | solution.py:43
  14.2 0.0 collective-permute-start.4
  14.2 0.1 collective-permute-start.5
  14.3 0.1 collective-permute-start.6
  14.4 0.5 %query.1 = (bf16[256,512]{1,0:T(8,128)(2,1)S(1)}, f32[512,1024]{1,0:T(8,128)S(1)}) custom-call(bf16[512,256]{1,0:T(8,128)(2,1)S(1)} %get-tuple-element.39.points_ref.refs_9_, bf16[512,256]{1,0:T(8,128)(2,1)S(1)} %get-tuple-element.40.skip_ref, bf16[256,256]{1,0:T(8,128)(2,1)S(1)} %get-tuple-element.41.w_query_ref, ...), custom_call_target="tpu_custom_call" | custom-call | flops 335544320 | bytes 3571712 | tf_op jit(solution)/shard_map/query/pallas_call | solution.py:70
  14.9 1.4 %collective-permute-done.3.refs_1_ = bf16[64,256]{1,0:T(8,128)(2,1)S(1)} collective-permute-done((bf16[64,256]{1,0:T(8,128)(2,1)S(1)}, bf16[64,256]{1,0:T(8,128)(2,1)S(1)}, u32[]{:S(2)}, u32[]{:S(2)}) %collective-permute-start.3) | collective-permute-done | bytes 32800 | tf_op jit(solution)/shard_map/ppermute | solution.py:43
  16.3 3.0 %collective-permute-done.4.refs_2_ = bf16[64,256]{1,0:T(8,128)(2,1)S(1)} collective-permute-done((bf16[64,256]{1,0:T(8,128)(2,1)S(1)}, bf16[64,256]{1,0:T(8,128)(2,1)S(1)}, u32[]{:S(2)}, u32[]{:S(2)}) %collective-permute-start.4) | collective-permute-done | bytes 32800 | tf_op jit(solution)/shard_map/ppermute | solution.py:43
  19.4 0.0 collective-permute-done.5.refs_3_
  19.4 0.0 collective-permute-done.6.refs_4_
  19.4 3.8 %far_row.1 = (f32[256,256]{1,0:T(8,128)S(1)}, bf16[256,256]{1,0:T(8,128)(2,1)S(1)}, bf16[320,256]{1,0:T(8,128)(2,1)S(1)}, bf16[256,320]{1,0:T(8,128)(2,1)S(1)}) custom-call(bf16[64,256]{1,0:T(8,128)(2,1)S(1)} %pad_maximum_fusion.after_ref.refs_0_, bf16[64,256]{1,0:T(8,128)(2,1)S(1)} %collective-permute-done.3.refs_1_, ...), custom_call_target="tpu_custom_call" | custom-call | flops 511705088 | bytes 5603328 | tf_op jit(solution)/shard_map/far_row/pallas_call | solution.py:70
  23.1 0.7 %collective-permute-start.8 = (bf16[256,256]{1,0:T(8,128)(2,1)S(1)}, bf16[256,256]{1,0:T(8,128)(2,1)S(1)}, u32[]{:S(2)}, u32[]{:S(2)}) collective-permute-start(bf16[256,256]{1,0:T(8,128)(2,1)S(1)} %get-tuple-element.52.far_ref), channel_id=1, source_target_pairs={{0,0},{1,2},{2,1},{3,3},{4,4},{5,6},{6,5},{7,7},{8,8},{9,10},{10,9... | collective-permute-start | bytes 393224 | tf_op jit(solution)/shard_map/ppermute | solution.py:43
  23.8 3.5 %near_row.1 = (f32[256,256]{1,0:T(8,128)S(1)}, bf16[256,256]{1,0:T(8,128)(2,1)S(1)}, bf16[2,256]{1,0:T(2,128)(2,1)S(1)}) custom-call(bf16[320,256]{1,0:T(8,128)(2,1)S(1)} %get-tuple-element.49.keys_ref, bf16[256,320]{1,0:T(8,128)(2,1)S(1)} %get-tuple-element.50.values_ref, bf16[256,512]{1,0:T(8,128)(2,1)S(1)} %get-tuple-element.43.refs_7_.q_ref, ...), custom_call_target="tpu_custom_call" | custom-call | flops 511705088 | bytes 5178368 | tf_op jit(solution)/shard_map/near_row/pallas_call | solution.py:70
  27.3 3.3 %collective-permute-start.7 = (bf16[256,256]{1,0:T(8,128)(2,1)S(1)}, bf16[256,256]{1,0:T(8,128)(2,1)S(1)}, u32[]{:S(2)}, u32[]{:S(2)}) collective-permute-start(bf16[256,256]{1,0:T(8,128)(2,1)S(1)} %get-tuple-element.51.near_ref), channel_id=1, source_target_pairs={{0,1},{1,0},{2,3},{3,2},{4,5},{5,4},{6,7},{7,6},{8,9},{9,8},{10,11... | collective-permute-start | bytes 393224 | tf_op jit(solution)/shard_map/ppermute | solution.py:43
  30.6 0.1 collective-permute-start.9
  30.6 3.5 %collective-permute-done.9.halo_ends_ref = bf16[2,256]{1,0:T(2,128)(2,1)S(1)} collective-permute-done((bf16[2,256]{1,0:T(2,128)(2,1)S(1)}, bf16[2,256]{1,0:T(2,128)(2,1)S(1)}, u32[]{:S(2)}, u32[]{:S(2)}) %collective-permute-start.9) | collective-permute-done | bytes 1056 | tf_op jit(solution)/shard_map/ppermute | solution.py:43
  34.1 0.0 collective-permute-done.8.far_halo_ref.far_ref
  34.1 0.1 collective-permute-start.10
  34.2 1.5 %collective-permute-start.11 = (bf16[4,256]{1,0:T(4,128)(2,1)S(1)}, bf16[4,256]{1,0:T(4,128)(2,1)S(1)}, u32[]{:S(2)}, u32[]{:S(2)}) collective-permute-start(bf16[4,256]{1,0:T(4,128)(2,1)S(1)} %get-tuple-element.55), channel_id=1, source_target_pairs={{0,28},{4,8},{8,4},{12,16},{16,12},{20,24},{24,20},{28,0},{1,29},{... | collective-permute-start | bytes 6152 | tf_op jit(solution)/shard_map/ppermute | solution.py:43
  35.7 0.6 %inside.1 = (f32[256,256]{1,0:T(8,128)S(1)}, f32[256,256]{1,0:T(8,128)S(1)}) custom-call(s32[1]{0:T(128)} %bitcast.el_ref.refs_0_, bf16[256,256]{1,0:T(8,128)(2,1)S(1)} %get-tuple-element.51.near_ref, bf16[256,256]{1,0:T(8,128)(2,1)S(1)} %get-tuple-element.52.far_ref, f32[256,256]{1,0:T(8,128)S(1)} %get-tuple-element.56.joined_near_ref, ...), custom_call_target="tpu_custom_call" | custom-call | flops 402653184 | bytes 2490372 | tf_op jit(solution)/shard_map/inside/pallas_call | solution.py:70
  36.3 0.0 collective-permute-done.7.near_ref
  36.3 0.0 collective-permute-done.10.inner_ref
  36.3 2.8 %collective-permute-done.11.outer_ref = bf16[4,256]{1,0:T(4,128)(2,1)S(1)} collective-permute-done((bf16[4,256]{1,0:T(4,128)(2,1)S(1)}, bf16[4,256]{1,0:T(4,128)(2,1)S(1)}, u32[]{:S(2)}, u32[]{:S(2)}) %collective-permute-start.11) | collective-permute-done | bytes 2080 | tf_op jit(solution)/shard_map/ppermute | solution.py:43
  39.1 1.2 %border.1 = bf16[2,256,256]{2,1,0:T(8,128)(2,1)} custom-call(s32[1]{0:T(128)} %bitcast.el_ref.refs_0_, s32[1]{0:T(128)} %bitcast.1.az_ref.refs_1_, bf16[256,256]{1,0:T(8,128)(2,1)S(1)} %collective-permute-done.7.near_ref, bf16[256,256]{1,0:T(8,128)(2,1)S(1)} %collective-permute-done.8.far_halo_ref.far_ref, ...), custom_call_target="tpu_custom_call" | custom-call | flops 201326592 | bytes 2232328 | tf_op jit(solution)/shard_map/border/pallas_call | solution.py:70
  (10 shorter events, 0.1 us)
Async XLA Ops:
  1.1 6.9 %collective-permute-start = (bf16[5,16,256]{2,1,0:T(8,128)(2,1)S(1)}, bf16[5,16,256]{2,1,0:T(8,128)(2,1)S(1)}, u32[]{:S(2)}, u32[]{:S(2)}) collective-permute-start(bf16[5,16,256]{2,1,0:T(8,128)(2,1)S(1)} %get-tuple-element.34), channel_id=1, source_target_pairs={{0,1},{1,0},{2,3},{3,2},{4,5},{5,4},{6,7},{7,6},{8,9},{9,8},{10,11... | collective-permute-start | bytes 122888 | tf_op jit(solution)/shard_map/ppermute | solution.py:43
  4.1 4.0 %collective-permute-start.1 = (bf16[5,16,256]{2,1,0:T(8,128)(2,1)S(1)}, bf16[5,16,256]{2,1,0:T(8,128)(2,1)S(1)}, u32[]{:S(2)}, u32[]{:S(2)}) collective-permute-start(bf16[5,16,256]{2,1,0:T(8,128)(2,1)S(1)} %get-tuple-element.35), channel_id=1, source_target_pairs={{0,2},{1,3},{2,0},{3,1},{4,6},{5,7},{6,4},{7,5},{8,10},{9,11},{10,... | collective-permute-start | bytes 122888 | tf_op jit(solution)/shard_map/ppermute | solution.py:43
  5.6 4.9 %collective-permute-start.2 = (bf16[5,16,256]{2,1,0:T(8,128)(2,1)S(1)}, bf16[5,16,256]{2,1,0:T(8,128)(2,1)S(1)}, u32[]{:S(2)}, u32[]{:S(2)}) collective-permute-start(bf16[5,16,256]{2,1,0:T(8,128)(2,1)S(1)} %get-tuple-element.36), channel_id=1, source_target_pairs={{0,3},{1,2},{2,1},{3,0},{4,7},{5,6},{6,5},{7,4},{8,11},{9,10},{10,... | collective-permute-start | bytes 122888 | tf_op jit(solution)/shard_map/ppermute | solution.py:43
  10.6 5.8 %collective-permute-start.3 = (bf16[64,256]{1,0:T(8,128)(2,1)S(1)}, bf16[64,256]{1,0:T(8,128)(2,1)S(1)}, u32[]{:S(2)}, u32[]{:S(2)}) collective-permute-start(bf16[64,256]{1,0:T(8,128)(2,1)S(1)} %pad_maximum_fusion.1), channel_id=1, source_target_pairs={{0,24},{4,28},{8,16},{12,20},{16,8},{20,12},{24,0},{28,4},{1,25},{... | collective-permute-start | bytes 98312 | tf_op jit(solution)/shard_map/ppermute | solution.py:43
  14.2 5.1 %collective-permute-start.4 = (bf16[64,256]{1,0:T(8,128)(2,1)S(1)}, bf16[64,256]{1,0:T(8,128)(2,1)S(1)}, u32[]{:S(2)}, u32[]{:S(2)}) collective-permute-start(bf16[64,256]{1,0:T(8,128)(2,1)S(1)} %pad_maximum_fusion.2), channel_id=1, source_target_pairs={{0,28},{4,8},{8,4},{12,16},{16,12},{20,24},{24,20},{28,0},{1,29},{... | collective-permute-start | bytes 98312 | tf_op jit(solution)/shard_map/ppermute | solution.py:43
  14.2 5.1 %collective-permute-start.5 = (bf16[64,256]{1,0:T(8,128)(2,1)S(1)}, bf16[64,256]{1,0:T(8,128)(2,1)S(1)}, u32[]{:S(2)}, u32[]{:S(2)}) collective-permute-start(bf16[64,256]{1,0:T(8,128)(2,1)S(1)} %pad_maximum_fusion.3), channel_id=1, source_target_pairs={{0,8},{4,12},{8,0},{12,4},{16,24},{20,28},{24,16},{28,20},{1,9},{5... | collective-permute-start | bytes 98312 | tf_op jit(solution)/shard_map/ppermute | solution.py:43
  14.3 5.0 %collective-permute-start.6 = (bf16[64,256]{1,0:T(8,128)(2,1)S(1)}, bf16[64,256]{1,0:T(8,128)(2,1)S(1)}, u32[]{:S(2)}, u32[]{:S(2)}) collective-permute-start(bf16[64,256]{1,0:T(8,128)(2,1)S(1)} %pad_maximum_fusion.4), channel_id=1, source_target_pairs={{0,4},{4,0},{8,12},{12,8},{16,20},{20,16},{24,28},{28,24},{1,5},{5... | collective-permute-start | bytes 98312 | tf_op jit(solution)/shard_map/ppermute | solution.py:43
  23.1 11.0 %collective-permute-start.8 = (bf16[256,256]{1,0:T(8,128)(2,1)S(1)}, bf16[256,256]{1,0:T(8,128)(2,1)S(1)}, u32[]{:S(2)}, u32[]{:S(2)}) collective-permute-start(bf16[256,256]{1,0:T(8,128)(2,1)S(1)} %get-tuple-element.52.far_ref), channel_id=1, source_target_pairs={{0,0},{1,2},{2,1},{3,3},{4,4},{5,6},{6,5},{7,7},{8,8},{9,10},{10,9... | collective-permute-start | bytes 393224 | tf_op jit(solution)/shard_map/ppermute | solution.py:43
  27.3 9.0 %collective-permute-start.7 = (bf16[256,256]{1,0:T(8,128)(2,1)S(1)}, bf16[256,256]{1,0:T(8,128)(2,1)S(1)}, u32[]{:S(2)}, u32[]{:S(2)}) collective-permute-start(bf16[256,256]{1,0:T(8,128)(2,1)S(1)} %get-tuple-element.51.near_ref), channel_id=1, source_target_pairs={{0,1},{1,0},{2,3},{3,2},{4,5},{5,4},{6,7},{7,6},{8,9},{9,8},{10,11... | collective-permute-start | bytes 393224 | tf_op jit(solution)/shard_map/ppermute | solution.py:43
  30.6 3.6 %collective-permute-start.9 = (bf16[2,256]{1,0:T(2,128)(2,1)S(1)}, bf16[2,256]{1,0:T(2,128)(2,1)S(1)}, u32[]{:S(2)}, u32[]{:S(2)}) collective-permute-start(bf16[2,256]{1,0:T(2,128)(2,1)S(1)} %get-tuple-element.53), channel_id=1, source_target_pairs={{0,1},{1,0},{2,3},{3,2},{4,5},{5,4},{6,7},{7,6},{8,9},{9,8},{10,11... | collective-permute-start | bytes 3080 | tf_op jit(solution)/shard_map/ppermute | solution.py:43
  34.1 2.2 %collective-permute-start.10 = (bf16[4,256]{1,0:T(4,128)(2,1)S(1)}, bf16[4,256]{1,0:T(4,128)(2,1)S(1)}, u32[]{:S(2)}, u32[]{:S(2)}) collective-permute-start(bf16[4,256]{1,0:T(4,128)(2,1)S(1)} %get-tuple-element.54), channel_id=1, source_target_pairs={{0,4},{4,0},{8,12},{12,8},{16,20},{20,16},{24,28},{28,24},{1,5},{5... | collective-permute-start | bytes 6152 | tf_op jit(solution)/shard_map/ppermute | solution.py:43
  34.2 4.9 %collective-permute-start.11 = (bf16[4,256]{1,0:T(4,128)(2,1)S(1)}, bf16[4,256]{1,0:T(4,128)(2,1)S(1)}, u32[]{:S(2)}, u32[]{:S(2)}) collective-permute-start(bf16[4,256]{1,0:T(4,128)(2,1)S(1)} %get-tuple-element.55), channel_id=1, source_target_pairs={{0,28},{4,8},{8,4},{12,16},{16,12},{20,24},{24,20},{28,0},{1,29},{... | collective-permute-start | bytes 6152 | tf_op jit(solution)/shard_map/ppermute | solution.py:43

commit v6 on v4

--- a/solution.py
+++ b/solution.py
@@ -74,7 +74,7 @@
         out_specs=[pl.BlockSpec(memory_space=VMEM) for _ in outs],
         scratch_shapes=list(scratch),
         input_output_aliases=aliases or {},
-        compiler_params=pltpu.CompilerParams(vmem_limit_bytes=20 * 1024 * 1024),
+        compiler_params=pltpu.CompilerParams(vmem_limit_bytes=32 * 1024 * 1024),
         cost_estimate=pl.CostEstimate(
             flops=flops, bytes_accessed=moved, transcendentals=transcendentals
         ),
@@ -163,6 +163,49 @@
     side_ref[...] = dot(skip_ref[...], w_skip_ref[...])
 
 
+def attend(keys, values_t, q_ref, bias_ref, score_ref, weight_ref, att_ref):
+    table, width = keys.shape
+    count = q_ref.shape[1]
+    head_width = width // HEADS
+    lanes = 128
+    for head in range(HEADS):
+        low, high = head * head_width, (head + 1) * head_width
+        score_ref[head] = dot(keys[:, low:high], q_ref[low:high, :]) + bias_ref[...]
+    for head in range(HEADS):
+        for start in range(0, count, lanes):
+            x = score_ref[head, :, start : start + lanes]
+            top = jnp.max(jnp.max(x.reshape(table // 64, 8, 8, lanes), axis=0), axis=0)
+            top = jnp.max(top, axis=0, keepdims=True)
+            weight_ref[head, :, start : start + lanes] = jnp.exp2(x - top).astype(BF16)
+    ones = jnp.ones((16, table), BF16)
+    for head in range(HEADS):
+        low, high = head * head_width, (head + 1) * head_width
+        lhs = jnp.concatenate([values_t[low:high, :], ones], axis=0)
+        mixed = dot(lhs, weight_ref[head])
+        scale = 1.0 / mixed[head_width : head_width + 1]
+        att_ref[low:high, :] = (mixed[:head_width] * scale).astype(BF16)
+
+
+def join(points_ref, side_ref, att_ref, w_out_ref, w_hid_ref, w_down_ref):
+    count = points_ref.shape[0]
+    size = count // 2
+    c1 = math.sqrt(2.0 / math.pi)
+    residuals, pres, out = [], [], []
+    for start in range(0, count, size):
+        part = slice(start, start + size)
+        residuals.append(
+            points_ref[part].astype(F32) + dot(att_ref[:, part], w_out_ref[...], ((0,), (0,)))
+        )
+    for at, residual in enumerate(residuals):
+        part = slice(at * size, (at + 1) * size)
+        pres.append(dot(rms(residual).astype(BF16), w_hid_ref[...]) + side_ref[part])
+    for residual, pre in zip(residuals, pres):
+        half = 0.5 * pre
+        inner = half + half * jnp.tanh(pre * (c1 + (c1 * 0.044715) * (pre * pre)))
+        out.append(residual + dot(inner.astype(BF16), w_down_ref[...]))
+    return out
+
+
 def main_body(az_ref, *refs, pieces):
     piece_refs = refs[:pieces]
     (
@@ -180,38 +223,26 @@
         far_ref,
         inner_edge_ref,
         outer_edge_ref,
+        score_ref,
+        weight_ref,
         att_ref,
     ) = refs[pieces:]
     width, count = q_ref.shape
-    head_width = width // HEADS
     received = jnp.concatenate([r[...] for r in piece_refs], axis=0)
-    table = received.shape[0]
     keys = dot(received, w_key_ref[...]).astype(BF16)
     normed_tokens = rms(received.astype(F32)).astype(BF16)
     values_t = dot(w_value_ref[...], normed_tokens, ((0,), (1,))).astype(BF16)
-    ones = jnp.ones((16, table), BF16)
-    for head in range(HEADS):
-        low, high = head * head_width, (head + 1) * head_width
-        scores = dot(keys[:, low:high], q_ref[low:high, :]) + bias_ref[...]
-        top = jnp.max(scores, axis=0, keepdims=True)
-        weights = jnp.exp2(scores - top).astype(BF16)
-        lhs = jnp.concatenate([values_t[low:high, :], ones], axis=0)
-        mixed = dot(lhs, weights)
-        att_ref[low:high, :] = (mixed[:head_width] / mixed[head_width : head_width + 1]).astype(BF16)
-    residual = points_ref[...].astype(F32) + dot(att_ref[...], w_out_ref[...], ((0,), (0,)))
-    normed = rms(residual).astype(BF16)
-    pre = dot(normed, w_hid_ref[...]) + side_ref[...]
-    c1 = math.sqrt(2.0 / math.pi)
-    half = 0.5 * pre
-    inner = (half + half * jnp.tanh(pre * (c1 + (c1 * 0.044715) * (pre * pre)))).astype(BF16)
-    joined = residual + dot(inner, w_down_ref[...])
-    conv = rms(joined)
-    joined_ref[...] = joined.reshape(joined_ref.shape)
+    attend(keys, values_t, q_ref, bias_ref, score_ref, weight_ref, att_ref)
+    joined = join(points_ref, side_ref, att_ref, w_out_ref, w_hid_ref, w_down_ref)
+    conv = []
+    for at, x in enumerate(joined):
+        joined_ref[at] = x
+        conv.append(rms(x))
     cols = count // 2
-    near_ref[0:cols] = conv[:cols].astype(BF16)
-    far_ref[0:cols] = conv[cols:].astype(BF16)
-    left = jnp.concatenate([conv[0:1], conv[cols : cols + 1]], axis=0)
-    right = jnp.concatenate([conv[cols - 1 : cols], conv[2 * cols - 1 :]], axis=0)
+    near_ref[0:cols] = conv[0].astype(BF16)
+    far_ref[0:cols] = conv[1].astype(BF16)
+    left = jnp.concatenate([x[:1] for x in conv], axis=0)
+    right = jnp.concatenate([x[cols - 1 :] for x in conv], axis=0)
     odd = lax.rem(az_ref[0], 2) == 1
     inner_edge_ref[...] = jnp.where(odd, left, right).astype(BF16)
     outer_edge_ref[...] = jnp.where(odd, right, left).astype(BF16)
@@ -340,7 +371,11 @@
         "main",
         (10 * table * count * width + 2 * count * width * 13 * width, table * count * HEADS),
         [SMEM] + [VMEM] * (len(pieces) + 9),
-        [VMEM((width, count), BF16)],
+        [
+            VMEM((HEADS, table, count), F32),
+            VMEM((HEADS, table, count), BF16),
+            VMEM((width, count), BF16),
+        ],
     )
     outer_got = swap(outer_edge, "az", next_chip)
     inner_got = swap(inner_edge, "az", same_chip)

time: 37 us -> 36.2 us (0.978)
  Pallas kernels: 10 us -> 9.2 us
    pallas_call x7, Pallas kernels: 10 us -> 9.2 us  [call(): pl.pallas_call(body, out_shape=outs, in_specs=[pl.BlockSpec(memory_space=...]
  transfers between devices with their start and end apart: 11 -> 11, of which waited for: 6 -> 6; matrix products, arithmetic and copies ran while one was open for 0% -> 0% of each run, Pallas kernels for 9% -> 10%
where the time goes in v6:
time: 36.2 us; the launch traced here: 35.9 us
  waiting for transfers between devices  14 us (39%)
  starting transfers between devices  12.6 us (35%)
  Pallas kernels  9.2 us (25%)
    ppermute x11, waiting for transfers between devices, swap(): return lax.ppermute(x, axis, [(i, partner(i, n)) for i in range(n)])  14 us
    ppermute x11, starting transfers between devices, swap(): return lax.ppermute(x, axis, [(i, partner(i, n)) for i in range(n)])  12.6 us
    pallas_call x7, Pallas kernels, call(): pl.pallas_call(body, out_shape=outs, in_specs=[pl.BlockSpec(memory_space=...  9.2 us
  transfers between devices with their start and end apart: 11, of which 6 were waited for; matrix products, arithmetic and copies ran while one was open for 0% of the time, Pallas kernels for 10%

profile of v6, /device:TPU:2, one launch (start us, length us, event | category | flops | bytes accessed | tf_op | source)
XLA Modules:
  0.0 35.9 jit_solution(8399408739618890986)
XLA Ops:
  0.0 1.1 %gather.1 = (bf16[5,16,256]{2,1,0:T(8,128)(2,1)S(1)}, bf16[5,16,256]{2,1,0:T(8,128)(2,1)S(1)}, bf16[5,16,256]{2,1,0:T(8,128)(2,1)S(1)}, bf16[5,16,256]{2,1,0:T(8,128)(2,1)S(1)}) custom-call(s32[1]{0:T(128)} %bitcast.el_ref.refs_0_, s32[1]{0:T(128)} %bitcast.1.az_ref.refs_1_, bf16[128,256]{1,0:T(8,128)(2,1)} %bitcast.46, s32[5,4,16]{2,1,0:T(4,128)} %bitcast.47), custom_call_target="tpu_custom_call" | custom-call | flops 20971520 | bytes 230664 | tf_op jit(solution)/shard_map/gather/pallas_call | solution.py:70
  1.1 0.1 collective-permute-start
  1.2 2.0 %collective-permute-start.1 = (bf16[5,16,256]{2,1,0:T(8,128)(2,1)S(1)}, bf16[5,16,256]{2,1,0:T(8,128)(2,1)S(1)}, u32[]{:S(2)}, u32[]{:S(2)}) collective-permute-start(bf16[5,16,256]{2,1,0:T(8,128)(2,1)S(1)} %get-tuple-element.31), channel_id=1, source_target_pairs={{0,2},{1,3},{2,0},{3,1},{4,6},{5,7},{6,4},{7,5},{8,10},{9,11},{10,... | collective-permute-start | bytes 122888 | tf_op jit(solution)/shard_map/ppermute | solution.py:43
  3.2 1.4 %collective-permute-start.2 = (bf16[5,16,256]{2,1,0:T(8,128)(2,1)S(1)}, bf16[5,16,256]{2,1,0:T(8,128)(2,1)S(1)}, u32[]{:S(2)}, u32[]{:S(2)}) collective-permute-start(bf16[5,16,256]{2,1,0:T(8,128)(2,1)S(1)} %get-tuple-element.32), channel_id=1, source_target_pairs={{0,3},{1,2},{2,1},{3,0},{4,7},{5,6},{6,5},{7,4},{8,11},{9,10},{10,... | collective-permute-start | bytes 122888 | tf_op jit(solution)/shard_map/ppermute | solution.py:43
  4.7 2.3 %load.1 = (f32[320,512]{1,0:T(8,128)S(1)}, bf16[512,256]{1,0:T(8,128)(2,1)S(1)}, bf16[512,256]{1,0:T(8,128)(2,1)S(1)}, bf16[256,256]{1,0:T(8,128)(2,1)S(1)}, bf1...) custom-call(s32[1]{0:T(128)} %bitcast.el_ref.refs_0_, ...), custom_call_target="tpu_custom_call" | custom-call | flops 7864320 | bytes 8290312 | tf_op jit(solution)/shard_map/load/pallas_call | solution.py:70
  7.0 0.0 collective-permute-done
  7.0 0.0 collective-permute-done.1
  7.1 1.1 %collective-permute-done.2 = bf16[5,16,256]{2,1,0:T(8,128)(2,1)S(1)} collective-permute-done((bf16[5,16,256]{2,1,0:T(8,128)(2,1)S(1)}, bf16[5,16,256]{2,1,0:T(8,128)(2,1)S(1)}, u32[]{:S(2)}, u32[]{:S(2)}) %collective-permute-start.2) | collective-permute-done | bytes 40992 | tf_op jit(solution)/shard_map/ppermute | solution.py:43
  8.2 3.7 %collective-permute-start.3 = (bf16[64,256]{1,0:T(8,128)(2,1)S(1)}, bf16[64,256]{1,0:T(8,128)(2,1)S(1)}, u32[]{:S(2)}, u32[]{:S(2)}) collective-permute-start(bf16[64,256]{1,0:T(8,128)(2,1)S(1)} %pad_maximum_fusion.1), channel_id=1, source_target_pairs={{0,24},{4,28},{8,16},{12,20},{16,8},{20,12},{24,0},{28,4},{1,25},{... | collective-permute-start | bytes 98312 | tf_op jit(solution)/shard_map/ppermute | solution.py:43
  11.8 0.0 collective-permute-start.4
  11.8 0.1 collective-permute-start.5
  11.9 0.1 collective-permute-start.6
  12.0 0.5 %query.1 = (bf16[256,512]{1,0:T(8,128)(2,1)S(1)}, f32[512,1024]{1,0:T(8,128)S(1)}) custom-call(bf16[512,256]{1,0:T(8,128)(2,1)S(1)} %get-tuple-element.33.points_ref.refs_7_, bf16[512,256]{1,0:T(8,128)(2,1)S(1)} %get-tuple-element.34.skip_ref, bf16[256,256]{1,0:T(8,128)(2,1)S(1)} %get-tuple-element.35.w_query_ref, ...), custom_call_target="tpu_custom_call" | custom-call | flops 335544320 | bytes 3571712 | tf_op jit(solution)/shard_map/query/pallas_call | solution.py:70
  12.5 1.4 %collective-permute-done.3.refs_1_ = bf16[64,256]{1,0:T(8,128)(2,1)S(1)} collective-permute-done((bf16[64,256]{1,0:T(8,128)(2,1)S(1)}, bf16[64,256]{1,0:T(8,128)(2,1)S(1)}, u32[]{:S(2)}, u32[]{:S(2)}) %collective-permute-start.3) | collective-permute-done | bytes 32800 | tf_op jit(solution)/shard_map/ppermute | solution.py:43
  13.9 3.0 %collective-permute-done.4.refs_2_ = bf16[64,256]{1,0:T(8,128)(2,1)S(1)} collective-permute-done((bf16[64,256]{1,0:T(8,128)(2,1)S(1)}, bf16[64,256]{1,0:T(8,128)(2,1)S(1)}, u32[]{:S(2)}, u32[]{:S(2)}) %collective-permute-start.4) | collective-permute-done | bytes 32800 | tf_op jit(solution)/shard_map/ppermute | solution.py:43
  17.0 0.0 collective-permute-done.5.refs_3_
  17.0 0.0 collective-permute-done.6.refs_4_
  17.0 3.5 %main.1 = (f32[2,256,256]{2,1,0:T(8,128)S(1)}, bf16[272,256]{1,0:T(8,128)(2,1)S(1)}, bf16[272,256]{1,0:T(8,128)(2,1)S(1)}, bf16[2,256]{1,0:T(2,128)(2,1)S(1)}, bf16[2,256]{1,0:T(2,128)(2,1)S(1)}) custom-call(s32[1]{0:T(128)} %bitcast.1.az_ref.refs_1_, bf16[64,256]{1,0:T(8,128)(2,1)S(1)} %pad_maximum_fusion.after_ref.refs_0_, ...), custom_call_target="tpu_custom_call" | custom-call | flops 1291845632 | bytes 5687300 | tf_op jit(solution)/shard_map/main/pallas_call | solution.py:70
  20.5 0.1 collective-permute-start.7
  20.6 1.2 %collective-permute-start.8 = (bf16[2,256]{1,0:T(2,128)(2,1)S(1)}, bf16[2,256]{1,0:T(2,128)(2,1)S(1)}, u32[]{:S(2)}, u32[]{:S(2)}) collective-permute-start(bf16[2,256]{1,0:T(2,128)(2,1)S(1)} %get-tuple-element.46), channel_id=1, source_target_pairs={{0,28},{4,8},{8,4},{12,16},{16,12},{20,24},{24,20},{28,0},{1,29},{... | collective-permute-start | bytes 3080 | tf_op jit(solution)/shard_map/ppermute | solution.py:43
  21.8 0.0 collective-permute-done.7.inner_ref
  21.8 3.6 %collective-permute-done.8.outer_ref = bf16[2,256]{1,0:T(2,128)(2,1)S(1)} collective-permute-done((bf16[2,256]{1,0:T(2,128)(2,1)S(1)}, bf16[2,256]{1,0:T(2,128)(2,1)S(1)}, u32[]{:S(2)}, u32[]{:S(2)}) %collective-permute-start.8) | collective-permute-done | bytes 1056 | tf_op jit(solution)/shard_map/ppermute | solution.py:43
  25.5 1.6 %collective-permute-start.9 = (bf16[272,256]{1,0:T(8,128)(2,1)S(1)}, bf16[272,256]{1,0:T(8,128)(2,1)S(1)}, u32[]{:S(2)}, u32[]{:S(2)}) collective-permute-start(bf16[272,256]{1,0:T(8,128)(2,1)S(1)} %get-tuple-element.49.near_ref), channel_id=1, source_target_pairs={{0,1},{1,0},{2,3},{3,2},{4,5},{5,4},{6,7},{7,6},{8,9},{9,8},{10,11... | collective-permute-start | bytes 417800 | tf_op jit(solution)/shard_map/ppermute | solution.py:43
  27.0 2.4 %collective-permute-start.10 = (bf16[272,256]{1,0:T(8,128)(2,1)S(1)}, bf16[272,256]{1,0:T(8,128)(2,1)S(1)}, u32[]{:S(2)}, u32[]{:S(2)}) collective-permute-start(bf16[272,256]{1,0:T(8,128)(2,1)S(1)} %get-tuple-element.50.far_ref), channel_id=1, source_target_pairs={{0,0},{1,2},{2,1},{3,3},{4,4},{5,6},{6,5},{7,7},{8,8},{9,10},{10,9... | collective-permute-start | bytes 417800 | tf_op jit(solution)/shard_map/ppermute | solution.py:43
  29.4 0.6 %inside.1.part_ref = f32[2,256,256]{2,1,0:T(8,128)S(1)} custom-call(s32[1]{0:T(128)} %bitcast.el_ref.refs_0_, bf16[272,256]{1,0:T(8,128)(2,1)S(1)} %get-tuple-element.49.near_ref, bf16[272,256]{1,0:T(8,128)(2,1)S(1)} %get-tuple-element.50.far_ref, f32[2,256,256]{2,1,0:T(8,128)S(1)} %get-tuple-element.51.joined_ref, ...), custom_call_target="tpu_custom_call" | custom-call | flops 402653184 | bytes 2506756 | tf_op jit(solution)/shard_map/inside/pallas_call | solution.py:70
  30.0 0.8 %collective-permute-done.9.near_ref = bf16[272,256]{1,0:T(8,128)(2,1)S(1)} collective-permute-done((bf16[272,256]{1,0:T(8,128)(2,1)S(1)}, bf16[272,256]{1,0:T(8,128)(2,1)S(1)}, u32[]{:S(2)}, u32[]{:S(2)}) %collective-permute-start.9) | collective-permute-done | bytes 139296 | tf_op jit(solution)/shard_map/ppermute | solution.py:43
  30.8 4.0 %collective-permute-done.10.far_ref = bf16[272,256]{1,0:T(8,128)(2,1)S(1)} collective-permute-done((bf16[272,256]{1,0:T(8,128)(2,1)S(1)}, bf16[272,256]{1,0:T(8,128)(2,1)S(1)}, u32[]{:S(2)}, u32[]{:S(2)}) %collective-permute-start.10) | collective-permute-done | bytes 139296 | tf_op jit(solution)/shard_map/ppermute | solution.py:43
  34.8 1.1 %border.1 = bf16[2,256,256]{2,1,0:T(8,128)(2,1)} custom-call(s32[1]{0:T(128)} %bitcast.el_ref.refs_0_, bf16[272,256]{1,0:T(8,128)(2,1)S(1)} %collective-permute-done.9.near_ref, bf16[272,256]{1,0:T(8,128)(2,1)S(1)} %collective-permute-done.10.far_ref, f32[2,256,256]{2,1,0:T(8,128)S(1)} %inside.1.part_ref, bf16[9,256,256]{2,1,0:T(8,128)(2,1)S(1)} %get-tuple-element.52.w_ref), custom_call_target="tpu_custom_call" | custom-call | flops 201326592 | bytes 2244612 | tf_op jit(solution)/shard_map/border/pallas_call | solution.py:70
  (10 shorter events, 0.1 us)
Async XLA Ops:
  1.1 5.9 %collective-permute-start = (bf16[5,16,256]{2,1,0:T(8,128)(2,1)S(1)}, bf16[5,16,256]{2,1,0:T(8,128)(2,1)S(1)}, u32[]{:S(2)}, u32[]{:S(2)}) collective-permute-start(bf16[5,16,256]{2,1,0:T(8,128)(2,1)S(1)} %get-tuple-element.30), channel_id=1, source_target_pairs={{0,1},{1,0},{2,3},{3,2},{4,5},{5,4},{6,7},{7,6},{8,9},{9,8},{10,11... | collective-permute-start | bytes 122888 | tf_op jit(solution)/shard_map/ppermute | solution.py:43
  1.2 5.8 %collective-permute-start.1 = (bf16[5,16,256]{2,1,0:T(8,128)(2,1)S(1)}, bf16[5,16,256]{2,1,0:T(8,128)(2,1)S(1)}, u32[]{:S(2)}, u32[]{:S(2)}) collective-permute-start(bf16[5,16,256]{2,1,0:T(8,128)(2,1)S(1)} %get-tuple-element.31), channel_id=1, source_target_pairs={{0,2},{1,3},{2,0},{3,1},{4,6},{5,7},{6,4},{7,5},{8,10},{9,11},{10,... | collective-permute-start | bytes 122888 | tf_op jit(solution)/shard_map/ppermute | solution.py:43
  3.2 4.9 %collective-permute-start.2 = (bf16[5,16,256]{2,1,0:T(8,128)(2,1)S(1)}, bf16[5,16,256]{2,1,0:T(8,128)(2,1)S(1)}, u32[]{:S(2)}, u32[]{:S(2)}) collective-permute-start(bf16[5,16,256]{2,1,0:T(8,128)(2,1)S(1)} %get-tuple-element.32), channel_id=1, source_target_pairs={{0,3},{1,2},{2,1},{3,0},{4,7},{5,6},{6,5},{7,4},{8,11},{9,10},{10,... | collective-permute-start | bytes 122888 | tf_op jit(solution)/shard_map/ppermute | solution.py:43
  8.2 5.8 %collective-permute-start.3 = (bf16[64,256]{1,0:T(8,128)(2,1)S(1)}, bf16[64,256]{1,0:T(8,128)(2,1)S(1)}, u32[]{:S(2)}, u32[]{:S(2)}) collective-permute-start(bf16[64,256]{1,0:T(8,128)(2,1)S(1)} %pad_maximum_fusion.1), channel_id=1, source_target_pairs={{0,24},{4,28},{8,16},{12,20},{16,8},{20,12},{24,0},{28,4},{1,25},{... | collective-permute-start | bytes 98312 | tf_op jit(solution)/shard_map/ppermute | solution.py:43
  11.8 5.1 %collective-permute-start.4 = (bf16[64,256]{1,0:T(8,128)(2,1)S(1)}, bf16[64,256]{1,0:T(8,128)(2,1)S(1)}, u32[]{:S(2)}, u32[]{:S(2)}) collective-permute-start(bf16[64,256]{1,0:T(8,128)(2,1)S(1)} %pad_maximum_fusion.2), channel_id=1, source_target_pairs={{0,28},{4,8},{8,4},{12,16},{16,12},{20,24},{24,20},{28,0},{1,29},{... | collective-permute-start | bytes 98312 | tf_op jit(solution)/shard_map/ppermute | solution.py:43
  11.8 5.1 %collective-permute-start.5 = (bf16[64,256]{1,0:T(8,128)(2,1)S(1)}, bf16[64,256]{1,0:T(8,128)(2,1)S(1)}, u32[]{:S(2)}, u32[]{:S(2)}) collective-permute-start(bf16[64,256]{1,0:T(8,128)(2,1)S(1)} %pad_maximum_fusion.3), channel_id=1, source_target_pairs={{0,8},{4,12},{8,0},{12,4},{16,24},{20,28},{24,16},{28,20},{1,9},{5... | collective-permute-start | bytes 98312 | tf_op jit(solution)/shard_map/ppermute | solution.py:43
  11.9 5.0 %collective-permute-start.6 = (bf16[64,256]{1,0:T(8,128)(2,1)S(1)}, bf16[64,256]{1,0:T(8,128)(2,1)S(1)}, u32[]{:S(2)}, u32[]{:S(2)}) collective-permute-start(bf16[64,256]{1,0:T(8,128)(2,1)S(1)} %pad_maximum_fusion.4), channel_id=1, source_target_pairs={{0,4},{4,0},{8,12},{12,8},{16,20},{20,16},{24,28},{28,24},{1,5},{5... | collective-permute-start | bytes 98312 | tf_op jit(solution)/shard_map/ppermute | solution.py:43
  20.5 1.3 %collective-permute-start.7 = (bf16[2,256]{1,0:T(2,128)(2,1)S(1)}, bf16[2,256]{1,0:T(2,128)(2,1)S(1)}, u32[]{:S(2)}, u32[]{:S(2)}) collective-permute-start(bf16[2,256]{1,0:T(2,128)(2,1)S(1)} %get-tuple-element.45), channel_id=1, source_target_pairs={{0,4},{4,0},{8,12},{12,8},{16,20},{20,16},{24,28},{28,24},{1,5},{5... | collective-permute-start | bytes 3080 | tf_op jit(solution)/shard_map/ppermute | solution.py:43
  20.6 4.9 %collective-permute-start.8 = (bf16[2,256]{1,0:T(2,128)(2,1)S(1)}, bf16[2,256]{1,0:T(2,128)(2,1)S(1)}, u32[]{:S(2)}, u32[]{:S(2)}) collective-permute-start(bf16[2,256]{1,0:T(2,128)(2,1)S(1)} %get-tuple-element.46), channel_id=1, source_target_pairs={{0,28},{4,8},{8,4},{12,16},{16,12},{20,24},{24,20},{28,0},{1,29},{... | collective-permute-start | bytes 3080 | tf_op jit(solution)/shard_map/ppermute | solution.py:43
  25.5 5.4 %collective-permute-start.9 = (bf16[272,256]{1,0:T(8,128)(2,1)S(1)}, bf16[272,256]{1,0:T(8,128)(2,1)S(1)}, u32[]{:S(2)}, u32[]{:S(2)}) collective-permute-start(bf16[272,256]{1,0:T(8,128)(2,1)S(1)} %get-tuple-element.49.near_ref), channel_id=1, source_target_pairs={{0,1},{1,0},{2,3},{3,2},{4,5},{5,4},{6,7},{7,6},{8,9},{9,8},{10,11... | collective-permute-start | bytes 417800 | tf_op jit(solution)/shard_map/ppermute | solution.py:43
  27.0 7.8 %collective-permute-start.10 = (bf16[272,256]{1,0:T(8,128)(2,1)S(1)}, bf16[272,256]{1,0:T(8,128)(2,1)S(1)}, u32[]{:S(2)}, u32[]{:S(2)}) collective-permute-start(bf16[272,256]{1,0:T(8,128)(2,1)S(1)} %get-tuple-element.50.far_ref), channel_id=1, source_target_pairs={{0,0},{1,2},{2,1},{3,3},{4,4},{5,6},{6,5},{7,7},{8,8},{9,10},{10,9... | collective-permute-start | bytes 417800 | tf_op jit(solution)/shard_map/ppermute | solution.py:43

commit v7 on v5

--- a/solution.py
+++ b/solution.py
@@ -74,7 +74,7 @@
         out_specs=[pl.BlockSpec(memory_space=VMEM) for _ in outs],
         scratch_shapes=list(scratch),
         input_output_aliases=aliases or {},
-        compiler_params=pltpu.CompilerParams(vmem_limit_bytes=20 * 1024 * 1024),
+        compiler_params=pltpu.CompilerParams(vmem_limit_bytes=32 * 1024 * 1024),
         cost_estimate=pl.CostEstimate(
             flops=flops, bytes_accessed=moved, transcendentals=transcendentals
         ),
@@ -124,17 +124,30 @@
     cols = points_ref.shape[0] // 2
     count = 2 * cols
     first, later = [], []
+    turn = cols // 4
+    spans = [
+        (even, turn, 0, 2 * turn),
+        (even, 3 * turn, 2 * turn, turn),
+        (even, 0, 3 * turn, turn),
+        (1 - even, 0, cols, cols),
+    ]
     for r, at in enumerate((even, 1 - even)):
-        rows = pl.ds(r * cols, cols)
         first.append(pltpu.make_async_copy(idx_hbm.at[at], idx_ref.at[r], sems.at[r]))
-        later.append(pltpu.make_async_copy(points_hbm.at[at], points_ref.at[rows], sems.at[2 + r]))
-        later.append(pltpu.make_async_copy(skip_hbm.at[at], skip_ref.at[rows], sems.at[4 + r]))
+    for r, (at, low, to, size) in enumerate(spans):
+        rows, place = pl.ds(low, size), pl.ds(to, size)
+        later.append(
+            pltpu.make_async_copy(points_hbm.at[at, rows], points_ref.at[place], sems.at[2 + r])
+        )
+        later.append(
+            pltpu.make_async_copy(skip_hbm.at[at, rows], skip_ref.at[place], sems.at[6 + r])
+        )
     for k in range(held):
-        later.append(pltpu.make_async_copy(held_hbm[k], held_refs[k], sems.at[6 + k]))
+        later.append(pltpu.make_async_copy(held_hbm[k], held_refs[k], sems.at[10 + k]))
     for c in first + later:
         c.start()
     for c in first:
         c.wait()
+    idx_ref[0] = pltpu.roll(idx_ref[0], cols - turn, 1)
     near = idx_ref.shape[1]
     lanes = 128
     for piece in range(bias_ref.shape[0] // (groups * capacity)):
@@ -163,23 +176,89 @@
     side_ref[...] = dot(skip_ref[...], w_skip_ref[...])
 
 
-def table_body(*refs, pieces):
+def attend(keys, values_t, q_ref, bias_ref, score_ref, weight_ref, att_ref, first):
+    table, width = keys.shape
+    count = att_ref.shape[1]
+    part = slice(first, first + count)
+    head_width = width // HEADS
+    lanes = 128
+    for head in range(HEADS):
+        low, high = head * head_width, (head + 1) * head_width
+        score_ref[head] = dot(keys[:, low:high], q_ref[low:high, part]) + bias_ref[:, part]
+    for head in range(HEADS):
+        for start in range(0, count, lanes):
+            x = score_ref[head, :, start : start + lanes]
+            top = jnp.max(jnp.max(x.reshape(table // 64, 8, 8, lanes), axis=0), axis=0)
+            top = jnp.max(top, axis=0, keepdims=True)
+            weight_ref[head, :, start : start + lanes] = jnp.exp2(x - top).astype(BF16)
+    ones = jnp.ones((16, table), BF16)
+    for head in range(HEADS):
+        low, high = head * head_width, (head + 1) * head_width
+        lhs = jnp.concatenate([values_t[low:high, :], ones], axis=0)
+        mixed = dot(lhs, weight_ref[head])
+        scale = 1.0 / mixed[head_width : head_width + 1]
+        att_ref[low:high, :] = (mixed[:head_width] * scale).astype(BF16)
+
+
+def join(points_ref, side_ref, att_ref, w_out_ref, w_hid_ref, w_down_ref, first, sizes):
+    c1 = math.sqrt(2.0 / math.pi)
+    residuals, pres, out = [], [], []
+    starts = [sum(sizes[:k]) for k in range(len(sizes))]
+    for start, size in zip(starts, sizes):
+        rows = slice(first + start, first + start + size)
+        mixed = att_ref[:, start : start + size]
+        residuals.append(
+            points_ref[rows].astype(F32) + dot(mixed, w_out_ref[...], ((0,), (0,)))
+        )
+    for start, size, residual in zip(starts, sizes, residuals):
+        rows = slice(first + start, first + start + size)
+        pres.append(dot(rms(residual).astype(BF16), w_hid_ref[...]) + side_ref[rows])
+    for residual, pre in zip(residuals, pres):
+        half = 0.5 * pre
+        inner = half + half * jnp.tanh(pre * (c1 + (c1 * 0.044715) * (pre * pre)))
+        out.append(residual + dot(inner.astype(BF16), w_down_ref[...]))
+    return out
+
+
+def block_body(*refs, pieces, first):
     (
         w_key_ref,
         w_value_ref,
-        *rest,
+        q_ref,
+        bias_ref,
+        points_ref,
+        side_ref,
+        w_out_ref,
+        w_hid_ref,
+        w_down_ref,
+        joined_ref,
+        block_ref,
+        ends_ref,
         keys_ref,
         values_ref,
+        score_ref,
+        weight_ref,
         att_ref,
     ) = refs[pieces:]
     received = jnp.concatenate([r[...] for r in refs[:pieces]], axis=0)
-    keys_ref[...] = dot(received, w_key_ref[...]).astype(BF16)
+    keys = dot(received, w_key_ref[...]).astype(BF16)
     normed_tokens = rms(received.astype(F32)).astype(BF16)
-    values_ref[...] = dot(w_value_ref[...], normed_tokens, ((0,), (1,))).astype(BF16)
-    row_body(keys_ref, values_ref, *rest, att_ref, row=1)
-
-
-def row_body(
+    values_t = dot(w_value_ref[...], normed_tokens, ((0,), (1,))).astype(BF16)
+    keys_ref[...], values_ref[...] = keys, values_t
+    attend(keys, values_t, q_ref, bias_ref, score_ref, weight_ref, att_ref, first)
+    size = block_ref.shape[0]
+    (joined,) = join(
+        points_ref, side_ref, att_ref, w_out_ref, w_hid_ref, w_down_ref, first, (size,)
+    )
+    joined_ref[...] = joined
+    block = rms(joined)
+    block_ref[...] = block.astype(BF16)
+    turn = size // 2
+    ends = jnp.concatenate([block[turn : turn + 1], block[turn - 1 : turn]], axis=0)
+    ends_ref[...] = ends.astype(BF16)
+
+
+def far_body(
     keys_ref,
     values_ref,
     q_ref,
@@ -190,36 +269,57 @@
     w_hid_ref,
     w_down_ref,
     joined_ref,
-    conv_ref,
-    *refs,
-    row,
+    far_ref,
+    score_ref,
+    weight_ref,
+    att_ref,
 ):
-    att_ref = refs[-1]
-    width, cols = att_ref.shape
-    lanes = slice(row * cols, (row + 1) * cols)
-    head_width = width // HEADS
-    keys = keys_ref[...]
-    ones = jnp.ones((16, keys.shape[0]), BF16)
-    for head in range(HEADS):
-        low, high = head * head_width, (head + 1) * head_width
-        scores = dot(keys[:, low:high], q_ref[low:high, lanes]) + bias_ref[:, lanes]
-        top = jnp.max(scores, axis=0, keepdims=True)
-        weights = jnp.exp2(scores - top).astype(BF16)
-        lhs = jnp.concatenate([values_ref[low:high, :], ones], axis=0)
-        mixed = dot(lhs, weights)
-        att_ref[low:high, :] = (mixed[:head_width] / mixed[head_width : head_width + 1]).astype(BF16)
-    residual = points_ref[lanes].astype(F32) + dot(att_ref[...], w_out_ref[...], ((0,), (0,)))
-    normed = rms(residual).astype(BF16)
-    pre = dot(normed, w_hid_ref[...]) + side_ref[lanes]
-    c1 = math.sqrt(2.0 / math.pi)
-    half = 0.5 * pre
-    inner = (half + half * jnp.tanh(pre * (c1 + (c1 * 0.044715) * (pre * pre)))).astype(BF16)
-    joined = residual + dot(inner, w_down_ref[...])
-    conv = rms(joined)
-    joined_ref[...] = joined
-    conv_ref[...] = conv.astype(BF16)
-    if len(refs) == 2:
-        refs[0][...] = jnp.concatenate([conv[:1], conv[cols - 1 :]], axis=0).astype(BF16)
+    cols = far_ref.shape[0]
+    attend(
+        keys_ref[...], values_ref[...], q_ref, bias_ref, score_ref, weight_ref, att_ref, cols
+    )
+    half = cols // 2
+    parts = join(
+        points_ref, side_ref, att_ref, w_out_ref, w_hid_ref, w_down_ref, cols, (half, half)
+    )
+    for at, part in enumerate(parts):
+        joined_ref[at * half : (at + 1) * half] = part
+        far_ref[at * half : (at + 1) * half] = rms(part).astype(BF16)
+
+
+def near_body(
+    keys_ref,
+    values_ref,
+    joined_ends_ref,
+    block_ref,
+    q_ref,
+    bias_ref,
+    points_ref,
+    side_ref,
+    w_out_ref,
+    w_hid_ref,
+    w_down_ref,
+    joined_ref,
+    near_ref,
+    score_ref,
+    weight_ref,
+    att_ref,
+):
+    attend(
+        keys_ref[...], values_ref[...], q_ref, bias_ref, score_ref, weight_ref, att_ref, 0
+    )
+    size = block_ref.shape[0]
+    turn = size // 2
+    (middle,) = join(
+        points_ref, side_ref, att_ref, w_out_ref, w_hid_ref, w_down_ref, 0, (size,)
+    )
+    for ref, inner, ends_ref in (
+        (joined_ref, middle, joined_ends_ref),
+        (near_ref, rms(middle).astype(BF16), block_ref),
+    ):
+        ref[turn : turn + size] = inner
+        ref[turn + size :] = ends_ref[:turn]
+        ref[:turn] = ends_ref[turn:]
 
 
 def ends_of(ref):
@@ -351,7 +451,7 @@
         "load",
         (table * count * 48, table * count),
         [SMEM, SMEM] + [HBM] * (3 + len(held)),
-        [VMEM(idx.shape, jnp.int32), dma((6 + len(held),))],
+        [VMEM(idx.shape, jnp.int32), dma((10 + len(held),))],
     )
     query_t, side = call(
         query_body,
@@ -361,29 +461,56 @@
         (2 * count * width * 5 * width, 0),
     )
     w_key, w_value, w_out, w_hid, w_down, w_conv = held[2:]
+    half = cols // 2
     row_f32, row_bf16 = shape((cols, width), F32), shape((cols, width), BF16)
-    work = (5 * table * count * width + count * width * 9 * width, table * cols * HEADS)
+
+    def work(points):
+        return (10 * table * points * width + 18 * points * width * width, table * points * HEADS)
+
+    def room(points):
+        return [
+            VMEM((HEADS, table, points), F32),
+            VMEM((HEADS, table, points), BF16),
+            VMEM((width, points), BF16),
+        ]
+
     shared = [query_t, bias, points_v, side, w_out, w_hid, w_down]
-    joined_far, far, keys, values = call(
-        functools.partial(table_body, pieces=len(pieces)),
-        [row_f32, row_bf16, shape((table, width), BF16), shape((width, table), BF16)],
+    joined_block, block, near_ends, keys, values = call(
+        functools.partial(block_body, pieces=len(pieces), first=half),
+        [
+            shape((half, width), F32),
+            shape((half, width), BF16),
+            shape((2, width), BF16),
+            shape((table, width), BF16),
+            shape((width, table), BF16),
+        ],
         pieces + [w_key, w_value] + shared,
+        "near_ends",
+        work(half),
+        None,
+        room(half),
+    )
+    halo_ends = swap(near_ends, "el", same_chip)
+    joined_far, far = call(
+        far_body,
+        [row_f32, row_bf16],
+        [keys, values] + shared,
         "far_row",
-        work,
+        work(cols),
         None,
-        [VMEM((width, cols), BF16)],
-    )
+        room(cols),
+    )
+    far, halo_ends = lax.optimization_barrier((far, halo_ends))
     far_got = swap(far, "el", inner_pair)
-    joined_near, near, near_ends = call(
-        functools.partial(row_body, row=0),
-        [row_f32, row_bf16, shape((2, width), BF16)],
-        [keys, values] + shared,
+    joined_near, near = call(
+        near_body,
+        [row_f32, row_bf16],
+        [keys, values, joined_block, block] + shared,
         "near_row",
-        work,
+        work(half),
         None,
-        [VMEM((width, cols), BF16)],
-    )
-    halo_ends = swap(near_ends, "el", same_chip)
+        room(half),
+    )
     near_got = swap(near, "el", same_chip)
     inner_edge, outer_edge = call(
         edges_body,

time: 40.6 us -> 36.7 us (0.904)
  the two profiles are of different devices: /device:TPU:0 before, /device:TPU:2 now
where the time goes in v7:
time: 36.7 us; the launch traced here: 36.3 us
  starting transfers between devices  14.5 us (40%)
  Pallas kernels  11.2 us (31%)
  waiting for transfers between devices  10.4 us (28%)
    ppermute x12, starting transfers between devices, swap(): return lax.ppermute(x, axis, [(i, partner(i, n)) for i in range(n)])  14.5 us
    pallas_call x9, Pallas kernels, call(): pl.pallas_call(body, out_shape=outs, in_specs=[pl.BlockSpec(memory_space=...  11.2 us
    ppermute x12, waiting for transfers between devices, swap(): return lax.ppermute(x, axis, [(i, partner(i, n)) for i in range(n)])  10.4 us
  transfers between devices with their start and end apart: 12, of which 5 were waited for; matrix products, arithmetic and copies ran while one was open for 0% of the time, Pallas kernels for 20%

profile of v7, /device:TPU:2, one launch (start us, length us, event | category | flops | bytes accessed | tf_op | source)
XLA Modules:
  0.0 36.3 jit_solution(16398477405022631841)
XLA Ops:
  0.0 1.1 %gather.1 = (bf16[5,16,256]{2,1,0:T(8,128)(2,1)S(1)}, bf16[5,16,256]{2,1,0:T(8,128)(2,1)S(1)}, bf16[5,16,256]{2,1,0:T(8,128)(2,1)S(1)}, bf16[5,16,256]{2,1,0:T(8,128)(2,1)S(1)}) custom-call(s32[1]{0:T(128)} %bitcast.el_ref.refs_0_, s32[1]{0:T(128)} %bitcast.1.az_ref.refs_1_, bf16[128,256]{1,0:T(8,128)(2,1)} %bitcast.46, s32[5,4,16]{2,1,0:T(4,128)} %bitcast.47), custom_call_target="tpu_custom_call" | custom-call | flops 20971520 | bytes 230664 | tf_op jit(solution)/shard_map/gather/pallas_call | solution.py:70
  1.1 0.1 collective-permute-start
  1.2 2.0 %collective-permute-start.1 = (bf16[5,16,256]{2,1,0:T(8,128)(2,1)S(1)}, bf16[5,16,256]{2,1,0:T(8,128)(2,1)S(1)}, u32[]{:S(2)}, u32[]{:S(2)}) collective-permute-start(bf16[5,16,256]{2,1,0:T(8,128)(2,1)S(1)} %get-tuple-element.39), channel_id=1, source_target_pairs={{0,2},{1,3},{2,0},{3,1},{4,6},{5,7},{6,4},{7,5},{8,10},{9,11},{10,... | collective-permute-start | bytes 122888 | tf_op jit(solution)/shard_map/ppermute | solution.py:43
  3.2 1.4 %collective-permute-start.2 = (bf16[5,16,256]{2,1,0:T(8,128)(2,1)S(1)}, bf16[5,16,256]{2,1,0:T(8,128)(2,1)S(1)}, u32[]{:S(2)}, u32[]{:S(2)}) collective-permute-start(bf16[5,16,256]{2,1,0:T(8,128)(2,1)S(1)} %get-tuple-element.40), channel_id=1, source_target_pairs={{0,3},{1,2},{2,1},{3,0},{4,7},{5,6},{6,5},{7,4},{8,11},{9,10},{10,... | collective-permute-start | bytes 122888 | tf_op jit(solution)/shard_map/ppermute | solution.py:43
  4.7 2.4 %load.1 = (f32[320,512]{1,0:T(8,128)S(1)}, bf16[512,256]{1,0:T(8,128)(2,1)S(1)}, bf16[512,256]{1,0:T(8,128)(2,1)S(1)}, bf16[256,256]{1,0:T(8,128)(2,1)S(1)}, bf1...) custom-call(s32[1]{0:T(128)} %bitcast.el_ref.refs_0_, ...), custom_call_target="tpu_custom_call" | custom-call | flops 7864320 | bytes 8290312 | tf_op jit(solution)/shard_map/load/pallas_call | solution.py:70
  7.1 0.0 collective-permute-done
  7.1 0.0 collective-permute-done.1
  7.1 1.0 %collective-permute-done.2 = bf16[5,16,256]{2,1,0:T(8,128)(2,1)S(1)} collective-permute-done((bf16[5,16,256]{2,1,0:T(8,128)(2,1)S(1)}, bf16[5,16,256]{2,1,0:T(8,128)(2,1)S(1)}, u32[]{:S(2)}, u32[]{:S(2)}) %collective-permute-start.2) | collective-permute-done | bytes 40992 | tf_op jit(solution)/shard_map/ppermute | solution.py:43
  8.2 3.7 %collective-permute-start.3 = (bf16[64,256]{1,0:T(8,128)(2,1)S(1)}, bf16[64,256]{1,0:T(8,128)(2,1)S(1)}, u32[]{:S(2)}, u32[]{:S(2)}) collective-permute-start(bf16[64,256]{1,0:T(8,128)(2,1)S(1)} %pad_maximum_fusion.1), channel_id=1, source_target_pairs={{0,24},{4,28},{8,16},{12,20},{16,8},{20,12},{24,0},{28,4},{1,25},{... | collective-permute-start | bytes 98312 | tf_op jit(solution)/shard_map/ppermute | solution.py:43
  11.8 0.0 collective-permute-start.4
  11.8 0.1 collective-permute-start.5
  11.9 0.1 collective-permute-start.6
  12.0 0.5 %query.1 = (bf16[256,512]{1,0:T(8,128)(2,1)S(1)}, f32[512,1024]{1,0:T(8,128)S(1)}) custom-call(bf16[512,256]{1,0:T(8,128)(2,1)S(1)} %get-tuple-element.43.points_ref.refs_9_, bf16[512,256]{1,0:T(8,128)(2,1)S(1)} %get-tuple-element.44.skip_ref, bf16[256,256]{1,0:T(8,128)(2,1)S(1)} %get-tuple-element.45.w_query_ref, ...), custom_call_target="tpu_custom_call" | custom-call | flops 335544320 | bytes 3571712 | tf_op jit(solution)/shard_map/query/pallas_call | solution.py:70
  12.5 1.4 %collective-permute-done.3.refs_1_ = bf16[64,256]{1,0:T(8,128)(2,1)S(1)} collective-permute-done((bf16[64,256]{1,0:T(8,128)(2,1)S(1)}, bf16[64,256]{1,0:T(8,128)(2,1)S(1)}, u32[]{:S(2)}, u32[]{:S(2)}) %collective-permute-start.3) | collective-permute-done | bytes 32800 | tf_op jit(solution)/shard_map/ppermute | solution.py:43
  13.9 3.0 %collective-permute-done.4.refs_2_ = bf16[64,256]{1,0:T(8,128)(2,1)S(1)} collective-permute-done((bf16[64,256]{1,0:T(8,128)(2,1)S(1)}, bf16[64,256]{1,0:T(8,128)(2,1)S(1)}, u32[]{:S(2)}, u32[]{:S(2)}) %collective-permute-start.4) | collective-permute-done | bytes 32800 | tf_op jit(solution)/shard_map/ppermute | solution.py:43
  17.0 0.0 collective-permute-done.5.refs_3_
  17.0 0.0 collective-permute-done.6.refs_4_
  17.0 1.8 %near_ends.1 = (f32[128,256]{1,0:T(8,128)S(1)}, bf16[128,256]{1,0:T(8,128)(2,1)S(1)}, bf16[2,256]{1,0:T(2,128)(2,1)S(1)}, bf16[320,256]{1,0:T(8,128)(2,1)S(1)}, bf16[256,320]{1,0:T(8,128)(2,1)S(1)}) custom-call(bf16[64,256]{1,0:T(8,128)(2,1)S(1)} %pad_maximum_fusion.after_ref.refs_0_, bf16[64,256]{1,0:T(8,128)(2,1)S(1)} %collective-permute-done.3.refs_1_, ...), custom_call_target="tpu_custom_call" | custom-call | flops 255852544 | bytes 5407744 | tf_op jit(solution)/shard_map/near_ends/pallas_call | solution.py:70
  18.7 1.6 %collective-permute-start.8 = (bf16[2,256]{1,0:T(2,128)(2,1)S(1)}, bf16[2,256]{1,0:T(2,128)(2,1)S(1)}, u32[]{:S(2)}, u32[]{:S(2)}) collective-permute-start(bf16[2,256]{1,0:T(2,128)(2,1)S(1)} %get-tuple-element.59), channel_id=1, source_target_pairs={{0,1},{1,0},{2,3},{3,2},{4,5},{5,4},{6,7},{7,6},{8,9},{9,8},{10,11... | collective-permute-start | bytes 3080 | tf_op jit(solution)/shard_map/ppermute | solution.py:43
  20.3 2.1 %far_row.1 = (f32[256,256]{1,0:T(8,128)S(1)}, bf16[256,256]{1,0:T(8,128)(2,1)S(1)}) custom-call(bf16[320,256]{1,0:T(8,128)(2,1)S(1)} %get-tuple-element.53.keys_ref, bf16[256,320]{1,0:T(8,128)(2,1)S(1)} %get-tuple-element.54.values_ref, bf16[256,512]{1,0:T(8,128)(2,1)S(1)} %get-tuple-element.47.refs_7_.q_ref, ...), custom_call_target="tpu_custom_call" | custom-call | flops 511705088 | bytes 5177344 | tf_op jit(solution)/shard_map/far_row/pallas_call | solution.py:70
  22.4 0.0 collective-permute-done.8.halo_ends_ref
  22.4 3.3 %collective-permute-start.9 = (bf16[256,256]{1,0:T(8,128)(2,1)S(1)}, bf16[256,256]{1,0:T(8,128)(2,1)S(1)}, u32[]{:S(2)}, u32[]{:S(2)}) collective-permute-start(bf16[256,256]{1,0:T(8,128)(2,1)S(1)} %get-tuple-element.60.far_ref), channel_id=1, source_target_pairs={{0,0},{1,2},{2,1},{3,3},{4,4},{5,6},{6,5},{7,7},{8,8},{9,10},{10,9... | collective-permute-start | bytes 393224 | tf_op jit(solution)/shard_map/ppermute | solution.py:43
  25.7 1.6 %near_row.1 = (f32[256,256]{1,0:T(8,128)S(1)}, bf16[256,256]{1,0:T(8,128)(2,1)S(1)}) custom-call(bf16[320,256]{1,0:T(8,128)(2,1)S(1)} %get-tuple-element.53.keys_ref, bf16[256,320]{1,0:T(8,128)(2,1)S(1)} %get-tuple-element.54.values_ref, f32[128,256]{1,0:T(8,128)S(1)} %get-tuple-element.55.joined_ends_ref, bf16[128,256]{1,0:T(8,128)(2,1)S(1)} %get-tuple-element.56.block_ref, ...), custom_call_target="tpu_custom_call" | custom-call | flops 255852544 | bytes 5373952 | tf_op jit(solution)/shard_map/near_row/pallas_call | solution.py:70
  27.3 0.1 collective-permute-start.7
  27.4 2.8 %collective-permute-done.9.far_halo_ref.far_ref = bf16[256,256]{1,0:T(8,128)(2,1)S(1)} collective-permute-done((bf16[256,256]{1,0:T(8,128)(2,1)S(1)}, bf16[256,256]{1,0:T(8,128)(2,1)S(1)}, u32[]{:S(2)}, u32[]{:S(2)}) %collective-permute-start.9) | collective-permute-done | bytes 131104 | tf_op jit(solution)/shard_map/ppermute | solution.py:43
  30.1 0.1 collective-permute-start.10
  30.2 2.1 %collective-permute-start.11 = (bf16[4,256]{1,0:T(4,128)(2,1)S(1)}, bf16[4,256]{1,0:T(4,128)(2,1)S(1)}, u32[]{:S(2)}, u32[]{:S(2)}) collective-permute-start(bf16[4,256]{1,0:T(4,128)(2,1)S(1)} %get-tuple-element.63), channel_id=1, source_target_pairs={{0,28},{4,8},{8,4},{12,16},{16,12},{20,24},{24,20},{28,0},{1,29},{... | collective-permute-start | bytes 6152 | tf_op jit(solution)/shard_map/ppermute | solution.py:43
  32.3 0.6 %inside.1 = (f32[256,256]{1,0:T(8,128)S(1)}, f32[256,256]{1,0:T(8,128)S(1)}) custom-call(s32[1]{0:T(128)} %bitcast.el_ref.refs_0_, bf16[256,256]{1,0:T(8,128)(2,1)S(1)} %get-tuple-element.57.near_ref, bf16[256,256]{1,0:T(8,128)(2,1)S(1)} %get-tuple-element.60.far_ref, f32[256,256]{1,0:T(8,128)S(1)} %get-tuple-element.64.joined_near_ref, ...), custom_call_target="tpu_custom_call" | custom-call | flops 402653184 | bytes 2490372 | tf_op jit(solution)/shard_map/inside/pallas_call | solution.py:70
  32.9 0.0 collective-permute-done.7.near_ref
  32.9 0.0 collective-permute-done.10.inner_ref
  32.9 2.2 %collective-permute-done.11.outer_ref = bf16[4,256]{1,0:T(4,128)(2,1)S(1)} collective-permute-done((bf16[4,256]{1,0:T(4,128)(2,1)S(1)}, bf16[4,256]{1,0:T(4,128)(2,1)S(1)}, u32[]{:S(2)}, u32[]{:S(2)}) %collective-permute-start.11) | collective-permute-done | bytes 2080 | tf_op jit(solution)/shard_map/ppermute | solution.py:43
  35.1 1.2 %border.1 = bf16[2,256,256]{2,1,0:T(8,128)(2,1)} custom-call(s32[1]{0:T(128)} %bitcast.el_ref.refs_0_, s32[1]{0:T(128)} %bitcast.1.az_ref.refs_1_, bf16[256,256]{1,0:T(8,128)(2,1)S(1)} %collective-permute-done.7.near_ref, bf16[256,256]{1,0:T(8,128)(2,1)S(1)} %collective-permute-done.9.far_halo_ref.far_ref, ...), custom_call_target="tpu_custom_call" | custom-call | flops 201326592 | bytes 2232328 | tf_op jit(solution)/shard_map/border/pallas_call | solution.py:70
  (10 shorter events, 0.1 us)
Async XLA Ops:
  1.1 5.9 %collective-permute-start = (bf16[5,16,256]{2,1,0:T(8,128)(2,1)S(1)}, bf16[5,16,256]{2,1,0:T(8,128)(2,1)S(1)}, u32[]{:S(2)}, u32[]{:S(2)}) collective-permute-start(bf16[5,16,256]{2,1,0:T(8,128)(2,1)S(1)} %get-tuple-element.38), channel_id=1, source_target_pairs={{0,1},{1,0},{2,3},{3,2},{4,5},{5,4},{6,7},{7,6},{8,9},{9,8},{10,11... | collective-permute-start | bytes 122888 | tf_op jit(solution)/shard_map/ppermute | solution.py:43
  1.2 5.9 %collective-permute-start.1 = (bf16[5,16,256]{2,1,0:T(8,128)(2,1)S(1)}, bf16[5,16,256]{2,1,0:T(8,128)(2,1)S(1)}, u32[]{:S(2)}, u32[]{:S(2)}) collective-permute-start(bf16[5,16,256]{2,1,0:T(8,128)(2,1)S(1)} %get-tuple-element.39), channel_id=1, source_target_pairs={{0,2},{1,3},{2,0},{3,1},{4,6},{5,7},{6,4},{7,5},{8,10},{9,11},{10,... | collective-permute-start | bytes 122888 | tf_op jit(solution)/shard_map/ppermute | solution.py:43
  3.2 4.9 %collective-permute-start.2 = (bf16[5,16,256]{2,1,0:T(8,128)(2,1)S(1)}, bf16[5,16,256]{2,1,0:T(8,128)(2,1)S(1)}, u32[]{:S(2)}, u32[]{:S(2)}) collective-permute-start(bf16[5,16,256]{2,1,0:T(8,128)(2,1)S(1)} %get-tuple-element.40), channel_id=1, source_target_pairs={{0,3},{1,2},{2,1},{3,0},{4,7},{5,6},{6,5},{7,4},{8,11},{9,10},{10,... | collective-permute-start | bytes 122888 | tf_op jit(solution)/shard_map/ppermute | solution.py:43
  8.2 5.8 %collective-permute-start.3 = (bf16[64,256]{1,0:T(8,128)(2,1)S(1)}, bf16[64,256]{1,0:T(8,128)(2,1)S(1)}, u32[]{:S(2)}, u32[]{:S(2)}) collective-permute-start(bf16[64,256]{1,0:T(8,128)(2,1)S(1)} %pad_maximum_fusion.1), channel_id=1, source_target_pairs={{0,24},{4,28},{8,16},{12,20},{16,8},{20,12},{24,0},{28,4},{1,25},{... | collective-permute-start | bytes 98312 | tf_op jit(solution)/shard_map/ppermute | solution.py:43
  11.8 5.1 %collective-permute-start.4 = (bf16[64,256]{1,0:T(8,128)(2,1)S(1)}, bf16[64,256]{1,0:T(8,128)(2,1)S(1)}, u32[]{:S(2)}, u32[]{:S(2)}) collective-permute-start(bf16[64,256]{1,0:T(8,128)(2,1)S(1)} %pad_maximum_fusion.2), channel_id=1, source_target_pairs={{0,28},{4,8},{8,4},{12,16},{16,12},{20,24},{24,20},{28,0},{1,29},{... | collective-permute-start | bytes 98312 | tf_op jit(solution)/shard_map/ppermute | solution.py:43
  11.8 5.1 %collective-permute-start.5 = (bf16[64,256]{1,0:T(8,128)(2,1)S(1)}, bf16[64,256]{1,0:T(8,128)(2,1)S(1)}, u32[]{:S(2)}, u32[]{:S(2)}) collective-permute-start(bf16[64,256]{1,0:T(8,128)(2,1)S(1)} %pad_maximum_fusion.3), channel_id=1, source_target_pairs={{0,8},{4,12},{8,0},{12,4},{16,24},{20,28},{24,16},{28,20},{1,9},{5... | collective-permute-start | bytes 98312 | tf_op jit(solution)/shard_map/ppermute | solution.py:43
  11.9 5.0 %collective-permute-start.6 = (bf16[64,256]{1,0:T(8,128)(2,1)S(1)}, bf16[64,256]{1,0:T(8,128)(2,1)S(1)}, u32[]{:S(2)}, u32[]{:S(2)}) collective-permute-start(bf16[64,256]{1,0:T(8,128)(2,1)S(1)} %pad_maximum_fusion.4), channel_id=1, source_target_pairs={{0,4},{4,0},{8,12},{12,8},{16,20},{20,16},{24,28},{28,24},{1,5},{5... | collective-permute-start | bytes 98312 | tf_op jit(solution)/shard_map/ppermute | solution.py:43
  18.7 3.6 %collective-permute-start.8 = (bf16[2,256]{1,0:T(2,128)(2,1)S(1)}, bf16[2,256]{1,0:T(2,128)(2,1)S(1)}, u32[]{:S(2)}, u32[]{:S(2)}) collective-permute-start(bf16[2,256]{1,0:T(2,128)(2,1)S(1)} %get-tuple-element.59), channel_id=1, source_target_pairs={{0,1},{1,0},{2,3},{3,2},{4,5},{5,4},{6,7},{7,6},{8,9},{9,8},{10,11... | collective-permute-start | bytes 3080 | tf_op jit(solution)/shard_map/ppermute | solution.py:43
  22.4 7.8 %collective-permute-start.9 = (bf16[256,256]{1,0:T(8,128)(2,1)S(1)}, bf16[256,256]{1,0:T(8,128)(2,1)S(1)}, u32[]{:S(2)}, u32[]{:S(2)}) collective-permute-start(bf16[256,256]{1,0:T(8,128)(2,1)S(1)} %get-tuple-element.60.far_ref), channel_id=1, source_target_pairs={{0,0},{1,2},{2,1},{3,3},{4,4},{5,6},{6,5},{7,7},{8,8},{9,10},{10,9... | collective-permute-start | bytes 393224 | tf_op jit(solution)/shard_map/ppermute | solution.py:43
  27.3 5.6 %collective-permute-start.7 = (bf16[256,256]{1,0:T(8,128)(2,1)S(1)}, bf16[256,256]{1,0:T(8,128)(2,1)S(1)}, u32[]{:S(2)}, u32[]{:S(2)}) collective-permute-start(bf16[256,256]{1,0:T(8,128)(2,1)S(1)} %get-tuple-element.57.near_ref), channel_id=1, source_target_pairs={{0,1},{1,0},{2,3},{3,2},{4,5},{5,4},{6,7},{7,6},{8,9},{9,8},{10,11... | collective-permute-start | bytes 393224 | tf_op jit(solution)/shard_map/ppermute | solution.py:43
  30.1 2.8 %collective-permute-start.10 = (bf16[4,256]{1,0:T(4,128)(2,1)S(1)}, bf16[4,256]{1,0:T(4,128)(2,1)S(1)}, u32[]{:S(2)}, u32[]{:S(2)}) collective-permute-start(bf16[4,256]{1,0:T(4,128)(2,1)S(1)} %get-tuple-element.62), channel_id=1, source_target_pairs={{0,4},{4,0},{8,12},{12,8},{16,20},{20,16},{24,28},{28,24},{1,5},{5... | collective-permute-start | bytes 6152 | tf_op jit(solution)/shard_map/ppermute | solution.py:43
  30.2 4.9 %collective-permute-start.11 = (bf16[4,256]{1,0:T(4,128)(2,1)S(1)}, bf16[4,256]{1,0:T(4,128)(2,1)S(1)}, u32[]{:S(2)}, u32[]{:S(2)}) collective-permute-start(bf16[4,256]{1,0:T(4,128)(2,1)S(1)} %get-tuple-element.63), channel_id=1, source_target_pairs={{0,28},{4,8},{8,4},{12,16},{16,12},{20,24},{24,20},{28,0},{1,29},{... | collective-permute-start | bytes 6152 | tf_op jit(solution)/shard_map/ppermute | solution.py:43

commit v8 on v6

--- a/solution.py
+++ b/solution.py
@@ -124,19 +124,32 @@
     cols = points_ref.shape[0] // 2
     count = 2 * cols
     first, later = [], []
+    turn, half = cols // 4, cols // 2
+    spans = []
     for r, at in enumerate((even, 1 - even)):
-        rows = pl.ds(r * cols, cols)
+        spans.append((at, turn, r * half, half))
+        spans.append((at, 3 * turn, (2 + r) * half, turn))
+        spans.append((at, 0, (2 + r) * half + turn, turn))
+    for r, at in enumerate((even, 1 - even)):
         first.append(pltpu.make_async_copy(idx_hbm.at[at], idx_ref.at[r], sems.at[r]))
-        later.append(pltpu.make_async_copy(points_hbm.at[at], points_ref.at[rows], sems.at[2 + r]))
-        later.append(pltpu.make_async_copy(skip_hbm.at[at], skip_ref.at[rows], sems.at[4 + r]))
+    for r, (at, low, to, size) in enumerate(spans):
+        rows, place = pl.ds(low, size), pl.ds(to, size)
+        later.append(
+            pltpu.make_async_copy(points_hbm.at[at, rows], points_ref.at[place], sems.at[2 + r])
+        )
+        later.append(
+            pltpu.make_async_copy(skip_hbm.at[at, rows], skip_ref.at[place], sems.at[8 + r])
+        )
     for k in range(held):
-        later.append(pltpu.make_async_copy(held_hbm[k], held_refs[k], sems.at[6 + k]))
+        later.append(pltpu.make_async_copy(held_hbm[k], held_refs[k], sems.at[14 + k]))
     for c in first + later:
         c.start()
     for c in first:
         c.wait()
+    for r in range(2):
+        idx_ref[r] = pltpu.roll(idx_ref[r], cols - turn, 1)
     near = idx_ref.shape[1]
-    lanes = 128
+    lanes = half
     for piece in range(bias_ref.shape[0] // (groups * capacity)):
         offset = 2 * REACH - sent_offset(az, piece)
         for step in range(groups):
@@ -145,7 +158,7 @@
             slot = low + lax.broadcasted_iota(jnp.int32, (capacity, lanes), 0)
             place = (piece * groups + step) * capacity
             for start in range(0, count, lanes):
-                row, col = divmod(start, cols)
+                row, col = start // half % 2, start // cols * half
                 total = jnp.zeros((capacity, lanes), F32)
                 for n in range(near):
                     index = idx_ref[row, n : n + 1, col : col + lanes]
@@ -163,14 +176,15 @@
     side_ref[...] = dot(skip_ref[...], w_skip_ref[...])
 
 
-def attend(keys, values_t, q_ref, bias_ref, score_ref, weight_ref, att_ref):
+def attend(keys, values_t, q_ref, bias_ref, score_ref, weight_ref, att_ref, first):
     table, width = keys.shape
-    count = q_ref.shape[1]
+    count = att_ref.shape[1]
+    part = slice(first, first + count)
     head_width = width // HEADS
     lanes = 128
     for head in range(HEADS):
         low, high = head * head_width, (head + 1) * head_width
-        score_ref[head] = dot(keys[:, low:high], q_ref[low:high, :]) + bias_ref[...]
+        score_ref[head] = dot(keys[:, low:high], q_ref[low:high, part]) + bias_ref[:, part]
     for head in range(HEADS):
         for start in range(0, count, lanes):
             x = score_ref[head, :, start : start + lanes]
@@ -186,19 +200,19 @@
         att_ref[low:high, :] = (mixed[:head_width] * scale).astype(BF16)
 
 
-def join(points_ref, side_ref, att_ref, w_out_ref, w_hid_ref, w_down_ref):
-    count = points_ref.shape[0]
-    size = count // 2
+def join(points_ref, side_ref, att_ref, w_out_ref, w_hid_ref, w_down_ref, first, sizes):
     c1 = math.sqrt(2.0 / math.pi)
     residuals, pres, out = [], [], []
-    for start in range(0, count, size):
-        part = slice(start, start + size)
+    starts = [sum(sizes[:k]) for k in range(len(sizes))]
+    for start, size in zip(starts, sizes):
+        rows = slice(first + start, first + start + size)
+        mixed = att_ref[:, start : start + size]
         residuals.append(
-            points_ref[part].astype(F32) + dot(att_ref[:, part], w_out_ref[...], ((0,), (0,)))
+            points_ref[rows].astype(F32) + dot(mixed, w_out_ref[...], ((0,), (0,)))
         )
-    for at, residual in enumerate(residuals):
-        part = slice(at * size, (at + 1) * size)
-        pres.append(dot(rms(residual).astype(BF16), w_hid_ref[...]) + side_ref[part])
+    for start, size, residual in zip(starts, sizes, residuals):
+        rows = slice(first + start, first + start + size)
+        pres.append(dot(rms(residual).astype(BF16), w_hid_ref[...]) + side_ref[rows])
     for residual, pre in zip(residuals, pres):
         half = 0.5 * pre
         inner = half + half * jnp.tanh(pre * (c1 + (c1 * 0.044715) * (pre * pre)))
@@ -206,46 +220,84 @@
     return out
 
 
-def main_body(az_ref, *refs, pieces):
-    piece_refs = refs[:pieces]
+def ends_body(az_ref, *refs, pieces):
     (
+        w_key_ref,
+        w_value_ref,
         q_ref,
         bias_ref,
         points_ref,
         side_ref,
-        w_key_ref,
-        w_value_ref,
         w_out_ref,
         w_hid_ref,
         w_down_ref,
         joined_ref,
-        near_ref,
-        far_ref,
+        block_ref,
         inner_edge_ref,
         outer_edge_ref,
+        keys_ref,
+        values_ref,
         score_ref,
         weight_ref,
         att_ref,
     ) = refs[pieces:]
-    width, count = q_ref.shape
-    received = jnp.concatenate([r[...] for r in piece_refs], axis=0)
+    received = jnp.concatenate([r[...] for r in refs[:pieces]], axis=0)
     keys = dot(received, w_key_ref[...]).astype(BF16)
     normed_tokens = rms(received.astype(F32)).astype(BF16)
     values_t = dot(w_value_ref[...], normed_tokens, ((0,), (1,))).astype(BF16)
-    attend(keys, values_t, q_ref, bias_ref, score_ref, weight_ref, att_ref)
-    joined = join(points_ref, side_ref, att_ref, w_out_ref, w_hid_ref, w_down_ref)
-    conv = []
-    for at, x in enumerate(joined):
-        joined_ref[at] = x
-        conv.append(rms(x))
-    cols = count // 2
-    near_ref[0:cols] = conv[0].astype(BF16)
-    far_ref[0:cols] = conv[1].astype(BF16)
-    left = jnp.concatenate([x[:1] for x in conv], axis=0)
-    right = jnp.concatenate([x[cols - 1 :] for x in conv], axis=0)
+    keys_ref[...], values_ref[...] = keys, values_t
+    half = block_ref.shape[1]
+    first = 2 * half
+    attend(keys, values_t, q_ref, bias_ref, score_ref, weight_ref, att_ref, first)
+    joined = join(
+        points_ref, side_ref, att_ref, w_out_ref, w_hid_ref, w_down_ref, first, (half, half)
+    )
+    blocks = [rms(x) for x in joined]
+    for at in range(2):
+        joined_ref[at] = joined[at]
+        block_ref[at] = blocks[at].astype(BF16)
+    turn = half // 2
+    left = jnp.concatenate([x[turn : turn + 1] for x in blocks], axis=0)
+    right = jnp.concatenate([x[turn - 1 : turn] for x in blocks], axis=0)
     odd = lax.rem(az_ref[0], 2) == 1
     inner_edge_ref[...] = jnp.where(odd, left, right).astype(BF16)
     outer_edge_ref[...] = jnp.where(odd, right, left).astype(BF16)
+
+
+def middle_body(
+    keys_ref,
+    values_ref,
+    joined_ends_ref,
+    block_ref,
+    q_ref,
+    bias_ref,
+    points_ref,
+    side_ref,
+    w_out_ref,
+    w_hid_ref,
+    w_down_ref,
+    joined_ref,
+    near_ref,
+    far_ref,
+    score_ref,
+    weight_ref,
+    att_ref,
+):
+    attend(
+        keys_ref[...], values_ref[...], q_ref, bias_ref, score_ref, weight_ref, att_ref, 0
+    )
+    half = block_ref.shape[1]
+    turn = half // 2
+    joined = join(
+        points_ref, side_ref, att_ref, w_out_ref, w_hid_ref, w_down_ref, 0, (half, half)
+    )
+    for at, (x, ref) in enumerate(zip(joined, (near_ref, far_ref))):
+        joined_ref[at, turn : turn + half] = x
+        joined_ref[at, turn + half :] = joined_ends_ref[at, :turn]
+        joined_ref[at, :turn] = joined_ends_ref[at, turn:]
+        ref[turn : turn + half] = rms(x).astype(BF16)
+        ref[turn + half : 2 * half] = block_ref[at, :turn]
+        ref[:turn] = block_ref[at, turn:]
 
 
 def pack_body(az_ref, inner_ref, outer_ref, near_in, far_in, near_ref, far_ref):
@@ -349,7 +401,7 @@
         "load",
         (table * count * 48, table * count),
         [SMEM, SMEM] + [HBM] * (3 + len(held)),
-        [VMEM(idx.shape, jnp.int32), dma((6 + len(held),))],
+        [VMEM(idx.shape, jnp.int32), dma((14 + len(held),))],
     )
     query_t, side = call(
         query_body,
@@ -358,27 +410,46 @@
         "query",
         (2 * count * width * 5 * width, 0),
     )
-    joined, near, far, inner_edge, outer_edge = call(
-        functools.partial(main_body, pieces=len(pieces)),
+    w_key, w_value, w_out, w_hid, w_down, w_conv = held[2:]
+    half = cols // 2
+    work = (10 * table * cols * width + 18 * cols * width * width, table * cols * HEADS)
+    room = [
+        VMEM((HEADS, table, cols), F32),
+        VMEM((HEADS, table, cols), BF16),
+        VMEM((width, cols), BF16),
+    ]
+    shared = [query_t, bias, points_v, side, w_out, w_hid, w_down]
+    joined_ends, blocks, inner_edge, outer_edge, keys, values = call(
+        functools.partial(ends_body, pieces=len(pieces)),
+        [
+            shape((rows, half, width), F32),
+            shape((rows, half, width), BF16),
+            shape((2, width), BF16),
+            shape((2, width), BF16),
+            shape((table, width), BF16),
+            shape((width, table), BF16),
+        ],
+        [az] + pieces + [w_key, w_value] + shared,
+        "ends",
+        work,
+        [SMEM] + [VMEM] * (len(pieces) + 2 + len(shared)),
+        room,
+    )
+    outer_got = swap(outer_edge, "az", next_chip)
+    inner_got = swap(inner_edge, "az", same_chip)
+    joined, near, far = call(
+        middle_body,
         [
             shape((rows, cols, width), F32),
             shape((cols + PAD, width), BF16),
             shape((cols + PAD, width), BF16),
-            shape((2, width), BF16),
-            shape((2, width), BF16),
         ],
-        [az] + pieces + [query_t, bias, points_v, side] + held[2:-1],
-        "main",
-        (10 * table * count * width + 2 * count * width * 13 * width, table * count * HEADS),
-        [SMEM] + [VMEM] * (len(pieces) + 9),
-        [
-            VMEM((HEADS, table, count), F32),
-            VMEM((HEADS, table, count), BF16),
-            VMEM((width, count), BF16),
-        ],
-    )
-    outer_got = swap(outer_edge, "az", next_chip)
-    inner_got = swap(inner_edge, "az", same_chip)
+        [keys, values, joined_ends, blocks] + shared,
+        "middle",
+        work,
+        None,
+        room,
+    )
     near, far = call(
         pack_body,
         [shape((cols + PAD, width), BF16)] * 2,
@@ -394,7 +465,7 @@
     (partial,) = call(
         inside_body,
         [shape((rows, cols, width), F32)],
-        [el, near, far, joined, held[-1]],
+        [el, near, far, joined, w_conv],
         "inside",
         (2 * count * width * width * 6, 0),
         [SMEM] + [VMEM] * 4,
@@ -402,7 +473,7 @@
     (out,) = call(
         functools.partial(border_body, last=lax.axis_size("el") - 1),
         [shape((rows, cols, width), BF16)],
-        [el, near_got, far_got, partial, held[-1]],
+        [el, near_got, far_got, partial, w_conv],
         "border",
         (2 * count * width * width * 3, 0),
         [SMEM] + [VMEM] * 4,

time: 36.2 us -> 35 us (0.967)
  waiting for transfers between devices: 14 us -> 11.8 us
  Pallas kernels: 9.2 us -> 10.1 us
    ppermute x11, waiting for transfers between devices: 14 us -> 11.8 us  [swap(): return lax.ppermute(x, axis, [(i, partner(i, n)) for i in range(n)])]
    pallas_call x7 -> x8, Pallas kernels: 9.2 us -> 10.1 us  [call(): pl.pallas_call(body, out_shape=outs, in_specs=[pl.BlockSpec(memory_space=...]
  transfers between devices with their start and end apart: 11 -> 11, of which waited for: 6 -> 6; matrix products, arithmetic and copies ran while one was open for 0% -> 0% of each run, Pallas kernels for 10% -> 16%
where the time goes in v8:
time: 35 us; the launch traced here: 34.7 us
  starting transfers between devices  12.6 us (36%)
  waiting for transfers between devices  11.8 us (34%)
  Pallas kernels  10.1 us (29%)
    ppermute x11, starting transfers between devices, swap(): return lax.ppermute(x, axis, [(i, partner(i, n)) for i in range(n)])  12.6 us
    ppermute x11, waiting for transfers between devices, swap(): return lax.ppermute(x, axis, [(i, partner(i, n)) for i in range(n)])  11.8 us
    pallas_call x8, Pallas kernels, call(): pl.pallas_call(body, out_shape=outs, in_specs=[pl.BlockSpec(memory_space=...  10.1 us
  transfers between devices with their start and end apart: 11, of which 6 were waited for; matrix products, arithmetic and copies ran while one was open for 0% of the time, Pallas kernels for 16%

profile of v8, /device:TPU:2, one launch (start us, length us, event | category | flops | bytes accessed | tf_op | source)
XLA Modules:
  0.0 34.7 jit_solution(3296071868157118270)
XLA Ops:
  0.0 1.1 %gather.1 = (bf16[5,16,256]{2,1,0:T(8,128)(2,1)S(1)}, bf16[5,16,256]{2,1,0:T(8,128)(2,1)S(1)}, bf16[5,16,256]{2,1,0:T(8,128)(2,1)S(1)}, bf16[5,16,256]{2,1,0:T(8,128)(2,1)S(1)}) custom-call(s32[1]{0:T(128)} %bitcast.el_ref.refs_0_, s32[1]{0:T(128)} %bitcast.1.az_ref.refs_1_, bf16[128,256]{1,0:T(8,128)(2,1)} %bitcast.46, s32[5,4,16]{2,1,0:T(4,128)} %bitcast.47), custom_call_target="tpu_custom_call" | custom-call | flops 20971520 | bytes 230664 | tf_op jit(solution)/shard_map/gather/pallas_call | solution.py:70
  1.1 0.1 collective-permute-start
  1.2 2.0 %collective-permute-start.1 = (bf16[5,16,256]{2,1,0:T(8,128)(2,1)S(1)}, bf16[5,16,256]{2,1,0:T(8,128)(2,1)S(1)}, u32[]{:S(2)}, u32[]{:S(2)}) collective-permute-start(bf16[5,16,256]{2,1,0:T(8,128)(2,1)S(1)} %get-tuple-element.35), channel_id=1, source_target_pairs={{0,2},{1,3},{2,0},{3,1},{4,6},{5,7},{6,4},{7,5},{8,10},{9,11},{10,... | collective-permute-start | bytes 122888 | tf_op jit(solution)/shard_map/ppermute | solution.py:43
  3.2 1.4 %collective-permute-start.2 = (bf16[5,16,256]{2,1,0:T(8,128)(2,1)S(1)}, bf16[5,16,256]{2,1,0:T(8,128)(2,1)S(1)}, u32[]{:S(2)}, u32[]{:S(2)}) collective-permute-start(bf16[5,16,256]{2,1,0:T(8,128)(2,1)S(1)} %get-tuple-element.36), channel_id=1, source_target_pairs={{0,3},{1,2},{2,1},{3,0},{4,7},{5,6},{6,5},{7,4},{8,11},{9,10},{10,... | collective-permute-start | bytes 122888 | tf_op jit(solution)/shard_map/ppermute | solution.py:43
  4.7 2.4 %load.1 = (f32[320,512]{1,0:T(8,128)S(1)}, bf16[512,256]{1,0:T(8,128)(2,1)S(1)}, bf16[512,256]{1,0:T(8,128)(2,1)S(1)}, bf16[256,256]{1,0:T(8,128)(2,1)S(1)}, bf1...) custom-call(s32[1]{0:T(128)} %bitcast.el_ref.refs_0_, ...), custom_call_target="tpu_custom_call" | custom-call | flops 7864320 | bytes 8290312 | tf_op jit(solution)/shard_map/load/pallas_call | solution.py:70
  7.1 0.0 collective-permute-done
  7.1 0.0 collective-permute-done.1
  7.1 1.0 %collective-permute-done.2 = bf16[5,16,256]{2,1,0:T(8,128)(2,1)S(1)} collective-permute-done((bf16[5,16,256]{2,1,0:T(8,128)(2,1)S(1)}, bf16[5,16,256]{2,1,0:T(8,128)(2,1)S(1)}, u32[]{:S(2)}, u32[]{:S(2)}) %collective-permute-start.2) | collective-permute-done | bytes 40992 | tf_op jit(solution)/shard_map/ppermute | solution.py:43
  8.2 3.7 %collective-permute-start.3 = (bf16[64,256]{1,0:T(8,128)(2,1)S(1)}, bf16[64,256]{1,0:T(8,128)(2,1)S(1)}, u32[]{:S(2)}, u32[]{:S(2)}) collective-permute-start(bf16[64,256]{1,0:T(8,128)(2,1)S(1)} %pad_maximum_fusion.1), channel_id=1, source_target_pairs={{0,24},{4,28},{8,16},{12,20},{16,8},{20,12},{24,0},{28,4},{1,25},{... | collective-permute-start | bytes 98312 | tf_op jit(solution)/shard_map/ppermute | solution.py:43
  11.8 0.0 collective-permute-start.4
  11.8 0.1 collective-permute-start.5
  11.9 0.1 collective-permute-start.6
  12.0 0.5 %query.1 = (bf16[256,512]{1,0:T(8,128)(2,1)S(1)}, f32[512,1024]{1,0:T(8,128)S(1)}) custom-call(bf16[512,256]{1,0:T(8,128)(2,1)S(1)} %get-tuple-element.39.points_ref.refs_9_, bf16[512,256]{1,0:T(8,128)(2,1)S(1)} %get-tuple-element.40.skip_ref, bf16[256,256]{1,0:T(8,128)(2,1)S(1)} %get-tuple-element.41.w_query_ref, ...), custom_call_target="tpu_custom_call" | custom-call | flops 335544320 | bytes 3571712 | tf_op jit(solution)/shard_map/query/pallas_call | solution.py:70
  12.5 1.4 %collective-permute-done.3.refs_1_ = bf16[64,256]{1,0:T(8,128)(2,1)S(1)} collective-permute-done((bf16[64,256]{1,0:T(8,128)(2,1)S(1)}, bf16[64,256]{1,0:T(8,128)(2,1)S(1)}, u32[]{:S(2)}, u32[]{:S(2)}) %collective-permute-start.3) | collective-permute-done | bytes 32800 | tf_op jit(solution)/shard_map/ppermute | solution.py:43
  13.9 3.0 %collective-permute-done.4.refs_2_ = bf16[64,256]{1,0:T(8,128)(2,1)S(1)} collective-permute-done((bf16[64,256]{1,0:T(8,128)(2,1)S(1)}, bf16[64,256]{1,0:T(8,128)(2,1)S(1)}, u32[]{:S(2)}, u32[]{:S(2)}) %collective-permute-start.4) | collective-permute-done | bytes 32800 | tf_op jit(solution)/shard_map/ppermute | solution.py:43
  17.0 0.0 collective-permute-done.5.refs_3_
  17.0 0.0 collective-permute-done.6.refs_4_
  17.0 2.3 %ends.1 = (f32[2,128,256]{2,1,0:T(8,128)S(1)}, bf16[2,128,256]{2,1,0:T(8,128)(2,1)S(1)}, bf16[2,256]{1,0:T(2,128)(2,1)S(1)}, bf16[2,256]{1,0:T(2,128)(2,1)S(1)},...) custom-call(s32[1]{0:T(128)} %bitcast.1.az_ref.refs_1_, ...), custom_call_target="tpu_custom_call" | custom-call | flops 511705088 | bytes 5605380 | tf_op jit(solution)/shard_map/ends/pallas_call | solution.py:70
  19.3 0.1 collective-permute-start.7
  19.3 1.2 %collective-permute-start.8 = (bf16[2,256]{1,0:T(2,128)(2,1)S(1)}, bf16[2,256]{1,0:T(2,128)(2,1)S(1)}, u32[]{:S(2)}, u32[]{:S(2)}) collective-permute-start(bf16[2,256]{1,0:T(2,128)(2,1)S(1)} %get-tuple-element.50), channel_id=1, source_target_pairs={{0,28},{4,8},{8,4},{12,16},{16,12},{20,24},{24,20},{28,0},{1,29},{... | collective-permute-start | bytes 3080 | tf_op jit(solution)/shard_map/ppermute | solution.py:43
  20.6 2.1 %middle.1 = (f32[2,256,256]{2,1,0:T(8,128)S(1)}, bf16[272,256]{1,0:T(8,128)(2,1)S(1)}, bf16[272,256]{1,0:T(8,128)(2,1)S(1)}) custom-call(bf16[320,256]{1,0:T(8,128)(2,1)S(1)} %get-tuple-element.51.keys_ref, bf16[256,320]{1,0:T(8,128)(2,1)S(1)} %get-tuple-element.52.values_ref, f32[2,128,256]{2,1,0:T(8,128)S(1)} %get-tuple-element.53.joined_ends_ref, ...), custom_call_target="tpu_custom_call" | custom-call | flops 511705088 | bytes 5980160 | tf_op jit(solution)/shard_map/middle/pallas_call | solution.py:70
  22.6 0.0 collective-permute-done.7.inner_ref
  22.7 1.5 %collective-permute-done.8.outer_ref = bf16[2,256]{1,0:T(2,128)(2,1)S(1)} collective-permute-done((bf16[2,256]{1,0:T(2,128)(2,1)S(1)}, bf16[2,256]{1,0:T(2,128)(2,1)S(1)}, u32[]{:S(2)}, u32[]{:S(2)}) %collective-permute-start.8) | collective-permute-done | bytes 1056 | tf_op jit(solution)/shard_map/ppermute | solution.py:43
  24.2 1.6 %collective-permute-start.9 = (bf16[272,256]{1,0:T(8,128)(2,1)S(1)}, bf16[272,256]{1,0:T(8,128)(2,1)S(1)}, u32[]{:S(2)}, u32[]{:S(2)}) collective-permute-start(bf16[272,256]{1,0:T(8,128)(2,1)S(1)} %get-tuple-element.57.near_ref), channel_id=1, source_target_pairs={{0,1},{1,0},{2,3},{3,2},{4,5},{5,4},{6,7},{7,6},{8,9},{9,8},{10,11... | collective-permute-start | bytes 417800 | tf_op jit(solution)/shard_map/ppermute | solution.py:43
  25.8 2.4 %collective-permute-start.10 = (bf16[272,256]{1,0:T(8,128)(2,1)S(1)}, bf16[272,256]{1,0:T(8,128)(2,1)S(1)}, u32[]{:S(2)}, u32[]{:S(2)}) collective-permute-start(bf16[272,256]{1,0:T(8,128)(2,1)S(1)} %get-tuple-element.58.far_ref), channel_id=1, source_target_pairs={{0,0},{1,2},{2,1},{3,3},{4,4},{5,6},{6,5},{7,7},{8,8},{9,10},{10,9... | collective-permute-start | bytes 417800 | tf_op jit(solution)/shard_map/ppermute | solution.py:43
  28.2 0.6 %inside.1.part_ref = f32[2,256,256]{2,1,0:T(8,128)S(1)} custom-call(s32[1]{0:T(128)} %bitcast.el_ref.refs_0_, bf16[272,256]{1,0:T(8,128)(2,1)S(1)} %get-tuple-element.57.near_ref, bf16[272,256]{1,0:T(8,128)(2,1)S(1)} %get-tuple-element.58.far_ref, f32[2,256,256]{2,1,0:T(8,128)S(1)} %get-tuple-element.59.joined_ref, ...), custom_call_target="tpu_custom_call" | custom-call | flops 402653184 | bytes 2506756 | tf_op jit(solution)/shard_map/inside/pallas_call | solution.py:70
  28.8 0.8 %collective-permute-done.9.near_ref = bf16[272,256]{1,0:T(8,128)(2,1)S(1)} collective-permute-done((bf16[272,256]{1,0:T(8,128)(2,1)S(1)}, bf16[272,256]{1,0:T(8,128)(2,1)S(1)}, u32[]{:S(2)}, u32[]{:S(2)}) %collective-permute-start.9) | collective-permute-done | bytes 139296 | tf_op jit(solution)/shard_map/ppermute | solution.py:43
  29.6 4.0 %collective-permute-done.10.far_ref = bf16[272,256]{1,0:T(8,128)(2,1)S(1)} collective-permute-done((bf16[272,256]{1,0:T(8,128)(2,1)S(1)}, bf16[272,256]{1,0:T(8,128)(2,1)S(1)}, u32[]{:S(2)}, u32[]{:S(2)}) %collective-permute-start.10) | collective-permute-done | bytes 139296 | tf_op jit(solution)/shard_map/ppermute | solution.py:43
  33.6 1.1 %border.1 = bf16[2,256,256]{2,1,0:T(8,128)(2,1)} custom-call(s32[1]{0:T(128)} %bitcast.el_ref.refs_0_, bf16[272,256]{1,0:T(8,128)(2,1)S(1)} %collective-permute-done.9.near_ref, bf16[272,256]{1,0:T(8,128)(2,1)S(1)} %collective-permute-done.10.far_ref, f32[2,256,256]{2,1,0:T(8,128)S(1)} %inside.1.part_ref, bf16[9,256,256]{2,1,0:T(8,128)(2,1)S(1)} %get-tuple-element.60.w_ref), custom_call_target="tpu_custom_call" | custom-call | flops 201326592 | bytes 2244612 | tf_op jit(solution)/shard_map/border/pallas_call | solution.py:70
  (10 shorter events, 0.1 us)
Async XLA Ops:
  1.1 6.0 %collective-permute-start = (bf16[5,16,256]{2,1,0:T(8,128)(2,1)S(1)}, bf16[5,16,256]{2,1,0:T(8,128)(2,1)S(1)}, u32[]{:S(2)}, u32[]{:S(2)}) collective-permute-start(bf16[5,16,256]{2,1,0:T(8,128)(2,1)S(1)} %get-tuple-element.34), channel_id=1, source_target_pairs={{0,1},{1,0},{2,3},{3,2},{4,5},{5,4},{6,7},{7,6},{8,9},{9,8},{10,11... | collective-permute-start | bytes 122888 | tf_op jit(solution)/shard_map/ppermute | solution.py:43
  1.2 5.9 %collective-permute-start.1 = (bf16[5,16,256]{2,1,0:T(8,128)(2,1)S(1)}, bf16[5,16,256]{2,1,0:T(8,128)(2,1)S(1)}, u32[]{:S(2)}, u32[]{:S(2)}) collective-permute-start(bf16[5,16,256]{2,1,0:T(8,128)(2,1)S(1)} %get-tuple-element.35), channel_id=1, source_target_pairs={{0,2},{1,3},{2,0},{3,1},{4,6},{5,7},{6,4},{7,5},{8,10},{9,11},{10,... | collective-permute-start | bytes 122888 | tf_op jit(solution)/shard_map/ppermute | solution.py:43
  3.2 4.9 %collective-permute-start.2 = (bf16[5,16,256]{2,1,0:T(8,128)(2,1)S(1)}, bf16[5,16,256]{2,1,0:T(8,128)(2,1)S(1)}, u32[]{:S(2)}, u32[]{:S(2)}) collective-permute-start(bf16[5,16,256]{2,1,0:T(8,128)(2,1)S(1)} %get-tuple-element.36), channel_id=1, source_target_pairs={{0,3},{1,2},{2,1},{3,0},{4,7},{5,6},{6,5},{7,4},{8,11},{9,10},{10,... | collective-permute-start | bytes 122888 | tf_op jit(solution)/shard_map/ppermute | solution.py:43
  8.2 5.8 %collective-permute-start.3 = (bf16[64,256]{1,0:T(8,128)(2,1)S(1)}, bf16[64,256]{1,0:T(8,128)(2,1)S(1)}, u32[]{:S(2)}, u32[]{:S(2)}) collective-permute-start(bf16[64,256]{1,0:T(8,128)(2,1)S(1)} %pad_maximum_fusion.1), channel_id=1, source_target_pairs={{0,24},{4,28},{8,16},{12,20},{16,8},{20,12},{24,0},{28,4},{1,25},{... | collective-permute-start | bytes 98312 | tf_op jit(solution)/shard_map/ppermute | solution.py:43
  11.8 5.1 %collective-permute-start.4 = (bf16[64,256]{1,0:T(8,128)(2,1)S(1)}, bf16[64,256]{1,0:T(8,128)(2,1)S(1)}, u32[]{:S(2)}, u32[]{:S(2)}) collective-permute-start(bf16[64,256]{1,0:T(8,128)(2,1)S(1)} %pad_maximum_fusion.2), channel_id=1, source_target_pairs={{0,28},{4,8},{8,4},{12,16},{16,12},{20,24},{24,20},{28,0},{1,29},{... | collective-permute-start | bytes 98312 | tf_op jit(solution)/shard_map/ppermute | solution.py:43
  11.8 5.1 %collective-permute-start.5 = (bf16[64,256]{1,0:T(8,128)(2,1)S(1)}, bf16[64,256]{1,0:T(8,128)(2,1)S(1)}, u32[]{:S(2)}, u32[]{:S(2)}) collective-permute-start(bf16[64,256]{1,0:T(8,128)(2,1)S(1)} %pad_maximum_fusion.3), channel_id=1, source_target_pairs={{0,8},{4,12},{8,0},{12,4},{16,24},{20,28},{24,16},{28,20},{1,9},{5... | collective-permute-start | bytes 98312 | tf_op jit(solution)/shard_map/ppermute | solution.py:43
  11.9 5.0 %collective-permute-start.6 = (bf16[64,256]{1,0:T(8,128)(2,1)S(1)}, bf16[64,256]{1,0:T(8,128)(2,1)S(1)}, u32[]{:S(2)}, u32[]{:S(2)}) collective-permute-start(bf16[64,256]{1,0:T(8,128)(2,1)S(1)} %pad_maximum_fusion.4), channel_id=1, source_target_pairs={{0,4},{4,0},{8,12},{12,8},{16,20},{20,16},{24,28},{28,24},{1,5},{5... | collective-permute-start | bytes 98312 | tf_op jit(solution)/shard_map/ppermute | solution.py:43
  19.3 3.4 %collective-permute-start.7 = (bf16[2,256]{1,0:T(2,128)(2,1)S(1)}, bf16[2,256]{1,0:T(2,128)(2,1)S(1)}, u32[]{:S(2)}, u32[]{:S(2)}) collective-permute-start(bf16[2,256]{1,0:T(2,128)(2,1)S(1)} %get-tuple-element.49), channel_id=1, source_target_pairs={{0,4},{4,0},{8,12},{12,8},{16,20},{20,16},{24,28},{28,24},{1,5},{5... | collective-permute-start | bytes 3080 | tf_op jit(solution)/shard_map/ppermute | solution.py:43
  19.3 4.9 %collective-permute-start.8 = (bf16[2,256]{1,0:T(2,128)(2,1)S(1)}, bf16[2,256]{1,0:T(2,128)(2,1)S(1)}, u32[]{:S(2)}, u32[]{:S(2)}) collective-permute-start(bf16[2,256]{1,0:T(2,128)(2,1)S(1)} %get-tuple-element.50), channel_id=1, source_target_pairs={{0,28},{4,8},{8,4},{12,16},{16,12},{20,24},{24,20},{28,0},{1,29},{... | collective-permute-start | bytes 3080 | tf_op jit(solution)/shard_map/ppermute | solution.py:43
  24.2 5.4 %collective-permute-start.9 = (bf16[272,256]{1,0:T(8,128)(2,1)S(1)}, bf16[272,256]{1,0:T(8,128)(2,1)S(1)}, u32[]{:S(2)}, u32[]{:S(2)}) collective-permute-start(bf16[272,256]{1,0:T(8,128)(2,1)S(1)} %get-tuple-element.57.near_ref), channel_id=1, source_target_pairs={{0,1},{1,0},{2,3},{3,2},{4,5},{5,4},{6,7},{7,6},{8,9},{9,8},{10,11... | collective-permute-start | bytes 417800 | tf_op jit(solution)/shard_map/ppermute | solution.py:43
  25.8 7.8 %collective-permute-start.10 = (bf16[272,256]{1,0:T(8,128)(2,1)S(1)}, bf16[272,256]{1,0:T(8,128)(2,1)S(1)}, u32[]{:S(2)}, u32[]{:S(2)}) collective-permute-start(bf16[272,256]{1,0:T(8,128)(2,1)S(1)} %get-tuple-element.58.far_ref), channel_id=1, source_target_pairs={{0,0},{1,2},{2,1},{3,3},{4,4},{5,6},{6,5},{7,7},{8,8},{9,10},{10,9... | collective-permute-start | bytes 417800 | tf_op jit(solution)/shard_map/ppermute | solution.py:43

commit v9 on v8

--- a/solution.py
+++ b/solution.py
@@ -59,7 +59,7 @@
     return x * lax.rsqrt(jnp.mean(x * x, axis=-1, keepdims=True) + 1e-06)
 
 
-def call(body, outs, ins, name, cost, spaces=None, scratch=(), aliases=None):
+def call(body, outs, ins, name, cost, spaces=None, scratch=(), aliases=None, out_space=VMEM):
     spaces = spaces or [VMEM] * len(ins)
     flops, transcendentals = cost
     moved = sum(x.size * x.dtype.itemsize for x in list(ins) + list(outs))
@@ -71,7 +71,7 @@
         body,
         out_shape=outs,
         in_specs=[pl.BlockSpec(memory_space=s) for s in spaces],
-        out_specs=[pl.BlockSpec(memory_space=VMEM) for _ in outs],
+        out_specs=[pl.BlockSpec(memory_space=out_space) for _ in outs],
         scratch_shapes=list(scratch),
         input_output_aliases=aliases or {},
         compiler_params=pltpu.CompilerParams(vmem_limit_bytes=32 * 1024 * 1024),
@@ -80,6 +80,10 @@
         ),
         name=name,
     )(*ins)
+
+
+def swap_order(groups):
+    return sorted(range(groups), key=lambda s: (s > 0, -s.bit_count(), s))
 
 
 def gather_body(el_ref, az_ref, tokens_hbm, slots_hbm, *refs):
@@ -100,7 +104,7 @@
     for c in copies:
         c.wait()
     tokens = tokens_ref[...]
-    for step in range(groups):
+    for place, step in enumerate(swap_order(groups)):
         target = lax.bitwise_xor(el, step)
         picks = []
         for piece in range(offsets):
@@ -110,7 +114,7 @@
             picks.append(jnp.where(column == lane, 1.0, 0.0))
         one_hot = jnp.concatenate(picks, axis=0).astype(BF16)
         chosen = dot(one_hot, tokens).astype(BF16)
-        out_refs[step][...] = chosen.reshape(out_refs[step].shape)
+        out_refs[place][...] = chosen.reshape(out_refs[place].shape)
 
 
 def load_body(*refs, groups, capacity, held):
@@ -152,11 +156,11 @@
     lanes = half
     for piece in range(bias_ref.shape[0] // (groups * capacity)):
         offset = 2 * REACH - sent_offset(az, piece)
-        for step in range(groups):
+        for block, step in enumerate(swap_order(groups)):
             source = lax.bitwise_xor(el, step)
             low = (offset * groups + source) * capacity
             slot = low + lax.broadcasted_iota(jnp.int32, (capacity, lanes), 0)
-            place = (piece * groups + step) * capacity
+            place = (piece * groups + block) * capacity
             for start in range(0, count, lanes):
                 row, col = start // half % 2, start // cols * half
                 total = jnp.zeros((capacity, lanes), F32)
@@ -335,15 +339,24 @@
     out_ref[1] = joined_ref[1] + conv_rows([(far, w_ref, 3), (near, w_ref, 6 - 6 * odd)], cols)
 
 
-def border_body(el_ref, near_ref, far_ref, part_ref, w_ref, out_ref, *, last):
+def near_border_body(el_ref, near_ref, part_ref, w_ref, out_ref):
+    odd = lax.rem(el_ref[0], 2)
+    near = part_ref[0] + conv_rows([(near_ref[...], w_ref, 6 - 6 * odd)], part_ref.shape[1])
+    out_ref[...] = near.astype(BF16)
+
+
+def far_border_body(el_ref, near_ref, far_ref, part_ref, w_ref, out_hbm, row_ref, sems, *, last):
     el = el_ref[0]
     odd = lax.rem(el, 2)
-    cols = part_ref.shape[1]
-    near = part_ref[0] + conv_rows([(near_ref[...], w_ref, 6 - 6 * odd)], cols)
-    out_ref[1 - odd] = near.astype(BF16)
-    far = conv_rows([(far_ref[...], w_ref, 6 * odd)], cols)
+    first = pltpu.make_async_copy(near_ref, out_hbm.at[1 - odd], sems.at[0])
+    first.start()
+    far = conv_rows([(far_ref[...], w_ref, 6 * odd)], part_ref.shape[1])
     ends = jnp.logical_or(el == 0, el == last)
-    out_ref[odd] = (part_ref[1] + jnp.where(ends, 0.0, far)).astype(BF16)
+    row_ref[...] = (part_ref[1] + jnp.where(ends, 0.0, far)).astype(BF16)
+    second = pltpu.make_async_copy(row_ref, out_hbm.at[odd], sems.at[1])
+    second.start()
+    first.wait()
+    second.wait()
 
 
 def per_device(
@@ -380,12 +393,12 @@
         [SMEM, SMEM, HBM, HBM],
         [VMEM(own_tokens.shape, BF16), VMEM(slots.shape, jnp.int32), dma((2,))],
     )
-    got = {0: sent[0]}
-    for s in reversed(range(1, groups)):
-        got[s] = swap(sent[s], "el", lambda i, n, s=s: i ^ s)
+    got = []
+    for block, step in zip(sent, swap_order(groups)):
+        got.append(swap(block, "el", lambda i, n, step=step: i ^ step) if step else block)
     pieces = []
     for piece in range(offsets):
-        bundle = jnp.concatenate([got[s][piece] for s in range(groups)], axis=0)
+        bundle = jnp.concatenate([block[piece] for block in got], axis=0)
         pieces.append(swap(bundle, "az", MATCHES[piece]) if piece else bundle)
     held = [w_query, w_skip, w_key, w_value, w_out, w_hid, w_down, w_conv]
     idx = jnp.swapaxes(recv_idx, 1, 2)
@@ -470,13 +483,23 @@
         (2 * count * width * width * 6, 0),
         [SMEM] + [VMEM] * 4,
     )
+    (near_row,) = call(
+        near_border_body,
+        [shape((cols, width), BF16)],
+        [el, near_got, partial, w_conv],
+        "near_border",
+        (cols * width * width * 6, 0),
+        [SMEM] + [VMEM] * 3,
+    )
     (out,) = call(
-        functools.partial(border_body, last=lax.axis_size("el") - 1),
+        functools.partial(far_border_body, last=lax.axis_size("el") - 1),
         [shape((rows, cols, width), BF16)],
-        [el, near_got, far_got, partial, w_conv],
-        "border",
-        (2 * count * width * width * 3, 0),
+        [el, near_row, far_got, partial, w_conv],
+        "far_border",
+        (cols * width * width * 6, 0),
         [SMEM] + [VMEM] * 4,
+        [VMEM((cols, width), BF16), dma((2,))],
+        out_space=HBM,
     )
     return out
 

time: 35 us -> 33.9 us (0.969)
  waiting for transfers between devices: 11.8 us -> 10.6 us
    ppermute x11, waiting for transfers between devices: 11.8 us -> 10.6 us  [swap(): return lax.ppermute(x, axis, [(i, partner(i, n)) for i in range(n)])]
    pallas_call x8 -> x9, Pallas kernels: 10.1 us -> 10.2 us  [call(): pl.pallas_call(body, out_shape=outs, in_specs=[pl.BlockSpec(memory_space=...]
  transfers between devices with their start and end apart: 11 -> 11, of which waited for: 6 -> 6; matrix products, arithmetic and copies ran while one was open for 0% -> 0% of each run, Pallas kernels for 16% -> 17%
where the time goes in v9:
time: 33.9 us; the launch traced here: 33.6 us
  starting transfers between devices  12.6 us (37%)
  waiting for transfers between devices  10.6 us (31%)
  Pallas kernels  10.2 us (30%)
    ppermute x11, starting transfers between devices, swap(): return lax.ppermute(x, axis, [(i, partner(i, n)) for i in range(n)])  12.6 us
    ppermute x11, waiting for transfers between devices, swap(): return lax.ppermute(x, axis, [(i, partner(i, n)) for i in range(n)])  10.6 us
    pallas_call x9, Pallas kernels, call(): pl.pallas_call(body, out_shape=outs, in_specs=[pl.BlockSpec(memory_space=...  10.2 us
  transfers between devices with their start and end apart: 11, of which 6 were waited for; matrix products, arithmetic and copies ran while one was open for 0% of the time, Pallas kernels for 17%

profile of v9, /device:TPU:2, one launch (start us, length us, event | category | flops | bytes accessed | tf_op | source)
XLA Modules:
  0.0 33.6 jit_solution(5033601163841192693)
XLA Ops:
  0.0 1.1 %gather.1 = (bf16[5,16,256]{2,1,0:T(8,128)(2,1)S(1)}, bf16[5,16,256]{2,1,0:T(8,128)(2,1)S(1)}, bf16[5,16,256]{2,1,0:T(8,128)(2,1)S(1)}, bf16[5,16,256]{2,1,0:T(8,128)(2,1)S(1)}) custom-call(s32[1]{0:T(128)} %bitcast.el_ref.refs_0_, s32[1]{0:T(128)} %bitcast.1.az_ref.refs_1_, bf16[128,256]{1,0:T(8,128)(2,1)} %bitcast.46, s32[5,4,16]{2,1,0:T(4,128)} %bitcast.47), custom_call_target="tpu_custom_call" | custom-call | flops 20971520 | bytes 230664 | tf_op jit(solution)/shard_map/gather/pallas_call | solution.py:70
  1.1 1.6 %collective-permute-start = (bf16[5,16,256]{2,1,0:T(8,128)(2,1)S(1)}, bf16[5,16,256]{2,1,0:T(8,128)(2,1)S(1)}, u32[]{:S(2)}, u32[]{:S(2)}) collective-permute-start(bf16[5,16,256]{2,1,0:T(8,128)(2,1)S(1)} %get-tuple-element.34), channel_id=1, source_target_pairs={{0,3},{1,2},{2,1},{3,0},{4,7},{5,6},{6,5},{7,4},{8,11},{9,10},{10,... | collective-permute-start | bytes 122888 | tf_op jit(solution)/shard_map/ppermute | solution.py:43
  2.7 1.5 %collective-permute-start.1 = (bf16[5,16,256]{2,1,0:T(8,128)(2,1)S(1)}, bf16[5,16,256]{2,1,0:T(8,128)(2,1)S(1)}, u32[]{:S(2)}, u32[]{:S(2)}) collective-permute-start(bf16[5,16,256]{2,1,0:T(8,128)(2,1)S(1)} %get-tuple-element.35), channel_id=1, source_target_pairs={{0,1},{1,0},{2,3},{3,2},{4,5},{5,4},{6,7},{7,6},{8,9},{9,8},{10,11... | collective-permute-start | bytes 122888 | tf_op jit(solution)/shard_map/ppermute | solution.py:43
  4.2 0.5 %collective-permute-start.2 = (bf16[5,16,256]{2,1,0:T(8,128)(2,1)S(1)}, bf16[5,16,256]{2,1,0:T(8,128)(2,1)S(1)}, u32[]{:S(2)}, u32[]{:S(2)}) collective-permute-start(bf16[5,16,256]{2,1,0:T(8,128)(2,1)S(1)} %get-tuple-element.36), channel_id=1, source_target_pairs={{0,2},{1,3},{2,0},{3,1},{4,6},{5,7},{6,4},{7,5},{8,10},{9,11},{10,... | collective-permute-start | bytes 122888 | tf_op jit(solution)/shard_map/ppermute | solution.py:43
  4.7 2.4 %load.1 = (f32[320,512]{1,0:T(8,128)S(1)}, bf16[512,256]{1,0:T(8,128)(2,1)S(1)}, bf16[512,256]{1,0:T(8,128)(2,1)S(1)}, bf16[256,256]{1,0:T(8,128)(2,1)S(1)}, bf1...) custom-call(s32[1]{0:T(128)} %bitcast.el_ref.refs_0_, ...), custom_call_target="tpu_custom_call" | custom-call | flops 7864320 | bytes 8290312 | tf_op jit(solution)/shard_map/load/pallas_call | solution.py:70
  7.1 0.0 collective-permute-done
  7.1 0.0 collective-permute-done.1
  7.1 1.0 %collective-permute-done.2 = bf16[5,16,256]{2,1,0:T(8,128)(2,1)S(1)} collective-permute-done((bf16[5,16,256]{2,1,0:T(8,128)(2,1)S(1)}, bf16[5,16,256]{2,1,0:T(8,128)(2,1)S(1)}, u32[]{:S(2)}, u32[]{:S(2)}) %collective-permute-start.2) | collective-permute-done | bytes 40992 | tf_op jit(solution)/shard_map/ppermute | solution.py:43
  8.2 3.7 %collective-permute-start.3 = (bf16[64,256]{1,0:T(8,128)(2,1)S(1)}, bf16[64,256]{1,0:T(8,128)(2,1)S(1)}, u32[]{:S(2)}, u32[]{:S(2)}) collective-permute-start(bf16[64,256]{1,0:T(8,128)(2,1)S(1)} %pad_maximum_fusion.1), channel_id=1, source_target_pairs={{0,24},{4,28},{8,16},{12,20},{16,8},{20,12},{24,0},{28,4},{1,25},{... | collective-permute-start | bytes 98312 | tf_op jit(solution)/shard_map/ppermute | solution.py:43
  11.9 0.0 collective-permute-start.4
  11.9 0.1 collective-permute-start.5
  12.0 0.1 collective-permute-start.6
  12.0 0.5 %query.1 = (bf16[256,512]{1,0:T(8,128)(2,1)S(1)}, f32[512,1024]{1,0:T(8,128)S(1)}) custom-call(bf16[512,256]{1,0:T(8,128)(2,1)S(1)} %get-tuple-element.39.points_ref.refs_9_, bf16[512,256]{1,0:T(8,128)(2,1)S(1)} %get-tuple-element.40.skip_ref, bf16[256,256]{1,0:T(8,128)(2,1)S(1)} %get-tuple-element.41.w_query_ref, ...), custom_call_target="tpu_custom_call" | custom-call | flops 335544320 | bytes 3571712 | tf_op jit(solution)/shard_map/query/pallas_call | solution.py:70
  12.6 1.4 %collective-permute-done.3.refs_1_ = bf16[64,256]{1,0:T(8,128)(2,1)S(1)} collective-permute-done((bf16[64,256]{1,0:T(8,128)(2,1)S(1)}, bf16[64,256]{1,0:T(8,128)(2,1)S(1)}, u32[]{:S(2)}, u32[]{:S(2)}) %collective-permute-start.3) | collective-permute-done | bytes 32800 | tf_op jit(solution)/shard_map/ppermute | solution.py:43
  14.0 3.0 %collective-permute-done.4.refs_2_ = bf16[64,256]{1,0:T(8,128)(2,1)S(1)} collective-permute-done((bf16[64,256]{1,0:T(8,128)(2,1)S(1)}, bf16[64,256]{1,0:T(8,128)(2,1)S(1)}, u32[]{:S(2)}, u32[]{:S(2)}) %collective-permute-start.4) | collective-permute-done | bytes 32800 | tf_op jit(solution)/shard_map/ppermute | solution.py:43
  17.0 0.0 collective-permute-done.5.refs_3_
  17.0 0.0 collective-permute-done.6.refs_4_
  17.0 2.3 %ends.1 = (f32[2,128,256]{2,1,0:T(8,128)S(1)}, bf16[2,128,256]{2,1,0:T(8,128)(2,1)S(1)}, bf16[2,256]{1,0:T(2,128)(2,1)S(1)}, bf16[2,256]{1,0:T(2,128)(2,1)S(1)},...) custom-call(s32[1]{0:T(128)} %bitcast.1.az_ref.refs_1_, ...), custom_call_target="tpu_custom_call" | custom-call | flops 511705088 | bytes 5605380 | tf_op jit(solution)/shard_map/ends/pallas_call | solution.py:70
  19.3 0.1 collective-permute-start.7
  19.4 1.2 %collective-permute-start.8 = (bf16[2,256]{1,0:T(2,128)(2,1)S(1)}, bf16[2,256]{1,0:T(2,128)(2,1)S(1)}, u32[]{:S(2)}, u32[]{:S(2)}) collective-permute-start(bf16[2,256]{1,0:T(2,128)(2,1)S(1)} %get-tuple-element.50), channel_id=1, source_target_pairs={{0,28},{4,8},{8,4},{12,16},{16,12},{20,24},{24,20},{28,0},{1,29},{... | collective-permute-start | bytes 3080 | tf_op jit(solution)/shard_map/ppermute | solution.py:43
  20.6 2.1 %middle.1 = (f32[2,256,256]{2,1,0:T(8,128)S(1)}, bf16[272,256]{1,0:T(8,128)(2,1)S(1)}, bf16[272,256]{1,0:T(8,128)(2,1)S(1)}) custom-call(bf16[320,256]{1,0:T(8,128)(2,1)S(1)} %get-tuple-element.51.keys_ref, bf16[256,320]{1,0:T(8,128)(2,1)S(1)} %get-tuple-element.52.values_ref, f32[2,128,256]{2,1,0:T(8,128)S(1)} %get-tuple-element.53.joined_ends_ref, ...), custom_call_target="tpu_custom_call" | custom-call | flops 511705088 | bytes 5980160 | tf_op jit(solution)/shard_map/middle/pallas_call | solution.py:70
  22.7 0.0 collective-permute-done.7.inner_ref
  22.7 1.5 %collective-permute-done.8.outer_ref = bf16[2,256]{1,0:T(2,128)(2,1)S(1)} collective-permute-done((bf16[2,256]{1,0:T(2,128)(2,1)S(1)}, bf16[2,256]{1,0:T(2,128)(2,1)S(1)}, u32[]{:S(2)}, u32[]{:S(2)}) %collective-permute-start.8) | collective-permute-done | bytes 1056 | tf_op jit(solution)/shard_map/ppermute | solution.py:43
  24.2 0.6 %collective-permute-start.9 = (bf16[272,256]{1,0:T(8,128)(2,1)S(1)}, bf16[272,256]{1,0:T(8,128)(2,1)S(1)}, u32[]{:S(2)}, u32[]{:S(2)}) collective-permute-start(bf16[272,256]{1,0:T(8,128)(2,1)S(1)} %get-tuple-element.57.near_ref), channel_id=1, source_target_pairs={{0,1},{1,0},{2,3},{3,2},{4,5},{5,4},{6,7},{7,6},{8,9},{9,8},{10,11... | collective-permute-start | bytes 417800 | tf_op jit(solution)/shard_map/ppermute | solution.py:43
  24.8 3.3 %collective-permute-start.10 = (bf16[272,256]{1,0:T(8,128)(2,1)S(1)}, bf16[272,256]{1,0:T(8,128)(2,1)S(1)}, u32[]{:S(2)}, u32[]{:S(2)}) collective-permute-start(bf16[272,256]{1,0:T(8,128)(2,1)S(1)} %get-tuple-element.58.far_ref), channel_id=1, source_target_pairs={{0,0},{1,2},{2,1},{3,3},{4,4},{5,6},{6,5},{7,7},{8,8},{9,10},{10,9... | collective-permute-start | bytes 417800 | tf_op jit(solution)/shard_map/ppermute | solution.py:43
  28.2 0.6 %inside.1.part_ref = f32[2,256,256]{2,1,0:T(8,128)S(1)} custom-call(s32[1]{0:T(128)} %bitcast.el_ref.refs_0_, bf16[272,256]{1,0:T(8,128)(2,1)S(1)} %get-tuple-element.57.near_ref, bf16[272,256]{1,0:T(8,128)(2,1)S(1)} %get-tuple-element.58.far_ref, f32[2,256,256]{2,1,0:T(8,128)S(1)} %get-tuple-element.59.joined_ref, ...), custom_call_target="tpu_custom_call" | custom-call | flops 402653184 | bytes 2506756 | tf_op jit(solution)/shard_map/inside/pallas_call | solution.py:70
  28.8 0.6 %collective-permute-done.9.near_ref = bf16[272,256]{1,0:T(8,128)(2,1)S(1)} collective-permute-done((bf16[272,256]{1,0:T(8,128)(2,1)S(1)}, bf16[272,256]{1,0:T(8,128)(2,1)S(1)}, u32[]{:S(2)}, u32[]{:S(2)}) %collective-permute-start.9) | collective-permute-done | bytes 139296 | tf_op jit(solution)/shard_map/ppermute | solution.py:43
  29.4 0.3 near_border.1.near_ref
  29.6 3.0 %collective-permute-done.10.far_ref = bf16[272,256]{1,0:T(8,128)(2,1)S(1)} collective-permute-done((bf16[272,256]{1,0:T(8,128)(2,1)S(1)}, bf16[272,256]{1,0:T(8,128)(2,1)S(1)}, u32[]{:S(2)}, u32[]{:S(2)}) %collective-permute-start.10) | collective-permute-done | bytes 139296 | tf_op jit(solution)/shard_map/ppermute | solution.py:43
  32.7 1.0 %far_border.1 = bf16[2,256,256]{2,1,0:T(8,128)(2,1)} custom-call(s32[1]{0:T(128)} %bitcast.el_ref.refs_0_, bf16[256,256]{1,0:T(8,128)(2,1)S(1)} %near_border.1.near_ref, bf16[272,256]{1,0:T(8,128)(2,1)S(1)} %collective-permute-done.10.far_ref, f32[2,256,256]{2,1,0:T(8,128)S(1)} %inside.1.part_ref, bf16[9,256,256]{2,1,0:T(8,128)(2,1)S(1)} %get-tuple-element.60.w_ref), custom_call_target="tpu_custom_call" | custom-call | flops 100663296 | bytes 2236420 | tf_op jit(solution)/shard_map/far_border/pallas_call | solution.py:70
  (10 shorter events, 0.1 us)
Async XLA Ops:
  1.1 6.0 %collective-permute-start = (bf16[5,16,256]{2,1,0:T(8,128)(2,1)S(1)}, bf16[5,16,256]{2,1,0:T(8,128)(2,1)S(1)}, u32[]{:S(2)}, u32[]{:S(2)}) collective-permute-start(bf16[5,16,256]{2,1,0:T(8,128)(2,1)S(1)} %get-tuple-element.34), channel_id=1, source_target_pairs={{0,3},{1,2},{2,1},{3,0},{4,7},{5,6},{6,5},{7,4},{8,11},{9,10},{10,... | collective-permute-start | bytes 122888 | tf_op jit(solution)/shard_map/ppermute | solution.py:43
  2.7 4.4 %collective-permute-start.1 = (bf16[5,16,256]{2,1,0:T(8,128)(2,1)S(1)}, bf16[5,16,256]{2,1,0:T(8,128)(2,1)S(1)}, u32[]{:S(2)}, u32[]{:S(2)}) collective-permute-start(bf16[5,16,256]{2,1,0:T(8,128)(2,1)S(1)} %get-tuple-element.35), channel_id=1, source_target_pairs={{0,1},{1,0},{2,3},{3,2},{4,5},{5,4},{6,7},{7,6},{8,9},{9,8},{10,11... | collective-permute-start | bytes 122888 | tf_op jit(solution)/shard_map/ppermute | solution.py:43
  4.2 4.0 %collective-permute-start.2 = (bf16[5,16,256]{2,1,0:T(8,128)(2,1)S(1)}, bf16[5,16,256]{2,1,0:T(8,128)(2,1)S(1)}, u32[]{:S(2)}, u32[]{:S(2)}) collective-permute-start(bf16[5,16,256]{2,1,0:T(8,128)(2,1)S(1)} %get-tuple-element.36), channel_id=1, source_target_pairs={{0,2},{1,3},{2,0},{3,1},{4,6},{5,7},{6,4},{7,5},{8,10},{9,11},{10,... | collective-permute-start | bytes 122888 | tf_op jit(solution)/shard_map/ppermute | solution.py:43
  8.2 5.8 %collective-permute-start.3 = (bf16[64,256]{1,0:T(8,128)(2,1)S(1)}, bf16[64,256]{1,0:T(8,128)(2,1)S(1)}, u32[]{:S(2)}, u32[]{:S(2)}) collective-permute-start(bf16[64,256]{1,0:T(8,128)(2,1)S(1)} %pad_maximum_fusion.1), channel_id=1, source_target_pairs={{0,24},{4,28},{8,16},{12,20},{16,8},{20,12},{24,0},{28,4},{1,25},{... | collective-permute-start | bytes 98312 | tf_op jit(solution)/shard_map/ppermute | solution.py:43
  11.9 5.1 %collective-permute-start.4 = (bf16[64,256]{1,0:T(8,128)(2,1)S(1)}, bf16[64,256]{1,0:T(8,128)(2,1)S(1)}, u32[]{:S(2)}, u32[]{:S(2)}) collective-permute-start(bf16[64,256]{1,0:T(8,128)(2,1)S(1)} %pad_maximum_fusion.2), channel_id=1, source_target_pairs={{0,28},{4,8},{8,4},{12,16},{16,12},{20,24},{24,20},{28,0},{1,29},{... | collective-permute-start | bytes 98312 | tf_op jit(solution)/shard_map/ppermute | solution.py:43
  11.9 5.1 %collective-permute-start.5 = (bf16[64,256]{1,0:T(8,128)(2,1)S(1)}, bf16[64,256]{1,0:T(8,128)(2,1)S(1)}, u32[]{:S(2)}, u32[]{:S(2)}) collective-permute-start(bf16[64,256]{1,0:T(8,128)(2,1)S(1)} %pad_maximum_fusion.3), channel_id=1, source_target_pairs={{0,8},{4,12},{8,0},{12,4},{16,24},{20,28},{24,16},{28,20},{1,9},{5... | collective-permute-start | bytes 98312 | tf_op jit(solution)/shard_map/ppermute | solution.py:43
  12.0 5.0 %collective-permute-start.6 = (bf16[64,256]{1,0:T(8,128)(2,1)S(1)}, bf16[64,256]{1,0:T(8,128)(2,1)S(1)}, u32[]{:S(2)}, u32[]{:S(2)}) collective-permute-start(bf16[64,256]{1,0:T(8,128)(2,1)S(1)} %pad_maximum_fusion.4), channel_id=1, source_target_pairs={{0,4},{4,0},{8,12},{12,8},{16,20},{20,16},{24,28},{28,24},{1,5},{5... | collective-permute-start | bytes 98312 | tf_op jit(solution)/shard_map/ppermute | solution.py:43
  19.3 3.4 %collective-permute-start.7 = (bf16[2,256]{1,0:T(2,128)(2,1)S(1)}, bf16[2,256]{1,0:T(2,128)(2,1)S(1)}, u32[]{:S(2)}, u32[]{:S(2)}) collective-permute-start(bf16[2,256]{1,0:T(2,128)(2,1)S(1)} %get-tuple-element.49), channel_id=1, source_target_pairs={{0,4},{4,0},{8,12},{12,8},{16,20},{20,16},{24,28},{28,24},{1,5},{5... | collective-permute-start | bytes 3080 | tf_op jit(solution)/shard_map/ppermute | solution.py:43
  19.4 4.9 %collective-permute-start.8 = (bf16[2,256]{1,0:T(2,128)(2,1)S(1)}, bf16[2,256]{1,0:T(2,128)(2,1)S(1)}, u32[]{:S(2)}, u32[]{:S(2)}) collective-permute-start(bf16[2,256]{1,0:T(2,128)(2,1)S(1)} %get-tuple-element.50), channel_id=1, source_target_pairs={{0,28},{4,8},{8,4},{12,16},{16,12},{20,24},{24,20},{28,0},{1,29},{... | collective-permute-start | bytes 3080 | tf_op jit(solution)/shard_map/ppermute | solution.py:43
  24.2 5.1 %collective-permute-start.9 = (bf16[272,256]{1,0:T(8,128)(2,1)S(1)}, bf16[272,256]{1,0:T(8,128)(2,1)S(1)}, u32[]{:S(2)}, u32[]{:S(2)}) collective-permute-start(bf16[272,256]{1,0:T(8,128)(2,1)S(1)} %get-tuple-element.57.near_ref), channel_id=1, source_target_pairs={{0,1},{1,0},{2,3},{3,2},{4,5},{5,4},{6,7},{7,6},{8,9},{9,8},{10,11... | collective-permute-start | bytes 417800 | tf_op jit(solution)/shard_map/ppermute | solution.py:43
  24.8 7.8 %collective-permute-start.10 = (bf16[272,256]{1,0:T(8,128)(2,1)S(1)}, bf16[272,256]{1,0:T(8,128)(2,1)S(1)}, u32[]{:S(2)}, u32[]{:S(2)}) collective-permute-start(bf16[272,256]{1,0:T(8,128)(2,1)S(1)} %get-tuple-element.58.far_ref), channel_id=1, source_target_pairs={{0,0},{1,2},{2,1},{3,3},{4,4},{5,6},{6,5},{7,7},{8,8},{9,10},{10,9... | collective-permute-start | bytes 417800 | tf_op jit(solution)/shard_map/ppermute | solution.py:43

commit v10 on v9

--- a/solution.py
+++ b/solution.py
@@ -339,21 +339,20 @@
     out_ref[1] = joined_ref[1] + conv_rows([(far, w_ref, 3), (near, w_ref, 6 - 6 * odd)], cols)
 
 
-def near_border_body(el_ref, near_ref, part_ref, w_ref, out_ref):
+def far_border_body(el_ref, far_ref, part_ref, w_ref, out_ref, *, last):
+    el = el_ref[0]
+    far = conv_rows([(far_ref[...], w_ref, 6 * lax.rem(el, 2))], part_ref.shape[1])
+    ends = jnp.logical_or(el == 0, el == last)
+    out_ref[...] = (part_ref[1] + jnp.where(ends, 0.0, far)).astype(BF16)
+
+
+def near_border_body(el_ref, far_row_ref, near_ref, part_ref, w_ref, out_hbm, row_ref, sems):
     odd = lax.rem(el_ref[0], 2)
-    near = part_ref[0] + conv_rows([(near_ref[...], w_ref, 6 - 6 * odd)], part_ref.shape[1])
-    out_ref[...] = near.astype(BF16)
-
-
-def far_border_body(el_ref, near_ref, far_ref, part_ref, w_ref, out_hbm, row_ref, sems, *, last):
-    el = el_ref[0]
-    odd = lax.rem(el, 2)
-    first = pltpu.make_async_copy(near_ref, out_hbm.at[1 - odd], sems.at[0])
+    first = pltpu.make_async_copy(far_row_ref, out_hbm.at[odd], sems.at[0])
     first.start()
-    far = conv_rows([(far_ref[...], w_ref, 6 * odd)], part_ref.shape[1])
-    ends = jnp.logical_or(el == 0, el == last)
-    row_ref[...] = (part_ref[1] + jnp.where(ends, 0.0, far)).astype(BF16)
-    second = pltpu.make_async_copy(row_ref, out_hbm.at[odd], sems.at[1])
+    near = conv_rows([(near_ref[...], w_ref, 6 - 6 * odd)], part_ref.shape[1])
+    row_ref[...] = (part_ref[0] + near).astype(BF16)
+    second = pltpu.make_async_copy(row_ref, out_hbm.at[1 - odd], sems.at[1])
     second.start()
     first.wait()
     second.wait()
@@ -483,19 +482,19 @@
         (2 * count * width * width * 6, 0),
         [SMEM] + [VMEM] * 4,
     )
-    (near_row,) = call(
-        near_border_body,
+    (far_row,) = call(
+        functools.partial(far_border_body, last=lax.axis_size("el") - 1),
         [shape((cols, width), BF16)],
-        [el, near_got, partial, w_conv],
-        "near_border",
+        [el, far_got, partial, w_conv],
+        "far_border",
         (cols * width * width * 6, 0),
         [SMEM] + [VMEM] * 3,
     )
     (out,) = call(
-        functools.partial(far_border_body, last=lax.axis_size("el") - 1),
+        near_border_body,
         [shape((rows, cols, width), BF16)],
-        [el, near_row, far_got, partial, w_conv],
-        "far_border",
+        [el, far_row, near_got, partial, w_conv],
+        "near_border",
         (cols * width * width * 6, 0),
         [SMEM] + [VMEM] * 4,
         [VMEM((cols, width), BF16), dma((2,))],

time: 33.9 us -> 36 us (1.062)
  the two profiles are of different devices: /device:TPU:2 before, /device:TPU:0 now
where the time goes in v10:
time: 36 us; the launch traced here: 35.7 us
  starting transfers between devices  13.7 us (38%)
  waiting for transfers between devices  11.6 us (32%)
  Pallas kernels  10.2 us (28%)
    ppermute x11, starting transfers between devices, swap(): return lax.ppermute(x, axis, [(i, partner(i, n)) for i in range(n)])  13.7 us
    ppermute x11, waiting for transfers between devices, swap(): return lax.ppermute(x, axis, [(i, partner(i, n)) for i in range(n)])  11.6 us
    pallas_call x9, Pallas kernels, call(): pl.pallas_call(body, out_shape=outs, in_specs=[pl.BlockSpec(memory_space=...  10.2 us
  transfers between devices with their start and end apart: 11, of which 6 were waited for; matrix products, arithmetic and copies ran while one was open for 0% of the time, Pallas kernels for 16%

profile of v10, /device:TPU:0, one launch (start us, length us, event | category | flops | bytes accessed | tf_op | source)
XLA Modules:
  0.0 35.7 jit_solution(14302519666605571587)
XLA Ops:
  0.0 1.1 %gather.1 = (bf16[5,16,256]{2,1,0:T(8,128)(2,1)S(1)}, bf16[5,16,256]{2,1,0:T(8,128)(2,1)S(1)}, bf16[5,16,256]{2,1,0:T(8,128)(2,1)S(1)}, bf16[5,16,256]{2,1,0:T(8,128)(2,1)S(1)}) custom-call(s32[1]{0:T(128)} %bitcast.el_ref.refs_0_, s32[1]{0:T(128)} %bitcast.1.az_ref.refs_1_, bf16[128,256]{1,0:T(8,128)(2,1)} %bitcast.46, s32[5,4,16]{2,1,0:T(4,128)} %bitcast.47), custom_call_target="tpu_custom_call" | custom-call | flops 20971520 | bytes 230664 | tf_op jit(solution)/shard_map/gather/pallas_call | solution.py:70
  1.1 4.0 %collective-permute-start = (bf16[5,16,256]{2,1,0:T(8,128)(2,1)S(1)}, bf16[5,16,256]{2,1,0:T(8,128)(2,1)S(1)}, u32[]{:S(2)}, u32[]{:S(2)}) collective-permute-start(bf16[5,16,256]{2,1,0:T(8,128)(2,1)S(1)} %get-tuple-element.34), channel_id=1, source_target_pairs={{0,3},{1,2},{2,1},{3,0},{4,7},{5,6},{6,5},{7,4},{8,11},{9,10},{10,... | collective-permute-start | bytes 122888 | tf_op jit(solution)/shard_map/ppermute | solution.py:43
  5.1 0.5 %collective-permute-start.1 = (bf16[5,16,256]{2,1,0:T(8,128)(2,1)S(1)}, bf16[5,16,256]{2,1,0:T(8,128)(2,1)S(1)}, u32[]{:S(2)}, u32[]{:S(2)}) collective-permute-start(bf16[5,16,256]{2,1,0:T(8,128)(2,1)S(1)} %get-tuple-element.35), channel_id=1, source_target_pairs={{0,1},{1,0},{2,3},{3,2},{4,5},{5,4},{6,7},{7,6},{8,9},{9,8},{10,11... | collective-permute-start | bytes 122888 | tf_op jit(solution)/shard_map/ppermute | solution.py:43
  5.6 0.1 collective-permute-start.2
  5.7 2.4 %load.1 = (f32[320,512]{1,0:T(8,128)S(1)}, bf16[512,256]{1,0:T(8,128)(2,1)S(1)}, bf16[512,256]{1,0:T(8,128)(2,1)S(1)}, bf16[256,256]{1,0:T(8,128)(2,1)S(1)}, bf1...) custom-call(s32[1]{0:T(128)} %bitcast.el_ref.refs_0_, ...), custom_call_target="tpu_custom_call" | custom-call | flops 7864320 | bytes 8290312 | tf_op jit(solution)/shard_map/load/pallas_call | solution.py:70
  8.1 0.0 collective-permute-done
  8.2 0.9 %collective-permute-done.1 = bf16[5,16,256]{2,1,0:T(8,128)(2,1)S(1)} collective-permute-done((bf16[5,16,256]{2,1,0:T(8,128)(2,1)S(1)}, bf16[5,16,256]{2,1,0:T(8,128)(2,1)S(1)}, u32[]{:S(2)}, u32[]{:S(2)}) %collective-permute-start.1) | collective-permute-done | bytes 40992 | tf_op jit(solution)/shard_map/ppermute | solution.py:43
  9.1 0.5 %collective-permute-done.2 = bf16[5,16,256]{2,1,0:T(8,128)(2,1)S(1)} collective-permute-done((bf16[5,16,256]{2,1,0:T(8,128)(2,1)S(1)}, bf16[5,16,256]{2,1,0:T(8,128)(2,1)S(1)}, u32[]{:S(2)}, u32[]{:S(2)}) %collective-permute-start.2) | collective-permute-done | bytes 40992 | tf_op jit(solution)/shard_map/ppermute | solution.py:43
  9.6 3.7 %collective-permute-start.3 = (bf16[64,256]{1,0:T(8,128)(2,1)S(1)}, bf16[64,256]{1,0:T(8,128)(2,1)S(1)}, u32[]{:S(2)}, u32[]{:S(2)}) collective-permute-start(bf16[64,256]{1,0:T(8,128)(2,1)S(1)} %pad_maximum_fusion.1), channel_id=1, source_target_pairs={{0,24},{4,28},{8,16},{12,20},{16,8},{20,12},{24,0},{28,4},{1,25},{... | collective-permute-start | bytes 98312 | tf_op jit(solution)/shard_map/ppermute | solution.py:43
  13.3 0.0 collective-permute-start.4
  13.3 0.1 collective-permute-start.5
  13.4 0.1 collective-permute-start.6
  13.5 0.5 %query.1 = (bf16[256,512]{1,0:T(8,128)(2,1)S(1)}, f32[512,1024]{1,0:T(8,128)S(1)}) custom-call(bf16[512,256]{1,0:T(8,128)(2,1)S(1)} %get-tuple-element.39.points_ref.refs_9_, bf16[512,256]{1,0:T(8,128)(2,1)S(1)} %get-tuple-element.40.skip_ref, bf16[256,256]{1,0:T(8,128)(2,1)S(1)} %get-tuple-element.41.w_query_ref, ...), custom_call_target="tpu_custom_call" | custom-call | flops 335544320 | bytes 3571712 | tf_op jit(solution)/shard_map/query/pallas_call | solution.py:70
  14.0 1.4 %collective-permute-done.3.refs_1_ = bf16[64,256]{1,0:T(8,128)(2,1)S(1)} collective-permute-done((bf16[64,256]{1,0:T(8,128)(2,1)S(1)}, bf16[64,256]{1,0:T(8,128)(2,1)S(1)}, u32[]{:S(2)}, u32[]{:S(2)}) %collective-permute-start.3) | collective-permute-done | bytes 32800 | tf_op jit(solution)/shard_map/ppermute | solution.py:43
  15.4 3.0 %collective-permute-done.4.refs_2_ = bf16[64,256]{1,0:T(8,128)(2,1)S(1)} collective-permute-done((bf16[64,256]{1,0:T(8,128)(2,1)S(1)}, bf16[64,256]{1,0:T(8,128)(2,1)S(1)}, u32[]{:S(2)}, u32[]{:S(2)}) %collective-permute-start.4) | collective-permute-done | bytes 32800 | tf_op jit(solution)/shard_map/ppermute | solution.py:43
  18.4 0.0 collective-permute-done.5.refs_3_
  18.4 0.0 collective-permute-done.6.refs_4_
  18.4 2.3 %ends.1 = (f32[2,128,256]{2,1,0:T(8,128)S(1)}, bf16[2,128,256]{2,1,0:T(8,128)(2,1)S(1)}, bf16[2,256]{1,0:T(2,128)(2,1)S(1)}, bf16[2,256]{1,0:T(2,128)(2,1)S(1)},...) custom-call(s32[1]{0:T(128)} %bitcast.1.az_ref.refs_1_, ...), custom_call_target="tpu_custom_call" | custom-call | flops 511705088 | bytes 5605380 | tf_op jit(solution)/shard_map/ends/pallas_call | solution.py:70
  20.7 0.1 collective-permute-start.7
  20.8 1.2 %collective-permute-start.8 = (bf16[2,256]{1,0:T(2,128)(2,1)S(1)}, bf16[2,256]{1,0:T(2,128)(2,1)S(1)}, u32[]{:S(2)}, u32[]{:S(2)}) collective-permute-start(bf16[2,256]{1,0:T(2,128)(2,1)S(1)} %get-tuple-element.50), channel_id=1, source_target_pairs={{0,28},{4,8},{8,4},{12,16},{16,12},{20,24},{24,20},{28,0},{1,29},{... | collective-permute-start | bytes 3080 | tf_op jit(solution)/shard_map/ppermute | solution.py:43
  22.0 2.1 %middle.1 = (f32[2,256,256]{2,1,0:T(8,128)S(1)}, bf16[272,256]{1,0:T(8,128)(2,1)S(1)}, bf16[272,256]{1,0:T(8,128)(2,1)S(1)}) custom-call(bf16[320,256]{1,0:T(8,128)(2,1)S(1)} %get-tuple-element.51.keys_ref, bf16[256,320]{1,0:T(8,128)(2,1)S(1)} %get-tuple-element.52.values_ref, f32[2,128,256]{2,1,0:T(8,128)S(1)} %get-tuple-element.53.joined_ends_ref, ...), custom_call_target="tpu_custom_call" | custom-call | flops 511705088 | bytes 5980160 | tf_op jit(solution)/shard_map/middle/pallas_call | solution.py:70
  24.1 0.0 collective-permute-done.7.inner_ref
  24.1 1.5 %collective-permute-done.8.outer_ref = bf16[2,256]{1,0:T(2,128)(2,1)S(1)} collective-permute-done((bf16[2,256]{1,0:T(2,128)(2,1)S(1)}, bf16[2,256]{1,0:T(2,128)(2,1)S(1)}, u32[]{:S(2)}, u32[]{:S(2)}) %collective-permute-start.8) | collective-permute-done | bytes 1056 | tf_op jit(solution)/shard_map/ppermute | solution.py:43
  25.7 0.7 %collective-permute-start.9 = (bf16[272,256]{1,0:T(8,128)(2,1)S(1)}, bf16[272,256]{1,0:T(8,128)(2,1)S(1)}, u32[]{:S(2)}, u32[]{:S(2)}) collective-permute-start(bf16[272,256]{1,0:T(8,128)(2,1)S(1)} %get-tuple-element.57.far_ref), channel_id=1, source_target_pairs={{0,0},{1,2},{2,1},{3,3},{4,4},{5,6},{6,5},{7,7},{8,8},{9,10},{10,9... | collective-permute-start | bytes 417800 | tf_op jit(solution)/shard_map/ppermute | solution.py:43
  26.4 3.3 %collective-permute-start.10 = (bf16[272,256]{1,0:T(8,128)(2,1)S(1)}, bf16[272,256]{1,0:T(8,128)(2,1)S(1)}, u32[]{:S(2)}, u32[]{:S(2)}) collective-permute-start(bf16[272,256]{1,0:T(8,128)(2,1)S(1)} %get-tuple-element.58.near_ref), channel_id=1, source_target_pairs={{0,1},{1,0},{2,3},{3,2},{4,5},{5,4},{6,7},{7,6},{8,9},{9,8},{10,11... | collective-permute-start | bytes 417800 | tf_op jit(solution)/shard_map/ppermute | solution.py:43
  29.6 0.6 %inside.1.part_ref = f32[2,256,256]{2,1,0:T(8,128)S(1)} custom-call(s32[1]{0:T(128)} %bitcast.el_ref.refs_0_, bf16[272,256]{1,0:T(8,128)(2,1)S(1)} %get-tuple-element.58.near_ref, bf16[272,256]{1,0:T(8,128)(2,1)S(1)} %get-tuple-element.57.far_ref, f32[2,256,256]{2,1,0:T(8,128)S(1)} %get-tuple-element.59.joined_ref, ...), custom_call_target="tpu_custom_call" | custom-call | flops 402653184 | bytes 2506756 | tf_op jit(solution)/shard_map/inside/pallas_call | solution.py:70
  30.3 0.0 collective-permute-done.9.far_ref
  30.3 0.3 far_border.1.far_row_ref
  30.6 4.2 %collective-permute-done.10.near_ref = bf16[272,256]{1,0:T(8,128)(2,1)S(1)} collective-permute-done((bf16[272,256]{1,0:T(8,128)(2,1)S(1)}, bf16[272,256]{1,0:T(8,128)(2,1)S(1)}, u32[]{:S(2)}, u32[]{:S(2)}) %collective-permute-start.10) | collective-permute-done | bytes 139296 | tf_op jit(solution)/shard_map/ppermute | solution.py:43
  34.7 1.0 %near_border.1 = bf16[2,256,256]{2,1,0:T(8,128)(2,1)} custom-call(s32[1]{0:T(128)} %bitcast.el_ref.refs_0_, bf16[256,256]{1,0:T(8,128)(2,1)S(1)} %far_border.1.far_row_ref, bf16[272,256]{1,0:T(8,128)(2,1)S(1)} %collective-permute-done.10.near_ref, f32[2,256,256]{2,1,0:T(8,128)S(1)} %inside.1.part_ref, bf16[9,256,256]{2,1,0:T(8,128)(2,1)S(1)} %get-tuple-element.60.w_ref), custom_call_target="tpu_custom_call" | custom-call | flops 100663296 | bytes 2236420 | tf_op jit(solution)/shard_map/near_border/pallas_call | solution.py:70
  (10 shorter events, 0.1 us)
Async XLA Ops:
  1.1 7.0 %collective-permute-start = (bf16[5,16,256]{2,1,0:T(8,128)(2,1)S(1)}, bf16[5,16,256]{2,1,0:T(8,128)(2,1)S(1)}, u32[]{:S(2)}, u32[]{:S(2)}) collective-permute-start(bf16[5,16,256]{2,1,0:T(8,128)(2,1)S(1)} %get-tuple-element.34), channel_id=1, source_target_pairs={{0,3},{1,2},{2,1},{3,0},{4,7},{5,6},{6,5},{7,4},{8,11},{9,10},{10,... | collective-permute-start | bytes 122888 | tf_op jit(solution)/shard_map/ppermute | solution.py:43
  5.1 4.0 %collective-permute-start.1 = (bf16[5,16,256]{2,1,0:T(8,128)(2,1)S(1)}, bf16[5,16,256]{2,1,0:T(8,128)(2,1)S(1)}, u32[]{:S(2)}, u32[]{:S(2)}) collective-permute-start(bf16[5,16,256]{2,1,0:T(8,128)(2,1)S(1)} %get-tuple-element.35), channel_id=1, source_target_pairs={{0,1},{1,0},{2,3},{3,2},{4,5},{5,4},{6,7},{7,6},{8,9},{9,8},{10,11... | collective-permute-start | bytes 122888 | tf_op jit(solution)/shard_map/ppermute | solution.py:43
  5.6 4.0 %collective-permute-start.2 = (bf16[5,16,256]{2,1,0:T(8,128)(2,1)S(1)}, bf16[5,16,256]{2,1,0:T(8,128)(2,1)S(1)}, u32[]{:S(2)}, u32[]{:S(2)}) collective-permute-start(bf16[5,16,256]{2,1,0:T(8,128)(2,1)S(1)} %get-tuple-element.36), channel_id=1, source_target_pairs={{0,2},{1,3},{2,0},{3,1},{4,6},{5,7},{6,4},{7,5},{8,10},{9,11},{10,... | collective-permute-start | bytes 122888 | tf_op jit(solution)/shard_map/ppermute | solution.py:43
  9.6 5.8 %collective-permute-start.3 = (bf16[64,256]{1,0:T(8,128)(2,1)S(1)}, bf16[64,256]{1,0:T(8,128)(2,1)S(1)}, u32[]{:S(2)}, u32[]{:S(2)}) collective-permute-start(bf16[64,256]{1,0:T(8,128)(2,1)S(1)} %pad_maximum_fusion.1), channel_id=1, source_target_pairs={{0,24},{4,28},{8,16},{12,20},{16,8},{20,12},{24,0},{28,4},{1,25},{... | collective-permute-start | bytes 98312 | tf_op jit(solution)/shard_map/ppermute | solution.py:43
  13.3 5.1 %collective-permute-start.4 = (bf16[64,256]{1,0:T(8,128)(2,1)S(1)}, bf16[64,256]{1,0:T(8,128)(2,1)S(1)}, u32[]{:S(2)}, u32[]{:S(2)}) collective-permute-start(bf16[64,256]{1,0:T(8,128)(2,1)S(1)} %pad_maximum_fusion.2), channel_id=1, source_target_pairs={{0,28},{4,8},{8,4},{12,16},{16,12},{20,24},{24,20},{28,0},{1,29},{... | collective-permute-start | bytes 98312 | tf_op jit(solution)/shard_map/ppermute | solution.py:43
  13.3 5.1 %collective-permute-start.5 = (bf16[64,256]{1,0:T(8,128)(2,1)S(1)}, bf16[64,256]{1,0:T(8,128)(2,1)S(1)}, u32[]{:S(2)}, u32[]{:S(2)}) collective-permute-start(bf16[64,256]{1,0:T(8,128)(2,1)S(1)} %pad_maximum_fusion.3), channel_id=1, source_target_pairs={{0,8},{4,12},{8,0},{12,4},{16,24},{20,28},{24,16},{28,20},{1,9},{5... | collective-permute-start | bytes 98312 | tf_op jit(solution)/shard_map/ppermute | solution.py:43
  13.4 5.0 %collective-permute-start.6 = (bf16[64,256]{1,0:T(8,128)(2,1)S(1)}, bf16[64,256]{1,0:T(8,128)(2,1)S(1)}, u32[]{:S(2)}, u32[]{:S(2)}) collective-permute-start(bf16[64,256]{1,0:T(8,128)(2,1)S(1)} %pad_maximum_fusion.4), channel_id=1, source_target_pairs={{0,4},{4,0},{8,12},{12,8},{16,20},{20,16},{24,28},{28,24},{1,5},{5... | collective-permute-start | bytes 98312 | tf_op jit(solution)/shard_map/ppermute | solution.py:43
  20.7 3.4 %collective-permute-start.7 = (bf16[2,256]{1,0:T(2,128)(2,1)S(1)}, bf16[2,256]{1,0:T(2,128)(2,1)S(1)}, u32[]{:S(2)}, u32[]{:S(2)}) collective-permute-start(bf16[2,256]{1,0:T(2,128)(2,1)S(1)} %get-tuple-element.49), channel_id=1, source_target_pairs={{0,4},{4,0},{8,12},{12,8},{16,20},{20,16},{24,28},{28,24},{1,5},{5... | collective-permute-start | bytes 3080 | tf_op jit(solution)/shard_map/ppermute | solution.py:43
  20.8 4.9 %collective-permute-start.8 = (bf16[2,256]{1,0:T(2,128)(2,1)S(1)}, bf16[2,256]{1,0:T(2,128)(2,1)S(1)}, u32[]{:S(2)}, u32[]{:S(2)}) collective-permute-start(bf16[2,256]{1,0:T(2,128)(2,1)S(1)} %get-tuple-element.50), channel_id=1, source_target_pairs={{0,28},{4,8},{8,4},{12,16},{16,12},{20,24},{24,20},{28,0},{1,29},{... | collective-permute-start | bytes 3080 | tf_op jit(solution)/shard_map/ppermute | solution.py:43
  25.7 4.6 %collective-permute-start.9 = (bf16[272,256]{1,0:T(8,128)(2,1)S(1)}, bf16[272,256]{1,0:T(8,128)(2,1)S(1)}, u32[]{:S(2)}, u32[]{:S(2)}) collective-permute-start(bf16[272,256]{1,0:T(8,128)(2,1)S(1)} %get-tuple-element.57.far_ref), channel_id=1, source_target_pairs={{0,0},{1,2},{2,1},{3,3},{4,4},{5,6},{6,5},{7,7},{8,8},{9,10},{10,9... | collective-permute-start | bytes 417800 | tf_op jit(solution)/shard_map/ppermute | solution.py:43
  26.4 8.4 %collective-permute-start.10 = (bf16[272,256]{1,0:T(8,128)(2,1)S(1)}, bf16[272,256]{1,0:T(8,128)(2,1)S(1)}, u32[]{:S(2)}, u32[]{:S(2)}) collective-permute-start(bf16[272,256]{1,0:T(8,128)(2,1)S(1)} %get-tuple-element.58.near_ref), channel_id=1, source_target_pairs={{0,1},{1,0},{2,3},{3,2},{4,5},{5,4},{6,7},{7,6},{8,9},{9,8},{10,11... | collective-permute-start | bytes 417800 | tf_op jit(solution)/shard_map/ppermute | solution.py:43

commit v11 on v9

--- a/solution.py
+++ b/solution.py
@@ -32,10 +32,6 @@
 
 def two_back(i, n):
     return (i - 2 if i // 2 % 2 == 0 else i + 2) % n
-
-
-def inner_pair(i, n):
-    return i if i in (0, n - 1) else next_chip(i, n)
 
 
 def swap(x, axis, partner):
@@ -473,7 +469,7 @@
         (),
         {3: 0, 4: 1},
     )
-    far_got = swap(far, "el", inner_pair)
+    far_got = swap(far, "el", next_chip)
     near_got = swap(near, "el", same_chip)
     (partial,) = call(
         inside_body,

time: 33.9 us -> 34.8 us (1.027)
  the two profiles are of different devices: /device:TPU:2 before, /device:TPU:0 now
where the time goes in v11:
time: 34.8 us; the launch traced here: 34.5 us
  waiting for transfers between devices  12.4 us (36%)
  starting transfers between devices  11.8 us (34%)
  Pallas kernels  10.2 us (29%)
    ppermute x11, waiting for transfers between devices, swap(): return lax.ppermute(x, axis, [(i, partner(i, n)) for i in range(n)])  12.4 us
    ppermute x11, starting transfers between devices, swap(): return lax.ppermute(x, axis, [(i, partner(i, n)) for i in range(n)])  11.8 us
    pallas_call x9, Pallas kernels, call(): pl.pallas_call(body, out_shape=outs, in_specs=[pl.BlockSpec(memory_space=...  10.2 us
  transfers between devices with their start and end apart: 11, of which 7 were waited for; matrix products, arithmetic and copies ran while one was open for 0% of the time, Pallas kernels for 17%

profile of v11, /device:TPU:0, one launch (start us, length us, event | category | flops | bytes accessed | tf_op | source)
XLA Modules:
  0.0 34.5 jit_solution(17599287734647215237)
XLA Ops:
  0.0 1.1 %gather.1 = (bf16[5,16,256]{2,1,0:T(8,128)(2,1)S(1)}, bf16[5,16,256]{2,1,0:T(8,128)(2,1)S(1)}, bf16[5,16,256]{2,1,0:T(8,128)(2,1)S(1)}, bf16[5,16,256]{2,1,0:T(8,128)(2,1)S(1)}) custom-call(s32[1]{0:T(128)} %bitcast.el_ref.refs_0_, s32[1]{0:T(128)} %bitcast.1.az_ref.refs_1_, bf16[128,256]{1,0:T(8,128)(2,1)} %bitcast.46, s32[5,4,16]{2,1,0:T(4,128)} %bitcast.47), custom_call_target="tpu_custom_call" | custom-call | flops 20971520 | bytes 230664 | tf_op jit(solution)/shard_map/gather/pallas_call | solution.py:66
  1.1 4.0 %collective-permute-start = (bf16[5,16,256]{2,1,0:T(8,128)(2,1)S(1)}, bf16[5,16,256]{2,1,0:T(8,128)(2,1)S(1)}, u32[]{:S(2)}, u32[]{:S(2)}) collective-permute-start(bf16[5,16,256]{2,1,0:T(8,128)(2,1)S(1)} %get-tuple-element.34), channel_id=1, source_target_pairs={{0,3},{1,2},{2,1},{3,0},{4,7},{5,6},{6,5},{7,4},{8,11},{9,10},{10,... | collective-permute-start | bytes 122888 | tf_op jit(solution)/shard_map/ppermute | solution.py:39
  5.1 0.5 %collective-permute-start.1 = (bf16[5,16,256]{2,1,0:T(8,128)(2,1)S(1)}, bf16[5,16,256]{2,1,0:T(8,128)(2,1)S(1)}, u32[]{:S(2)}, u32[]{:S(2)}) collective-permute-start(bf16[5,16,256]{2,1,0:T(8,128)(2,1)S(1)} %get-tuple-element.35), channel_id=1, source_target_pairs={{0,1},{1,0},{2,3},{3,2},{4,5},{5,4},{6,7},{7,6},{8,9},{9,8},{10,11... | collective-permute-start | bytes 122888 | tf_op jit(solution)/shard_map/ppermute | solution.py:39
  5.6 0.1 collective-permute-start.2
  5.7 2.4 %load.1 = (f32[320,512]{1,0:T(8,128)S(1)}, bf16[512,256]{1,0:T(8,128)(2,1)S(1)}, bf16[512,256]{1,0:T(8,128)(2,1)S(1)}, bf16[256,256]{1,0:T(8,128)(2,1)S(1)}, bf1...) custom-call(s32[1]{0:T(128)} %bitcast.el_ref.refs_0_, ...), custom_call_target="tpu_custom_call" | custom-call | flops 7864320 | bytes 8290312 | tf_op jit(solution)/shard_map/load/pallas_call | solution.py:66
  8.1 0.0 collective-permute-done
  8.2 0.9 %collective-permute-done.1 = bf16[5,16,256]{2,1,0:T(8,128)(2,1)S(1)} collective-permute-done((bf16[5,16,256]{2,1,0:T(8,128)(2,1)S(1)}, bf16[5,16,256]{2,1,0:T(8,128)(2,1)S(1)}, u32[]{:S(2)}, u32[]{:S(2)}) %collective-permute-start.1) | collective-permute-done | bytes 40992 | tf_op jit(solution)/shard_map/ppermute | solution.py:39
  9.1 0.5 %collective-permute-done.2 = bf16[5,16,256]{2,1,0:T(8,128)(2,1)S(1)} collective-permute-done((bf16[5,16,256]{2,1,0:T(8,128)(2,1)S(1)}, bf16[5,16,256]{2,1,0:T(8,128)(2,1)S(1)}, u32[]{:S(2)}, u32[]{:S(2)}) %collective-permute-start.2) | collective-permute-done | bytes 40992 | tf_op jit(solution)/shard_map/ppermute | solution.py:39
  9.6 3.7 %collective-permute-start.3 = (bf16[64,256]{1,0:T(8,128)(2,1)S(1)}, bf16[64,256]{1,0:T(8,128)(2,1)S(1)}, u32[]{:S(2)}, u32[]{:S(2)}) collective-permute-start(bf16[64,256]{1,0:T(8,128)(2,1)S(1)} %pad_maximum_fusion.1), channel_id=1, source_target_pairs={{0,24},{4,28},{8,16},{12,20},{16,8},{20,12},{24,0},{28,4},{1,25},{... | collective-permute-start | bytes 98312 | tf_op jit(solution)/shard_map/ppermute | solution.py:39
  13.3 0.0 collective-permute-start.4
  13.3 0.1 collective-permute-start.5
  13.4 0.1 collective-permute-start.6
  13.5 0.5 %query.1 = (bf16[256,512]{1,0:T(8,128)(2,1)S(1)}, f32[512,1024]{1,0:T(8,128)S(1)}) custom-call(bf16[512,256]{1,0:T(8,128)(2,1)S(1)} %get-tuple-element.39.points_ref.refs_9_, bf16[512,256]{1,0:T(8,128)(2,1)S(1)} %get-tuple-element.40.skip_ref, bf16[256,256]{1,0:T(8,128)(2,1)S(1)} %get-tuple-element.41.w_query_ref, ...), custom_call_target="tpu_custom_call" | custom-call | flops 335544320 | bytes 3571712 | tf_op jit(solution)/shard_map/query/pallas_call | solution.py:66
  14.0 1.4 %collective-permute-done.3.refs_1_ = bf16[64,256]{1,0:T(8,128)(2,1)S(1)} collective-permute-done((bf16[64,256]{1,0:T(8,128)(2,1)S(1)}, bf16[64,256]{1,0:T(8,128)(2,1)S(1)}, u32[]{:S(2)}, u32[]{:S(2)}) %collective-permute-start.3) | collective-permute-done | bytes 32800 | tf_op jit(solution)/shard_map/ppermute | solution.py:39
  15.4 3.0 %collective-permute-done.4.refs_2_ = bf16[64,256]{1,0:T(8,128)(2,1)S(1)} collective-permute-done((bf16[64,256]{1,0:T(8,128)(2,1)S(1)}, bf16[64,256]{1,0:T(8,128)(2,1)S(1)}, u32[]{:S(2)}, u32[]{:S(2)}) %collective-permute-start.4) | collective-permute-done | bytes 32800 | tf_op jit(solution)/shard_map/ppermute | solution.py:39
  18.4 0.0 collective-permute-done.5.refs_3_
  18.4 0.0 collective-permute-done.6.refs_4_
  18.4 2.3 %ends.1 = (f32[2,128,256]{2,1,0:T(8,128)S(1)}, bf16[2,128,256]{2,1,0:T(8,128)(2,1)S(1)}, bf16[2,256]{1,0:T(2,128)(2,1)S(1)}, bf16[2,256]{1,0:T(2,128)(2,1)S(1)},...) custom-call(s32[1]{0:T(128)} %bitcast.1.az_ref.refs_1_, ...), custom_call_target="tpu_custom_call" | custom-call | flops 511705088 | bytes 5605380 | tf_op jit(solution)/shard_map/ends/pallas_call | solution.py:66
  20.7 0.1 collective-permute-start.7
  20.8 1.2 %collective-permute-start.8 = (bf16[2,256]{1,0:T(2,128)(2,1)S(1)}, bf16[2,256]{1,0:T(2,128)(2,1)S(1)}, u32[]{:S(2)}, u32[]{:S(2)}) collective-permute-start(bf16[2,256]{1,0:T(2,128)(2,1)S(1)} %get-tuple-element.50), channel_id=1, source_target_pairs={{0,28},{4,8},{8,4},{12,16},{16,12},{20,24},{24,20},{28,0},{1,29},{... | collective-permute-start | bytes 3080 | tf_op jit(solution)/shard_map/ppermute | solution.py:39
  22.0 2.1 %middle.1 = (f32[2,256,256]{2,1,0:T(8,128)S(1)}, bf16[272,256]{1,0:T(8,128)(2,1)S(1)}, bf16[272,256]{1,0:T(8,128)(2,1)S(1)}) custom-call(bf16[320,256]{1,0:T(8,128)(2,1)S(1)} %get-tuple-element.51.keys_ref, bf16[256,320]{1,0:T(8,128)(2,1)S(1)} %get-tuple-element.52.values_ref, f32[2,128,256]{2,1,0:T(8,128)S(1)} %get-tuple-element.53.joined_ends_ref, ...), custom_call_target="tpu_custom_call" | custom-call | flops 511705088 | bytes 5980160 | tf_op jit(solution)/shard_map/middle/pallas_call | solution.py:66
  24.1 0.0 collective-permute-done.7.inner_ref
  24.1 1.5 %collective-permute-done.8.outer_ref = bf16[2,256]{1,0:T(2,128)(2,1)S(1)} collective-permute-done((bf16[2,256]{1,0:T(2,128)(2,1)S(1)}, bf16[2,256]{1,0:T(2,128)(2,1)S(1)}, u32[]{:S(2)}, u32[]{:S(2)}) %collective-permute-start.8) | collective-permute-done | bytes 1056 | tf_op jit(solution)/shard_map/ppermute | solution.py:39
  25.7 1.6 %collective-permute-start.9 = (bf16[272,256]{1,0:T(8,128)(2,1)S(1)}, bf16[272,256]{1,0:T(8,128)(2,1)S(1)}, u32[]{:S(2)}, u32[]{:S(2)}) collective-permute-start(bf16[272,256]{1,0:T(8,128)(2,1)S(1)} %get-tuple-element.57.near_ref), channel_id=1, source_target_pairs={{0,1},{1,0},{2,3},{3,2},{4,5},{5,4},{6,7},{7,6},{8,9},{9,8},{10,11... | collective-permute-start | bytes 417800 | tf_op jit(solution)/shard_map/ppermute | solution.py:39
  27.2 0.5 %collective-permute-start.10 = (bf16[272,256]{1,0:T(8,128)(2,1)S(1)}, bf16[272,256]{1,0:T(8,128)(2,1)S(1)}, u32[]{:S(2)}, u32[]{:S(2)}) collective-permute-start(bf16[272,256]{1,0:T(8,128)(2,1)S(1)} %get-tuple-element.58.far_ref), channel_id=1, source_target_pairs={{0,3},{1,2},{2,1},{3,0},{4,7},{5,6},{6,5},{7,4},{8,11},{9,10},{10,... | collective-permute-start | bytes 417800 | tf_op jit(solution)/shard_map/ppermute | solution.py:39
  27.7 0.6 %inside.1.part_ref = f32[2,256,256]{2,1,0:T(8,128)S(1)} custom-call(s32[1]{0:T(128)} %bitcast.el_ref.refs_0_, bf16[272,256]{1,0:T(8,128)(2,1)S(1)} %get-tuple-element.57.near_ref, bf16[272,256]{1,0:T(8,128)(2,1)S(1)} %get-tuple-element.58.far_ref, f32[2,256,256]{2,1,0:T(8,128)S(1)} %get-tuple-element.59.joined_ref, ...), custom_call_target="tpu_custom_call" | custom-call | flops 402653184 | bytes 2506756 | tf_op jit(solution)/shard_map/inside/pallas_call | solution.py:66
  28.3 3.1 %collective-permute-done.9.near_ref = bf16[272,256]{1,0:T(8,128)(2,1)S(1)} collective-permute-done((bf16[272,256]{1,0:T(8,128)(2,1)S(1)}, bf16[272,256]{1,0:T(8,128)(2,1)S(1)}, u32[]{:S(2)}, u32[]{:S(2)}) %collective-permute-start.9) | collective-permute-done | bytes 139296 | tf_op jit(solution)/shard_map/ppermute | solution.py:39
  31.4 0.3 near_border.1.near_ref
  31.7 1.8 %collective-permute-done.10.far_ref = bf16[272,256]{1,0:T(8,128)(2,1)S(1)} collective-permute-done((bf16[272,256]{1,0:T(8,128)(2,1)S(1)}, bf16[272,256]{1,0:T(8,128)(2,1)S(1)}, u32[]{:S(2)}, u32[]{:S(2)}) %collective-permute-start.10) | collective-permute-done | bytes 139296 | tf_op jit(solution)/shard_map/ppermute | solution.py:39
  33.6 1.0 %far_border.1 = bf16[2,256,256]{2,1,0:T(8,128)(2,1)} custom-call(s32[1]{0:T(128)} %bitcast.el_ref.refs_0_, bf16[256,256]{1,0:T(8,128)(2,1)S(1)} %near_border.1.near_ref, bf16[272,256]{1,0:T(8,128)(2,1)S(1)} %collective-permute-done.10.far_ref, f32[2,256,256]{2,1,0:T(8,128)S(1)} %inside.1.part_ref, bf16[9,256,256]{2,1,0:T(8,128)(2,1)S(1)} %get-tuple-element.60.w_ref), custom_call_target="tpu_custom_call" | custom-call | flops 100663296 | bytes 2236420 | tf_op jit(solution)/shard_map/far_border/pallas_call | solution.py:66
  (10 shorter events, 0.1 us)
Async XLA Ops:
  1.1 7.0 %collective-permute-start = (bf16[5,16,256]{2,1,0:T(8,128)(2,1)S(1)}, bf16[5,16,256]{2,1,0:T(8,128)(2,1)S(1)}, u32[]{:S(2)}, u32[]{:S(2)}) collective-permute-start(bf16[5,16,256]{2,1,0:T(8,128)(2,1)S(1)} %get-tuple-element.34), channel_id=1, source_target_pairs={{0,3},{1,2},{2,1},{3,0},{4,7},{5,6},{6,5},{7,4},{8,11},{9,10},{10,... | collective-permute-start | bytes 122888 | tf_op jit(solution)/shard_map/ppermute | solution.py:39
  5.1 4.0 %collective-permute-start.1 = (bf16[5,16,256]{2,1,0:T(8,128)(2,1)S(1)}, bf16[5,16,256]{2,1,0:T(8,128)(2,1)S(1)}, u32[]{:S(2)}, u32[]{:S(2)}) collective-permute-start(bf16[5,16,256]{2,1,0:T(8,128)(2,1)S(1)} %get-tuple-element.35), channel_id=1, source_target_pairs={{0,1},{1,0},{2,3},{3,2},{4,5},{5,4},{6,7},{7,6},{8,9},{9,8},{10,11... | collective-permute-start | bytes 122888 | tf_op jit(solution)/shard_map/ppermute | solution.py:39
  5.6 4.0 %collective-permute-start.2 = (bf16[5,16,256]{2,1,0:T(8,128)(2,1)S(1)}, bf16[5,16,256]{2,1,0:T(8,128)(2,1)S(1)}, u32[]{:S(2)}, u32[]{:S(2)}) collective-permute-start(bf16[5,16,256]{2,1,0:T(8,128)(2,1)S(1)} %get-tuple-element.36), channel_id=1, source_target_pairs={{0,2},{1,3},{2,0},{3,1},{4,6},{5,7},{6,4},{7,5},{8,10},{9,11},{10,... | collective-permute-start | bytes 122888 | tf_op jit(solution)/shard_map/ppermute | solution.py:39
  9.6 5.8 %collective-permute-start.3 = (bf16[64,256]{1,0:T(8,128)(2,1)S(1)}, bf16[64,256]{1,0:T(8,128)(2,1)S(1)}, u32[]{:S(2)}, u32[]{:S(2)}) collective-permute-start(bf16[64,256]{1,0:T(8,128)(2,1)S(1)} %pad_maximum_fusion.1), channel_id=1, source_target_pairs={{0,24},{4,28},{8,16},{12,20},{16,8},{20,12},{24,0},{28,4},{1,25},{... | collective-permute-start | bytes 98312 | tf_op jit(solution)/shard_map/ppermute | solution.py:39
  13.3 5.1 %collective-permute-start.4 = (bf16[64,256]{1,0:T(8,128)(2,1)S(1)}, bf16[64,256]{1,0:T(8,128)(2,1)S(1)}, u32[]{:S(2)}, u32[]{:S(2)}) collective-permute-start(bf16[64,256]{1,0:T(8,128)(2,1)S(1)} %pad_maximum_fusion.2), channel_id=1, source_target_pairs={{0,28},{4,8},{8,4},{12,16},{16,12},{20,24},{24,20},{28,0},{1,29},{... | collective-permute-start | bytes 98312 | tf_op jit(solution)/shard_map/ppermute | solution.py:39
  13.3 5.1 %collective-permute-start.5 = (bf16[64,256]{1,0:T(8,128)(2,1)S(1)}, bf16[64,256]{1,0:T(8,128)(2,1)S(1)}, u32[]{:S(2)}, u32[]{:S(2)}) collective-permute-start(bf16[64,256]{1,0:T(8,128)(2,1)S(1)} %pad_maximum_fusion.3), channel_id=1, source_target_pairs={{0,8},{4,12},{8,0},{12,4},{16,24},{20,28},{24,16},{28,20},{1,9},{5... | collective-permute-start | bytes 98312 | tf_op jit(solution)/shard_map/ppermute | solution.py:39
  13.4 5.0 %collective-permute-start.6 = (bf16[64,256]{1,0:T(8,128)(2,1)S(1)}, bf16[64,256]{1,0:T(8,128)(2,1)S(1)}, u32[]{:S(2)}, u32[]{:S(2)}) collective-permute-start(bf16[64,256]{1,0:T(8,128)(2,1)S(1)} %pad_maximum_fusion.4), channel_id=1, source_target_pairs={{0,4},{4,0},{8,12},{12,8},{16,20},{20,16},{24,28},{28,24},{1,5},{5... | collective-permute-start | bytes 98312 | tf_op jit(solution)/shard_map/ppermute | solution.py:39
  20.7 3.4 %collective-permute-start.7 = (bf16[2,256]{1,0:T(2,128)(2,1)S(1)}, bf16[2,256]{1,0:T(2,128)(2,1)S(1)}, u32[]{:S(2)}, u32[]{:S(2)}) collective-permute-start(bf16[2,256]{1,0:T(2,128)(2,1)S(1)} %get-tuple-element.49), channel_id=1, source_target_pairs={{0,4},{4,0},{8,12},{12,8},{16,20},{20,16},{24,28},{28,24},{1,5},{5... | collective-permute-start | bytes 3080 | tf_op jit(solution)/shard_map/ppermute | solution.py:39
  20.8 4.9 %collective-permute-start.8 = (bf16[2,256]{1,0:T(2,128)(2,1)S(1)}, bf16[2,256]{1,0:T(2,128)(2,1)S(1)}, u32[]{:S(2)}, u32[]{:S(2)}) collective-permute-start(bf16[2,256]{1,0:T(2,128)(2,1)S(1)} %get-tuple-element.50), channel_id=1, source_target_pairs={{0,28},{4,8},{8,4},{12,16},{16,12},{20,24},{24,20},{28,0},{1,29},{... | collective-permute-start | bytes 3080 | tf_op jit(solution)/shard_map/ppermute | solution.py:39
  25.7 5.8 %collective-permute-start.9 = (bf16[272,256]{1,0:T(8,128)(2,1)S(1)}, bf16[272,256]{1,0:T(8,128)(2,1)S(1)}, u32[]{:S(2)}, u32[]{:S(2)}) collective-permute-start(bf16[272,256]{1,0:T(8,128)(2,1)S(1)} %get-tuple-element.57.near_ref), channel_id=1, source_target_pairs={{0,1},{1,0},{2,3},{3,2},{4,5},{5,4},{6,7},{7,6},{8,9},{9,8},{10,11... | collective-permute-start | bytes 417800 | tf_op jit(solution)/shard_map/ppermute | solution.py:39
  27.2 6.3 %collective-permute-start.10 = (bf16[272,256]{1,0:T(8,128)(2,1)S(1)}, bf16[272,256]{1,0:T(8,128)(2,1)S(1)}, u32[]{:S(2)}, u32[]{:S(2)}) collective-permute-start(bf16[272,256]{1,0:T(8,128)(2,1)S(1)} %get-tuple-element.58.far_ref), channel_id=1, source_target_pairs={{0,3},{1,2},{2,1},{3,0},{4,7},{5,6},{6,5},{7,4},{8,11},{9,10},{10,... | collective-permute-start | bytes 417800 | tf_op jit(solution)/shard_map/ppermute | solution.py:39

commit v12 on v11

--- a/solution.py
+++ b/solution.py
@@ -37,6 +37,19 @@
 def swap(x, axis, partner):
     n = lax.axis_size(axis)
     return lax.ppermute(x, axis, [(i, partner(i, n)) for i in range(n)])
+
+
+def swap_inner(x):
+    columns, count = lax.axis_size("az"), lax.axis_size("el")
+    pairs = []
+    for az in range(columns):
+        for el in range(count):
+            if el in (0, count - 1):
+                to = same_chip(az, columns) * count + el
+            else:
+                to = az * count + next_chip(el, count)
+            pairs.append((az * count + el, to))
+    return lax.ppermute(x, ("az", "el"), pairs)
 
 
 def sent_offset(az, piece):
@@ -469,7 +482,7 @@
         (),
         {3: 0, 4: 1},
     )
-    far_got = swap(far, "el", next_chip)
+    far_got = swap_inner(far)
     near_got = swap(near, "el", same_chip)
     (partial,) = call(
         inside_body,

time: 34.8 us -> 33 us (0.948)
  the two profiles are of different devices: /device:TPU:0 before, /device:TPU:2 now
where the time goes in v12:
time: 33 us; the launch traced here: 32.4 us
  waiting for transfers between devices  11.3 us (34%)
  starting transfers between devices  10.7 us (32%)
  Pallas kernels  10.2 us (31%)
    pallas_call x9, Pallas kernels, call(): pl.pallas_call(body, out_shape=outs, in_specs=[pl.BlockSpec(memory_space=...  10.2 us
    ppermute x10, waiting for transfers between devices, swap(): return lax.ppermute(x, axis, [(i, partner(i, n)) for i in range(n)])  9.48 us
    ppermute x10, starting transfers between devices, swap(): return lax.ppermute(x, axis, [(i, partner(i, n)) for i in range(n)])  9.27 us
    ppermute x1, waiting for transfers between devices, swap_inner(): return lax.ppermute(x, ('az', 'el'), pairs)  1.8 us
    ppermute x1, starting transfers between devices, swap_inner(): return lax.ppermute(x, ('az', 'el'), pairs)  1.43 us
  transfers between devices with their start and end apart: 11, of which 6 were waited for; matrix products, arithmetic and copies ran while one was open for 0% of the time, Pallas kernels for 18%

profile of v12, /device:TPU:2, one launch (start us, length us, event | category | flops | bytes accessed | tf_op | source)
XLA Modules:
  0.0 32.4 jit_solution(2995403812535233178)
XLA Ops:
  0.0 1.1 %gather.1 = (bf16[5,16,256]{2,1,0:T(8,128)(2,1)S(1)}, bf16[5,16,256]{2,1,0:T(8,128)(2,1)S(1)}, bf16[5,16,256]{2,1,0:T(8,128)(2,1)S(1)}, bf16[5,16,256]{2,1,0:T(8,128)(2,1)S(1)}) custom-call(s32[1]{0:T(128)} %bitcast.el_ref.refs_0_, s32[1]{0:T(128)} %bitcast.1.az_ref.refs_1_, bf16[128,256]{1,0:T(8,128)(2,1)} %bitcast.46, s32[5,4,16]{2,1,0:T(4,128)} %bitcast.47), custom_call_target="tpu_custom_call" | custom-call | flops 20971520 | bytes 230664 | tf_op jit(solution)/shard_map/gather/pallas_call | solution.py:79
  1.1 1.6 %collective-permute-start = (bf16[5,16,256]{2,1,0:T(8,128)(2,1)S(1)}, bf16[5,16,256]{2,1,0:T(8,128)(2,1)S(1)}, u32[]{:S(2)}, u32[]{:S(2)}) collective-permute-start(bf16[5,16,256]{2,1,0:T(8,128)(2,1)S(1)} %get-tuple-element.34), channel_id=1, source_target_pairs={{0,3},{1,2},{2,1},{3,0},{4,7},{5,6},{6,5},{7,4},{8,11},{9,10},{10,... | collective-permute-start | bytes 122888 | tf_op jit(solution)/shard_map/ppermute | solution.py:39
  2.7 1.5 %collective-permute-start.1 = (bf16[5,16,256]{2,1,0:T(8,128)(2,1)S(1)}, bf16[5,16,256]{2,1,0:T(8,128)(2,1)S(1)}, u32[]{:S(2)}, u32[]{:S(2)}) collective-permute-start(bf16[5,16,256]{2,1,0:T(8,128)(2,1)S(1)} %get-tuple-element.35), channel_id=1, source_target_pairs={{0,1},{1,0},{2,3},{3,2},{4,5},{5,4},{6,7},{7,6},{8,9},{9,8},{10,11... | collective-permute-start | bytes 122888 | tf_op jit(solution)/shard_map/ppermute | solution.py:39
  4.2 0.5 %collective-permute-start.2 = (bf16[5,16,256]{2,1,0:T(8,128)(2,1)S(1)}, bf16[5,16,256]{2,1,0:T(8,128)(2,1)S(1)}, u32[]{:S(2)}, u32[]{:S(2)}) collective-permute-start(bf16[5,16,256]{2,1,0:T(8,128)(2,1)S(1)} %get-tuple-element.36), channel_id=1, source_target_pairs={{0,2},{1,3},{2,0},{3,1},{4,6},{5,7},{6,4},{7,5},{8,10},{9,11},{10,... | collective-permute-start | bytes 122888 | tf_op jit(solution)/shard_map/ppermute | solution.py:39
  4.7 2.4 %load.1 = (f32[320,512]{1,0:T(8,128)S(1)}, bf16[512,256]{1,0:T(8,128)(2,1)S(1)}, bf16[512,256]{1,0:T(8,128)(2,1)S(1)}, bf16[256,256]{1,0:T(8,128)(2,1)S(1)}, bf1...) custom-call(s32[1]{0:T(128)} %bitcast.el_ref.refs_0_, ...), custom_call_target="tpu_custom_call" | custom-call | flops 7864320 | bytes 8290312 | tf_op jit(solution)/shard_map/load/pallas_call | solution.py:79
  7.1 0.0 collective-permute-done
  7.1 0.0 collective-permute-done.1
  7.1 1.0 %collective-permute-done.2 = bf16[5,16,256]{2,1,0:T(8,128)(2,1)S(1)} collective-permute-done((bf16[5,16,256]{2,1,0:T(8,128)(2,1)S(1)}, bf16[5,16,256]{2,1,0:T(8,128)(2,1)S(1)}, u32[]{:S(2)}, u32[]{:S(2)}) %collective-permute-start.2) | collective-permute-done | bytes 40992 | tf_op jit(solution)/shard_map/ppermute | solution.py:39
  8.2 3.7 %collective-permute-start.3 = (bf16[64,256]{1,0:T(8,128)(2,1)S(1)}, bf16[64,256]{1,0:T(8,128)(2,1)S(1)}, u32[]{:S(2)}, u32[]{:S(2)}) collective-permute-start(bf16[64,256]{1,0:T(8,128)(2,1)S(1)} %pad_maximum_fusion.1), channel_id=1, source_target_pairs={{0,24},{4,28},{8,16},{12,20},{16,8},{20,12},{24,0},{28,4},{1,25},{... | collective-permute-start | bytes 98312 | tf_op jit(solution)/shard_map/ppermute | solution.py:39
  11.9 0.0 collective-permute-start.4
  11.9 0.1 collective-permute-start.5
  12.0 0.1 collective-permute-start.6
  12.0 0.5 %query.1 = (bf16[256,512]{1,0:T(8,128)(2,1)S(1)}, f32[512,1024]{1,0:T(8,128)S(1)}) custom-call(bf16[512,256]{1,0:T(8,128)(2,1)S(1)} %get-tuple-element.39.points_ref.refs_9_, bf16[512,256]{1,0:T(8,128)(2,1)S(1)} %get-tuple-element.40.skip_ref, bf16[256,256]{1,0:T(8,128)(2,1)S(1)} %get-tuple-element.41.w_query_ref, ...), custom_call_target="tpu_custom_call" | custom-call | flops 335544320 | bytes 3571712 | tf_op jit(solution)/shard_map/query/pallas_call | solution.py:79
  12.6 1.4 %collective-permute-done.3.refs_1_ = bf16[64,256]{1,0:T(8,128)(2,1)S(1)} collective-permute-done((bf16[64,256]{1,0:T(8,128)(2,1)S(1)}, bf16[64,256]{1,0:T(8,128)(2,1)S(1)}, u32[]{:S(2)}, u32[]{:S(2)}) %collective-permute-start.3) | collective-permute-done | bytes 32800 | tf_op jit(solution)/shard_map/ppermute | solution.py:39
  14.0 3.0 %collective-permute-done.4.refs_2_ = bf16[64,256]{1,0:T(8,128)(2,1)S(1)} collective-permute-done((bf16[64,256]{1,0:T(8,128)(2,1)S(1)}, bf16[64,256]{1,0:T(8,128)(2,1)S(1)}, u32[]{:S(2)}, u32[]{:S(2)}) %collective-permute-start.4) | collective-permute-done | bytes 32800 | tf_op jit(solution)/shard_map/ppermute | solution.py:39
  17.0 0.0 collective-permute-done.5.refs_3_
  17.0 0.0 collective-permute-done.6.refs_4_
  17.0 2.3 %ends.1 = (f32[2,128,256]{2,1,0:T(8,128)S(1)}, bf16[2,128,256]{2,1,0:T(8,128)(2,1)S(1)}, bf16[2,256]{1,0:T(2,128)(2,1)S(1)}, bf16[2,256]{1,0:T(2,128)(2,1)S(1)},...) custom-call(s32[1]{0:T(128)} %bitcast.1.az_ref.refs_1_, ...), custom_call_target="tpu_custom_call" | custom-call | flops 511705088 | bytes 5605380 | tf_op jit(solution)/shard_map/ends/pallas_call | solution.py:79
  19.3 0.1 collective-permute-start.7
  19.4 1.2 %collective-permute-start.8 = (bf16[2,256]{1,0:T(2,128)(2,1)S(1)}, bf16[2,256]{1,0:T(2,128)(2,1)S(1)}, u32[]{:S(2)}, u32[]{:S(2)}) collective-permute-start(bf16[2,256]{1,0:T(2,128)(2,1)S(1)} %get-tuple-element.50), channel_id=1, source_target_pairs={{0,28},{4,8},{8,4},{12,16},{16,12},{20,24},{24,20},{28,0},{1,29},{... | collective-permute-start | bytes 3080 | tf_op jit(solution)/shard_map/ppermute | solution.py:39
  20.6 2.1 %middle.1 = (f32[2,256,256]{2,1,0:T(8,128)S(1)}, bf16[272,256]{1,0:T(8,128)(2,1)S(1)}, bf16[272,256]{1,0:T(8,128)(2,1)S(1)}) custom-call(bf16[320,256]{1,0:T(8,128)(2,1)S(1)} %get-tuple-element.51.keys_ref, bf16[256,320]{1,0:T(8,128)(2,1)S(1)} %get-tuple-element.52.values_ref, f32[2,128,256]{2,1,0:T(8,128)S(1)} %get-tuple-element.53.joined_ends_ref, ...), custom_call_target="tpu_custom_call" | custom-call | flops 511705088 | bytes 5980160 | tf_op jit(solution)/shard_map/middle/pallas_call | solution.py:79
  22.7 0.0 collective-permute-done.7.inner_ref
  22.7 1.5 %collective-permute-done.8.outer_ref = bf16[2,256]{1,0:T(2,128)(2,1)S(1)} collective-permute-done((bf16[2,256]{1,0:T(2,128)(2,1)S(1)}, bf16[2,256]{1,0:T(2,128)(2,1)S(1)}, u32[]{:S(2)}, u32[]{:S(2)}) %collective-permute-start.8) | collective-permute-done | bytes 1056 | tf_op jit(solution)/shard_map/ppermute | solution.py:39
  24.2 0.6 %collective-permute-start.9 = (bf16[272,256]{1,0:T(8,128)(2,1)S(1)}, bf16[272,256]{1,0:T(8,128)(2,1)S(1)}, u32[]{:S(2)}, u32[]{:S(2)}) collective-permute-start(bf16[272,256]{1,0:T(8,128)(2,1)S(1)} %get-tuple-element.57.near_ref), channel_id=1, source_target_pairs={{0,1},{1,0},{2,3},{3,2},{4,5},{5,4},{6,7},{7,6},{8,9},{9,8},{10,11... | collective-permute-start | bytes 417800 | tf_op jit(solution)/shard_map/ppermute | solution.py:39
  24.8 1.4 %collective-permute-start.10 = (bf16[272,256]{1,0:T(8,128)(2,1)S(1)}, bf16[272,256]{1,0:T(8,128)(2,1)S(1)}, u32[]{:S(2)}, u32[]{:S(2)}) collective-permute-start(bf16[272,256]{1,0:T(8,128)(2,1)S(1)} %get-tuple-element.58.far_ref), channel_id=1, source_target_pairs={{0,4},{1,2},{2,1},{3,7},{4,0},{5,6},{6,5},{7,3},{8,12},{9,10},{10,... | collective-permute-start | bytes 417800 | tf_op jit(solution)/shard_map/ppermute | solution.py:52
  26.3 0.6 %inside.1.part_ref = f32[2,256,256]{2,1,0:T(8,128)S(1)} custom-call(s32[1]{0:T(128)} %bitcast.el_ref.refs_0_, bf16[272,256]{1,0:T(8,128)(2,1)S(1)} %get-tuple-element.57.near_ref, bf16[272,256]{1,0:T(8,128)(2,1)S(1)} %get-tuple-element.58.far_ref, f32[2,256,256]{2,1,0:T(8,128)S(1)} %get-tuple-element.59.joined_ref, ...), custom_call_target="tpu_custom_call" | custom-call | flops 402653184 | bytes 2506756 | tf_op jit(solution)/shard_map/inside/pallas_call | solution.py:79
  26.9 2.5 %collective-permute-done.9.near_ref = bf16[272,256]{1,0:T(8,128)(2,1)S(1)} collective-permute-done((bf16[272,256]{1,0:T(8,128)(2,1)S(1)}, bf16[272,256]{1,0:T(8,128)(2,1)S(1)}, u32[]{:S(2)}, u32[]{:S(2)}) %collective-permute-start.9) | collective-permute-done | bytes 139296 | tf_op jit(solution)/shard_map/ppermute | solution.py:39
  29.4 0.3 near_border.1.near_ref
  29.6 1.8 %collective-permute-done.10.far_ref = bf16[272,256]{1,0:T(8,128)(2,1)S(1)} collective-permute-done((bf16[272,256]{1,0:T(8,128)(2,1)S(1)}, bf16[272,256]{1,0:T(8,128)(2,1)S(1)}, u32[]{:S(2)}, u32[]{:S(2)}) %collective-permute-start.10) | collective-permute-done | bytes 139296 | tf_op jit(solution)/shard_map/ppermute | solution.py:52
  31.4 1.0 %far_border.1 = bf16[2,256,256]{2,1,0:T(8,128)(2,1)} custom-call(s32[1]{0:T(128)} %bitcast.el_ref.refs_0_, bf16[256,256]{1,0:T(8,128)(2,1)S(1)} %near_border.1.near_ref, bf16[272,256]{1,0:T(8,128)(2,1)S(1)} %collective-permute-done.10.far_ref, f32[2,256,256]{2,1,0:T(8,128)S(1)} %inside.1.part_ref, bf16[9,256,256]{2,1,0:T(8,128)(2,1)S(1)} %get-tuple-element.60.w_ref), custom_call_target="tpu_custom_call" | custom-call | flops 100663296 | bytes 2236420 | tf_op jit(solution)/shard_map/far_border/pallas_call | solution.py:79
  (10 shorter events, 0.1 us)
Async XLA Ops:
  1.1 6.0 %collective-permute-start = (bf16[5,16,256]{2,1,0:T(8,128)(2,1)S(1)}, bf16[5,16,256]{2,1,0:T(8,128)(2,1)S(1)}, u32[]{:S(2)}, u32[]{:S(2)}) collective-permute-start(bf16[5,16,256]{2,1,0:T(8,128)(2,1)S(1)} %get-tuple-element.34), channel_id=1, source_target_pairs={{0,3},{1,2},{2,1},{3,0},{4,7},{5,6},{6,5},{7,4},{8,11},{9,10},{10,... | collective-permute-start | bytes 122888 | tf_op jit(solution)/shard_map/ppermute | solution.py:39
  2.7 4.4 %collective-permute-start.1 = (bf16[5,16,256]{2,1,0:T(8,128)(2,1)S(1)}, bf16[5,16,256]{2,1,0:T(8,128)(2,1)S(1)}, u32[]{:S(2)}, u32[]{:S(2)}) collective-permute-start(bf16[5,16,256]{2,1,0:T(8,128)(2,1)S(1)} %get-tuple-element.35), channel_id=1, source_target_pairs={{0,1},{1,0},{2,3},{3,2},{4,5},{5,4},{6,7},{7,6},{8,9},{9,8},{10,11... | collective-permute-start | bytes 122888 | tf_op jit(solution)/shard_map/ppermute | solution.py:39
  4.2 4.0 %collective-permute-start.2 = (bf16[5,16,256]{2,1,0:T(8,128)(2,1)S(1)}, bf16[5,16,256]{2,1,0:T(8,128)(2,1)S(1)}, u32[]{:S(2)}, u32[]{:S(2)}) collective-permute-start(bf16[5,16,256]{2,1,0:T(8,128)(2,1)S(1)} %get-tuple-element.36), channel_id=1, source_target_pairs={{0,2},{1,3},{2,0},{3,1},{4,6},{5,7},{6,4},{7,5},{8,10},{9,11},{10,... | collective-permute-start | bytes 122888 | tf_op jit(solution)/shard_map/ppermute | solution.py:39
  8.2 5.8 %collective-permute-start.3 = (bf16[64,256]{1,0:T(8,128)(2,1)S(1)}, bf16[64,256]{1,0:T(8,128)(2,1)S(1)}, u32[]{:S(2)}, u32[]{:S(2)}) collective-permute-start(bf16[64,256]{1,0:T(8,128)(2,1)S(1)} %pad_maximum_fusion.1), channel_id=1, source_target_pairs={{0,24},{4,28},{8,16},{12,20},{16,8},{20,12},{24,0},{28,4},{1,25},{... | collective-permute-start | bytes 98312 | tf_op jit(solution)/shard_map/ppermute | solution.py:39
  11.9 5.1 %collective-permute-start.4 = (bf16[64,256]{1,0:T(8,128)(2,1)S(1)}, bf16[64,256]{1,0:T(8,128)(2,1)S(1)}, u32[]{:S(2)}, u32[]{:S(2)}) collective-permute-start(bf16[64,256]{1,0:T(8,128)(2,1)S(1)} %pad_maximum_fusion.2), channel_id=1, source_target_pairs={{0,28},{4,8},{8,4},{12,16},{16,12},{20,24},{24,20},{28,0},{1,29},{... | collective-permute-start | bytes 98312 | tf_op jit(solution)/shard_map/ppermute | solution.py:39
  11.9 5.1 %collective-permute-start.5 = (bf16[64,256]{1,0:T(8,128)(2,1)S(1)}, bf16[64,256]{1,0:T(8,128)(2,1)S(1)}, u32[]{:S(2)}, u32[]{:S(2)}) collective-permute-start(bf16[64,256]{1,0:T(8,128)(2,1)S(1)} %pad_maximum_fusion.3), channel_id=1, source_target_pairs={{0,8},{4,12},{8,0},{12,4},{16,24},{20,28},{24,16},{28,20},{1,9},{5... | collective-permute-start | bytes 98312 | tf_op jit(solution)/shard_map/ppermute | solution.py:39
  12.0 5.0 %collective-permute-start.6 = (bf16[64,256]{1,0:T(8,128)(2,1)S(1)}, bf16[64,256]{1,0:T(8,128)(2,1)S(1)}, u32[]{:S(2)}, u32[]{:S(2)}) collective-permute-start(bf16[64,256]{1,0:T(8,128)(2,1)S(1)} %pad_maximum_fusion.4), channel_id=1, source_target_pairs={{0,4},{4,0},{8,12},{12,8},{16,20},{20,16},{24,28},{28,24},{1,5},{5... | collective-permute-start | bytes 98312 | tf_op jit(solution)/shard_map/ppermute | solution.py:39
  19.3 3.4 %collective-permute-start.7 = (bf16[2,256]{1,0:T(2,128)(2,1)S(1)}, bf16[2,256]{1,0:T(2,128)(2,1)S(1)}, u32[]{:S(2)}, u32[]{:S(2)}) collective-permute-start(bf16[2,256]{1,0:T(2,128)(2,1)S(1)} %get-tuple-element.49), channel_id=1, source_target_pairs={{0,4},{4,0},{8,12},{12,8},{16,20},{20,16},{24,28},{28,24},{1,5},{5... | collective-permute-start | bytes 3080 | tf_op jit(solution)/shard_map/ppermute | solution.py:39
  19.4 4.9 %collective-permute-start.8 = (bf16[2,256]{1,0:T(2,128)(2,1)S(1)}, bf16[2,256]{1,0:T(2,128)(2,1)S(1)}, u32[]{:S(2)}, u32[]{:S(2)}) collective-permute-start(bf16[2,256]{1,0:T(2,128)(2,1)S(1)} %get-tuple-element.50), channel_id=1, source_target_pairs={{0,28},{4,8},{8,4},{12,16},{16,12},{20,24},{24,20},{28,0},{1,29},{... | collective-permute-start | bytes 3080 | tf_op jit(solution)/shard_map/ppermute | solution.py:39
  24.2 5.1 %collective-permute-start.9 = (bf16[272,256]{1,0:T(8,128)(2,1)S(1)}, bf16[272,256]{1,0:T(8,128)(2,1)S(1)}, u32[]{:S(2)}, u32[]{:S(2)}) collective-permute-start(bf16[272,256]{1,0:T(8,128)(2,1)S(1)} %get-tuple-element.57.near_ref), channel_id=1, source_target_pairs={{0,1},{1,0},{2,3},{3,2},{4,5},{5,4},{6,7},{7,6},{8,9},{9,8},{10,11... | collective-permute-start | bytes 417800 | tf_op jit(solution)/shard_map/ppermute | solution.py:39
  24.8 6.6 %collective-permute-start.10 = (bf16[272,256]{1,0:T(8,128)(2,1)S(1)}, bf16[272,256]{1,0:T(8,128)(2,1)S(1)}, u32[]{:S(2)}, u32[]{:S(2)}) collective-permute-start(bf16[272,256]{1,0:T(8,128)(2,1)S(1)} %get-tuple-element.58.far_ref), channel_id=1, source_target_pairs={{0,4},{1,2},{2,1},{3,7},{4,0},{5,6},{6,5},{7,3},{8,12},{9,10},{10,... | collective-permute-start | bytes 417800 | tf_op jit(solution)/shard_map/ppermute | solution.py:52

commit v13 on v12

--- a/solution.py
+++ b/solution.py
@@ -54,10 +54,10 @@
 
 def sent_offset(az, piece):
     odd, odd_chip = lax.rem(az, 2), lax.rem(lax.div(az, 2), 2)
-    return (REACH, 4 * odd_chip, 1 + 2 * odd, 4 - 4 * odd_chip, 3 - 2 * odd)[piece]
-
-
-MATCHES = (None, two_back, next_chip, two_on, same_chip)
+    return (REACH, 1 + 2 * odd, 4 * odd_chip, 4 - 4 * odd_chip, 3 - 2 * odd)[piece]
+
+
+MATCHES = (None, next_chip, two_back, two_on, same_chip)
 
 
 def dot(a, b, contract=((1,), (0,))):

time: 33 us -> 31.9 us (0.967)
  waiting for transfers between devices: 11.3 us -> 8.89 us
  starting transfers between devices: 10.7 us -> 12.4 us
    ppermute x10, waiting for transfers between devices: 9.48 us -> 6.87 us  [swap(): return lax.ppermute(x, axis, [(i, partner(i, n)) for i in range(n)])]
    ppermute x10, starting transfers between devices: 9.27 us -> 10.6 us  [swap(): return lax.ppermute(x, axis, [(i, partner(i, n)) for i in range(n)])]
  transfers between devices with their start and end apart: 11 -> 11, of which waited for: 6 -> 7; matrix products, arithmetic and copies ran while one was open for 0% -> 0% of each run, Pallas kernels for 18% -> 19%
where the time goes in v13:
time: 31.9 us; the launch traced here: 31.6 us
  starting transfers between devices  12.4 us (39%)
  Pallas kernels  10.2 us (32%)
  waiting for transfers between devices  8.89 us (28%)
    ppermute x10, starting transfers between devices, swap(): return lax.ppermute(x, axis, [(i, partner(i, n)) for i in range(n)])  10.6 us
    pallas_call x9, Pallas kernels, call(): pl.pallas_call(body, out_shape=outs, in_specs=[pl.BlockSpec(memory_space=...  10.2 us
    ppermute x10, waiting for transfers between devices, swap(): return lax.ppermute(x, axis, [(i, partner(i, n)) for i in range(n)])  6.87 us
    ppermute x1, waiting for transfers between devices, swap_inner(): return lax.ppermute(x, ('az', 'el'), pairs)  2.02 us
    ppermute x1, starting transfers between devices, swap_inner(): return lax.ppermute(x, ('az', 'el'), pairs)  1.72 us
  transfers between devices with their start and end apart: 11, of which 7 were waited for; matrix products, arithmetic and copies ran while one was open for 0% of the time, Pallas kernels for 19%

profile of v13, /device:TPU:2, one launch (start us, length us, event | category | flops | bytes accessed | tf_op | source)
XLA Modules:
  0.0 31.6 jit_solution(9490216247656460207)
XLA Ops:
  0.0 1.1 %gather.1 = (bf16[5,16,256]{2,1,0:T(8,128)(2,1)S(1)}, bf16[5,16,256]{2,1,0:T(8,128)(2,1)S(1)}, bf16[5,16,256]{2,1,0:T(8,128)(2,1)S(1)}, bf16[5,16,256]{2,1,0:T(8,128)(2,1)S(1)}) custom-call(s32[1]{0:T(128)} %bitcast.el_ref.refs_0_, s32[1]{0:T(128)} %bitcast.1.az_ref.refs_1_, bf16[128,256]{1,0:T(8,128)(2,1)} %bitcast.46, s32[5,4,16]{2,1,0:T(4,128)} %bitcast.47), custom_call_target="tpu_custom_call" | custom-call | flops 20971520 | bytes 230664 | tf_op jit(solution)/shard_map/gather/pallas_call | solution.py:79
  1.1 1.6 %collective-permute-start = (bf16[5,16,256]{2,1,0:T(8,128)(2,1)S(1)}, bf16[5,16,256]{2,1,0:T(8,128)(2,1)S(1)}, u32[]{:S(2)}, u32[]{:S(2)}) collective-permute-start(bf16[5,16,256]{2,1,0:T(8,128)(2,1)S(1)} %get-tuple-element.34), channel_id=1, source_target_pairs={{0,3},{1,2},{2,1},{3,0},{4,7},{5,6},{6,5},{7,4},{8,11},{9,10},{10,... | collective-permute-start | bytes 122888 | tf_op jit(solution)/shard_map/ppermute | solution.py:39
  2.7 1.5 %collective-permute-start.1 = (bf16[5,16,256]{2,1,0:T(8,128)(2,1)S(1)}, bf16[5,16,256]{2,1,0:T(8,128)(2,1)S(1)}, u32[]{:S(2)}, u32[]{:S(2)}) collective-permute-start(bf16[5,16,256]{2,1,0:T(8,128)(2,1)S(1)} %get-tuple-element.35), channel_id=1, source_target_pairs={{0,1},{1,0},{2,3},{3,2},{4,5},{5,4},{6,7},{7,6},{8,9},{9,8},{10,11... | collective-permute-start | bytes 122888 | tf_op jit(solution)/shard_map/ppermute | solution.py:39
  4.2 0.5 %collective-permute-start.2 = (bf16[5,16,256]{2,1,0:T(8,128)(2,1)S(1)}, bf16[5,16,256]{2,1,0:T(8,128)(2,1)S(1)}, u32[]{:S(2)}, u32[]{:S(2)}) collective-permute-start(bf16[5,16,256]{2,1,0:T(8,128)(2,1)S(1)} %get-tuple-element.36), channel_id=1, source_target_pairs={{0,2},{1,3},{2,0},{3,1},{4,6},{5,7},{6,4},{7,5},{8,10},{9,11},{10,... | collective-permute-start | bytes 122888 | tf_op jit(solution)/shard_map/ppermute | solution.py:39
  4.7 2.4 %load.1 = (f32[320,512]{1,0:T(8,128)S(1)}, bf16[512,256]{1,0:T(8,128)(2,1)S(1)}, bf16[512,256]{1,0:T(8,128)(2,1)S(1)}, bf16[256,256]{1,0:T(8,128)(2,1)S(1)}, bf1...) custom-call(s32[1]{0:T(128)} %bitcast.el_ref.refs_0_, ...), custom_call_target="tpu_custom_call" | custom-call | flops 7864320 | bytes 8290312 | tf_op jit(solution)/shard_map/load/pallas_call | solution.py:79
  7.1 0.0 collective-permute-done
  7.1 0.0 collective-permute-done.1
  7.1 1.0 %collective-permute-done.2 = bf16[5,16,256]{2,1,0:T(8,128)(2,1)S(1)} collective-permute-done((bf16[5,16,256]{2,1,0:T(8,128)(2,1)S(1)}, bf16[5,16,256]{2,1,0:T(8,128)(2,1)S(1)}, u32[]{:S(2)}, u32[]{:S(2)}) %collective-permute-start.2) | collective-permute-done | bytes 40992 | tf_op jit(solution)/shard_map/ppermute | solution.py:39
  8.2 1.7 %collective-permute-start.3 = (bf16[64,256]{1,0:T(8,128)(2,1)S(1)}, bf16[64,256]{1,0:T(8,128)(2,1)S(1)}, u32[]{:S(2)}, u32[]{:S(2)}) collective-permute-start(bf16[64,256]{1,0:T(8,128)(2,1)S(1)} %pad_maximum_fusion.1), channel_id=1, source_target_pairs={{0,28},{4,8},{8,4},{12,16},{16,12},{20,24},{24,20},{28,0},{1,29},{... | collective-permute-start | bytes 98312 | tf_op jit(solution)/shard_map/ppermute | solution.py:39
  9.9 2.0 %collective-permute-start.4 = (bf16[64,256]{1,0:T(8,128)(2,1)S(1)}, bf16[64,256]{1,0:T(8,128)(2,1)S(1)}, u32[]{:S(2)}, u32[]{:S(2)}) collective-permute-start(bf16[64,256]{1,0:T(8,128)(2,1)S(1)} %pad_maximum_fusion.2), channel_id=1, source_target_pairs={{0,24},{4,28},{8,16},{12,20},{16,8},{20,12},{24,0},{28,4},{1,25},{... | collective-permute-start | bytes 98312 | tf_op jit(solution)/shard_map/ppermute | solution.py:39
  11.9 0.0 collective-permute-start.5
  12.0 0.6 %collective-permute-start.6 = (bf16[64,256]{1,0:T(8,128)(2,1)S(1)}, bf16[64,256]{1,0:T(8,128)(2,1)S(1)}, u32[]{:S(2)}, u32[]{:S(2)}) collective-permute-start(bf16[64,256]{1,0:T(8,128)(2,1)S(1)} %pad_maximum_fusion.4), channel_id=1, source_target_pairs={{0,4},{4,0},{8,12},{12,8},{16,20},{20,16},{24,28},{28,24},{1,5},{5... | collective-permute-start | bytes 98312 | tf_op jit(solution)/shard_map/ppermute | solution.py:39
  12.6 0.5 %query.1 = (bf16[256,512]{1,0:T(8,128)(2,1)S(1)}, f32[512,1024]{1,0:T(8,128)S(1)}) custom-call(bf16[512,256]{1,0:T(8,128)(2,1)S(1)} %get-tuple-element.39.points_ref.refs_9_, bf16[512,256]{1,0:T(8,128)(2,1)S(1)} %get-tuple-element.40.skip_ref, bf16[256,256]{1,0:T(8,128)(2,1)S(1)} %get-tuple-element.41.w_query_ref, ...), custom_call_target="tpu_custom_call" | custom-call | flops 335544320 | bytes 3571712 | tf_op jit(solution)/shard_map/query/pallas_call | solution.py:79
  13.1 0.4 %collective-permute-done.3.refs_1_ = bf16[64,256]{1,0:T(8,128)(2,1)S(1)} collective-permute-done((bf16[64,256]{1,0:T(8,128)(2,1)S(1)}, bf16[64,256]{1,0:T(8,128)(2,1)S(1)}, u32[]{:S(2)}, u32[]{:S(2)}) %collective-permute-start.3) | collective-permute-done | bytes 32800 | tf_op jit(solution)/shard_map/ppermute | solution.py:39
  13.5 2.2 %collective-permute-done.4.refs_2_ = bf16[64,256]{1,0:T(8,128)(2,1)S(1)} collective-permute-done((bf16[64,256]{1,0:T(8,128)(2,1)S(1)}, bf16[64,256]{1,0:T(8,128)(2,1)S(1)}, u32[]{:S(2)}, u32[]{:S(2)}) %collective-permute-start.4) | collective-permute-done | bytes 32800 | tf_op jit(solution)/shard_map/ppermute | solution.py:39
  15.7 0.3 %collective-permute-done.5.refs_3_ = bf16[64,256]{1,0:T(8,128)(2,1)S(1)} collective-permute-done((bf16[64,256]{1,0:T(8,128)(2,1)S(1)}, bf16[64,256]{1,0:T(8,128)(2,1)S(1)}, u32[]{:S(2)}, u32[]{:S(2)}) %collective-permute-start.5) | collective-permute-done | bytes 32800 | tf_op jit(solution)/shard_map/ppermute | solution.py:39
  16.0 0.0 collective-permute-done.6.refs_4_
  16.0 2.3 %ends.1 = (f32[2,128,256]{2,1,0:T(8,128)S(1)}, bf16[2,128,256]{2,1,0:T(8,128)(2,1)S(1)}, bf16[2,256]{1,0:T(2,128)(2,1)S(1)}, bf16[2,256]{1,0:T(2,128)(2,1)S(1)},...) custom-call(s32[1]{0:T(128)} %bitcast.1.az_ref.refs_1_, ...), custom_call_target="tpu_custom_call" | custom-call | flops 511705088 | bytes 5605380 | tf_op jit(solution)/shard_map/ends/pallas_call | solution.py:79
  18.3 0.1 collective-permute-start.7
  18.4 2.1 %collective-permute-start.8 = (bf16[2,256]{1,0:T(2,128)(2,1)S(1)}, bf16[2,256]{1,0:T(2,128)(2,1)S(1)}, u32[]{:S(2)}, u32[]{:S(2)}) collective-permute-start(bf16[2,256]{1,0:T(2,128)(2,1)S(1)} %get-tuple-element.50), channel_id=1, source_target_pairs={{0,28},{4,8},{8,4},{12,16},{16,12},{20,24},{24,20},{28,0},{1,29},{... | collective-permute-start | bytes 3080 | tf_op jit(solution)/shard_map/ppermute | solution.py:39
  20.5 2.1 %middle.1 = (f32[2,256,256]{2,1,0:T(8,128)S(1)}, bf16[272,256]{1,0:T(8,128)(2,1)S(1)}, bf16[272,256]{1,0:T(8,128)(2,1)S(1)}) custom-call(bf16[320,256]{1,0:T(8,128)(2,1)S(1)} %get-tuple-element.51.keys_ref, bf16[256,320]{1,0:T(8,128)(2,1)S(1)} %get-tuple-element.52.values_ref, f32[2,128,256]{2,1,0:T(8,128)S(1)} %get-tuple-element.53.joined_ends_ref, ...), custom_call_target="tpu_custom_call" | custom-call | flops 511705088 | bytes 5980160 | tf_op jit(solution)/shard_map/middle/pallas_call | solution.py:79
  22.6 0.0 collective-permute-done.7.inner_ref
  22.6 0.7 %collective-permute-done.8.outer_ref = bf16[2,256]{1,0:T(2,128)(2,1)S(1)} collective-permute-done((bf16[2,256]{1,0:T(2,128)(2,1)S(1)}, bf16[2,256]{1,0:T(2,128)(2,1)S(1)}, u32[]{:S(2)}, u32[]{:S(2)}) %collective-permute-start.8) | collective-permute-done | bytes 1056 | tf_op jit(solution)/shard_map/ppermute | solution.py:39
  23.2 0.5 %collective-permute-start.9 = (bf16[272,256]{1,0:T(8,128)(2,1)S(1)}, bf16[272,256]{1,0:T(8,128)(2,1)S(1)}, u32[]{:S(2)}, u32[]{:S(2)}) collective-permute-start(bf16[272,256]{1,0:T(8,128)(2,1)S(1)} %get-tuple-element.57.near_ref), channel_id=1, source_target_pairs={{0,1},{1,0},{2,3},{3,2},{4,5},{5,4},{6,7},{7,6},{8,9},{9,8},{10,11... | collective-permute-start | bytes 417800 | tf_op jit(solution)/shard_map/ppermute | solution.py:39
  23.8 1.7 %collective-permute-start.10 = (bf16[272,256]{1,0:T(8,128)(2,1)S(1)}, bf16[272,256]{1,0:T(8,128)(2,1)S(1)}, u32[]{:S(2)}, u32[]{:S(2)}) collective-permute-start(bf16[272,256]{1,0:T(8,128)(2,1)S(1)} %get-tuple-element.58.far_ref), channel_id=1, source_target_pairs={{0,4},{1,2},{2,1},{3,7},{4,0},{5,6},{6,5},{7,3},{8,12},{9,10},{10,... | collective-permute-start | bytes 417800 | tf_op jit(solution)/shard_map/ppermute | solution.py:52
  25.5 0.6 %inside.1.part_ref = f32[2,256,256]{2,1,0:T(8,128)S(1)} custom-call(s32[1]{0:T(128)} %bitcast.el_ref.refs_0_, bf16[272,256]{1,0:T(8,128)(2,1)S(1)} %get-tuple-element.57.near_ref, bf16[272,256]{1,0:T(8,128)(2,1)S(1)} %get-tuple-element.58.far_ref, f32[2,256,256]{2,1,0:T(8,128)S(1)} %get-tuple-element.59.joined_ref, ...), custom_call_target="tpu_custom_call" | custom-call | flops 402653184 | bytes 2506756 | tf_op jit(solution)/shard_map/inside/pallas_call | solution.py:79
  26.1 2.2 %collective-permute-done.9.near_ref = bf16[272,256]{1,0:T(8,128)(2,1)S(1)} collective-permute-done((bf16[272,256]{1,0:T(8,128)(2,1)S(1)}, bf16[272,256]{1,0:T(8,128)(2,1)S(1)}, u32[]{:S(2)}, u32[]{:S(2)}) %collective-permute-start.9) | collective-permute-done | bytes 139296 | tf_op jit(solution)/shard_map/ppermute | solution.py:39
  28.4 0.3 near_border.1.near_ref
  28.6 2.0 %collective-permute-done.10.far_ref = bf16[272,256]{1,0:T(8,128)(2,1)S(1)} collective-permute-done((bf16[272,256]{1,0:T(8,128)(2,1)S(1)}, bf16[272,256]{1,0:T(8,128)(2,1)S(1)}, u32[]{:S(2)}, u32[]{:S(2)}) %collective-permute-start.10) | collective-permute-done | bytes 139296 | tf_op jit(solution)/shard_map/ppermute | solution.py:52
  30.7 1.0 %far_border.1 = bf16[2,256,256]{2,1,0:T(8,128)(2,1)} custom-call(s32[1]{0:T(128)} %bitcast.el_ref.refs_0_, bf16[256,256]{1,0:T(8,128)(2,1)S(1)} %near_border.1.near_ref, bf16[272,256]{1,0:T(8,128)(2,1)S(1)} %collective-permute-done.10.far_ref, f32[2,256,256]{2,1,0:T(8,128)S(1)} %inside.1.part_ref, bf16[9,256,256]{2,1,0:T(8,128)(2,1)S(1)} %get-tuple-element.60.w_ref), custom_call_target="tpu_custom_call" | custom-call | flops 100663296 | bytes 2236420 | tf_op jit(solution)/shard_map/far_border/pallas_call | solution.py:79
  (10 shorter events, 0.0 us)
Async XLA Ops:
  1.1 6.0 %collective-permute-start = (bf16[5,16,256]{2,1,0:T(8,128)(2,1)S(1)}, bf16[5,16,256]{2,1,0:T(8,128)(2,1)S(1)}, u32[]{:S(2)}, u32[]{:S(2)}) collective-permute-start(bf16[5,16,256]{2,1,0:T(8,128)(2,1)S(1)} %get-tuple-element.34), channel_id=1, source_target_pairs={{0,3},{1,2},{2,1},{3,0},{4,7},{5,6},{6,5},{7,4},{8,11},{9,10},{10,... | collective-permute-start | bytes 122888 | tf_op jit(solution)/shard_map/ppermute | solution.py:39
  2.7 4.4 %collective-permute-start.1 = (bf16[5,16,256]{2,1,0:T(8,128)(2,1)S(1)}, bf16[5,16,256]{2,1,0:T(8,128)(2,1)S(1)}, u32[]{:S(2)}, u32[]{:S(2)}) collective-permute-start(bf16[5,16,256]{2,1,0:T(8,128)(2,1)S(1)} %get-tuple-element.35), channel_id=1, source_target_pairs={{0,1},{1,0},{2,3},{3,2},{4,5},{5,4},{6,7},{7,6},{8,9},{9,8},{10,11... | collective-permute-start | bytes 122888 | tf_op jit(solution)/shard_map/ppermute | solution.py:39
  4.2 4.0 %collective-permute-start.2 = (bf16[5,16,256]{2,1,0:T(8,128)(2,1)S(1)}, bf16[5,16,256]{2,1,0:T(8,128)(2,1)S(1)}, u32[]{:S(2)}, u32[]{:S(2)}) collective-permute-start(bf16[5,16,256]{2,1,0:T(8,128)(2,1)S(1)} %get-tuple-element.36), channel_id=1, source_target_pairs={{0,2},{1,3},{2,0},{3,1},{4,6},{5,7},{6,4},{7,5},{8,10},{9,11},{10,... | collective-permute-start | bytes 122888 | tf_op jit(solution)/shard_map/ppermute | solution.py:39
  8.2 5.3 %collective-permute-start.3 = (bf16[64,256]{1,0:T(8,128)(2,1)S(1)}, bf16[64,256]{1,0:T(8,128)(2,1)S(1)}, u32[]{:S(2)}, u32[]{:S(2)}) collective-permute-start(bf16[64,256]{1,0:T(8,128)(2,1)S(1)} %pad_maximum_fusion.1), channel_id=1, source_target_pairs={{0,28},{4,8},{8,4},{12,16},{16,12},{20,24},{24,20},{28,0},{1,29},{... | collective-permute-start | bytes 98312 | tf_op jit(solution)/shard_map/ppermute | solution.py:39
  9.9 5.7 %collective-permute-start.4 = (bf16[64,256]{1,0:T(8,128)(2,1)S(1)}, bf16[64,256]{1,0:T(8,128)(2,1)S(1)}, u32[]{:S(2)}, u32[]{:S(2)}) collective-permute-start(bf16[64,256]{1,0:T(8,128)(2,1)S(1)} %pad_maximum_fusion.2), channel_id=1, source_target_pairs={{0,24},{4,28},{8,16},{12,20},{16,8},{20,12},{24,0},{28,4},{1,25},{... | collective-permute-start | bytes 98312 | tf_op jit(solution)/shard_map/ppermute | solution.py:39
  11.9 4.0 %collective-permute-start.5 = (bf16[64,256]{1,0:T(8,128)(2,1)S(1)}, bf16[64,256]{1,0:T(8,128)(2,1)S(1)}, u32[]{:S(2)}, u32[]{:S(2)}) collective-permute-start(bf16[64,256]{1,0:T(8,128)(2,1)S(1)} %pad_maximum_fusion.3), channel_id=1, source_target_pairs={{0,8},{4,12},{8,0},{12,4},{16,24},{20,28},{24,16},{28,20},{1,9},{5... | collective-permute-start | bytes 98312 | tf_op jit(solution)/shard_map/ppermute | solution.py:39
  12.0 4.0 %collective-permute-start.6 = (bf16[64,256]{1,0:T(8,128)(2,1)S(1)}, bf16[64,256]{1,0:T(8,128)(2,1)S(1)}, u32[]{:S(2)}, u32[]{:S(2)}) collective-permute-start(bf16[64,256]{1,0:T(8,128)(2,1)S(1)} %pad_maximum_fusion.4), channel_id=1, source_target_pairs={{0,4},{4,0},{8,12},{12,8},{16,20},{20,16},{24,28},{28,24},{1,5},{5... | collective-permute-start | bytes 98312 | tf_op jit(solution)/shard_map/ppermute | solution.py:39
  18.3 4.3 %collective-permute-start.7 = (bf16[2,256]{1,0:T(2,128)(2,1)S(1)}, bf16[2,256]{1,0:T(2,128)(2,1)S(1)}, u32[]{:S(2)}, u32[]{:S(2)}) collective-permute-start(bf16[2,256]{1,0:T(2,128)(2,1)S(1)} %get-tuple-element.49), channel_id=1, source_target_pairs={{0,4},{4,0},{8,12},{12,8},{16,20},{20,16},{24,28},{28,24},{1,5},{5... | collective-permute-start | bytes 3080 | tf_op jit(solution)/shard_map/ppermute | solution.py:39
  18.4 4.9 %collective-permute-start.8 = (bf16[2,256]{1,0:T(2,128)(2,1)S(1)}, bf16[2,256]{1,0:T(2,128)(2,1)S(1)}, u32[]{:S(2)}, u32[]{:S(2)}) collective-permute-start(bf16[2,256]{1,0:T(2,128)(2,1)S(1)} %get-tuple-element.50), channel_id=1, source_target_pairs={{0,28},{4,8},{8,4},{12,16},{16,12},{20,24},{24,20},{28,0},{1,29},{... | collective-permute-start | bytes 3080 | tf_op jit(solution)/shard_map/ppermute | solution.py:39
  23.2 5.1 %collective-permute-start.9 = (bf16[272,256]{1,0:T(8,128)(2,1)S(1)}, bf16[272,256]{1,0:T(8,128)(2,1)S(1)}, u32[]{:S(2)}, u32[]{:S(2)}) collective-permute-start(bf16[272,256]{1,0:T(8,128)(2,1)S(1)} %get-tuple-element.57.near_ref), channel_id=1, source_target_pairs={{0,1},{1,0},{2,3},{3,2},{4,5},{5,4},{6,7},{7,6},{8,9},{9,8},{10,11... | collective-permute-start | bytes 417800 | tf_op jit(solution)/shard_map/ppermute | solution.py:39
  23.8 6.9 %collective-permute-start.10 = (bf16[272,256]{1,0:T(8,128)(2,1)S(1)}, bf16[272,256]{1,0:T(8,128)(2,1)S(1)}, u32[]{:S(2)}, u32[]{:S(2)}) collective-permute-start(bf16[272,256]{1,0:T(8,128)(2,1)S(1)} %get-tuple-element.58.far_ref), channel_id=1, source_target_pairs={{0,4},{1,2},{2,1},{3,7},{4,0},{5,6},{6,5},{7,3},{8,12},{9,10},{10,... | collective-permute-start | bytes 417800 | tf_op jit(solution)/shard_map/ppermute | solution.py:52
